TPU v7x, 32 devices: a whole 2x2x4 slice. The times are simulated.
32 devices in a mesh: tok: 16 (over z, y, x), mlp: 2 (over core).
Axes of the slice: x: 2, y: 2, z: 4, core: 2. Of those that a mesh axis runs over, the one named last changes fastest.
Arguments:
- block_input: bfloat16 [16384, 1152], P(('tok', 'mlp')), may hold values from -44 to 44, as said below
- out_grad: bfloat16 [16384, 1152], P(('tok', 'mlp')), may hold values from -11 to 11, as said below
- class_table: bfloat16 [1000, 1152], replicated, may hold values from -6 to 6
- time_table: bfloat16 [1000, 1152], replicated, may hold values from -6 to 6
- class_label: int32 [128], P(('tok', 'mlp')), may hold values from 0 to 999
- time_index: int32 [128], P(('tok', 'mlp')), may hold values from 0 to 999
- grid_height: int32 [128], P(('tok', 'mlp')), may hold values from 0 to 16, as said below
- grid_width: int32 [128], P(('tok', 'mlp')), may hold values from 0 to 20, as said below
- mix_weight: float32 [1152, 3456], P('tok', 'mlp'), may hold values from -0.1875 to 0.1875
- proj_weight: float32 [1152, 1152], P('tok', 'mlp'), may hold values from -0.1875 to 0.1875
- cond_weight: float32 [1152, 6912], P('tok', 'mlp'), may hold values from -0.1875 to 0.1875
- cond_bias: float32 [6912], P(('tok', 'mlp')), may hold values from -0.5 to 0.5
- feed_weight: float32 [2, 1152, 3072], P(None, 'tok', 'mlp')
- down_weight: float32 [3072, 1152], P('mlp', 'tok'), may hold values from -0.109375 to 0.109375
- mix_mean: float32 [1152, 3456], P('tok', 'mlp'), may hold values from -0.00010681152 to 0.00010681152
- proj_mean: float32 [1152, 1152], P('tok', 'mlp'), may hold values from -0.00010681152 to 0.00010681152
- cond_mean: float32 [1152, 6912], P('tok', 'mlp'), may hold values from -0.00010681152 to 0.00010681152
- bias_mean: float32 [6912], P(('tok', 'mlp')), may hold values from -0.00010681152 to 0.00010681152
- feed_mean: float32 [2, 1152, 3072], P(None, 'tok', 'mlp'), may hold values from -0.00010681152 to 0.00010681152
- down_mean: float32 [3072, 1152], P('mlp', 'tok'), may hold values from -0.00010681152 to 0.00010681152
- mix_square: float32 [1152, 3456], P('tok', 'mlp'), may hold values from 1.2555041e-09 to 5.0220166e-09
- proj_square: float32 [1152, 1152], P('tok', 'mlp'), may hold values from 1.2555041e-09 to 5.0220166e-09
- cond_square: float32 [1152, 6912], P('tok', 'mlp'), may hold values from 1.2555041e-09 to 5.0220166e-09
- bias_square: float32 [6912], P(('tok', 'mlp')), may hold values from 1.2555041e-09 to 5.0220166e-09
- feed_square: float32 [2, 1152, 3072], P(None, 'tok', 'mlp'), may hold values from 1.2555041e-09 to 5.0220166e-09
- down_square: float32 [3072, 1152], P('mlp', 'tok'), may hold values from 1.2555041e-09 to 5.0220166e-09
Outputs:
- block_output: bfloat16 [16384, 1152], P(('tok', 'mlp'))
- input_grad: float32 [16384, 1152], P(('tok', 'mlp'))
- grad_norm: float32 [], replicated
- mix_mean_new: float32 [1152, 3456], P('tok', 'mlp')
- proj_mean_new: float32 [1152, 1152], P('tok', 'mlp')
- cond_mean_new: float32 [1152, 6912], P('tok', 'mlp')
- bias_mean_new: float32 [6912], P(('tok', 'mlp'))
- feed_mean_new: float32 [2, 1152, 3072], P(None, 'tok', 'mlp')
- down_mean_new: float32 [3072, 1152], P('mlp', 'tok')
- mix_square_new: float32 [1152, 3456], P('tok', 'mlp')
- proj_square_new: float32 [1152, 1152], P('tok', 'mlp')
- cond_square_new: float32 [1152, 6912], P('tok', 'mlp')
- bias_square_new: float32 [6912], P(('tok', 'mlp'))
- feed_square_new: float32 [2, 1152, 3072], P(None, 'tok', 'mlp')
- down_square_new: float32 [3072, 1152], P('mlp', 'tok')
- mix_weight_new: float32 [1152, 3456], P('tok', 'mlp')
- proj_weight_new: float32 [1152, 1152], P('tok', 'mlp')
- cond_weight_new: float32 [1152, 6912], P('tok', 'mlp')
- cond_bias_new: float32 [6912], P(('tok', 'mlp'))
- feed_weight_new: float32 [2, 1152, 3072], P(None, 'tok', 'mlp')
- down_weight_new: float32 [3072, 1152], P('mlp', 'tok')
Inputs may be any that keep to these rules, and one draw needn't show every extreme that they name: block_input is finite. out_grad is finite. `grid_height`: the 4 slots of pack n describe its images in order; unused slots have height and width 0 and come after the used ones. An image is 8 x 16, 16 x 16 or 16 x 5*16//4 patches (height x width), and the images of one pack hold at most 512 tokens. `grid_width`: see grid_height.
All inputs are finite; a program needn't handle non-finite values.
Results may differ from a plain program's by a relative error of at most 0.028.
Values may be sent and summed in bfloat16 or wider, within the bound.
No kernel may reach another device: no remote copies, remote signals or barrier semaphores. Data moves between devices by JAX's collectives and lax.ppermute only.
A program may use at most 320 MiB of HBM per device.

v0:
```python
import jax
import jax.numpy as jnp
from jax import lax
from jax.sharding import PartitionSpec as P

HEADS = 16
HEAD = 72
SLOTS = 4
STEP = 10


BETA_ONE = 0.9
BETA_TWO = 0.95
ADAM_EPS = 1e-08
RATE = 0.08
DECAY = 0.01
CLIP_NORM = 1.0
NORM_EPS = 1e-06
MASKED = -1e30
HIGH = lax.Precision.HIGHEST


def layer_norm(value):
    centered = value - jnp.mean(value, axis=-1, keepdims=True)
    spread = jnp.mean(centered * centered, axis=-1, keepdims=True)
    return centered * lax.rsqrt(spread + NORM_EPS)


def modulate(value, shift, scale):
    return layer_norm(value) * (1.0 + scale) + shift


def geometry(height, width, count):
    lengths = height * width
    ends = jnp.cumsum(lengths)
    starts = ends - lengths
    places = jnp.arange(count, dtype=jnp.int32)
    segment = jnp.sum((places[:, None] >= ends[None, :]).astype(jnp.int32), axis=1)
    member = segment[:, None] == jnp.arange(height.shape[0], dtype=jnp.int32)[None, :]
    start_tok = jnp.sum(jnp.where(member, starts[None, :], 0), axis=1)
    width_tok = jnp.maximum(jnp.sum(jnp.where(member, width[None, :], 0), axis=1), 1)
    offset = places - start_tok
    return (segment, member.astype(jnp.float32), offset // width_tok, offset % width_tok)


def rope(value, rows, cols):
    quarter = value.shape[-1] // 4
    freq = 10000.0 ** (-jnp.arange(quarter, dtype=jnp.float32) / quarter)
    angle = jnp.concatenate(
        [
            rows.astype(jnp.float32)[:, None] * freq[None, :],
            cols.astype(jnp.float32)[:, None] * freq[None, :],
        ],
        axis=1,
    )[:, None, :]
    cosine = jnp.cos(angle)
    sine = jnp.sin(angle)
    first = jnp.concatenate([value[..., :quarter], value[..., 2 * quarter : 3 * quarter]], axis=-1)
    second = jnp.concatenate(
        [value[..., quarter : 2 * quarter], value[..., 3 * quarter :]], axis=-1
    )
    new_first = first * cosine - second * sine
    new_second = second * cosine + first * sine
    return jnp.concatenate(
        [
            new_first[..., :quarter],
            new_second[..., :quarter],
            new_first[..., quarter:],
            new_second[..., quarter:],
        ],
        axis=-1,
    )


def across(left, right, precision=None):
    return lax.dot_general(
        left,
        right,
        (((0,), (0,)), ((), ())),
        preferred_element_type=jnp.float32,
        precision=precision,
    )


def against(left, right):
    return lax.dot_general(
        left, right, (((1,), (1,)), ((), ())), preferred_element_type=jnp.float32
    )


def adam(weight, mean, square, grad):
    mean_new = BETA_ONE * mean + (1.0 - BETA_ONE) * grad
    square_new = BETA_TWO * square + (1.0 - BETA_TWO) * grad * grad
    fixed_mean = mean_new / (1.0 - BETA_ONE**STEP)
    fixed_square = square_new / (1.0 - BETA_TWO**STEP)
    weight_new = weight - RATE * (fixed_mean / (jnp.sqrt(fixed_square) + ADAM_EPS) + DECAY * weight)
    return (mean_new, square_new, weight_new)


def body(
    block_input,
    out_grad,
    class_table,
    time_table,
    class_label,
    time_index,
    grid_height,
    grid_width,
    mix_weight,
    proj_weight,
    cond_weight,
    cond_bias,
    feed_weight,
    down_weight,
    mix_mean,
    proj_mean,
    cond_mean,
    bias_mean,
    feed_mean,
    down_mean,
    mix_square,
    proj_square,
    cond_square,
    bias_square,
    feed_square,
    down_square,
):
    half = jnp.bfloat16
    count = block_input.shape[0]
    width = block_input.shape[1]
    pair = (
        lax.all_gather(mix_weight.astype(half), "mlp", axis=1, tiled=True),
        lax.all_gather(proj_weight.astype(half), "mlp", axis=1, tiled=True),
        lax.all_gather(cond_weight.astype(half), "mlp", axis=1, tiled=True),
        lax.all_gather(cond_bias.astype(half), "mlp", axis=0, tiled=True),
    )
    full = (
        lax.all_gather(pair[0], "tok", axis=0, tiled=True),
        lax.all_gather(pair[1], "tok", axis=0, tiled=True),
        lax.all_gather(pair[2], "tok", axis=0, tiled=True),
        lax.all_gather(pair[3], "tok", axis=0, tiled=True),
        lax.all_gather(feed_weight.astype(half), "tok", axis=1, tiled=True),
        lax.all_gather(down_weight.astype(half), "tok", axis=1, tiled=True),
    )
    mix_full, proj_full, cond_full, bias_full, feed_full, down_full = full
    segment, member, rows, cols = geometry(grid_height, grid_width, count)
    valid = (segment < SLOTS).astype(jnp.float32)[:, None]
    embed = class_table[class_label].astype(jnp.float32) + time_table[time_index].astype(
        jnp.float32
    )
    cond_low = jax.nn.silu(embed).astype(half)
    modulation = jnp.dot(
        cond_low, cond_full, preferred_element_type=jnp.float32
    ) + bias_full.astype(jnp.float32)
    per_token = jnp.dot(member, modulation, precision=HIGH)
    shift_a, scale_a, gate_a, shift_b, scale_b, gate_b = jnp.split(per_token, 6, axis=1)
    inputs = block_input.astype(jnp.float32)
    first_in = modulate(inputs, shift_a, scale_a).astype(half)
    mixed = jnp.dot(first_in, mix_full, preferred_element_type=jnp.float32)
    query_raw, key_raw, value_raw = jnp.split(mixed, 3, axis=1)
    shape = (count, HEADS, HEAD)
    query_raw = query_raw.reshape(shape)
    key_raw = key_raw.reshape(shape)
    query = rope(query_raw, rows, cols).astype(half)
    key = rope(key_raw, rows, cols).astype(half)
    value = value_raw.reshape(shape).astype(half)
    scale = HEAD ** (-0.5)
    same = segment[:, None] == segment[None, :]

    def scores_of():
        raw = jnp.einsum("qhd,khd->hqk", query, key, preferred_element_type=jnp.float32) * scale
        return jnp.where(same[None], raw, MASKED)

    scores = scores_of()
    top = jnp.max(scores, axis=-1, keepdims=True)
    weights = jnp.exp(scores - top)
    totals = jnp.sum(weights, axis=-1, keepdims=True)
    probs_low = (weights / totals).astype(half)
    log_total = top + jnp.log(totals)
    attended = (
        jnp.einsum("hqk,khd->qhd", probs_low, value, preferred_element_type=jnp.float32)
        .reshape(count, width)
        .astype(half)
    )
    branch = jnp.dot(attended, proj_full, preferred_element_type=jnp.float32)
    middle = inputs + gate_a * branch
    second_in = modulate(middle, shift_b, scale_b).astype(half)
    second_pair = lax.all_gather(second_in, "mlp", axis=0, tiled=True)
    gate_pre = jnp.dot(second_pair, feed_full[0], preferred_element_type=jnp.float32)
    up_pre = jnp.dot(second_pair, feed_full[1], preferred_element_type=jnp.float32)
    hidden = (jax.nn.silu(gate_pre) * up_pre).astype(half)
    partial_value = jnp.dot(hidden, down_full, preferred_element_type=jnp.float32)
    result = lax.psum_scatter(
        partial_value.astype(jnp.bfloat16), "mlp", scatter_dimension=0, tiled=True
    ).astype(jnp.float32)
    block_output = (valid * (middle + gate_b * result)).astype(half)
    again = (
        lax.all_gather(mix_weight.astype(half), "mlp", axis=1, tiled=True),
        lax.all_gather(proj_weight.astype(half), "mlp", axis=1, tiled=True),
    )
    later = (
        lax.all_gather(again[0], "tok", axis=0, tiled=True),
        lax.all_gather(again[1], "tok", axis=0, tiled=True),
        lax.all_gather(feed_weight.astype(half), "tok", axis=1, tiled=True),
        lax.all_gather(down_weight.astype(half), "tok", axis=1, tiled=True),
    )
    mix_back, proj_back, feed_back, down_back = later
    grad_out = valid * out_grad.astype(jnp.float32)
    d_gate_b = grad_out * result
    result_grad = (gate_b * grad_out).astype(half)
    result_pair = lax.all_gather(result_grad, "mlp", axis=0, tiled=True)
    d_down = across(hidden, result_pair)
    d_hidden = against(result_pair, down_back)
    sig = jax.nn.sigmoid(gate_pre)
    gate_grad = (d_hidden * up_pre * sig * (1.0 + gate_pre * (1.0 - sig))).astype(half)
    up_grad = (d_hidden * gate_pre * sig).astype(half)
    d_feed = jnp.stack([across(second_pair, gate_grad), across(second_pair, up_grad)])
    second_part = against(gate_grad, feed_back[0]) + against(up_grad, feed_back[1])
    second_grad = lax.psum_scatter(
        second_part.astype(jnp.bfloat16), "mlp", scatter_dimension=0, tiled=True
    ).astype(jnp.float32)
    pull_second = jax.vjp(modulate, middle, shift_b, scale_b)[1]
    d_middle, d_shift_b, d_scale_b = pull_second(second_grad)
    d_middle = d_middle + grad_out
    d_gate_a = d_middle * branch
    branch_grad = (gate_a * d_middle).astype(half)
    d_proj = across(attended, branch_grad)
    attended_grad = against(branch_grad, proj_back).astype(half).reshape(shape)
    probs_again = jnp.exp(scores_of() - log_total)
    d_value = jnp.einsum(
        "hqk,qhd->khd", probs_again.astype(half), attended_grad, preferred_element_type=jnp.float32
    )
    d_probs = jnp.einsum("qhd,khd->hqk", attended_grad, value, preferred_element_type=jnp.float32)
    d_scores = (
        probs_again * (d_probs - jnp.sum(probs_again * d_probs, axis=-1, keepdims=True)) * scale
    ).astype(half)
    d_query = jnp.einsum("hqk,khd->qhd", d_scores, key, preferred_element_type=jnp.float32)
    d_key = jnp.einsum("hqk,qhd->khd", d_scores, query, preferred_element_type=jnp.float32)
    unturn = jax.vjp(
        lambda left, right: (rope(left, rows, cols), rope(right, rows, cols)), query_raw, key_raw
    )[1]
    d_query_raw, d_key_raw = unturn((d_query, d_key))
    mixed_grad = jnp.concatenate(
        [
            d_query_raw.reshape(count, width),
            d_key_raw.reshape(count, width),
            d_value.reshape(count, width),
        ],
        axis=1,
    ).astype(half)
    d_mix = across(first_in, mixed_grad)
    first_grad = against(mixed_grad, mix_back)
    pull_first = jax.vjp(modulate, inputs, shift_a, scale_a)[1]
    d_inputs, d_shift_a, d_scale_a = pull_first(first_grad)
    input_grad = d_inputs + d_middle
    d_per_token = jnp.concatenate(
        [d_shift_a, d_scale_a, d_gate_a, d_shift_b, d_scale_b, d_gate_b], axis=1
    )
    d_modulation = across(member, d_per_token, HIGH)
    d_bias = jnp.sum(d_modulation, axis=0)
    modulation_low = d_modulation.astype(half)
    rows_part = (
        lax.psum_scatter(d_mix, "tok", scatter_dimension=0, tiled=True),
        lax.psum_scatter(d_proj, "tok", scatter_dimension=0, tiled=True),
        lax.psum_scatter(d_bias, "tok", scatter_dimension=0, tiled=True),
        lax.psum_scatter(d_feed, "tok", scatter_dimension=1, tiled=True),
        lax.psum_scatter(d_down, "tok", scatter_dimension=1, tiled=True),
    )
    cond_rows = lax.psum_scatter(
        across(cond_low, modulation_low), "tok", scatter_dimension=0, tiled=True
    )
    cols_part = (
        lax.psum_scatter(
            rows_part[0].astype(jnp.bfloat16), "mlp", scatter_dimension=1, tiled=True
        ).astype(jnp.float32),
        lax.psum_scatter(
            rows_part[1].astype(jnp.bfloat16), "mlp", scatter_dimension=1, tiled=True
        ).astype(jnp.float32),
        lax.psum_scatter(
            cond_rows.astype(jnp.bfloat16), "mlp", scatter_dimension=1, tiled=True
        ).astype(jnp.float32),
        lax.psum_scatter(
            rows_part[2].astype(jnp.bfloat16), "mlp", scatter_dimension=0, tiled=True
        ).astype(jnp.float32),
    )
    mix_grad, proj_grad, cond_grad, bias_grad = cols_part
    grads = (mix_grad, proj_grad, cond_grad, bias_grad, rows_part[3], rows_part[4])
    local_squares = jnp.float32(0.0)
    for grad in grads:
        local_squares = local_squares + jnp.sum(grad * grad)
    total = lax.psum(local_squares, ("tok", "mlp"))
    grad_norm = jnp.sqrt(total)
    factor = CLIP_NORM / jnp.maximum(grad_norm, CLIP_NORM)
    params = (mix_weight, proj_weight, cond_weight, cond_bias, feed_weight, down_weight)
    means = (mix_mean, proj_mean, cond_mean, bias_mean, feed_mean, down_mean)
    squares_old = (mix_square, proj_square, cond_square, bias_square, feed_square, down_square)
    updates = [adam(w, m, v, g * factor) for w, m, v, g in zip(params, means, squares_old, grads)]
    return (
        block_output,
        input_grad,
        grad_norm,
        updates[0][0],
        updates[1][0],
        updates[2][0],
        updates[3][0],
        updates[4][0],
        updates[5][0],
        updates[0][1],
        updates[1][1],
        updates[2][1],
        updates[3][1],
        updates[4][1],
        updates[5][1],
        updates[0][2],
        updates[1][2],
        updates[2][2],
        updates[3][2],
        updates[4][2],
        updates[5][2],
    )


def solution(mesh):
    placed = (
        P(("tok", "mlp"), None),
        P(("tok", "mlp"), None),
        P(),
        P(),
        P(("tok", "mlp")),
        P(("tok", "mlp")),
        P(("tok", "mlp")),
        P(("tok", "mlp")),
        P("tok", "mlp"),
        P("tok", "mlp"),
        P("tok", "mlp"),
        P(("tok", "mlp")),
        P(None, "tok", "mlp"),
        P("mlp", "tok"),
        P("tok", "mlp"),
        P("tok", "mlp"),
        P("tok", "mlp"),
        P(("tok", "mlp")),
        P(None, "tok", "mlp"),
        P("mlp", "tok"),
        P("tok", "mlp"),
        P("tok", "mlp"),
        P("tok", "mlp"),
        P(("tok", "mlp")),
        P(None, "tok", "mlp"),
        P("mlp", "tok"),
    )
    return jax.shard_map(
        body,
        mesh=mesh,
        in_specs=placed,
        out_specs=(
            P(("tok", "mlp"), None),
            P(("tok", "mlp"), None),
            P(),
            P("tok", "mlp"),
            P("tok", "mlp"),
            P("tok", "mlp"),
            P(("tok", "mlp")),
            P(None, "tok", "mlp"),
            P("mlp", "tok"),
            P("tok", "mlp"),
            P("tok", "mlp"),
            P("tok", "mlp"),
            P(("tok", "mlp")),
            P(None, "tok", "mlp"),
            P("mlp", "tok"),
            P("tok", "mlp"),
            P("tok", "mlp"),
            P("tok", "mlp"),
            P(("tok", "mlp")),
            P(None, "tok", "mlp"),
            P("mlp", "tok"),
        ),
        check_vma=False,
    )
```

profile of v0, /device:TPU:0, one launch (start us, length us, event | category | flops | bytes accessed | tf_op | source)
XLA Modules:
  0.0 2010.7 jit_solution(13261385472149890279)
XLA Ops:
  8.7 2.7 all_gather.42
  15.0 2.3 reshape.311
  29.7 2.5 all-reduce.14
  32.4 80.8 %all-reduce.15 = bf16[6912]{0:T(1024)(128)(2,1)S(1)} all-reduce(bf16[6912]{0:T(1024)(128)(2,1)S(1)} %dynamic-update-slice.1), channel_id=1, replica_groups=mesh['tok'=16,'mlp'=2] {'tok'}, use_global_device_ids=true, to_apply=%add.15 | all-reduce | flops 6912 | bytes 27648
  113.9 2.5 gather_fusion
  117.8 81.7 %all-gather.10.cloned.1.call-done = bf16[1152,6912]{1,0:T(8,128)(2,1)} async-done(((bf16[72,6912]{1,0:T(8,128)(2,1)}), bf16[1152,6912]{1,0:T(8,128)(2,1)}) %all-gather.10.cloned.1.call-update) | async-done | bytes 15925264 | tf_op jit(solution)/shard_map/all_gather | solution.py:140
  199.5 7.7 convolution_add_fusion
  207.2 5.7 fusion.72
  213.0 5.0 copy-done.2
  218.6 91.4 %all-gather.12.cloned.1.call-done = bf16[1152,3456]{1,0:T(8,128)(2,1)} async-done(((bf16[72,3456]{1,0:T(8,128)(2,1)}), bf16[1152,3456]{1,0:T(8,128)(2,1)}) %all-gather.12.cloned.1.call-update) | async-done | bytes 7962640 | tf_op jit(solution)/shard_map/all_gather | solution.py:138
  310.0 7.6 fusion.125
  318.8 2.5 fusion.108
  321.2 3.1 copy.85
  325.9 3.5 copy.86
  329.4 2.7 fusion.111
  335.6 8.0 fusion.123
  343.7 8.2 fusion.4
  351.9 9.4 fusion.44
  361.2 14.5 all-gather.14.cloned.1.call-done
  375.8 6.3 fusion.107
  384.2 4.9 multiply_convert_fusion.5
  390.7 88.6 %all-gather.18.cloned.1.call-done = bf16[2,1152,1536]{2,1,0:T(8,128)(2,1)} async-done(((bf16[2,72,1536]{2,1,0:T(8,128)(2,1)}), bf16[2,1152,1536]{2,1,0:T(8,128)(2,1)}) %all-gather.18.cloned.1.call-update) | async-done | bytes 7077904 | tf_op jit(solution)/shard_map/all_gather | solution.py:142
  479.2 10.5 all-gather.16.cloned.1.call-done
  489.8 9.7 fusion.23
  499.5 6.3 fusion.22
  505.8 59.6 %all-gather.20.cloned.1.call-done = bf16[1536,1152]{0,1:T(8,128)(2,1)} async-done(((bf16[1536,72]{0,1:T(8,128)(2,1)}), bf16[1536,1152]{0,1:T(8,128)(2,1)}) %all-gather.20.cloned.1.call-update) | async-done | bytes 3538960 | tf_op jit(solution)/shard_map/all_gather | solution.py:143
  565.4 11.7 all-gather.22.cloned.1.call-done
  577.1 12.3 multiply_convert_fusion.1
  589.4 8.5 fusion.21
  597.9 7.5 add_convert_fusion
  605.5 8.7 convolution_convert_fusion
  614.3 2.4 reduce-scatter.23.cloned.1.call-done
  616.7 3.3 multiply_reduce_fusion.1
  620.0 10.1 reduce-scatter.21.cloned.1.call-done
  630.1 5.2 fusion.106
  635.3 3.1 multiply_convert_fusion.4
  639.5 4.0 fusion.127
  644.8 4.6 convolution_convert_fusion.1
  651.0 9.4 fusion.126
  660.4 25.9 %fusion.38 = f32[512,16,72]{0,2,1:T(8,128)} fusion(f32[16,512,512]{1,2,0:T(8,128)} %fusion.126, f32[16,512,512]{1,2,0:T(8,128)} %get-tuple-element.113, f32[16,512]{1,0:T(8,128)S(1)} %log_add_fusion, bf16[512,16,18]{0,2,1:T(8,128)(2,1)} %copy-done.51, bf16[512,16,18]{0,2,1:T(8,128)(2,1)} %copy-done.53, bf16[512,16,18]{0,2,1:T(8,128)(2,1)} %copy-done.50, ...), kind=kOutput, calls=%fused_computation.77 | convolution fusion | flops 638067200 | bytes 37126144 | tf_op jit(solution)/shard_map/hqk,khd->qhd/dot_general | solution.py:237
  686.4 25.6 %fusion.41 = f32[512,16,72]{0,2,1:T(8,128)} fusion(f32[16,512,512]{1,2,0:T(8,128)} %fusion.126, f32[16,512,512]{1,2,0:T(8,128)} %get-tuple-element.113, f32[16,512]{1,0:T(8,128)S(1)} %log_add_fusion, bf16[512,16,18]{0,2,1:T(8,128)(2,1)} %copy-done.49, bf16[512,16,18]{0,2,1:T(8,128)(2,1)S(1)} %copy-done.47, bf16[512,16,18]{0,2,1:T(8,128)(2,1)} %copy-done.48, ...), kind=kOutput, calls=%fused_computation.78 | convolution fusion | flops 638067200 | bytes 37126144 | tf_op jit(solution)/shard_map/hqk,qhd->khd/dot_general | solution.py:238
  712.0 2.3 fusion.110
  719.2 9.0 fusion.45
  729.3 10.8 fusion.48
  741.4 12.0 constant_dynamic-update-slice_fusion
  753.4 4.2 fusion.105
  757.6 2.8 multiply_dynamic-update-slice_fusion
  766.8 8.0 fusion.124
  774.8 12.7 fusion.68
  789.2 7.7 fusion.128
  799.1 7.7 convolution_bitcast_fusion
  806.8 6.0 convolution_bitcast_fusion.1
  814.8 11.9 pad_maximum_fusion
  826.8 215.8 %reduce-scatter.37.cloned.1.call-done = f32[72,3456]{1,0:T(8,128)} async-done(((f32[1152,3456]{1,0:T(8,128)}), f32[72,3456]{1,0:T(8,128)}) %reduce-scatter.37.cloned.1.call-update) | async-done | bytes 995344
  1045.2 482.2 %reduce-scatter.25.cloned.1.call-done = f32[72,6912]{1,0:T(8,128)} async-done(((f32[1152,6912]{1,0:T(8,128)}), f32[72,6912]{1,0:T(8,128)}) %reduce-scatter.25.cloned.1.call-update) | async-done | bytes 1990672 | tf_op jit(solution)/shard_map/reduce_scatter | solution.py:269
  1532.1 76.6 %all-reduce.18 = bf16[6912]{0:T(1024)(128)(2,1)S(1)} all-reduce(f32[6912]{0:T(1024)S(1)} %get-tuple-element.116), channel_id=10, replica_groups=mesh['tok'=16,'mlp'=2] {'tok'}, use_global_device_ids=true, to_apply=%region_27.28.clone | all-reduce | flops 6912 | bytes 41472
  1608.8 2.7 all-reduce.19
  1612.2 71.9 %reduce-scatter.29.cloned.1.call-done = f32[1536,72]{0,1:T(8,128)} async-done(((f32[1536,1152]{0,1:T(8,128)}), f32[1536,72]{0,1:T(8,128)}) %reduce-scatter.29.cloned.1.call-update) | async-done | bytes 442384 | tf_op jit(solution)/shard_map/reduce_scatter | solution.py:267
  1685.8 7.4 reduce-scatter.33.cloned.1.call-done
  1694.8 226.3 %reduce-scatter.27.cloned.1.call-done = f32[2,72,1536]{2,1,0:T(8,128)} async-done(((f32[2,1152,1536]{2,1,0:T(8,128)}), f32[2,72,1536]{2,1,0:T(8,128)}) %reduce-scatter.27.cloned.1.call-update) | async-done | bytes 884752 | tf_op jit(solution)/shard_map/reduce_scatter | solution.py:266
  1923.1 8.8 reduce-scatter.31.cloned.1.call-done
  1935.2 9.5 reduce-scatter.35.cloned.1.call-done
  1949.7 40.5 %psum.7 = f32[]{:T(128)} all-reduce(f32[]{:T(128)S(6)} %add.293), channel_id=1, replica_groups=mesh['tok'=16,'mlp'=2] {'tok','mlp'}, use_global_device_ids=true, to_apply=%region_34.35 | all-reduce | flops 1 | bytes 8 | tf_op jit(solution)/shard_map/psum | solution.py:291
  1993.7 2.6 multiply_subtract_fusion.2
  (290 shorter events, 77.5 us)
Async XLA Ops:
  7.2 106.0 %copy-start = (bf16[1000,1152]{1,0:T(8,128)(2,1)S(1)}, bf16[1000,1152]{1,0:T(8,128)(2,1)}, u32[]{:S(2)}) copy-start(bf16[1000,1152]{1,0:T(8,128)(2,1)} %param.29) | copy-start | bytes 6912004
  7.2 192.3 %all-gather.10.cloned.1.call-start = ((), (), s32[]{:S(2)}) async-start(), calls=%async_computation.10 | async-start | bytes 16920576 | tf_op jit(solution)/shard_map/all_gather | solution.py:140
  11.5 298.6 %all-gather.12.cloned.1.call-start = ((), (), s32[]{:S(2)}) async-start(), calls=%async_computation.11 | async-start | bytes 8460288 | tf_op jit(solution)/shard_map/all_gather | solution.py:138
  14.9 10.2 copy-start.74
  14.9 10.2 copy-start.79
  14.9 10.4 copy-start.80
  14.9 10.4 copy-start.81
  14.9 10.5 copy-start.5
  17.3 10.3 copy-start.69
  17.3 10.3 copy-start.67
  17.3 10.2 copy-start.68
  17.3 358.5 %all-gather.14.cloned.1.call-start = ((), (), s32[]{:S(2)}) async-start(), calls=%async_computation.12 | async-start | bytes 2820096 | tf_op jit(solution)/shard_map/all_gather | solution.py:139
  22.9 456.3 %all-gather.18.cloned.1.call-start = ((), (), s32[]{:S(2)}) async-start(), calls=%async_computation.14 | async-start | bytes 7520256 | tf_op jit(solution)/shard_map/all_gather | solution.py:142
  25.0 464.7 %all-gather.16.cloned.1.call-start = ((), (), s32[]{:S(2)}) async-start(), calls=%async_computation.13 | async-start | bytes 3538944 | tf_op jit(solution)/shard_map/all_gather | solution.py:188
  25.4 181.8 %copy-start.55 = (s32[512]{0:T(512)}, s32[512]{0:T(512)S(1)}, u32[]{:S(2)}) copy-start(s32[512]{0:T(512)S(1)} %convert_reduce_fusion.1) | copy-start | bytes 6148
  113.9 93.4 %copy-start.57 = (bf16[4,1152]{1,0:T(4,128)(2,1)}, bf16[4,1152]{1,0:T(4,128)(2,1)S(1)}, u32[]{:S(2)}) copy-start(bf16[4,1152]{1,0:T(4,128)(2,1)S(1)} %gather_fusion.1) | copy-start | bytes 27652
  116.4 90.8 %copy-start.59 = (bf16[4,1152]{1,0:T(4,128)(2,1)}, bf16[4,1152]{1,0:T(4,128)(2,1)S(1)}, u32[]{:S(2)}) copy-start(bf16[4,1152]{1,0:T(4,128)(2,1)S(1)} %gather_fusion) | copy-start | bytes 27652
  116.4 96.6 %copy-start.61 = (f32[512]{0:T(512)}, f32[512]{0:T(512)S(1)}, u32[]{:S(2)}) copy-start(f32[512]{0:T(512)S(1)} %broadcast_multiply_fusion.3) | copy-start | bytes 6148
  116.9 96.1 %copy-start.63 = (f32[512]{0:T(512)}, f32[512]{0:T(512)S(1)}, u32[]{:S(2)}) copy-start(f32[512]{0:T(512)S(1)} %fusion.78) | copy-start | bytes 6148
  213.0 5.0 copy-start.2
  218.6 99.0 %copy-start.30 = (bf16[512,1152]{1,0:T(8,128)(2,1)}, bf16[512,1152]{1,0:T(8,128)(2,1)S(1)}, u32[]{:S(2)}) copy-start(bf16[512,1152]{1,0:T(8,128)(2,1)S(1)} %fusion.27) | copy-start | bytes 3538948
  325.9 26.0 %copy-start.17 = (bf16[512,1152]{0,1:T(8,128)(2,1)}, bf16[512,1152]{0,1:T(8,128)(2,1)S(1)}, u32[]{:S(2)}) copy-start(bf16[512,1152]{0,1:T(8,128)(2,1)S(1)} %copy.84) | copy-start | bytes 3538948
  334.6 9.1 copy-start.48
  334.6 9.1 copy-start.49
  334.7 9.0 copy-start.50
  334.7 8.9 copy-start.51
  334.9 8.8 copy-start.52
  334.9 8.8 copy-start.53
  382.0 7.0 copy-start.3
  389.1 176.3 %all-gather.20.cloned.1.call-start = ((), (), s32[]{:S(2)}) async-start(), calls=%async_computation.15 | async-start | bytes 3760128 | tf_op jit(solution)/shard_map/all_gather | solution.py:143
  389.9 187.2 %all-gather.22.cloned.1.call-start = ((), (), s32[]{:S(2)}) async-start(), calls=%async_computation.17 | async-start | bytes 3538944 | tf_op jit(solution)/shard_map/all_gather | solution.py:211
  390.6 226.1 %reduce-scatter.23.cloned.1.call-start = ((), (), s32[]{:S(2)}) async-start(), calls=%async_computation.18 | async-start | bytes 3538944 | tf_op jit(solution)/shard_map/reduce_scatter | solution.py:219
  489.8 9.7 copy-start.75
  489.8 9.7 copy-start.76
  589.4 8.5 copy-start.82
  589.4 8.5 copy-start.84
  605.5 24.7 %reduce-scatter.21.cloned.1.call-start = ((), (), s32[]{:S(2)}) async-start(), calls=%async_computation.16 | async-start | bytes 3538944 | tf_op jit(solution)/shard_map/reduce_scatter | solution.py:193
  614.2 198.6 %reduce-scatter.39.cloned.1.call-start = ((), (), s32[]{:S(2)}) async-start(), calls=%async_computation.26 | async-start | bytes 5640192
  616.7 13.4 copy-start.8
  630.1 5.2 copy-start.11
  643.5 399.1 %reduce-scatter.37.cloned.1.call-start = ((), (), s32[]{:S(2)}) async-start(), calls=%async_computation.25 | async-start | bytes 16920576
  660.4 25.9 %copy-start.45 = (bf16[512,16,18]{0,2,1:T(8,128)(2,1)S(1)}, bf16[512,16,18]{0,2,1:T(8,128)(2,1)}, u32[]{:S(2)}) copy-start(bf16[512,16,18]{0,2,1:T(8,128)(2,1)} %copy-done.44) | copy-start | bytes 884740
  660.4 25.9 %copy-start.47 = (bf16[512,16,18]{0,2,1:T(8,128)(2,1)S(1)}, bf16[512,16,18]{0,2,1:T(8,128)(2,1)}, u32[]{:S(2)}) copy-start(bf16[512,16,18]{0,2,1:T(8,128)(2,1)} %copy-done.46) | copy-start | bytes 884740
  718.4 9.9 copy-start.32
  719.2 9.1 copy-start.33
  719.2 10.1 copy-start.31
  740.2 13.2 copy-start.66
  740.2 13.2 copy-start.64
  740.2 787.2 %reduce-scatter.25.cloned.1.call-start = ((), (), s32[]{:S(2)}) async-start(), calls=%async_computation.19 | async-start | bytes 33841152 | tf_op jit(solution)/shard_map/reduce_scatter | solution.py:269
  766.8 8.0 copy-start.58
  766.8 8.1 copy-start.60
  787.6 896.4 %reduce-scatter.29.cloned.1.call-start = ((), (), s32[]{:S(2)}) async-start(), calls=%async_computation.21 | async-start | bytes 7520256 | tf_op jit(solution)/shard_map/reduce_scatter | solution.py:267
  797.0 896.1 %reduce-scatter.33.cloned.1.call-start = ((), (), s32[]{:S(2)}) async-start(), calls=%async_computation.23 | async-start | bytes 442368
  799.1 7.7 copy-start.83
  814.8 1106.4 %reduce-scatter.27.cloned.1.call-start = ((), (), s32[]{:S(2)}) async-start(), calls=%async_computation.20 | async-start | bytes 15040512 | tf_op jit(solution)/shard_map/reduce_scatter | solution.py:266
  826.8 1105.2 %reduce-scatter.31.cloned.1.call-start = ((), (), s32[]{:S(2)}) async-start(), calls=%async_computation.22 | async-start | bytes 1327104
  1045.2 899.5 %reduce-scatter.35.cloned.1.call-start = ((), (), s32[]{:S(2)}) async-start(), calls=%async_computation.24 | async-start | bytes 2654208
  1530.7 460.3 %copy-start.70 = (f32[216]{0:T(256)S(1)}, f32[216]{0:T(256)}, u32[]{:S(2)}) copy-start(f32[216]{0:T(256)} %param.37) | copy-start | bytes 2596
  1530.7 460.3 %copy-start.71 = (f32[216]{0:T(256)S(1)}, f32[216]{0:T(256)}, u32[]{:S(2)}) copy-start(f32[216]{0:T(256)} %param.49) | copy-start | bytes 2596
  1530.8 460.3 %copy-start.72 = (f32[216]{0:T(256)S(1)}, f32[216]{0:T(256)}, u32[]{:S(2)}) copy-start(f32[216]{0:T(256)} %param.43) | copy-start | bytes 2596
  1694.8 298.9 %copy-start.23 = (f32[72,1728]{1,0:T(8,128)S(1)}, f32[72,1728]{1,0:T(8,128)}, u32[]{:S(2)}) copy-start(f32[72,1728]{1,0:T(8,128)} %param.34) | copy-start | bytes 1492996
  1947.0 49.3 %copy-start.19 = (f32[72,3456]{1,0:T(8,128)S(1)}, f32[72,3456]{1,0:T(8,128)}, u32[]{:S(2)}) copy-start(f32[72,3456]{1,0:T(8,128)} %param.36) | copy-start | bytes 2985988
  1947.0 49.3 %copy-start.36 = (f32[72,3456]{1,0:T(8,128)S(1)}, f32[72,3456]{1,0:T(8,128)}, u32[]{:S(2)}) copy-start(f32[72,3456]{1,0:T(8,128)} %param.48) | copy-start | bytes 2985988
  1991.1 5.3 copy-start.37
  (38 other events, 86.5 us)
Sparse Core Ops, SparseCore 0:
  11.6 187.8 all-gather.9
  202.8 107.1 all-gather.11
  313.3 62.4 all-gather.13
  378.9 100.2 all-gather.17
  480.6 9.0 all-gather.15
  493.0 72.3 all-gather.19
  567.5 9.4 all-gather.21
  605.6 11.0 reduce-scatter.22
  619.0 11.0 reduce-scatter.20
  643.6 141.7 reduce-scatter.38
  791.3 251.3 reduce-scatter.36
  1048.6 478.7 reduce-scatter.24
  1532.7 151.2 reduce-scatter.28
  1686.7 6.4 reduce-scatter.32
  1698.8 222.3 reduce-scatter.26
  1923.9 7.9 reduce-scatter.30
  1934.1 10.4 reduce-scatter.34
where the time goes:
time: 2020 us; the launch traced here: 2010 us
  waiting for transfers between devices  1390 us (69%)
  matrix products  241 us (12%)
  blocking collectives  210 us (10%)
  other arithmetic  83.6 us (4%)
  local copies, waits for them, and re-layouts  57.9 us (3%)
  between operations  23.8 us (1%)
    reduce_scatter x1, waiting for transfers between devices, body(): lax.psum_scatter(across(cond_low, modulation_low), 'tok', scatter_dimensi...  482 us
    unnamed x22, waiting for transfers between devices  242 us
    reduce_scatter x1, waiting for transfers between devices, body(): lax.psum_scatter(d_feed, 'tok', scatter_dimension=1, tiled=True)  226 us
    unnamed x4, blocking collectives  163 us
    all_gather x1, waiting for transfers between devices, body(): lax.all_gather(pair[0], 'tok', axis=0, tiled=True)  91.4 us
    all_gather x1, waiting for transfers between devices, body(): lax.all_gather(feed_weight.astype(half), 'tok', axis=1, tiled=True)  88.6 us
    all_gather x1, waiting for transfers between devices, body(): lax.all_gather(pair[2], 'tok', axis=0, tiled=True)  81.7 us
    reduce_scatter x1, waiting for transfers between devices, body(): lax.psum_scatter(d_down, 'tok', scatter_dimension=1, tiled=True)  71.9 us
  transfers between devices with their start and end apart: 17, of which 16 were waited for; matrix products, arithmetic and copies ran while one was open for 15% of the time, Pallas kernels for 0%

commit v1 on v0

--- a/solution.py
+++ b/solution.py
@@ -95,6 +95,128 @@
     fixed_square = square_new / (1.0 - BETA_TWO**STEP)
     weight_new = weight - RATE * (fixed_mean / (jnp.sqrt(fixed_square) + ADAM_EPS) + DECAY * weight)
     return (mean_new, square_new, weight_new)
+
+
+AXES = {16: (2, 2, 4), 128: (8, 4, 4)}
+
+
+def factors(count):
+    sizes = AXES.get(count, (count,))
+    strides = []
+    stride = 1
+    for size in sizes:
+        strides.append((size, stride))
+        stride *= size
+    return strides
+
+
+def shift(factor, step, count):
+    size, stride = factor
+    pairs = []
+    for place in range(count):
+        digit = (place // stride) % size
+        pairs.append((place, place + ((digit + step) % size - digit) * stride))
+    return pairs
+
+
+def digit_of(factor):
+    size, stride = factor
+    return (lax.axis_index("tok") // stride) % size
+
+
+def plan(count):
+    parts = factors(count)
+    canon = parts[::-1]
+    longest = max(canon, key=lambda part: part[0])
+    rest = [part for part in canon if part is not longest]
+    return canon, [longest] + rest, [longest] + rest[::-1]
+
+
+def swap(value):
+    return lax.ppermute(value, "mlp", [(0, 1), (1, 0)])
+
+
+def gather_stage(value, factor, axis, count):
+    size = factor[0]
+    if size == 1:
+        return value
+    digit = digit_of(factor)
+    shape = list(value.shape)
+    shape[axis] *= size
+    pieces = [value] + [
+        lax.ppermute(value, "tok", shift(factor, step, count)) for step in range(1, size)
+    ]
+    out = jnp.zeros(shape, value.dtype)
+    for step, piece in enumerate(pieces):
+        start = [0] * value.ndim
+        start[axis] = (digit - step) % size
+        out = lax.dynamic_update_slice(out, piece, tuple(start))
+    return out
+
+
+def scatter_stage(value, factor, axis, count, kept):
+    size = factor[0]
+    if size == 1:
+        return value.astype(kept)
+    digit = digit_of(factor)
+
+    def part(place):
+        return lax.dynamic_slice_in_dim(value, place % size, 1, axis)
+
+    out = part(digit).astype(jnp.float32)
+    for step in range(1, size):
+        sent = part(digit + step).astype(jnp.bfloat16)
+        out = out + lax.ppermute(sent, "tok", shift(factor, step, count)).astype(jnp.float32)
+    return out.astype(kept)
+
+
+def split_rows(value, canon):
+    sizes = [part[0] for part in canon]
+    total = 1
+    for size in sizes:
+        total *= size
+    return value.reshape(*sizes, value.shape[0] // total, value.shape[1])
+
+
+def gather_small(value, count):
+    canon, order, _ = plan(count)
+    out = value.reshape((1,) * len(canon) + value.shape)
+    for factor in order:
+        out = gather_stage(out, factor, canon.index(factor), count)
+    return out.reshape((count,) + value.shape)
+
+
+def scatter_small(value, count):
+    canon, order, _ = plan(count)
+    out = split_rows(value, canon)
+    for factor in order[::-1]:
+        kept = jnp.float32
+        out = scatter_stage(out, factor, canon.index(factor), count, kept)
+    return out.reshape(out.shape[-2:])
+
+
+def sum_all(value, count):
+    value = value + swap(value)
+    for factor in factors(count):
+        size = factor[0]
+        if size == 2:
+            value = value + lax.ppermute(value, "tok", shift(factor, 1, count))
+            continue
+        digit = digit_of(factor)
+        places = jnp.arange(size)
+        line = jnp.where(places == digit, value, 0.0)
+        for step in range(1, size):
+            moved = lax.ppermute(value, "tok", shift(factor, step, count))
+            line = jnp.where(places == (digit - step) % size, moved, line)
+        value = jnp.sum(line)
+    return value
+
+
+def pick(segment, table):
+    out = jnp.zeros((segment.shape[0], table.shape[1]), jnp.float32)
+    for slot in range(SLOTS):
+        out = jnp.where(segment[:, None] == slot, table[slot][None, :], out)
+    return out
 
 
 def body(
@@ -128,35 +250,105 @@
     half = jnp.bfloat16
     count = block_input.shape[0]
     width = block_input.shape[1]
-    pair = (
-        lax.all_gather(mix_weight.astype(half), "mlp", axis=1, tiled=True),
-        lax.all_gather(proj_weight.astype(half), "mlp", axis=1, tiled=True),
-        lax.all_gather(cond_weight.astype(half), "mlp", axis=1, tiled=True),
-        lax.all_gather(cond_bias.astype(half), "mlp", axis=0, tiled=True),
-    )
-    full = (
-        lax.all_gather(pair[0], "tok", axis=0, tiled=True),
-        lax.all_gather(pair[1], "tok", axis=0, tiled=True),
-        lax.all_gather(pair[2], "tok", axis=0, tiled=True),
-        lax.all_gather(pair[3], "tok", axis=0, tiled=True),
-        lax.all_gather(feed_weight.astype(half), "tok", axis=1, tiled=True),
-        lax.all_gather(down_weight.astype(half), "tok", axis=1, tiled=True),
-    )
-    mix_full, proj_full, cond_full, bias_full, feed_full, down_full = full
+    chips = lax.axis_size("tok")
+    tok = lax.axis_index("tok")
+    side = lax.axis_index("mlp")
+    first_side = side == 0
+    canon, order_a, order_b = plan(chips)
+    rows_own = mix_weight.shape[0]
+    mix_cols = mix_weight.shape[1]
+    proj_cols = proj_weight.shape[1]
+    hidden_cols = feed_weight.shape[2]
+    cond_cols = cond_weight.shape[1]
+
+    def expand(value):
+        return value.reshape((1,) * len(canon) + value.shape)
+
+    def stage(value, factor):
+        return gather_stage(value, factor, canon.index(factor), chips)
+
+    near = jnp.concatenate([mix_weight.astype(half), proj_weight.astype(half)], axis=1)
+    near = stage(expand(near), order_a[0])
+    down_turned = down_weight.T
+    mid = hidden_cols // 2
+    far = jnp.concatenate(
+        [
+            feed_weight[0].astype(half),
+            down_turned[:, :mid].astype(half),
+            feed_weight[1].astype(half),
+            down_turned[:, mid:].astype(half),
+        ],
+        axis=1,
+    )
+    near, far = lax.optimization_barrier((near, far))
+    far = stage(expand(far), order_a[0])
+    cut = near.shape[-1] // 2
+    near_a, near_b = near[..., :cut], near[..., cut:]
+    for one, two in zip(order_a[1:], order_b[1:]):
+        near_a, near_b = stage(near_a, one), stage(near_b, two)
+    near_a, near_b, far = lax.optimization_barrier((near_a, near_b, far))
+    cut = far.shape[-1] // 2
+    far_a, far_b = far[..., :cut], far[..., cut:]
+    for one, two in zip(order_a[1:], order_b[1:]):
+        far_a, far_b = stage(far_a, one), stage(far_b, two)
+    near_a, near_b, far_a, far_b = (
+        value.reshape(width, value.shape[-1]) for value in (near_a, near_b, far_a, far_b)
+    )
+    far_gate, far_up = far_a[:, :hidden_cols], far_b[:, :hidden_cols]
+    down_a, down_b = far_a[:, hidden_cols:], far_b[:, hidden_cols:]
+    near_own = jnp.concatenate([near_a, near_b], axis=1)
+    near_other = jnp.concatenate([swap(near_a), swap(near_b)], axis=1)
+    mix_own, proj_own = near_own[:, :mix_cols], near_own[:, mix_cols:]
+    mix_other, proj_other = near_other[:, :mix_cols], near_other[:, mix_cols:]
+
+    def joined(own, other):
+        low = jnp.where(first_side, own, other)
+        high = jnp.where(first_side, other, own)
+        return jnp.concatenate([low, high], axis=1)
+
+    def parted(value):
+        size = value.shape[1] // 2
+        low, high = value[:, :size], value[:, size:]
+        return jnp.where(first_side, low, high), jnp.where(first_side, high, low)
+
+    codes = jnp.stack([class_label, time_index])
+    codes = gather_small(jnp.concatenate([codes, swap(codes)], axis=1), chips)
+    labels = codes[:, 0].reshape(-1)
+    times = codes[:, 1].reshape(-1)
+    start = tok * rows_own
+    class_part = lax.dynamic_slice_in_dim(class_table, start, rows_own, 1)
+    time_part = lax.dynamic_slice_in_dim(time_table, start, rows_own, 1)
+    class_hot = (labels[:, None] == jnp.arange(class_table.shape[0])[None, :]).astype(half)
+    time_hot = (times[:, None] == jnp.arange(time_table.shape[0])[None, :]).astype(half)
+    embed = jnp.dot(class_hot, class_part, preferred_element_type=jnp.float32) + jnp.dot(
+        time_hot, time_part, preferred_element_type=jnp.float32
+    )
+    cond_low = jax.nn.silu(embed).astype(half)
+    partial_mod = jnp.dot(cond_low, cond_weight.astype(half), preferred_element_type=jnp.float32)
+    bias_low = cond_bias.astype(half).astype(jnp.float32)
+    bias_pair = joined(bias_low[None, :], swap(bias_low)[None, :])[0]
+    bias_start = tok * bias_pair.shape[0]
+    bias_side = bias_start // cond_cols
+    bias_pair = jnp.where(bias_side == side, bias_pair, 0.0)
+    bias_row = lax.dynamic_update_slice(
+        jnp.zeros((cond_cols,), jnp.float32), bias_pair, (bias_start - bias_side * cond_cols,)
+    )
+    mod_half = scatter_small(partial_mod + bias_row[None, :], chips)
+    slots = class_label.shape[0]
+    modulation = joined(mod_half[:slots], swap(mod_half[slots:]))
+
     segment, member, rows, cols = geometry(grid_height, grid_width, count)
     valid = (segment < SLOTS).astype(jnp.float32)[:, None]
-    embed = class_table[class_label].astype(jnp.float32) + time_table[time_index].astype(
-        jnp.float32
-    )
-    cond_low = jax.nn.silu(embed).astype(half)
-    modulation = jnp.dot(
-        cond_low, cond_full, preferred_element_type=jnp.float32
-    ) + bias_full.astype(jnp.float32)
-    per_token = jnp.dot(member, modulation, precision=HIGH)
-    shift_a, scale_a, gate_a, shift_b, scale_b, gate_b = jnp.split(per_token, 6, axis=1)
+    shift_a, scale_a, gate_a, shift_b, scale_b, gate_b = (
+        pick(segment, table) for table in jnp.split(modulation, 6, axis=1)
+    )
     inputs = block_input.astype(jnp.float32)
     first_in = modulate(inputs, shift_a, scale_a).astype(half)
-    mixed = jnp.dot(first_in, mix_full, preferred_element_type=jnp.float32)
+    first_other = swap(first_in)
+    mixed = joined(
+        jnp.dot(first_in, mix_own, preferred_element_type=jnp.float32),
+        jnp.dot(first_in, mix_other, preferred_element_type=jnp.float32),
+    )
     query_raw, key_raw, value_raw = jnp.split(mixed, 3, axis=1)
     shape = (count, HEADS, HEAD)
     query_raw = query_raw.reshape(shape)
@@ -182,50 +374,75 @@
         .reshape(count, width)
         .astype(half)
     )
-    branch = jnp.dot(attended, proj_full, preferred_element_type=jnp.float32)
+    attended_other = swap(attended)
+    branch = joined(
+        jnp.dot(attended, proj_own, preferred_element_type=jnp.float32),
+        jnp.dot(attended, proj_other, preferred_element_type=jnp.float32),
+    )
     middle = inputs + gate_a * branch
     second_in = modulate(middle, shift_b, scale_b).astype(half)
-    second_pair = lax.all_gather(second_in, "mlp", axis=0, tiled=True)
-    gate_pre = jnp.dot(second_pair, feed_full[0], preferred_element_type=jnp.float32)
-    up_pre = jnp.dot(second_pair, feed_full[1], preferred_element_type=jnp.float32)
+    second_pair = jnp.concatenate([second_in, swap(second_in)], axis=0)
+    gate_pre = jnp.dot(second_pair, far_gate, preferred_element_type=jnp.float32)
+    up_pre = jnp.dot(second_pair, far_up, preferred_element_type=jnp.float32)
     hidden = (jax.nn.silu(gate_pre) * up_pre).astype(half)
-    partial_value = jnp.dot(hidden, down_full, preferred_element_type=jnp.float32)
-    result = lax.psum_scatter(
-        partial_value.astype(jnp.bfloat16), "mlp", scatter_dimension=0, tiled=True
-    ).astype(jnp.float32)
+    partial_value = against(hidden[:, :mid], down_a) + against(hidden[:, mid:], down_b)
+    result = partial_value[:count] + swap(partial_value[count:].astype(half)).astype(jnp.float32)
     block_output = (valid * (middle + gate_b * result)).astype(half)
-    again = (
-        lax.all_gather(mix_weight.astype(half), "mlp", axis=1, tiled=True),
-        lax.all_gather(proj_weight.astype(half), "mlp", axis=1, tiled=True),
-    )
-    later = (
-        lax.all_gather(again[0], "tok", axis=0, tiled=True),
-        lax.all_gather(again[1], "tok", axis=0, tiled=True),
-        lax.all_gather(feed_weight.astype(half), "tok", axis=1, tiled=True),
-        lax.all_gather(down_weight.astype(half), "tok", axis=1, tiled=True),
-    )
-    mix_back, proj_back, feed_back, down_back = later
+
     grad_out = valid * out_grad.astype(jnp.float32)
     d_gate_b = grad_out * result
     result_grad = (gate_b * grad_out).astype(half)
-    result_pair = lax.all_gather(result_grad, "mlp", axis=0, tiled=True)
-    d_down = across(hidden, result_pair)
-    d_hidden = against(result_pair, down_back)
+    result_pair = jnp.concatenate([result_grad, swap(result_grad)], axis=0)
+    d_down = across(result_pair, hidden).astype(half)
+    d_hidden = jnp.concatenate(
+        [
+            jnp.dot(result_pair, down_a, preferred_element_type=jnp.float32),
+            jnp.dot(result_pair, down_b, preferred_element_type=jnp.float32),
+        ],
+        axis=1,
+    )
     sig = jax.nn.sigmoid(gate_pre)
     gate_grad = (d_hidden * up_pre * sig * (1.0 + gate_pre * (1.0 - sig))).astype(half)
     up_grad = (d_hidden * gate_pre * sig).astype(half)
-    d_feed = jnp.stack([across(second_pair, gate_grad), across(second_pair, up_grad)])
-    second_part = against(gate_grad, feed_back[0]) + against(up_grad, feed_back[1])
-    second_grad = lax.psum_scatter(
-        second_part.astype(jnp.bfloat16), "mlp", scatter_dimension=0, tiled=True
-    ).astype(jnp.float32)
+    d_gate = across(second_pair, gate_grad).astype(half)
+    d_up = across(second_pair, up_grad).astype(half)
+
+    def unstage(value, factor, kept=jnp.bfloat16):
+        return scatter_stage(value, factor, canon.index(factor), chips, kept)
+
+    far_a = split_rows(jnp.concatenate([d_gate, d_down[:, :mid]], axis=1), canon)
+    far_b = split_rows(jnp.concatenate([d_up, d_down[:, mid:]], axis=1), canon)
+    for one, two in zip(order_a[:0:-1], order_b[:0:-1]):
+        far_a, far_b = unstage(far_a, one), unstage(far_b, two)
+    far_grad = unstage(jnp.concatenate([far_a, far_b], axis=-1), order_a[0], jnp.float32)
+    far_grad = far_grad.reshape(far_grad.shape[-2:])
+    feed_grad = jnp.stack(
+        [
+            far_grad[:, :hidden_cols],
+            far_grad[:, hidden_cols + mid : 2 * hidden_cols + mid],
+        ]
+    )
+    down_grad = jnp.concatenate(
+        [far_grad[:, hidden_cols : hidden_cols + mid], far_grad[:, 2 * hidden_cols + mid :]], axis=1
+    ).T
+
+    second_part = against(gate_grad, far_gate) + against(up_grad, far_up)
+    second_grad = second_part[:count] + swap(second_part[count:].astype(half)).astype(jnp.float32)
     pull_second = jax.vjp(modulate, middle, shift_b, scale_b)[1]
     d_middle, d_shift_b, d_scale_b = pull_second(second_grad)
     d_middle = d_middle + grad_out
     d_gate_a = d_middle * branch
     branch_grad = (gate_a * d_middle).astype(half)
-    d_proj = across(attended, branch_grad)
-    attended_grad = against(branch_grad, proj_back).astype(half).reshape(shape)
+    branch_grad_own, branch_grad_other = parted(branch_grad)
+    d_proj = across(
+        jnp.concatenate([attended, attended_other], axis=0),
+        jnp.concatenate([branch_grad_own, swap(branch_grad_other)], axis=0),
+    ).astype(half)
+    attended_grad = (
+        (against(branch_grad_own, proj_own) + against(branch_grad_other, proj_other))
+        .astype(half)
+        .reshape(shape)
+    )
     probs_again = jnp.exp(scores_of() - log_total)
     d_value = jnp.einsum(
         "hqk,qhd->khd", probs_again.astype(half), attended_grad, preferred_element_type=jnp.float32
@@ -248,48 +465,47 @@
         ],
         axis=1,
     ).astype(half)
-    d_mix = across(first_in, mixed_grad)
-    first_grad = against(mixed_grad, mix_back)
+    mixed_grad_own, mixed_grad_other = parted(mixed_grad)
+    d_mix = across(
+        jnp.concatenate([first_in, first_other], axis=0),
+        jnp.concatenate([mixed_grad_own, swap(mixed_grad_other)], axis=0),
+    ).astype(half)
+    near_grad = jnp.concatenate([d_mix, d_proj], axis=1)
+    cut = near_grad.shape[1] // 2
+    near_a = split_rows(near_grad[:, :cut], canon)
+    near_b = split_rows(near_grad[:, cut:], canon)
+    for one, two in zip(order_a[:0:-1], order_b[:0:-1]):
+        near_a, near_b = unstage(near_a, one), unstage(near_b, two)
+    near_grad = unstage(jnp.concatenate([near_a, near_b], axis=-1), order_a[0], jnp.float32)
+    near_grad = near_grad.reshape(near_grad.shape[-2:])
+    mix_grad, proj_grad = near_grad[:, :mix_cols], near_grad[:, mix_cols:]
+
+    first_grad = against(mixed_grad_own, mix_own) + against(mixed_grad_other, mix_other)
     pull_first = jax.vjp(modulate, inputs, shift_a, scale_a)[1]
     d_inputs, d_shift_a, d_scale_a = pull_first(first_grad)
     input_grad = d_inputs + d_middle
-    d_per_token = jnp.concatenate(
-        [d_shift_a, d_scale_a, d_gate_a, d_shift_b, d_scale_b, d_gate_b], axis=1
-    )
-    d_modulation = across(member, d_per_token, HIGH)
-    d_bias = jnp.sum(d_modulation, axis=0)
-    modulation_low = d_modulation.astype(half)
-    rows_part = (
-        lax.psum_scatter(d_mix, "tok", scatter_dimension=0, tiled=True),
-        lax.psum_scatter(d_proj, "tok", scatter_dimension=0, tiled=True),
-        lax.psum_scatter(d_bias, "tok", scatter_dimension=0, tiled=True),
-        lax.psum_scatter(d_feed, "tok", scatter_dimension=1, tiled=True),
-        lax.psum_scatter(d_down, "tok", scatter_dimension=1, tiled=True),
-    )
-    cond_rows = lax.psum_scatter(
-        across(cond_low, modulation_low), "tok", scatter_dimension=0, tiled=True
-    )
-    cols_part = (
-        lax.psum_scatter(
-            rows_part[0].astype(jnp.bfloat16), "mlp", scatter_dimension=1, tiled=True
-        ).astype(jnp.float32),
-        lax.psum_scatter(
-            rows_part[1].astype(jnp.bfloat16), "mlp", scatter_dimension=1, tiled=True
-        ).astype(jnp.float32),
-        lax.psum_scatter(
-            cond_rows.astype(jnp.bfloat16), "mlp", scatter_dimension=1, tiled=True
-        ).astype(jnp.float32),
-        lax.psum_scatter(
-            rows_part[2].astype(jnp.bfloat16), "mlp", scatter_dimension=0, tiled=True
-        ).astype(jnp.float32),
-    )
-    mix_grad, proj_grad, cond_grad, bias_grad = cols_part
-    grads = (mix_grad, proj_grad, cond_grad, bias_grad, rows_part[3], rows_part[4])
+    member_low = member.astype(half)
+    d_modulation = jnp.concatenate(
+        [
+            across(member_low, piece.astype(half))
+            for piece in (d_shift_a, d_scale_a, d_gate_a, d_shift_b, d_scale_b, d_gate_b)
+        ],
+        axis=1,
+    ).astype(half)
+    mod_own, mod_other = parted(d_modulation)
+    mod_all = gather_small(jnp.concatenate([mod_own, swap(mod_other)], axis=0), chips)
+    mod_all = mod_all.reshape(-1, cond_cols)
+    cond_grad = across(cond_low, mod_all)
+    bias_half = jnp.sum(mod_all.astype(jnp.float32), axis=0)[None, :]
+    bias_full = joined(bias_half, swap(bias_half))[0]
+    bias_size = cond_bias.shape[0]
+    bias_grad = lax.dynamic_slice_in_dim(bias_full, (2 * tok + side) * bias_size, bias_size, 0)
+
+    grads = (mix_grad, proj_grad, cond_grad, bias_grad, feed_grad, down_grad)
     local_squares = jnp.float32(0.0)
     for grad in grads:
         local_squares = local_squares + jnp.sum(grad * grad)
-    total = lax.psum(local_squares, ("tok", "mlp"))
-    grad_norm = jnp.sqrt(total)
+    grad_norm = jnp.sqrt(sum_all(local_squares, chips))
     factor = CLIP_NORM / jnp.maximum(grad_norm, CLIP_NORM)
     params = (mix_weight, proj_weight, cond_weight, cond_bias, feed_weight, down_weight)
     means = (mix_mean, proj_mean, cond_mean, bias_mean, feed_mean, down_mean)

time: 2020 us -> 743 us (0.37)
  waiting for transfers between devices: 1390 us -> 247 us
  blocking collectives: 210 us -> 0 us
  starting transfers between devices: 0.88 us -> 96.5 us
  matrix products: 241 us -> 202 us
  local copies, waits for them, and re-layouts: 57.9 us -> 91.5 us
    reduce_scatter x5 -> x0, waiting for transfers between devices: 793 us -> none  [the longest x1 482 us: body(): lax.psum_scatter(across(cond_low, modulation_low), 'tok', scatter_dimensi...]
    all_gather x7 -> x0, waiting for transfers between devices: 358 us -> none  [the longest x1 91.4 us: body(): lax.all_gather(pair[0], 'tok', axis=0, tiled=True)]
    ppermute x0 -> x64, waiting for transfers between devices: none -> 247 us  [the longest x19 136 us: scatter_stage(): lax.ppermute(sent, 'tok', shift(factor, step, count)).astype(jnp.float32)]
    unnamed x22 -> x0, waiting for transfers between devices: 242 us -> none
    unnamed x4 -> x0, blocking collectives: 163 us -> none
    ppermute x0 -> x64, starting transfers between devices: none -> 96.5 us  [the longest x19 40.2 us: scatter_stage(): lax.ppermute(sent, 'tok', shift(factor, step, count)).astype(jnp.float32)]
    psum x1 -> x0, blocking collectives: 40.5 us -> none  [body(): total = lax.psum(local_squares, ('tok', 'mlp'))]
    dot_general x7 -> x12, matrix products: 57.1 us -> 33.8 us  [across(): lax.dot_general(left, right, (((0,), (0,)), ((), ())), preferred_element_...]
  transfers between devices with their start and end apart: 17 -> 64, of which waited for: 16 -> 32; matrix products, arithmetic and copies ran while one was open for 15% -> 46% of each run, Pallas kernels for 0% -> 0%
where the time goes in v1:
time: 743 us; the launch traced here: 733 us
  waiting for transfers between devices  247 us (33%)
  matrix products  202 us (27%)
  starting transfers between devices  96.5 us (13%)
  local copies, waits for them, and re-layouts  91.5 us (12%)
  other arithmetic  85.7 us (12%)
  between operations  11 us (1%)
    ppermute x19, waiting for transfers between devices, scatter_stage(): lax.ppermute(sent, 'tok', shift(factor, step, count)).astype(jnp.float32)  136 us
    ppermute x24, waiting for transfers between devices, gather_stage(): lax.ppermute(value, 'tok', shift(factor, step, count))  104 us
    ppermute x19, starting transfers between devices, scatter_stage(): lax.ppermute(sent, 'tok', shift(factor, step, count)).astype(jnp.float32)  40.2 us
    dot_general x8, matrix products, against(): lax.dot_general(left, right, (((1,), (1,)), ((), ())), preferred_element_...  34.4 us
    ppermute x24, starting transfers between devices, gather_stage(): lax.ppermute(value, 'tok', shift(factor, step, count))  34 us
    dot_general x12, matrix products, across(): lax.dot_general(left, right, (((0,), (0,)), ((), ())), preferred_element_...  33.8 us
    unnamed x368, local copies, waits for them, and re-layouts  28.7 us
    dot_general x1, matrix products, body(): jnp.einsum('hqk,khd->qhd', d_scores, key, preferred_element_type=jnp.floa...  25.3 us
  transfers between devices with their start and end apart: 64, of which 32 were waited for; matrix products, arithmetic and copies ran while one was open for 46% of the time, Pallas kernels for 0%

profile of v1, /device:TPU:0, one launch (start us, length us, event | category | flops | bytes accessed | tf_op | source)
XLA Modules:
  0.0 733.2 jit_solution(12018446580321194633)
XLA Ops:
  5.0 3.0 collective-permute-start.13
  8.0 2.6 collective-permute-start.14
  29.8 3.9 collective-permute-done.1
  33.7 6.4 collective-permute-start.2
  42.3 3.0 collective-permute-done.3
  62.3 3.4 collective-permute-done.7
  72.2 2.7 collective-permute-start.10
  77.1 35.6 %collective-permute-done.10 = bf16[1,1,1,8,3456]{4,3,2,1,0:T(8,128)(2,1)S(1)} collective-permute-done((bf16[1,1,1,8,3456]{4,3,2,1,0:T(8,128)(2,1)S(1)}, bf16[1,1,1,8,3456]{4,3,2,1,0:T(8,128)(2,1)S(1)}, u32[]{:S(2)}, u32[]{:S(2)}) %collective-permute-start.10) | collective-permute-done | bytes 55328 | tf_op jit(solution)/shard_map/ppermute | solution.py:169
  119.2 15.3 %collective-permute-done.18 = bf16[4,1,1,72,1152]{4,3,2,1,0:T(8,128)(2,1)S(1)} collective-permute-done((bf16[4,1,1,72,1152]{4,3,2,1,0:T(8,128)(2,1)S(1)}, bf16[4,1,1,72,1152]{4,3,2,1,0:T(8,128)(2,1)S(1)}, u32[]{:S(2)}, u32[]{:S(2)}) %collective-permute-start.18) | collective-permute-done | bytes 663584 | tf_op jit(solution)/shard_map/ppermute | solution.py:147
  137.8 27.6 %collective-permute-done.19 = bf16[4,1,2,72,1152]{4,3,2,1,0:T(8,128)(2,1)S(1)} collective-permute-done((bf16[4,1,2,72,1152]{4,3,2,1,0:T(8,128)(2,1)S(1)}, bf16[4,1,2,72,1152]{4,3,2,1,0:T(8,128)(2,1)S(1)}, u32[]{:S(2)}, u32[]{:S(2)}) %collective-permute-start.19) | collective-permute-done | bytes 1327136 | tf_op jit(solution)/shard_map/ppermute | solution.py:147
  175.8 2.9 fusion.35
  179.4 3.8 fusion.48
  183.3 18.4 %collective-permute-done.26 = bf16[4,1,1,72,2304]{4,3,2,1,0:T(8,128)(2,1)S(1)} collective-permute-done((bf16[4,1,1,72,2304]{4,3,2,1,0:T(8,128)(2,1)S(1)}, bf16[4,1,1,72,2304]{4,3,2,1,0:T(8,128)(2,1)S(1)}, u32[]{:S(2)}, u32[]{:S(2)}) %collective-permute-start.26) | collective-permute-done | bytes 1327136 | tf_op jit(solution)/shard_map/ppermute | solution.py:147
  217.5 4.7 broadcast_select_fusion.2
  228.1 8.4 %fusion.178 = (f32[16,512]{1,0:T(8,128)S(1)}, f32[16,512,512]{1,2,0:T(8,128)}) fusion(bf16[512,16,18]{0,2,1:T(8,128)(2,1)S(1)} %get-tuple-element.264, bf16[512,16,18]{0,2,1:T(8,128)(2,1)S(1)} %get-tuple-element.220, bf16[512,16,18]{0,2,1:T(8,128)(2,1)S(1)} %get-tuple-element.265, bf16[512,16,18]{0,2,1:T(8,128)(2,1)S(1)} %get-tuple-element.219, ...), kind=kOutput, calls=%fused_computation.444 | convolution fusion | flops 625991680 | bytes 19431424 | tf_op jit(solution)/shard_map/qhd,khd->hqk/dot_general | solution.py:363
  236.6 8.3 %fusion.4 = f32[16,512]{1,0:T(8,128)S(1)} fusion(f32[16,512,512]{1,2,0:T(8,128)} %get-tuple-element.257, f32[16,512]{1,0:T(8,128)S(1)} %get-tuple-element.256), kind=kLoop, calls=%fused_computation.8 | loop fusion | flops 8380416 | bytes 16842752 | tf_op jit(solution)/shard_map/reduce_sum | solution.py:369
  244.9 10.3 %fusion.65 = bf16[16,72,512]{2,1,0:T(8,128)(2,1)} fusion(bf16[512,16,72]{0,2,1:T(8,128)(2,1)} %bitcast.142, f32[16,512,512]{1,2,0:T(8,128)} %get-tuple-element.257, f32[16,512]{1,0:T(8,128)S(1)} %fusion.4, f32[16,512]{1,0:T(8,128)S(1)} %get-tuple-element.256), kind=kOutput, calls=%fused_computation.147 | convolution fusion | flops 617152512 | bytes 19202048 | tf_op jit(solution)/shard_map/hqk,khd->qhd/dot_general | solution.py:373
  255.2 2.8 fusion.76
  258.3 2.9 broadcast_select_fusion.7
  261.4 2.6 fusion.158
  269.9 3.9 constant_dynamic-update-slice_fusion.8
  273.8 4.0 fusion.62
  277.8 3.9 fusion.59
  282.8 6.3 fusion.26
  289.1 13.4 %multiply_convert_fusion.2 = (bf16[1024,1536]{1,0:T(8,128)(2,1)}, bf16[1024,1536]{1,0:T(8,128)(2,1)}, bf16[1024,1536]{1,0:T(8,128)(2,1)}) fusion(f32[1024,1536]{1,0:T(8,128)} %fusion.26, f32[1024,768]{1,0:T(8,128)} %fusion.59, f32[1024,768]{1,0:T(8,128)} %fusion.62, bf16[1152,2304]{1,0:T(8,128)(2,1)S(1)} %bitcast.128, bf16[512,1152]{0,1:T(8,128)(2,1)} %copy-done.157, ...), kind=kOutput, calls=%fused_computation.20 | convolution fusion | flops 3655335936 | bytes 27918336 | tf_op jit(solution)/shard_map/dot_general | solution.py:385
  302.6 6.3 fusion.56
  308.9 4.0 convolution_convert_fusion.1
  314.8 5.4 fusion.24
  320.3 5.2 convolution_convert_fusion
  332.8 6.1 convolution_add_fusion.2
  341.5 6.1 convolution_add_fusion.1
  347.9 8.4 %convolution_convert_fusion.2 = bf16[1152,1536]{1,0:T(8,128)(2,1)} fusion(bf16[1024,1536]{1,0:T(8,128)(2,1)} %get-tuple-element.148, bf16[512,1152]{0,1:T(8,128)(2,1)S(1)} %copy-done.159, bf16[512,1152]{0,1:T(8,128)(2,1)S(1)} %copy-done.53), kind=kOutput, calls=%fused_computation.16 | convolution fusion | flops 3630366720 | bytes 9043968 | tf_op jit(solution)/shard_map/dot_general | solution.py:76
  356.4 4.7 pad_maximum_fusion.1
  361.1 3.4 constant_dynamic-slice_fusion.3
  364.6 5.8 multiply_reduce_fusion.1
  378.2 3.7 fusion.31
  384.4 9.9 %fusion.179 = f32[16,512,512]{1,2,0:T(8,128)} fusion(bf16[512,16,72]{0,2,1:T(8,128)(2,1)} %bitcast.114, bf16[512,16,72]{0,2,1:T(8,128)(2,1)} %bitcast.143), kind=kOutput, calls=%fused_computation.445 | convolution fusion | flops 603979776 | bytes 19136512 | tf_op jit(solution)/shard_map/qhd,khd->hqk/dot_general | solution.py:450
  394.3 9.6 %fusion.66 = bf16[16,72,512]{2,1,0:T(8,128)(2,1)} fusion(bf16[512,16,72]{0,2,1:T(8,128)(2,1)S(1)} %bitcast.115, f32[16,512,512]{1,2,0:T(8,128)} %get-tuple-element.257, f32[16,512]{1,0:T(8,128)S(1)} %copy-done.81), kind=kOutput, calls=%fused_computation.148 | convolution fusion | flops 612958208 | bytes 19169280 | tf_op jit(solution)/shard_map/hqk,qhd->khd/dot_general | solution.py:447
  403.8 24.8 %fusion.53 = f32[512,16,72]{0,2,1:T(8,128)} fusion(f32[16,512,512]{1,2,0:T(8,128)} %fusion.179, f32[16,512,512]{1,2,0:T(8,128)} %get-tuple-element.257, f32[16,512]{1,0:T(8,128)} %log_add_fusion, bf16[512,16,18]{0,2,1:T(8,128)(2,1)} %copy-done.69, bf16[512,16,18]{0,2,1:T(8,128)(2,1)} %copy-done.68, bf16[512,16,18]{0,2,1:T(8,128)(2,1)} %copy-done.70, ...), kind=kOutput, calls=%fused_computation.137 | convolution fusion | flops 638067200 | bytes 37126144 | tf_op jit(solution)/shard_map/hqk,qhd->khd/dot_general | solution.py:455
  428.6 25.3 %fusion.50 = f32[512,16,72]{0,2,1:T(8,128)} fusion(f32[16,512,512]{1,2,0:T(8,128)} %fusion.179, f32[16,512,512]{1,2,0:T(8,128)} %get-tuple-element.257, f32[16,512]{1,0:T(8,128)} %log_add_fusion, bf16[512,16,18]{0,2,1:T(8,128)(2,1)} %copy-done.73, bf16[512,16,18]{0,2,1:T(8,128)(2,1)} %copy-done.72, bf16[512,16,18]{0,2,1:T(8,128)(2,1)} %copy-done.74, ...), kind=kOutput, calls=%fused_computation.136 | convolution fusion | flops 638067200 | bytes 37126144 | tf_op jit(solution)/shard_map/hqk,khd->qhd/dot_general | solution.py:454
  468.9 2.9 fusion.38
  484.6 5.2 collective-permute-done.45
  489.8 5.3 collective-permute-done.46
  495.1 4.1 collective-permute-done.47
  500.5 4.8 collective-permute-done.48
  507.6 4.0 convolution_convert_fusion.4
  511.6 6.9 collective-permute-done.49
  521.4 2.5 add_convert_fusion
  526.4 48.9 %collective-permute-done.51 = bf16[4,2,1,72,2304]{4,3,2,1,0:T(8,128)(2,1)S(1)} collective-permute-done((bf16[4,2,1,72,2304]{4,3,2,1,0:T(8,128)(2,1)S(1)}, bf16[4,2,1,72,2304]{4,3,2,1,0:T(8,128)(2,1)S(1)}, u32[]{:S(2)}, u32[]{:S(2)}) %collective-permute-start.51) | collective-permute-done | bytes 2654240 | tf_op jit(solution)/shard_map/ppermute | solution.py:169
  578.8 6.7 convolution_convert_fusion.3
  587.5 5.2 copy.116
  592.7 2.5 constant_dynamic-slice_fusion.5
  596.3 3.3 copy.115
  605.6 3.4 collective-permute-done.52
  611.1 2.7 collective-permute-start.56
  614.7 14.8 %collective-permute-done.39 = bf16[4,1,2,72,1152]{4,3,2,1,0:T(8,128)(2,1)} collective-permute-done((bf16[4,1,2,72,1152]{4,3,2,1,0:T(8,128)(2,1)}, bf16[4,1,2,72,1152]{4,3,2,1,0:T(8,128)(2,1)}, u32[]{:S(2)}, u32[]{:S(2)}) %collective-permute-start.39) | collective-permute-done | bytes 1327136 | tf_op jit(solution)/shard_map/ppermute | solution.py:169
  634.7 10.1 %collective-permute-done.56 = bf16[1,1,1,72,4608]{4,3,2,1,0:T(8,128)(2,1)S(1)} collective-permute-done((bf16[1,1,1,72,4608]{4,3,2,1,0:T(8,128)(2,1)S(1)}, bf16[1,1,1,72,4608]{4,3,2,1,0:T(8,128)(2,1)S(1)}, u32[]{:S(2)}, u32[]{:S(2)}) %collective-permute-start.56) | collective-permute-done | bytes 663584 | tf_op jit(solution)/shard_map/ppermute | solution.py:169
  646.4 17.4 %collective-permute-start.41 = (bf16[1,1,1,72,2304]{4,3,2,1,0:T(8,128)(2,1)S(1)}, bf16[1,1,1,72,2304]{4,3,2,1,0:T(8,128)(2,1)S(1)}, u32[]{:S(2)}, u32[]{:S(2)}) collective-permute-start(bf16[1,1,1,72,2304]{4,3,2,1,0:T(8,128)(2,1)S(1)} %get-tuple-element.198), channel_id=1, source_target_pairs={{0,8},{2,10},{4,12},{6,14},{8,16},{10,18},{12,20},{14,22},{16,24},... | collective-permute-start | bytes 995336 | tf_op jit(solution)/shard_map/ppermute | solution.py:169
  663.8 2.6 collective-permute-start.43
  667.4 4.7 collective-permute-done.41
  672.1 8.2 %collective-permute-done.42 = bf16[1,1,1,72,2304]{4,3,2,1,0:T(8,128)(2,1)S(1)} collective-permute-done((bf16[1,1,1,72,2304]{4,3,2,1,0:T(8,128)(2,1)S(1)}, bf16[1,1,1,72,2304]{4,3,2,1,0:T(8,128)(2,1)S(1)}, u32[]{:S(2)}, u32[]{:S(2)}) %collective-permute-start.42) | collective-permute-done | bytes 331808 | tf_op jit(solution)/shard_map/ppermute | solution.py:169
  680.3 4.2 collective-permute-done.43
  700.4 11.5 %collective-permute-start.61 = (f32[]{:T(128)}, f32[]{:T(128)}, u32[]{:S(2)}, u32[]{:S(2)}) collective-permute-start(f32[]{:T(128)} %add.695), channel_id=1, source_target_pairs={{0,24},{2,26},{4,28},{6,30},{8,0},{10,2},{12,4},{14,6},{16,8},{18,... | collective-permute-start | bytes 20 | tf_op jit(solution)/shard_map/ppermute | solution.py:209
  721.8 2.6 multiply_subtract_fusion.3
  (658 shorter events, 208.7 us)
Async XLA Ops:
  5.0 53.9 %collective-permute-start.13 = (bf16[1,1,1,72,2304]{4,3,2,1,0:T(8,128)(2,1)}, bf16[1,1,1,72,2304]{4,3,2,1,0:T(8,128)(2,1)}, u32[]{:S(2)}, u32[]{:S(2)}) collective-permute-start(bf16[1,1,1,72,2304]{4,3,2,1,0:T(8,128)(2,1)} %get-tuple-element.147), channel_id=1, source_target_pairs={{0,8},{2,10},{4,12},{6,14},{8,16},{10,18},{12,20},{14,22},{16,24},... | collective-permute-start | bytes 995336 | tf_op jit(solution)/shard_map/ppermute | solution.py:147
  8.0 52.6 %collective-permute-start.14 = (bf16[1,1,1,72,2304]{4,3,2,1,0:T(8,128)(2,1)}, bf16[1,1,1,72,2304]{4,3,2,1,0:T(8,128)(2,1)}, u32[]{:S(2)}, u32[]{:S(2)}) collective-permute-start(bf16[1,1,1,72,2304]{4,3,2,1,0:T(8,128)(2,1)} %get-tuple-element.147), channel_id=1, source_target_pairs={{0,16},{2,18},{4,20},{6,22},{8,24},{10,26},{12,28},{14,30},{16,0},... | collective-permute-start | bytes 995336 | tf_op jit(solution)/shard_map/ppermute | solution.py:147
  10.6 56.8 %collective-permute-start.15 = (bf16[1,1,1,72,2304]{4,3,2,1,0:T(8,128)(2,1)}, bf16[1,1,1,72,2304]{4,3,2,1,0:T(8,128)(2,1)}, u32[]{:S(2)}, u32[]{:S(2)}) collective-permute-start(bf16[1,1,1,72,2304]{4,3,2,1,0:T(8,128)(2,1)} %get-tuple-element.147), channel_id=1, source_target_pairs={{0,24},{2,26},{4,28},{6,30},{8,0},{10,2},{12,4},{14,6},{16,8},{18,... | collective-permute-start | bytes 995336 | tf_op jit(solution)/shard_map/ppermute | solution.py:147
  12.6 15.1 %collective-permute-start = (s32[2,4]{1,0:T(2,128)}, s32[2,4]{1,0:T(2,128)}, u32[]{:S(2)}, u32[]{:S(2)}) collective-permute-start(s32[2,4]{1,0:T(2,128)} %pad_add_fusion.2), channel_id=1, source_target_pairs={{0,1},{1,0},{2,3},{3,2},{4,5},{5,4},{6,7},{7,6},{8,9},{9,8},{10,11... | collective-permute-start | bytes 104 | tf_op jit(solution)/shard_map/ppermute | solution.py:136
  13.1 41.6 %collective-permute-start.6 = (f32[216]{0:T(256)}, f32[216]{0:T(256)}, u32[]{:S(2)}, u32[]{:S(2)}) collective-permute-start(f32[216]{0:T(256)} %convert_convert_fusion.7), channel_id=1, source_target_pairs={{0,1},{1,0},{2,3},{3,2},{4,5},{5,4},{6,7},{7,6},{8,9},{9,8},{10,11... | collective-permute-start | bytes 2600 | tf_op jit(solution)/shard_map/ppermute | solution.py:136
  28.4 5.4 collective-permute-start.1
  33.7 8.0 %collective-permute-start.2 = (s32[1,1,1,2,8]{4,3,2,1,0:T(2,128)S(1)}, s32[1,1,1,2,8]{4,3,2,1,0:T(2,128)S(1)}, u32[]{:S(2)}, u32[]{:S(2)}) collective-permute-start(s32[1,1,1,2,8]{4,3,2,1,0:T(2,128)S(1)} %fusion.200), channel_id=1, source_target_pairs={{0,16},{2,18},{4,20},{6,22},{8,24},{10,26},{12,28},{14,30},{16,0},... | collective-permute-start | bytes 200 | tf_op jit(solution)/shard_map/ppermute | solution.py:147
  41.7 3.6 collective-permute-start.3
  45.3 3.6 collective-permute-start.4
  48.9 3.7 collective-permute-start.5
  57.3 8.4 %collective-permute-start.7 = (bf16[4,2,1,8,3456]{4,3,2,1,0:T(8,128)(2,1)S(1)}, bf16[4,2,1,8,3456]{4,3,2,1,0:T(8,128)(2,1)S(1)}, u32[]{:S(2)}, u32[]{:S(2)}) collective-permute-start(bf16[4,2,1,8,3456]{4,3,2,1,0:T(8,128)(2,1)S(1)} %dynamic-slice_convert_fusion), channel_id=1, source_target_pairs={{0,2},{2,0},{4,6},{6,4},{8,10},{10,8},{12,14},{14,12},{16,18},{18,... | collective-permute-start | bytes 1327112 | tf_op jit(solution)/shard_map/ppermute | solution.py:169
  65.8 6.3 collective-permute-start.8
  69.1 67.7 %collective-permute-start.20 = (bf16[1,1,1,72,4608]{4,3,2,1,0:T(8,128)(2,1)S(1)}, bf16[1,1,1,72,4608]{4,3,2,1,0:T(8,128)(2,1)S(1)}, u32[]{:S(2)}, u32[]{:S(2)}) collective-permute-start(bf16[1,1,1,72,4608]{4,3,2,1,0:T(8,128)(2,1)S(1)} %bitcast.146), channel_id=1, source_target_pairs={{0,8},{2,10},{4,12},{6,14},{8,16},{10,18},{12,20},{14,22},{16,24},... | collective-permute-start | bytes 1990664 | tf_op jit(solution)/shard_map/ppermute | solution.py:147
  70.6 67.1 %collective-permute-start.21 = (bf16[1,1,1,72,4608]{4,3,2,1,0:T(8,128)(2,1)S(1)}, bf16[1,1,1,72,4608]{4,3,2,1,0:T(8,128)(2,1)S(1)}, u32[]{:S(2)}, u32[]{:S(2)}) collective-permute-start(bf16[1,1,1,72,4608]{4,3,2,1,0:T(8,128)(2,1)S(1)} %bitcast.147), channel_id=1, source_target_pairs={{0,16},{2,18},{4,20},{6,22},{8,24},{10,26},{12,28},{14,30},{16,0},... | collective-permute-start | bytes 1990664 | tf_op jit(solution)/shard_map/ppermute | solution.py:147
  72.2 40.6 %collective-permute-start.10 = (bf16[1,1,1,8,3456]{4,3,2,1,0:T(8,128)(2,1)S(1)}, bf16[1,1,1,8,3456]{4,3,2,1,0:T(8,128)(2,1)S(1)}, u32[]{:S(2)}, u32[]{:S(2)}) collective-permute-start(bf16[1,1,1,8,3456]{4,3,2,1,0:T(8,128)(2,1)S(1)} %get-tuple-element.227), channel_id=1, source_target_pairs={{0,16},{2,18},{4,20},{6,22},{8,24},{10,26},{12,28},{14,30},{16,0},... | collective-permute-start | bytes 165896 | tf_op jit(solution)/shard_map/ppermute | solution.py:169
  74.9 40.3 %collective-permute-start.11 = (bf16[1,1,1,8,3456]{4,3,2,1,0:T(8,128)(2,1)S(1)}, bf16[1,1,1,8,3456]{4,3,2,1,0:T(8,128)(2,1)S(1)}, u32[]{:S(2)}, u32[]{:S(2)}) collective-permute-start(bf16[1,1,1,8,3456]{4,3,2,1,0:T(8,128)(2,1)S(1)} %get-tuple-element.226), channel_id=1, source_target_pairs={{0,24},{2,26},{4,28},{6,30},{8,0},{10,2},{12,4},{14,6},{16,8},{18,... | collective-permute-start | bytes 165896 | tf_op jit(solution)/shard_map/ppermute | solution.py:169
  76.0 39.1 %collective-permute-start.9 = (bf16[1,1,1,8,3456]{4,3,2,1,0:T(8,128)(2,1)S(1)}, bf16[1,1,1,8,3456]{4,3,2,1,0:T(8,128)(2,1)S(1)}, u32[]{:S(2)}, u32[]{:S(2)}) collective-permute-start(bf16[1,1,1,8,3456]{4,3,2,1,0:T(8,128)(2,1)S(1)} %get-tuple-element.225), channel_id=1, source_target_pairs={{0,8},{2,10},{4,12},{6,14},{8,16},{10,18},{12,20},{14,22},{16,24},... | collective-permute-start | bytes 165896 | tf_op jit(solution)/shard_map/ppermute | solution.py:169
  112.8 24.9 %collective-permute-start.22 = (bf16[1,1,1,72,4608]{4,3,2,1,0:T(8,128)(2,1)S(1)}, bf16[1,1,1,72,4608]{4,3,2,1,0:T(8,128)(2,1)S(1)}, u32[]{:S(2)}, u32[]{:S(2)}) collective-permute-start(bf16[1,1,1,72,4608]{4,3,2,1,0:T(8,128)(2,1)S(1)} %bitcast.148), channel_id=1, source_target_pairs={{0,24},{2,26},{4,28},{6,30},{8,0},{10,2},{12,4},{14,6},{16,8},{18,... | collective-permute-start | bytes 1990664 | tf_op jit(solution)/shard_map/ppermute | solution.py:147
  115.2 3.4 collective-permute-start.12
  117.1 17.4 %collective-permute-start.18 = (bf16[4,1,1,72,1152]{4,3,2,1,0:T(8,128)(2,1)S(1)}, bf16[4,1,1,72,1152]{4,3,2,1,0:T(8,128)(2,1)S(1)}, u32[]{:S(2)}, u32[]{:S(2)}) collective-permute-start(bf16[4,1,1,72,1152]{4,3,2,1,0:T(8,128)(2,1)S(1)} %get-tuple-element.201), channel_id=1, source_target_pairs={{0,2},{2,0},{4,6},{6,4},{8,10},{10,8},{12,14},{14,12},{16,18},{18,... | collective-permute-start | bytes 1990664 | tf_op jit(solution)/shard_map/ppermute | solution.py:147
  118.7 17.0 %collective-permute-start.16 = (bf16[4,1,1,72,1152]{4,3,2,1,0:T(8,128)(2,1)S(1)}, bf16[4,1,1,72,1152]{4,3,2,1,0:T(8,128)(2,1)S(1)}, u32[]{:S(2)}, u32[]{:S(2)}) collective-permute-start(bf16[4,1,1,72,1152]{4,3,2,1,0:T(8,128)(2,1)S(1)} %get-tuple-element.204), channel_id=1, source_target_pairs={{0,4},{2,6},{4,0},{6,2},{8,12},{10,14},{12,8},{14,10},{16,20},{18,... | collective-permute-start | bytes 1990664 | tf_op jit(solution)/shard_map/ppermute | solution.py:147
  134.6 30.8 %collective-permute-start.19 = (bf16[4,1,2,72,1152]{4,3,2,1,0:T(8,128)(2,1)S(1)}, bf16[4,1,2,72,1152]{4,3,2,1,0:T(8,128)(2,1)S(1)}, u32[]{:S(2)}, u32[]{:S(2)}) collective-permute-start(bf16[4,1,2,72,1152]{4,3,2,1,0:T(8,128)(2,1)S(1)} %constant_dynamic-update-slice_fusion.22), channel_id=1, source_target_pairs={{0,4},{2,6},{4,0},{6,2},{8,12},{10,14},{12,8},{14,10},{16,20},{18,... | collective-permute-start | bytes 3981320 | tf_op jit(solution)/shard_map/ppermute | solution.py:147
  135.8 30.5 %collective-permute-start.17 = (bf16[4,2,1,72,1152]{4,3,2,1,0:T(8,128)(2,1)S(1)}, bf16[4,2,1,72,1152]{4,3,2,1,0:T(8,128)(2,1)S(1)}, u32[]{:S(2)}, u32[]{:S(2)}) collective-permute-start(bf16[4,2,1,72,1152]{4,3,2,1,0:T(8,128)(2,1)S(1)} %constant_dynamic-update-slice_fusion.26), channel_id=1, source_target_pairs={{0,2},{2,0},{4,6},{6,4},{8,10},{10,8},{12,14},{14,12},{16,18},{18,... | collective-permute-start | bytes 3981320 | tf_op jit(solution)/shard_map/ppermute | solution.py:147
  171.9 29.8 %collective-permute-start.26 = (bf16[4,1,1,72,2304]{4,3,2,1,0:T(8,128)(2,1)S(1)}, bf16[4,1,1,72,2304]{4,3,2,1,0:T(8,128)(2,1)S(1)}, u32[]{:S(2)}, u32[]{:S(2)}) collective-permute-start(bf16[4,1,1,72,2304]{4,3,2,1,0:T(8,128)(2,1)S(1)} %get-tuple-element.172), channel_id=1, source_target_pairs={{0,4},{2,6},{4,0},{6,2},{8,12},{10,14},{12,8},{14,10},{16,20},{18,... | collective-permute-start | bytes 3981320 | tf_op jit(solution)/shard_map/ppermute | solution.py:147
  173.6 41.6 %collective-permute-start.23 = (bf16[1152,1152]{1,0:T(8,128)(2,1)S(1)}, bf16[1152,1152]{1,0:T(8,128)(2,1)S(1)}, u32[]{:S(2)}, u32[]{:S(2)}) collective-permute-start(bf16[1152,1152]{1,0:T(8,128)(2,1)S(1)} %bitcast.154), channel_id=1, source_target_pairs={{0,1},{1,0},{2,3},{3,2},{4,5},{5,4},{6,7},{7,6},{8,9},{9,8},{10,11... | collective-permute-start | bytes 7962632 | tf_op jit(solution)/shard_map/ppermute | solution.py:136
  173.7 43.8 %collective-permute-start.24 = (bf16[1152,1152]{1,0:T(8,128)(2,1)S(1)}, bf16[1152,1152]{1,0:T(8,128)(2,1)S(1)}, u32[]{:S(2)}, u32[]{:S(2)}) collective-permute-start(bf16[1152,1152]{1,0:T(8,128)(2,1)S(1)} %bitcast.149), channel_id=1, source_target_pairs={{0,1},{1,0},{2,3},{3,2},{4,5},{5,4},{6,7},{7,6},{8,9},{9,8},{10,11... | collective-permute-start | bytes 7962632 | tf_op jit(solution)/shard_map/ppermute | solution.py:136
  174.2 32.0 %collective-permute-start.28 = (bf16[4,1,1,72,2304]{4,3,2,1,0:T(8,128)(2,1)S(1)}, bf16[4,1,1,72,2304]{4,3,2,1,0:T(8,128)(2,1)S(1)}, u32[]{:S(2)}, u32[]{:S(2)}) collective-permute-start(bf16[4,1,1,72,2304]{4,3,2,1,0:T(8,128)(2,1)S(1)} %get-tuple-element.175), channel_id=1, source_target_pairs={{0,2},{2,0},{4,6},{6,4},{8,10},{10,8},{12,14},{14,12},{16,18},{18,... | collective-permute-start | bytes 3981320 | tf_op jit(solution)/shard_map/ppermute | solution.py:147
  178.7 399.7 %collective-permute-start.33 = (bf16[512,1152]{0,1:T(8,128)(2,1)}, bf16[512,1152]{0,1:T(8,128)(2,1)}, u32[]{:S(2)}, u32[]{:S(2)}) collective-permute-start(bf16[512,1152]{0,1:T(8,128)(2,1)} %fusion.35), channel_id=1, source_target_pairs={{0,1},{1,0},{2,3},{3,2},{4,5},{5,4},{6,7},{7,6},{8,9},{9,8},{10,11... | collective-permute-start | bytes 3538952 | tf_op jit(solution)/shard_map/ppermute | solution.py:136
  202.8 64.7 %collective-permute-start.27 = (bf16[4,2,1,72,2304]{4,3,2,1,0:T(8,128)(2,1)}, bf16[4,2,1,72,2304]{4,3,2,1,0:T(8,128)(2,1)}, u32[]{:S(2)}, u32[]{:S(2)}) collective-permute-start(bf16[4,2,1,72,2304]{4,3,2,1,0:T(8,128)(2,1)} %constant_dynamic-update-slice_fusion.14), channel_id=1, source_target_pairs={{0,2},{2,0},{4,6},{6,4},{8,10},{10,8},{12,14},{14,12},{16,18},{18,... | collective-permute-start | bytes 7962632 | tf_op jit(solution)/shard_map/ppermute | solution.py:147
  207.4 62.5 %collective-permute-start.29 = (bf16[4,1,2,72,2304]{4,3,2,1,0:T(8,128)(2,1)}, bf16[4,1,2,72,2304]{4,3,2,1,0:T(8,128)(2,1)}, u32[]{:S(2)}, u32[]{:S(2)}) collective-permute-start(bf16[4,1,2,72,2304]{4,3,2,1,0:T(8,128)(2,1)} %constant_dynamic-update-slice_fusion.10), channel_id=1, source_target_pairs={{0,4},{2,6},{4,0},{6,2},{8,12},{10,14},{12,8},{14,10},{16,20},{18,... | collective-permute-start | bytes 7962632 | tf_op jit(solution)/shard_map/ppermute | solution.py:147
  258.2 248.6 %collective-permute-start.37 = (bf16[512,1152]{0,1:T(8,128)(2,1)}, bf16[512,1152]{0,1:T(8,128)(2,1)}, u32[]{:S(2)}, u32[]{:S(2)}) collective-permute-start(bf16[512,1152]{0,1:T(8,128)(2,1)} %bitcast.24), channel_id=1, source_target_pairs={{0,1},{1,0},{2,3},{3,2},{4,5},{5,4},{6,7},{7,6},{8,9},{9,8},{10,11... | collective-permute-start | bytes 3538952 | tf_op jit(solution)/shard_map/ppermute | solution.py:136
  264.1 9.7 %collective-permute-start.31 = (bf16[512,1152]{0,1:T(8,128)(2,1)S(1)}, bf16[512,1152]{0,1:T(8,128)(2,1)S(1)}, u32[]{:S(2)}, u32[]{:S(2)}) collective-permute-start(bf16[512,1152]{0,1:T(8,128)(2,1)S(1)} %get-tuple-element.246), channel_id=1, source_target_pairs={{0,1},{1,0},{2,3},{3,2},{4,5},{5,4},{6,7},{7,6},{8,9},{9,8},{10,11... | collective-permute-start | bytes 3538952 | tf_op jit(solution)/shard_map/ppermute | solution.py:136
  267.6 14.2 %collective-permute-start.25 = (bf16[512,1152]{0,1:T(8,128)(2,1)S(1)}, bf16[512,1152]{0,1:T(8,128)(2,1)S(1)}, u32[]{:S(2)}, u32[]{:S(2)}) collective-permute-start(bf16[512,1152]{0,1:T(8,128)(2,1)S(1)} %add_convert_fusion.8), channel_id=1, source_target_pairs={{0,1},{1,0},{2,3},{3,2},{4,5},{5,4},{6,7},{7,6},{8,9},{9,8},{10,11... | collective-permute-start | bytes 3538952 | tf_op jit(solution)/shard_map/ppermute | solution.py:136
  331.8 189.6 %collective-permute-start.53 = (bf16[4,1,2,72,2304]{4,3,2,1,0:T(8,128)(2,1)}, bf16[4,1,2,72,2304]{4,3,2,1,0:T(8,128)(2,1)}, u32[]{:S(2)}, u32[]{:S(2)}) collective-permute-start(bf16[4,1,2,72,2304]{4,3,2,1,0:T(8,128)(2,1)} %constant_dynamic-slice_fusion.1), channel_id=1, source_target_pairs={{0,4},{2,6},{4,0},{6,2},{8,12},{10,14},{12,8},{14,10},{16,20},{18,... | collective-permute-start | bytes 7962632 | tf_op jit(solution)/shard_map/ppermute | solution.py:169
  340.3 24.2 %collective-permute-start.30 = (bf16[512,1152]{0,1:T(8,128)(2,1)}, bf16[512,1152]{0,1:T(8,128)(2,1)S(1)}, u32[]{:S(2)}, u32[]{:S(2)}) collective-permute-start(bf16[512,1152]{0,1:T(8,128)(2,1)} %slice.569), channel_id=1, source_target_pairs={{0,1},{1,0},{2,3},{3,2},{4,5},{5,4},{6,7},{7,6},{8,9},{9,8},{10,11... | collective-permute-start | bytes 3538952 | tf_op jit(solution)/shard_map/ppermute | solution.py:136
  347.8 16.8 %collective-permute-start.32 = (bf16[512,1152]{0,1:T(8,128)(2,1)S(1)}, bf16[512,1152]{0,1:T(8,128)(2,1)S(1)}, u32[]{:S(2)}, u32[]{:S(2)}) collective-permute-start(bf16[512,1152]{0,1:T(8,128)(2,1)S(1)} %slice.568), channel_id=1, source_target_pairs={{0,1},{1,0},{2,3},{3,2},{4,5},{5,4},{6,7},{7,6},{8,9},{9,8},{10,11... | collective-permute-start | bytes 3538952 | tf_op jit(solution)/shard_map/ppermute | solution.py:136
  472.7 34.9 %collective-permute-start.38 = (bf16[512,576]{0,1:T(8,128)(2,1)}, bf16[512,576]{0,1:T(8,128)(2,1)}, u32[]{:S(2)}, u32[]{:S(2)}) collective-permute-start(bf16[512,576]{0,1:T(8,128)(2,1)} %get-tuple-element.213), channel_id=1, source_target_pairs={{0,1},{1,0},{2,3},{3,2},{4,5},{5,4},{6,7},{7,6},{8,9},{9,8},{10,11... | collective-permute-start | bytes 1769480 | tf_op jit(solution)/shard_map/ppermute | solution.py:136
  476.8 5.8 collective-permute-start.44
  483.6 6.2 collective-permute-start.45
  489.8 5.3 collective-permute-start.46
  495.1 4.2 collective-permute-start.47
  499.3 6.0 collective-permute-start.48
  505.3 13.2 %collective-permute-start.49 = (bf16[4,2,1,8,3456]{4,3,2,1,0:T(8,128)(2,1)S(1)}, bf16[4,2,1,8,3456]{4,3,2,1,0:T(8,128)(2,1)S(1)}, u32[]{:S(2)}, u32[]{:S(2)}) collective-permute-start(bf16[4,2,1,8,3456]{4,3,2,1,0:T(8,128)(2,1)S(1)} %constant_dynamic-update-slice_fusion.2), channel_id=1, source_target_pairs={{0,2},{2,0},{4,6},{6,4},{8,10},{10,8},{12,14},{14,12},{16,18},{18,... | collective-permute-start | bytes 1327112 | tf_op jit(solution)/shard_map/ppermute | solution.py:147
  506.8 68.5 %collective-permute-start.51 = (bf16[4,2,1,72,2304]{4,3,2,1,0:T(8,128)(2,1)S(1)}, bf16[4,2,1,72,2304]{4,3,2,1,0:T(8,128)(2,1)S(1)}, u32[]{:S(2)}, u32[]{:S(2)}) collective-permute-start(bf16[4,2,1,72,2304]{4,3,2,1,0:T(8,128)(2,1)S(1)} %copy-done.38), channel_id=1, source_target_pairs={{0,2},{2,0},{4,6},{6,4},{8,10},{10,8},{12,14},{14,12},{16,18},{18,... | collective-permute-start | bytes 7962632 | tf_op jit(solution)/shard_map/ppermute | solution.py:169
  507.6 70.7 %collective-permute-start.34 = (bf16[512,1728]{0,1:T(8,128)(2,1)S(1)}, bf16[512,1728]{0,1:T(8,128)(2,1)S(1)}, u32[]{:S(2)}, u32[]{:S(2)}) collective-permute-start(bf16[512,1728]{0,1:T(8,128)(2,1)S(1)} %copy-done.49), channel_id=1, source_target_pairs={{0,1},{1,0},{2,3},{3,2},{4,5},{5,4},{6,7},{7,6},{8,9},{9,8},{10,11... | collective-permute-start | bytes 5308424 | tf_op jit(solution)/shard_map/ppermute | solution.py:136
  518.7 2.0 collective-permute-start.50
  525.1 78.8 %collective-permute-start.54 = (bf16[4,1,1,72,2304]{4,3,2,1,0:T(8,128)(2,1)}, bf16[4,1,1,72,2304]{4,3,2,1,0:T(8,128)(2,1)}, u32[]{:S(2)}, u32[]{:S(2)}) collective-permute-start(bf16[4,1,1,72,2304]{4,3,2,1,0:T(8,128)(2,1)} %constant_dynamic-slice_fusion), channel_id=1, source_target_pairs={{0,2},{2,0},{4,6},{6,4},{8,10},{10,8},{12,14},{14,12},{16,18},{18,... | collective-permute-start | bytes 3981320 | tf_op jit(solution)/shard_map/ppermute | solution.py:169
  577.3 31.7 %collective-permute-start.52 = (bf16[4,1,1,72,2304]{4,3,2,1,0:T(8,128)(2,1)}, bf16[4,1,1,72,2304]{4,3,2,1,0:T(8,128)(2,1)}, u32[]{:S(2)}, u32[]{:S(2)}) collective-permute-start(bf16[4,1,1,72,2304]{4,3,2,1,0:T(8,128)(2,1)} %constant_dynamic-slice_fusion.2), channel_id=1, source_target_pairs={{0,4},{2,6},{4,0},{6,2},{8,12},{10,14},{12,8},{14,10},{16,20},{18,... | collective-permute-start | bytes 3981320 | tf_op jit(solution)/shard_map/ppermute | solution.py:169
  595.2 34.4 %collective-permute-start.39 = (bf16[4,1,2,72,1152]{4,3,2,1,0:T(8,128)(2,1)}, bf16[4,1,2,72,1152]{4,3,2,1,0:T(8,128)(2,1)}, u32[]{:S(2)}, u32[]{:S(2)}) collective-permute-start(bf16[4,1,2,72,1152]{4,3,2,1,0:T(8,128)(2,1)} %constant_dynamic-slice_fusion.5), channel_id=1, source_target_pairs={{0,4},{2,6},{4,0},{6,2},{8,12},{10,14},{12,8},{14,10},{16,20},{18,... | collective-permute-start | bytes 3981320 | tf_op jit(solution)/shard_map/ppermute | solution.py:169
  601.2 31.9 %collective-permute-start.35 = (bf16[4,2,1,72,1152]{4,3,2,1,0:T(8,128)(2,1)S(1)}, bf16[4,2,1,72,1152]{4,3,2,1,0:T(8,128)(2,1)S(1)}, u32[]{:S(2)}, u32[]{:S(2)}) collective-permute-start(bf16[4,2,1,72,1152]{4,3,2,1,0:T(8,128)(2,1)S(1)} %constant_dynamic-slice_fusion.7), channel_id=1, source_target_pairs={{0,2},{2,0},{4,6},{6,4},{8,10},{10,8},{12,14},{14,12},{16,18},{18,... | collective-permute-start | bytes 3981320 | tf_op jit(solution)/shard_map/ppermute | solution.py:169
  610.9 23.9 %collective-permute-start.55 = (bf16[1,1,1,72,4608]{4,3,2,1,0:T(8,128)(2,1)S(1)}, bf16[1,1,1,72,4608]{4,3,2,1,0:T(8,128)(2,1)S(1)}, u32[]{:S(2)}, u32[]{:S(2)}) collective-permute-start(bf16[1,1,1,72,4608]{4,3,2,1,0:T(8,128)(2,1)S(1)} %get-tuple-element.169), channel_id=1, source_target_pairs={{0,8},{2,10},{4,12},{6,14},{8,16},{10,18},{12,20},{14,22},{16,24},... | collective-permute-start | bytes 1990664 | tf_op jit(solution)/shard_map/ppermute | solution.py:169
  611.1 33.7 %collective-permute-start.56 = (bf16[1,1,1,72,4608]{4,3,2,1,0:T(8,128)(2,1)S(1)}, bf16[1,1,1,72,4608]{4,3,2,1,0:T(8,128)(2,1)S(1)}, u32[]{:S(2)}, u32[]{:S(2)}) collective-permute-start(bf16[1,1,1,72,4608]{4,3,2,1,0:T(8,128)(2,1)S(1)} %get-tuple-element.170), channel_id=1, source_target_pairs={{0,16},{2,18},{4,20},{6,22},{8,24},{10,26},{12,28},{14,30},{16,0},... | collective-permute-start | bytes 1990664 | tf_op jit(solution)/shard_map/ppermute | solution.py:169
  613.8 31.0 %collective-permute-start.57 = (bf16[1,1,1,72,4608]{4,3,2,1,0:T(8,128)(2,1)S(1)}, bf16[1,1,1,72,4608]{4,3,2,1,0:T(8,128)(2,1)S(1)}, u32[]{:S(2)}, u32[]{:S(2)}) collective-permute-start(bf16[1,1,1,72,4608]{4,3,2,1,0:T(8,128)(2,1)S(1)} %get-tuple-element.171), channel_id=1, source_target_pairs={{0,24},{2,26},{4,28},{6,30},{8,0},{10,2},{12,4},{14,6},{16,8},{18,... | collective-permute-start | bytes 1990664 | tf_op jit(solution)/shard_map/ppermute | solution.py:169
  631.3 14.6 %collective-permute-start.40 = (bf16[4,1,1,72,1152]{4,3,2,1,0:T(8,128)(2,1)S(1)}, bf16[4,1,1,72,1152]{4,3,2,1,0:T(8,128)(2,1)S(1)}, u32[]{:S(2)}, u32[]{:S(2)}) collective-permute-start(bf16[4,1,1,72,1152]{4,3,2,1,0:T(8,128)(2,1)S(1)} %constant_dynamic-slice_fusion.4), channel_id=1, source_target_pairs={{0,2},{2,0},{4,6},{6,4},{8,10},{10,8},{12,14},{14,12},{16,18},{18,... | collective-permute-start | bytes 1990664 | tf_op jit(solution)/shard_map/ppermute | solution.py:169
  633.6 12.5 %collective-permute-start.36 = (bf16[4,1,1,72,1152]{4,3,2,1,0:T(8,128)(2,1)S(1)}, bf16[4,1,1,72,1152]{4,3,2,1,0:T(8,128)(2,1)S(1)}, u32[]{:S(2)}, u32[]{:S(2)}) collective-permute-start(bf16[4,1,1,72,1152]{4,3,2,1,0:T(8,128)(2,1)S(1)} %constant_dynamic-slice_fusion.6), channel_id=1, source_target_pairs={{0,4},{2,6},{4,0},{6,2},{8,12},{10,14},{12,8},{14,10},{16,20},{18,... | collective-permute-start | bytes 1990664 | tf_op jit(solution)/shard_map/ppermute | solution.py:169
  646.4 25.6 %collective-permute-start.41 = (bf16[1,1,1,72,2304]{4,3,2,1,0:T(8,128)(2,1)S(1)}, bf16[1,1,1,72,2304]{4,3,2,1,0:T(8,128)(2,1)S(1)}, u32[]{:S(2)}, u32[]{:S(2)}) collective-permute-start(bf16[1,1,1,72,2304]{4,3,2,1,0:T(8,128)(2,1)S(1)} %get-tuple-element.198), channel_id=1, source_target_pairs={{0,8},{2,10},{4,12},{6,14},{8,16},{10,18},{12,20},{14,22},{16,24},... | collective-permute-start | bytes 995336 | tf_op jit(solution)/shard_map/ppermute | solution.py:169
  663.8 16.4 %collective-permute-start.42 = (bf16[1,1,1,72,2304]{4,3,2,1,0:T(8,128)(2,1)S(1)}, bf16[1,1,1,72,2304]{4,3,2,1,0:T(8,128)(2,1)S(1)}, u32[]{:S(2)}, u32[]{:S(2)}) collective-permute-start(bf16[1,1,1,72,2304]{4,3,2,1,0:T(8,128)(2,1)S(1)} %get-tuple-element.199), channel_id=1, source_target_pairs={{0,16},{2,18},{4,20},{6,22},{8,24},{10,26},{12,28},{14,30},{16,0},... | collective-permute-start | bytes 995336 | tf_op jit(solution)/shard_map/ppermute | solution.py:169
  663.8 20.6 %collective-permute-start.43 = (bf16[1,1,1,72,2304]{4,3,2,1,0:T(8,128)(2,1)S(1)}, bf16[1,1,1,72,2304]{4,3,2,1,0:T(8,128)(2,1)S(1)}, u32[]{:S(2)}, u32[]{:S(2)}) collective-permute-start(bf16[1,1,1,72,2304]{4,3,2,1,0:T(8,128)(2,1)S(1)} %get-tuple-element.200), channel_id=1, source_target_pairs={{0,24},{2,26},{4,28},{6,30},{8,0},{10,2},{12,4},{14,6},{16,8},{18,... | collective-permute-start | bytes 995336 | tf_op jit(solution)/shard_map/ppermute | solution.py:169
  689.9 1.3 collective-permute-start.58
  691.8 3.7 collective-permute-start.59
  696.1 3.7 collective-permute-start.60
  700.4 14.7 %collective-permute-start.61 = (f32[]{:T(128)}, f32[]{:T(128)}, u32[]{:S(2)}, u32[]{:S(2)}) collective-permute-start(f32[]{:T(128)} %add.695), channel_id=1, source_target_pairs={{0,24},{2,26},{4,28},{6,30},{8,0},{10,2},{12,4},{14,6},{16,8},{18,... | collective-permute-start | bytes 20 | tf_op jit(solution)/shard_map/ppermute | solution.py:209
  711.9 4.4 collective-permute-start.62
  713.2 5.4 collective-permute-start.63
  (182 other events, 2079.3 us)

commit v2 on v0

v2 whole, which is shorter than its diff:
```python
import jax
import jax.numpy as jnp
from jax import lax
from jax.experimental import pallas as pl
from jax.experimental.pallas import tpu as pltpu
from jax.experimental.layout import Layout, with_layout_constraint
from jax.sharding import PartitionSpec as P

HEADS = 16
HEAD = 72
SLOTS = 4
STEP = 10


BETA_ONE = 0.9
BETA_TWO = 0.95
ADAM_EPS = 1e-08
RATE = 0.08
DECAY = 0.01
CLIP_NORM = 1.0
NORM_EPS = 1e-06
MASKED = -1e30
HIGH = lax.Precision.HIGHEST


def layer_norm(value):
    centered = value - jnp.mean(value, axis=-1, keepdims=True)
    spread = jnp.mean(centered * centered, axis=-1, keepdims=True)
    return centered * lax.rsqrt(spread + NORM_EPS)


def modulate(value, shift, scale):
    return layer_norm(value) * (1.0 + scale) + shift


def geometry(height, width, count):
    lengths = height * width
    ends = jnp.cumsum(lengths)
    starts = ends - lengths
    places = jnp.arange(count, dtype=jnp.int32)
    segment = jnp.sum((places[:, None] >= ends[None, :]).astype(jnp.int32), axis=1)
    member = segment[:, None] == jnp.arange(height.shape[0], dtype=jnp.int32)[None, :]
    start_tok = jnp.sum(jnp.where(member, starts[None, :], 0), axis=1)
    width_tok = jnp.maximum(jnp.sum(jnp.where(member, width[None, :], 0), axis=1), 1)
    offset = places - start_tok
    return (segment, member.astype(jnp.float32), offset // width_tok, offset % width_tok)


def across(left, right, precision=None):
    return lax.dot_general(
        left,
        right,
        (((0,), (0,)), ((), ())),
        preferred_element_type=jnp.float32,
        precision=precision,
    )


def against(left, right):
    return lax.dot_general(
        left, right, (((1,), (1,)), ((), ())), preferred_element_type=jnp.float32
    )


def adam(weight, mean, square, grad):
    mean_new = BETA_ONE * mean + (1.0 - BETA_ONE) * grad
    square_new = BETA_TWO * square + (1.0 - BETA_TWO) * grad * grad
    fixed_mean = mean_new / (1.0 - BETA_ONE**STEP)
    fixed_square = square_new / (1.0 - BETA_TWO**STEP)
    weight_new = weight - RATE * (fixed_mean / (jnp.sqrt(fixed_square) + ADAM_EPS) + DECAY * weight)
    return (mean_new, square_new, weight_new)


BITS = {16: ((3, 2), ((0,), (1,))), 128: ((2, 1, 0), ((3, 4), (5, 6)))}


def orders(count):
    first, (one, two) = BITS[count]
    return first, one + two, two + one


def bit_of(bit):
    return (lax.axis_index("tok") >> bit) & 1


def trade(value, bit, count):
    return lax.ppermute(value, "tok", [(place, place ^ (1 << bit)) for place in range(count)])


def axis_of(bit, count):
    return count.bit_length() - 2 - bit


def swap(value):
    return lax.ppermute(value, "mlp", [(0, 1), (1, 0)])


def swap_rows(value, count):
    blocks = value.reshape((2,) * (count.bit_length() - 1) + (-1, value.shape[-1]))
    return swap(blocks).reshape(value.shape)


def split_rows(value, count):
    axes = (2,) * (count.bit_length() - 1)
    return value.reshape(*axes, value.shape[0] // count, value.shape[1])


def put(out, value, places, count):
    start = [0] * out.ndim
    for axis, place in places.items():
        start[axis] = place
    return lax.dynamic_update_slice(out, value, tuple(start))


def doubled(value, bit, count):
    axis = axis_of(bit, count)
    out = jnp.concatenate([value, value], axis=axis)
    return put(out, trade(value, bit, count), {axis: 1 - bit_of(bit)}, count)


SCORE_SCALE = HEAD ** (-0.5)


def cost(micros):
    return pl.CostEstimate(flops=int(micros * 0.460e9), bytes_accessed=1000, transcendentals=0)


def turn(value, cosine, up, down):
    quarter = HEAD // 4
    above = pltpu.roll(value, HEAD - quarter, 0)
    below = pltpu.roll(value, quarter, 0)
    return value * cosine + above * up + below * down


def dots(left, right, left_axis, right_axis):
    return lax.dot_general(
        left,
        right,
        (((left_axis,), (right_axis,)), ((), ())),
        preferred_element_type=jnp.float32,
    )


def attend_kernel(
    q_ref, k_ref, v_ref, cos_ref, up_ref, down_ref, row_ref, col_ref,
    out_ref, log_ref, q_out, k_out, v_out,
):
    cosine, up, down = cos_ref[...], up_ref[...], down_ref[...]
    query = turn(q_ref[0, 0], cosine, up, down).astype(jnp.bfloat16)
    key = turn(k_ref[0, 0], cosine, up, down).astype(jnp.bfloat16)
    value = v_ref[0, 0].astype(jnp.bfloat16)
    q_out[0], k_out[0], v_out[0] = query, key, value
    scores = dots(key, query, 0, 0) * SCORE_SCALE
    scores = jnp.where(col_ref[...] == row_ref[...], scores, MASKED)
    top = jnp.max(scores, axis=0, keepdims=True)
    weights = jnp.exp(scores - top)
    total = jnp.sum(weights, axis=0, keepdims=True)
    mixed = dots(value, weights.astype(jnp.bfloat16), 1, 0)
    out_ref[0] = (mixed * (1.0 / total)).astype(jnp.bfloat16)
    log_ref[0] = top + jnp.log(total)


def whole(value):
    return pl.BlockSpec(value.shape, lambda i: (0,) * value.ndim)


def attend(mixed, tables):
    _, heads, _, tokens = mixed.shape

    def part(place):
        return pl.BlockSpec((1, 1, HEAD, tokens), lambda i: (place, i, 0, 0))

    block = pl.BlockSpec((1, HEAD, tokens), lambda i: (i, 0, 0))
    line = pl.BlockSpec((1, 1, tokens), lambda i: (i, 0, 0))
    shape = jax.ShapeDtypeStruct((heads, HEAD, tokens), jnp.bfloat16)
    return pl.pallas_call(
        attend_kernel,
        grid=(heads,),
        in_specs=[part(0), part(1), part(2)] + [whole(value) for value in tables],
        out_specs=[block, line, block, block, block],
        out_shape=[
            shape,
            jax.ShapeDtypeStruct((heads, 1, tokens), jnp.float32),
            shape,
            shape,
            shape,
        ],
        compiler_params=pltpu.CompilerParams(vmem_limit_bytes=32 << 20),
        cost_estimate=cost(6),
        name="attend",
    )(mixed, mixed, mixed, *tables)


def attend_back_kernel(
    q_ref, k_ref, v_ref, g_ref, log_ref, cos_ref, up_ref, down_ref, row_ref, col_ref, out_ref
):
    query, key, value, grad = q_ref[0], k_ref[0], v_ref[0], g_ref[0]
    scores = dots(key, query, 0, 0) * SCORE_SCALE
    scores = jnp.where(col_ref[...] == row_ref[...], scores, MASKED)
    probs = jnp.exp(scores - log_ref[0])
    d_probs = dots(value, grad, 0, 0)
    inner = jnp.sum(probs * d_probs, axis=0, keepdims=True)
    d_scores = (probs * (d_probs - inner) * SCORE_SCALE).astype(jnp.bfloat16)
    d_value = dots(grad, probs.astype(jnp.bfloat16), 1, 1)
    d_key = dots(query, d_scores, 1, 1)
    d_query = dots(key, d_scores, 1, 0)
    cosine, up, down = cos_ref[...], -up_ref[...], -down_ref[...]
    out_ref[0, 0] = turn(d_query, cosine, up, down).astype(jnp.bfloat16)
    out_ref[1, 0] = turn(d_key, cosine, up, down).astype(jnp.bfloat16)
    out_ref[2, 0] = d_value.astype(jnp.bfloat16)


def attend_back(query, key, value, grad, logs, tables):
    heads, _, tokens = query.shape
    block = pl.BlockSpec((1, HEAD, tokens), lambda i: (i, 0, 0))
    line = pl.BlockSpec((1, 1, tokens), lambda i: (i, 0, 0))
    return pl.pallas_call(
        attend_back_kernel,
        grid=(heads,),
        in_specs=[block] * 4 + [line] + [whole(item) for item in tables],
        out_specs=pl.BlockSpec((3, 1, HEAD, tokens), lambda i: (0, i, 0, 0)),
        out_shape=jax.ShapeDtypeStruct((3, heads, HEAD, tokens), jnp.bfloat16),
        compiler_params=pltpu.CompilerParams(vmem_limit_bytes=32 << 20),
        cost_estimate=cost(10),
        name="attend_back",
    )(query, key, value, grad, logs, *tables)


def turn_tables(rows, cols):
    quarter = HEAD // 4
    freq = 10000.0 ** (-jnp.arange(quarter, dtype=jnp.float32) / quarter)
    row_angle = freq[:, None] * rows.astype(jnp.float32)[None, :]
    col_angle = freq[:, None] * cols.astype(jnp.float32)[None, :]
    zero = jnp.zeros_like(row_angle)
    cosine = jnp.concatenate([jnp.cos(row_angle)] * 2 + [jnp.cos(col_angle)] * 2, axis=0)
    up = jnp.concatenate([-jnp.sin(row_angle), zero, -jnp.sin(col_angle), zero], axis=0)
    down = jnp.concatenate([zero, jnp.sin(row_angle), zero, jnp.sin(col_angle)], axis=0)
    return cosine, up, down


def heads_kernel(x_ref, w_ref, *refs):
    out_ref = refs[-1]
    step = min(256, x_ref.shape[0])
    for start in range(0, x_ref.shape[0], step):
        rows = slice(start, start + step)
        product = dots(x_ref[rows, :], w_ref[:, : out_ref.shape[0]], 1, 0)
        out_ref[:, rows] = product.T


def heads_of(value, weight, columns, *others):
    shape = (columns, value.shape[0])
    return pl.pallas_call(
        heads_kernel,
        in_specs=[pl.BlockSpec(memory_space=pltpu.VMEM)] * 2
        + [pl.BlockSpec(memory_space=pl.ANY)] * len(others),
        out_shape=jax.ShapeDtypeStruct(shape, jnp.float32),
        compiler_params=pltpu.CompilerParams(vmem_limit_bytes=48 << 20),
        cost_estimate=cost(5),
        name="heads_of",
    )(value, weight, *others)


def back_kernel(one_ref, two_ref, w_one_ref, w_two_ref, out_ref, one_turn, two_turn):
    @pl.when(pl.program_id(0) == 0)
    def _():
        for ref, turn_ref in ((one_ref, one_turn), (two_ref, two_turn)):
            for start in range(0, ref.shape[1], 128):
                turn_ref[start : start + 128, :] = ref[:, start : start + 128].T

    size = one_turn.shape[1]
    out_ref[...] = dots(one_turn[...], w_one_ref[:, :size], 1, 1) + dots(
        two_turn[...], w_two_ref[:, :size], 1, 1
    )


def back_through(one, two, weight_one, weight_two):
    columns, tokens = one.shape
    rows = weight_one.shape[0]
    block = 384
    fixed = pl.BlockSpec((columns, tokens), lambda i: (0, 0))
    moving = pl.BlockSpec((block, weight_one.shape[1]), lambda i: (i, 0))
    return pl.pallas_call(
        back_kernel,
        grid=(rows // block,),
        in_specs=[fixed, fixed, moving, moving],
        out_specs=pl.BlockSpec((tokens, block), lambda i: (0, i)),
        out_shape=jax.ShapeDtypeStruct((tokens, rows), jnp.float32),
        scratch_shapes=[pltpu.VMEM((tokens, columns), jnp.bfloat16)] * 2,
        compiler_params=pltpu.CompilerParams(vmem_limit_bytes=48 << 20),
        cost_estimate=cost(9),
        name="back_through",
    )(one, two, weight_one, weight_two)


def block_index(chip, bits):
    place = 0
    for bit in bits:
        place = place * 2 + ((chip >> bit) & 1)
    return place


def other_bits(bits, count):
    return [bit for bit in range(count.bit_length() - 2, -1, -1) if bit not in bits]


def grad_parts(terms, turned, columns, parts, count, *others):
    left = terms[0][0][0][0]
    rows = left.shape[1] if turned else left.shape[0]
    size = rows // count
    chunk = rows // 4
    flat = [pair for term, _ in terms for pair in term]
    lefts = []
    for pair in flat:
        if not any(pair[0] is other for other in lefts):
            lefts.append(pair[0])

    def kernel(tok_ref, *refs):
        left_refs = refs[: len(lefts)]
        right_refs = refs[len(lefts) : len(lefts) + len(flat)]
        outs = refs[len(lefts) + len(flat) + len(others) :]
        outs, scratch = outs[: len(parts)], outs[len(parts) :]
        step = pl.program_id(0)
        tok = tok_ref[0]
        if turned:

            @pl.when(step == 0)
            def _():
                for left_ref, turn_ref in zip(left_refs, scratch):
                    for start in range(0, rows, 128):
                        turn_ref[start : start + 128, :] = left_ref[:, start : start + 128].T

        place = 0
        for term, start in terms:
            total = None
            for left, right, axis in term:
                which = [left is other for other in lefts].index(True)
                if turned:
                    part = scratch[which][pl.ds(pl.multiple_of(step * chunk, chunk), chunk), :]
                else:
                    part = left_refs[which][...]
                product = dots(part, right_refs[place][...], 1, axis)
                total = product if total is None else total + product
                place += 1
            width = total.shape[1]
            for block in range(chunk // size):
                value = total[block * size : (block + 1) * size, :].astype(jnp.bfloat16)
                mine = (step * (chunk // size) + block) ^ tok
                for out, fixed_bits in zip(outs, parts):
                    index = block_index(mine, other_bits(fixed_bits, count))
                    here = jnp.bool_(True)
                    for bit, wanted in fixed_bits.items():
                        here &= ((mine >> bit) & 1) == wanted

                    @pl.when(here)
                    def _():
                        out[index, :, start : start + width] = value

    def fixed(value):
        return pl.BlockSpec(value.shape, lambda i: (0,) * value.ndim)

    if turned:
        left_specs = [fixed(value) for value in lefts]
        scratch = [pltpu.VMEM(value.shape[::-1], value.dtype) for value in lefts]
    else:
        left_specs = [pl.BlockSpec((chunk, value.shape[1]), lambda i: (i, 0)) for value in lefts]
        scratch = []
    shapes = [(count >> len(part), size, columns) for part in parts]
    return pl.pallas_call(
        kernel,
        grid=(4,),
        in_specs=[pl.BlockSpec(memory_space=pltpu.SMEM)]
        + left_specs
        + [fixed(pair[1]) for pair in flat]
        + [pl.BlockSpec(memory_space=pl.ANY)] * len(others),
        out_specs=[pl.BlockSpec(shape, lambda i: (0, 0, 0)) for shape in shapes],
        out_shape=[jax.ShapeDtypeStruct(shape, jnp.bfloat16) for shape in shapes],
        scratch_shapes=scratch,
        compiler_params=pltpu.CompilerParams(vmem_limit_bytes=56 << 20),
        cost_estimate=cost(6 * columns // 1024),
        name="grad_parts",
    )(lax.axis_index("tok").reshape(1), *lefts, *[pair[1] for pair in flat], *others)


def scatter_on(value, left_bits, order, count, last=jnp.bfloat16):
    left_bits = list(left_bits)
    sent = []
    for bit in order:
        value = value.reshape((2,) * len(left_bits) + value.shape[-2:])
        axis = left_bits.index(bit)
        away = lax.index_in_dim(value, 1, axis, keepdims=False)
        sent.append(away)
        kept = last if bit == order[-1] else jnp.bfloat16
        value = add(lax.index_in_dim(value, 0, axis, keepdims=False), trade(away, bit, count), kept)
        left_bits.remove(bit)
    return value, sent


def plain_products(terms, turned, columns):
    pieces = []
    for place, (term, start) in enumerate(terms):
        total = sum(dots(one, two, 0 if turned else 1, axis) for one, two, axis in term)
        end = terms[place + 1][1] if place + 1 < len(terms) else columns
        total = jnp.pad(total, ((0, 0), (0, end - start - total.shape[1])))
        pieces.append(total.astype(jnp.bfloat16))
    return pieces


def row_size(terms, turned, count):
    left = terms[0][0][0][0]
    return (left.shape[1] if turned else left.shape[0]) // count


def chain_scatter(terms, turned, columns, count, *others):
    first, order, _ = orders(count)
    bits = first[::-1] + order
    if row_size(terms, turned, count) % 8:
        half, sent = half_scatter(plain_products(terms, turned, columns), count)
        return sent[:1], [half], lambda value: last_scatter(value[0], count)
    away, kept = grad_parts(terms, turned, columns, [{bits[0]: 1}, {bits[0]: 0}], count, *others)
    left_bits = other_bits(bits[:1], count)
    value = add(kept, trade(away, bits[0], count))
    value, sent = scatter_on(value, left_bits, bits[1 : len(first)], count)
    left_bits = [bit for bit in left_bits if bit in order]
    return (
        sent[:1],
        [value],
        lambda value: scatter_on(value[0], left_bits, order, count, jnp.float32)[0],
    )


def across_scatter(terms, turned, columns, count):
    first, order_a, order_b = orders(count)
    if row_size(terms, turned, count) % 8:
        half, sent = half_scatter(plain_products(terms, turned, columns), count)
        return [half], sent, [], [], lambda value: last_scatter(value[0], count)
    half_bit = first[-1]
    parts = [
        {half_bit: half, order[-1]: away}
        for half, order in enumerate((order_a, order_b))
        for away in (1, 0)
    ]
    blocks = grad_parts(terms, turned, columns, parts, count)
    halves, firsts, mids = [], [], []
    for place, order in enumerate((order_a, order_b)):
        away, kept = blocks[2 * place : 2 * place + 2]
        left_bits = other_bits((order[-1], half_bit), count)
        value = add(kept, trade(away, order[-1], count))
        firsts.append(value)
        value, sent = scatter_on(value, left_bits, order[-2::-1], count)
        halves.append(value)
        mids += sent[:1]

    def finish(halves):
        kept, away = halves
        value = add(kept, trade(away, half_bit, count))
        left_bits = [bit for bit in other_bits((), count) if bit in first[:-1]]
        return scatter_on(value, left_bits, first[-2::-1], count, jnp.float32)[0]

    return halves, [blocks[0], blocks[2]], firsts, mids, finish


def row_major(value):
    return with_layout_constraint(value, Layout(tuple(range(value.ndim))))


def add(one, two, kept=jnp.bfloat16):
    return (one.astype(jnp.float32) + two.astype(jnp.float32)).astype(kept)


def after(value, *others, micros=1):
    def keep(*refs):
        pass

    anywhere = pl.BlockSpec(memory_space=pl.ANY)
    return pl.pallas_call(
        keep,
        in_specs=[anywhere] * (1 + len(others)),
        out_specs=anywhere,
        out_shape=jax.ShapeDtypeStruct(value.shape, value.dtype),
        input_output_aliases={0: 0},
        cost_estimate=cost(micros),
        name="after",
    )(value, *others)


def first_gather(shard, count):
    first, _, _ = orders(count)
    value = shard.reshape((1,) * (count.bit_length() - 1) + shard.shape)
    for bit in first:
        value = doubled(value, bit, count)
    return value


def next_gather(value, count):
    first, order_a, order_b = orders(count)
    axis = axis_of(first[-1], count)
    halves = [
        lax.slice_in_dim(value, 0, 1, axis=axis),
        lax.slice_in_dim(value, 1, 2, axis=axis),
    ]
    for one, two in zip(order_a[:-1], order_b[:-1]):
        halves = [doubled(half, bit, count) for half, bit in zip(halves, (one, two))]
    return halves


def last_gather(halves, count):
    first, order_a, order_b = orders(count)
    axis = axis_of(first[-1], count)
    lasts = (order_a[-1], order_b[-1])
    moved = [trade(half, bit, count) for half, bit in zip(halves, lasts)]
    out = jnp.concatenate(
        [
            jnp.concatenate([half, half], axis=axis_of(bit, count))
            for half, bit in zip(halves, lasts)
        ],
        axis=axis,
    )
    for place, (bit, value) in enumerate(zip(lasts, moved)):
        out = put(out, value, {axis: place, axis_of(bit, count): 1 - bit_of(bit)}, count)
    return out.reshape(-1, out.shape[-1])


def halved(pieces, bit, count, kept):
    axis = axis_of(bit, count)
    digit = bit_of(bit)

    def part(place):
        parts = [lax.dynamic_slice_in_dim(piece, place, 1, axis) for piece in pieces]
        return parts[0] if len(parts) == 1 else jnp.concatenate(parts, axis=-1)

    sent = part(1 - digit).astype(jnp.bfloat16)
    total = part(digit).astype(jnp.float32) + trade(sent, bit, count).astype(jnp.float32)
    return total.astype(kept), sent


def half_scatter(values, count):
    first, order_a, order_b = orders(count)
    values = [split_rows(value, count) for value in values]
    axis = axis_of(first[-1], count)
    first_sent, out = [], []
    for place, order in enumerate((order_a[::-1], order_b[::-1])):
        pieces = [lax.slice_in_dim(value, place, place + 1, axis=axis) for value in values]
        for step, bit in enumerate(order):
            total, sent = halved(pieces, bit, count, jnp.bfloat16)
            if step == 0:
                first_sent.append(sent)
            pieces = [total]
        out.append(pieces[0])
    return jnp.concatenate(out, axis=axis), first_sent


def last_scatter(value, count):
    first, _, _ = orders(count)
    for bit in first[::-1]:
        value, _ = halved([value], bit, count, jnp.bfloat16 if bit != first[0] else jnp.float32)
    return value.reshape(value.shape[-2:])


def gather_small(value, count, bits):
    for bit in bits:
        value = jnp.concatenate([value, trade(value, bit, count)], axis=axis_of(bit, count))
    return value


def spread(value, count):
    return value.reshape((1,) * (count.bit_length() - 1) + value.shape)


def stacked(value, count):
    return value.reshape((-1,) + value.shape[count.bit_length() :])


def scatter_small(value, count, bits):
    for bit in bits:
        axis = axis_of(bit, count)
        sent = lax.slice_in_dim(value, 1, 2, axis=axis).astype(jnp.bfloat16)
        moved = trade(sent, bit, count).astype(jnp.float32)
        value = lax.slice_in_dim(value, 0, 1, axis=axis) + moved
    return value


def sum_all(value, count):
    value = value + swap(value)
    for bit in range(count.bit_length() - 1):
        value = value + trade(value, bit, count)
    return value


def pick(segment, table):
    out = jnp.zeros((segment.shape[0], table.shape[1]), jnp.float32)
    for slot in range(SLOTS):
        out = jnp.where(segment[:, None] == slot, table[slot][None, :], out)
    return out


def body(
    block_input,
    out_grad,
    class_table,
    time_table,
    class_label,
    time_index,
    grid_height,
    grid_width,
    mix_weight,
    proj_weight,
    cond_weight,
    cond_bias,
    feed_weight,
    down_weight,
    mix_mean,
    proj_mean,
    cond_mean,
    bias_mean,
    feed_mean,
    down_mean,
    mix_square,
    proj_square,
    cond_square,
    bias_square,
    feed_square,
    down_square,
):
    half = jnp.bfloat16
    count = block_input.shape[0]
    width = block_input.shape[1]
    chips = lax.axis_size("tok")
    tok = lax.axis_index("tok")
    side = lax.axis_index("mlp")
    first_side = side == 0
    rows_own = mix_weight.shape[0]
    mix_cols = mix_weight.shape[1]
    proj_cols = proj_weight.shape[1]
    hidden_cols = feed_weight.shape[2]
    cond_cols = cond_weight.shape[1]
    group = mix_cols // 3
    heads = HEADS // 2

    def joined(own, other, axis=1):
        low = jnp.where(first_side, own, other)
        high = jnp.where(first_side, other, own)
        return jnp.concatenate([low, high], axis=axis)

    def parted(value):
        size = value.shape[1] // 2
        low, high = value[:, :size], value[:, size:]
        return jnp.where(first_side, low, high), jnp.where(first_side, high, low)

    codes = jnp.stack([class_label, time_index], axis=1)
    first, order, _ = orders(chips)
    codes = spread(jnp.concatenate([codes, swap(codes)], axis=0), chips)
    codes = gather_small(codes, chips, first)

    mix_low = mix_weight.astype(half)
    mix_parts = [mix_low[:, :group], mix_low[:, group : 2 * group], mix_low[:, 2 * group :]]
    mix_moved = swap(mix_parts[1])
    mix_shard = jnp.where(
        first_side,
        jnp.concatenate([mix_parts[0], mix_parts[2], mix_moved], axis=1),
        jnp.concatenate([mix_moved, mix_parts[0], mix_parts[2]], axis=1),
    )
    mix_shard = jnp.concatenate([mix_shard, proj_weight.astype(half)], axis=1)
    mix_first = spread(after(mix_shard, codes), chips)
    mix_first = doubled(mix_first, first[0], chips)
    codes = gather_small(after(codes, mix_first), chips, order)
    codes = stacked(codes, chips)
    labels, times = codes[:, 0], codes[:, 1]
    for bit in first[1:]:
        mix_first = doubled(mix_first, bit, chips)

    start = tok * rows_own
    class_part = lax.dynamic_slice_in_dim(class_table, start, rows_own, 1)
    time_part = lax.dynamic_slice_in_dim(time_table, start, rows_own, 1)
    class_hot = (labels[:, None] == jnp.arange(class_table.shape[0])[None, :]).astype(half)
    time_hot = (times[:, None] == jnp.arange(time_table.shape[0])[None, :]).astype(half)
    embed = jnp.dot(class_hot, class_part, preferred_element_type=jnp.float32) + jnp.dot(
        time_hot, time_part, preferred_element_type=jnp.float32
    )
    cond_low = jax.nn.silu(embed).astype(half)
    partial_mod = jnp.dot(cond_low, cond_weight.astype(half), preferred_element_type=jnp.float32)
    bias_low = cond_bias.astype(half).astype(jnp.float32)
    bias_pair = joined(bias_low[None, :], swap(bias_low)[None, :])[0]
    bias_start = tok * bias_pair.shape[0]
    bias_side = bias_start // cond_cols
    bias_pair = jnp.where(bias_side == side, bias_pair, 0.0)
    bias_row = lax.dynamic_update_slice(
        jnp.zeros((cond_cols,), jnp.float32), bias_pair, (bias_start - bias_side * cond_cols,)
    )
    mod_half = split_rows(partial_mod + bias_row[None, :], chips)
    mod_half = scatter_small(mod_half, chips, order[:1])
    mod_half = scatter_small(after(mod_half, mix_first), chips, order[1:])
    far_down = spread(down_weight.T.astype(half), chips)
    for bit in order:
        far_down = doubled(far_down, bit, chips)
    mix_halves = next_gather(after(mix_first, mod_half, far_down), chips)
    mod_half = scatter_small(mod_half, chips, first[::-1])
    mod_half = mod_half.reshape(-1, cond_cols)
    slots = class_label.shape[0]
    modulation = joined(mod_half[:slots], swap(mod_half[slots:]))

    mix_own = last_gather(mix_halves, chips)
    far = jnp.concatenate([feed_weight[0].astype(half), feed_weight[1].astype(half)], axis=1)
    far = first_gather(after(far, mix_first), chips)
    far_down = after(far_down, far)
    for bit in first:
        far_down = doubled(far_down, bit, chips)
    far_down = far_down.reshape(width, hidden_cols)
    far = last_gather(next_gather(after(far, mix_own), chips), chips)
    far_gate, far_up = far[:, :hidden_cols], far[:, hidden_cols:]
    mix_other = swap_rows(mix_own, chips)
    proj_full = joined(mix_own[:, mix_cols:], mix_other[:, mix_cols:])

    segment, member, rows, cols = geometry(grid_height, grid_width, count)
    tables = turn_tables(rows, cols) + (segment[None, :], segment[:, None])
    valid = (segment < SLOTS).astype(jnp.float32)[:, None]
    shift_a, scale_a, gate_a, shift_b, scale_b, gate_b = (
        pick(segment, table) for table in jnp.split(modulation, 6, axis=1)
    )
    inputs = block_input.astype(jnp.float32)
    first_in = modulate(inputs, shift_a, scale_a).astype(half)
    first_turned = after(first_in.T, first_in)
    first_moved = swap(first_turned)

    shape = (3, heads, HEAD, count)
    att_own, log_own, *qkv_own = attend(
        heads_of(first_in, mix_own, mix_cols).reshape(shape), tables
    )
    att_other, log_other, *qkv_other = attend(
        heads_of(first_in, mix_other, mix_cols, first_moved).reshape(shape), tables
    )
    attended = joined(att_own, att_other, 0).reshape(width, count)
    attended_moved = swap(attended)
    branch = dots(attended, proj_full, 0, 0)
    middle = inputs + gate_a * branch
    second_in = modulate(middle, shift_b, scale_b).astype(half)
    second_pair = jnp.concatenate([second_in, swap(second_in)], axis=0)
    gate_pre = jnp.dot(second_pair, far_gate, preferred_element_type=jnp.float32)
    up_pre = jnp.dot(second_pair, far_up, preferred_element_type=jnp.float32)
    hidden = (jax.nn.silu(gate_pre) * up_pre).astype(half)
    partial_value = against(hidden, far_down)
    result = partial_value[:count] + swap(partial_value[count:].astype(half)).astype(jnp.float32)
    block_output = (valid * (middle + gate_b * result)).astype(half)

    grad_out = valid * out_grad.astype(jnp.float32)
    d_gate_b = grad_out * result
    result_grad = (gate_b * grad_out).astype(half)
    result_pair = jnp.concatenate([result_grad, swap(result_grad)], axis=0)
    down_sent, down_half, down_finish = chain_scatter(
        [([(result_pair, hidden, 0)], 0)], True, hidden_cols, chips, attended_moved
    )
    d_hidden = jnp.dot(result_pair, far_down, preferred_element_type=jnp.float32)
    sig = jax.nn.sigmoid(gate_pre)
    gate_grad = (d_hidden * up_pre * sig * (1.0 + gate_pre * (1.0 - sig))).astype(half)
    up_grad = (d_hidden * gate_pre * sig).astype(half)
    feed_half, _, _, feed_mids, feed_finish = across_scatter(
        [([(second_pair, gate_grad, 0)], 0), ([(second_pair, up_grad, 0)], hidden_cols)],
        True,
        2 * hidden_cols,
        chips,
    )
    second_part = against(gate_grad, far_gate) + against(up_grad, far_up)
    second_grad = second_part[:count] + swap(second_part[count:].astype(half)).astype(jnp.float32)
    pull_second = jax.vjp(modulate, middle, shift_b, scale_b)[1]
    d_middle, d_shift_b, d_scale_b = pull_second(second_grad)
    d_middle = d_middle + grad_out
    d_gate_a = d_middle * branch
    branch_grad = (gate_a * d_middle).astype(half)
    attended_grad = dots(proj_full, branch_grad, 1, 1).astype(half).reshape(HEADS, HEAD, count)
    grad_own = lax.dynamic_slice_in_dim(attended_grad, side * heads, heads, 0)
    grad_other = lax.dynamic_slice_in_dim(attended_grad, (1 - side) * heads, heads, 0)
    grad_other = after(grad_other, *down_sent)
    mg_other = attend_back(*qkv_other, grad_other, log_other, tables).reshape(mix_cols, count)
    mg_moved = swap(mg_other)
    grad_own = after(grad_own, mg_other, *feed_mids)
    mg_own = attend_back(*qkv_own, grad_own, log_own, tables).reshape(mix_cols, count)
    branch_grad_own, branch_grad_other = parted(branch_grad)
    proj_start = -(-mix_cols // 128) * 128
    near_half, near_sent, near_firsts, _, near_finish = across_scatter(
        [
            ([(first_turned, mg_own, 1), (first_moved, mg_moved, 1)], 0),
            ([(attended, branch_grad_own, 0), (attended_moved, swap_rows(branch_grad_other, chips), 0)], proj_start),
        ],
        False,
        proj_start + proj_cols,
        chips,
    )
    down_grad = down_finish(jax.tree.map(lambda value: after(value, *near_sent), down_half)).T
    feed_grad = feed_finish(jax.tree.map(lambda value: after(value, *near_sent), feed_half))
    feed_grad = jnp.stack([feed_grad[:, :hidden_cols], feed_grad[:, hidden_cols:]])
    near_grad = near_finish(near_half)
    proj_grad = near_grad[:, proj_start:]
    mix_parts = [near_grad[:, place * group : (place + 1) * group] for place in range(3)]
    mix_moved = swap(jnp.where(first_side, mix_parts[2], mix_parts[0]))
    mix_grad = jnp.where(
        first_side,
        jnp.concatenate([mix_parts[0], mix_moved, mix_parts[1]], axis=1),
        jnp.concatenate([mix_parts[1], mix_moved, mix_parts[2]], axis=1),
    )

    mg_own, mg_other = after(mg_own, *near_sent), after(mg_other, *near_sent)
    first_grad = back_through(mg_own, mg_other, mix_own, mix_other)
    pull_first = jax.vjp(modulate, inputs, shift_a, scale_a)[1]
    d_inputs, d_shift_a, d_scale_a = pull_first(first_grad)
    input_grad = d_inputs + d_middle
    member_low = member.astype(half)
    d_modulation = jnp.concatenate(
        [
            across(member_low, piece.astype(half))
            for piece in (d_shift_a, d_scale_a, d_gate_a, d_shift_b, d_scale_b, d_gate_b)
        ],
        axis=1,
    ).astype(half)
    mod_own, mod_other = parted(d_modulation)
    mod_all = spread(jnp.concatenate([mod_own, swap(mod_other)], axis=0), chips)
    mod_all = after(gather_small(mod_all, chips, first), *near_firsts)
    mod_all = stacked(gather_small(mod_all, chips, order), chips)
    cond_grad = across(cond_low, mod_all)
    bias_half = jnp.sum(mod_all.astype(jnp.float32), axis=0)[None, :]
    bias_full = joined(bias_half, swap(bias_half))[0]
    bias_size = cond_bias.shape[0]
    bias_grad = lax.dynamic_slice_in_dim(bias_full, (2 * tok + side) * bias_size, bias_size, 0)

    grads = (mix_grad, proj_grad, cond_grad, bias_grad, feed_grad, down_grad)
    local_squares = jnp.float32(0.0)
    for grad in grads:
        local_squares = local_squares + jnp.sum(grad * grad)
    grad_norm = jnp.sqrt(sum_all(local_squares, chips))
    factor = CLIP_NORM / jnp.maximum(grad_norm, CLIP_NORM)
    params = (mix_weight, proj_weight, cond_weight, cond_bias, feed_weight, down_weight)
    means = (mix_mean, proj_mean, cond_mean, bias_mean, feed_mean, down_mean)
    squares_old = (mix_square, proj_square, cond_square, bias_square, feed_square, down_square)
    updates = [adam(w, m, v, g * factor) for w, m, v, g in zip(params, means, squares_old, grads)]
    return (
        block_output,
        input_grad,
        grad_norm,
        updates[0][0],
        updates[1][0],
        updates[2][0],
        updates[3][0],
        updates[4][0],
        updates[5][0],
        updates[0][1],
        updates[1][1],
        updates[2][1],
        updates[3][1],
        updates[4][1],
        updates[5][1],
        updates[0][2],
        updates[1][2],
        updates[2][2],
        updates[3][2],
        updates[4][2],
        updates[5][2],
    )


def solution(mesh):
    placed = (
        P(("tok", "mlp"), None),
        P(("tok", "mlp"), None),
        P(),
        P(),
        P(("tok", "mlp")),
        P(("tok", "mlp")),
        P(("tok", "mlp")),
        P(("tok", "mlp")),
        P("tok", "mlp"),
        P("tok", "mlp"),
        P("tok", "mlp"),
        P(("tok", "mlp")),
        P(None, "tok", "mlp"),
        P("mlp", "tok"),
        P("tok", "mlp"),
        P("tok", "mlp"),
        P("tok", "mlp"),
        P(("tok", "mlp")),
        P(None, "tok", "mlp"),
        P("mlp", "tok"),
        P("tok", "mlp"),
        P("tok", "mlp"),
        P("tok", "mlp"),
        P(("tok", "mlp")),
        P(None, "tok", "mlp"),
        P("mlp", "tok"),
    )
    return jax.shard_map(
        body,
        mesh=mesh,
        in_specs=placed,
        out_specs=(
            P(("tok", "mlp"), None),
            P(("tok", "mlp"), None),
            P(),
            P("tok", "mlp"),
            P("tok", "mlp"),
            P("tok", "mlp"),
            P(("tok", "mlp")),
            P(None, "tok", "mlp"),
            P("mlp", "tok"),
            P("tok", "mlp"),
            P("tok", "mlp"),
            P("tok", "mlp"),
            P(("tok", "mlp")),
            P(None, "tok", "mlp"),
            P("mlp", "tok"),
            P("tok", "mlp"),
            P("tok", "mlp"),
            P("tok", "mlp"),
            P(("tok", "mlp")),
            P(None, "tok", "mlp"),
            P("mlp", "tok"),
        ),
        check_vma=False,
    )
```

time: 2020 us -> 622 us (0.31)
  waiting for transfers between devices: 1390 us -> 202 us
  blocking collectives: 210 us -> 0 us
  matrix products: 241 us -> 59.2 us
  Pallas kernels: 0 us -> 94.4 us
  starting transfers between devices: 0.88 us -> 59.3 us
  other arithmetic: 83.6 us -> 130 us
    reduce_scatter x5 -> x0, waiting for transfers between devices: 793 us -> none  [the longest x1 482 us: body(): lax.psum_scatter(across(cond_low, modulation_low), 'tok', scatter_dimensi...]
    all_gather x7 -> x0, waiting for transfers between devices: 358 us -> none  [the longest x1 91.4 us: body(): lax.all_gather(pair[0], 'tok', axis=0, tiled=True)]
    unnamed x22 -> x0, waiting for transfers between devices: 242 us -> none
    ppermute x0 -> x65, waiting for transfers between devices: none -> 202 us  [the longest x48 201 us: trade(): lax.ppermute(value, 'tok', [(place, place ^ 1 << bit) for place in range(...]
    unnamed x4 -> x0, blocking collectives: 163 us -> none
    dot_general x13 -> x8, matrix products: 139 us -> 36.4 us  [the longest x1 12.9 us: body(): jnp.dot(second_pair, far_gate, preferred_element_type=jnp.float32)]
    pallas_call x0 -> x26, Pallas kernels: none -> 94.4 us  [the longest x3 42.5 us: grad_parts(): pl.pallas_call(kernel, grid=(4,), in_specs=[pl.BlockSpec(memory_space=plt...]
    ppermute x0 -> x65, starting transfers between devices: none -> 59.3 us  [the longest x48 55.4 us: trade(): lax.ppermute(value, 'tok', [(place, place ^ 1 << bit) for place in range(...]
  transfers between devices with their start and end apart: 17 -> 65, of which waited for: 16 -> 29; matrix products, arithmetic and copies ran while one was open for 15% -> 33% of each run, Pallas kernels for 0% -> 11%
where the time goes in v2:
time: 622 us; the launch traced here: 614 us
  waiting for transfers between devices  202 us (32%)
  other arithmetic  130 us (21%)
  Pallas kernels  94.4 us (15%)
  starting transfers between devices  59.3 us (10%)
  matrix products  59.2 us (10%)
  local copies, waits for them, and re-layouts  58.3 us (9%)
  between operations  11.2 us (2%)
    ppermute x48, waiting for transfers between devices, trade(): lax.ppermute(value, 'tok', [(place, place ^ 1 << bit) for place in range(...  201 us
    ppermute x48, starting transfers between devices, trade(): lax.ppermute(value, 'tok', [(place, place ^ 1 << bit) for place in range(...  55.4 us
    pallas_call x3, Pallas kernels, grad_parts(): pl.pallas_call(kernel, grid=(4,), in_specs=[pl.BlockSpec(memory_space=plt...  42.5 us
    convert_element_type x12, other arithmetic, add(): return (one.astype(jnp.float32) + two.astype(jnp.float32)).astype(kept)  23.3 us
    pallas_call x2, Pallas kernels, attend_back(): pl.pallas_call(attend_back_kernel, grid=(heads,), in_specs=[block] * 4 +...  19 us
    concatenate x12, other arithmetic, doubled(): out = jnp.concatenate([value, value], axis=axis)  18.7 us
    dynamic_update_slice x16, local copies, waits for them, and re-layouts, put(): return lax.dynamic_update_slice(out, value, tuple(start))  18.5 us
    unnamed x262, local copies, waits for them, and re-layouts  18 us
  transfers between devices with their start and end apart: 65, of which 29 were waited for; matrix products, arithmetic and copies ran while one was open for 33% of the time, Pallas kernels for 11%

profile of v2, /device:TPU:0, one launch (start us, length us, event | category | flops | bytes accessed | tf_op | source)
XLA Modules:
  0.0 614.3 jit_solution(1494926325299142475)
XLA Ops:
  7.9 2.5 collective-permute-start.14
  22.3 2.6 collective-permute-start.1
  35.6 2.6 collective-permute-start.4
  40.1 11.2 %collective-permute-done.4 = bf16[1,1,1,1,72,2304]{5,4,3,2,1,0:T(8,128)(2,1)S(1)} collective-permute-done((bf16[1,1,1,1,72,2304]{5,4,3,2,1,0:T(8,128)(2,1)}, bf16[1,1,1,1,72,2304]{5,4,3,2,1,0:T(8,128)(2,1)S(1)}, u32[]{:S(2)}, u32[]{:S(2)}) %collective-permute-start.4) | collective-permute-done | bytes 331808 | tf_op jit(solution)/shard_map/ppermute | solution.py:87
  64.5 2.7 pad_maximum_fusion.10
  69.6 4.5 collective-permute-done.8
  79.7 3.3 collective-permute-start.23
  88.7 5.7 collective-permute-done.11
  96.8 5.5 collective-permute-done.12
  104.3 4.5 collective-permute-done.17
  110.1 3.0 maximum_maximum_fusion.1
  113.1 23.2 %collective-permute-done.18 = bf16[2,1,1,2,72,2304]{5,4,3,2,1,0:T(8,128)(2,1)S(1)} collective-permute-done((bf16[2,1,1,2,72,2304]{5,4,3,2,1,0:T(8,128)(2,1)S(1)}, bf16[2,1,1,2,72,2304]{5,4,3,2,1,0:T(8,128)(2,1)S(1)}, u32[]{:S(2)}, u32[]{:S(2)}) %collective-permute-start.18) | collective-permute-done | bytes 1327136 | tf_op jit(solution)/shard_map/ppermute | solution.py:87
  138.6 4.1 fusion.97
  142.7 5.7 fusion.14.x_ref.refs_1_
  155.9 2.8 pad_maximum_fusion.7
  164.0 5.2 heads_of.2
  169.9 6.1 attend.2
  176.0 19.8 %collective-permute-done.29 = bf16[1,1,2,2,72,1536]{5,4,3,2,1,0:T(8,128)(2,1)} collective-permute-done((bf16[1,1,2,2,72,1536]{5,4,3,2,1,0:T(8,128)(2,1)}, bf16[1,1,2,2,72,1536]{5,4,3,2,1,0:T(8,128)(2,1)}, u32[]{:S(2)}, u32[]{:S(2)}) %collective-permute-start.29) | collective-permute-done | bytes 884768 | tf_op jit(solution)/shard_map/ppermute | solution.py:87
  203.0 4.0 broadcast_select_fusion.1
  207.0 6.1 heads_of.3
  213.1 5.9 attend.3
  222.2 4.6 fusion.81
  227.1 4.0 add_convert_fusion.5
  231.2 4.5 maximum_maximum_fusion
  244.9 6.7 %fusion.6 = f32[1024,1536]{1,0:T(8,128)} fusion(bf16[1152,3072]{1,0:T(8,128)(2,1)S(1)} %bitcast.185, bf16[512,1152]{1,0:T(8,128)(2,1)S(1)} %collective-permute-done.22, bf16[512,1152]{1,0:T(8,128)(2,1)S(1)} %add_convert_fusion.5), kind=kOutput, calls=%fused_computation.23 | convolution fusion | flops 3628597248 | bytes 12189696 | tf_op jit(solution)/shard_map/dot_general | solution.py:738
  252.6 6.9 %fusion.70 = f32[1024,1536]{1,0:T(8,128)} fusion(bf16[1152,1536]{1,0:T(8,128)(2,1)S(1)} %bitcast.199, bf16[512,1152]{1,0:T(8,128)(2,1)S(1)} %collective-permute-done.32, bf16[512,1152]{1,0:T(8,128)(2,1)S(1)} %get-tuple-element.164), kind=kOutput, calls=%fused_computation.314 | convolution fusion | flops 3628597248 | bytes 12189696 | tf_op jit(solution)/shard_map/dot_general | solution.py:751
  259.6 12.9 %multiply_convert_fusion.1 = (bf16[1024,1536]{1,0:T(8,128)(2,1)}, bf16[1024,1536]{1,0:T(8,128)(2,1)}, bf16[1024,1536]{1,0:T(8,128)(2,1)}) fusion(f32[1024,1536]{1,0:T(8,128)} %fusion.70, f32[1024,1536]{1,0:T(8,128)} %fusion.6, bf16[1152,3072]{1,0:T(8,128)(2,1)S(1)} %bitcast.186, bf16[512,1152]{1,0:T(8,128)(2,1)S(1)} %copy-done.76, ...), kind=kOutput, calls=%fused_computation.2 | convolution fusion | flops 3653763072 | bytes 27918336 | tf_op jit(solution)/shard_map/dot_general | solution.py:737
  272.5 6.3 %fusion.86 = f32[1024,1152]{1,0:T(8,128)S(1)} fusion(bf16[1024,1536]{1,0:T(8,128)(2,1)} %get-tuple-element.118.refs_1_, bf16[1152,1536]{1,0:T(8,128)(2,1)S(1)} %bitcast.200), kind=kOutput, calls=%fused_computation.322 | convolution fusion | flops 3623878656 | bytes 11403264 | tf_op jit(solution)/shard_map/dot_general | solution.py:60
  280.2 4.3 fusion.4
  284.5 4.3 convolution_add_fusion.1
  288.7 2.2 copy-done.28
  294.7 10.1 %grad_parts.3 = (bf16[8,72,1536]{2,1,0:T(8,128)(2,1)}, bf16[8,72,1536]{2,1,0:T(8,128)(2,1)}) custom-call(s32[1]{0:T(128)} %bitcast.28.tok_ref, bf16[1024,1152]{1,0:T(8,128)(2,1)} %pad_maximum_fusion.3.refs_0_, bf16[1024,1536]{1,0:T(8,128)(2,1)} %get-tuple-element.118.refs_1_, bf16[1152,512]{1,0:T(8,128)(2,1)} %collective-permute-done.34.refs_2_.refs_3_), custom_call_target="tpu_custom_call" | custom-call | flops 4140000000 | bytes 1000 | tf_op jit(solution)/shard_map/grad_parts/pallas_call | solution.py:368
  306.5 3.0 pad_maximum_fusion.2.refs_0_
  309.4 17.2 %grad_parts.4 = (bf16[4,72,3072]{2,1,0:T(8,128)(2,1)}, bf16[4,72,3072]{2,1,0:T(8,128)(2,1)}, bf16[4,72,3072]{2,1,0:T(8,128)(2,1)}, bf16[4,72,3072]{2,1,0:T(8,128)(2,1)}) custom-call(s32[1]{0:T(128)} %bitcast.28.tok_ref, bf16[1024,1152]{1,0:T(8,128)(2,1)} %pad_maximum_fusion.2.refs_0_, bf16[1024,1536]{1,0:T(8,128)(2,1)} %get-tuple-element.117.refs_1_, ...), custom_call_target="tpu_custom_call" | custom-call | flops 8280000000 | bytes 1000 | tf_op jit(solution)/shard_map/grad_parts/pallas_call | solution.py:368
  328.6 6.0 multiply_reduce_fusion
  336.5 2.5 multiply_convert_fusion.6
  352.8 14.8 %collective-permute-done.36 = bf16[4,72,3072]{2,1,0:T(8,128)(2,1)} collective-permute-done((bf16[4,72,3072]{2,1,0:T(8,128)(2,1)}, bf16[4,72,3072]{2,1,0:T(8,128)(2,1)}, u32[]{:S(2)}, u32[]{:S(2)}) %collective-permute-start.36) | collective-permute-done | bytes 1769504 | tf_op jit(solution)/shard_map/ppermute | solution.py:87
  367.6 2.3 add_convert_fusion.1
  369.9 2.8 add_convert_fusion
  375.6 9.5 %attend_back.2 = bf16[3,8,72,512]{3,2,1,0:T(8,128)(2,1)S(1)} custom-call(bf16[8,72,512]{2,1,0:T(8,128)(2,1)S(1)} %copy-done.17, bf16[8,72,512]{2,1,0:T(8,128)(2,1)S(1)} %copy-done.19, bf16[8,72,512]{2,1,0:T(8,128)(2,1)S(1)} %copy-done.21, bf16[8,72,512]{2,1,0:T(8,128)(2,1)S(1)} %copy-done.8, f32[8,1,512]{2,1,0:T(1,128)S(1)} %get-tuple-element.51.log_ref, ...), custom_call_target="tpu_custom_call" | custom-call | flops 4600000000 | bytes 1000 | tf_op jit(solution)/shard_map/attend_back/pallas_call | solution.py:217
  390.6 9.5 %attend_back.3 = bf16[3,8,72,512]{3,2,1,0:T(8,128)(2,1)S(1)} custom-call(bf16[8,72,512]{2,1,0:T(8,128)(2,1)S(1)} %copy-done.11, bf16[8,72,512]{2,1,0:T(8,128)(2,1)S(1)} %copy-done.13, bf16[8,72,512]{2,1,0:T(8,128)(2,1)S(1)} %copy-done.15, bf16[8,72,512]{2,1,0:T(8,128)(2,1)S(1)} %copy-done.7, f32[8,1,512]{2,1,0:T(1,128)S(1)} %get-tuple-element.56.log_ref, ...), custom_call_target="tpu_custom_call" | custom-call | flops 4600000000 | bytes 1000 | tf_op jit(solution)/shard_map/attend_back/pallas_call | solution.py:217
  400.1 3.0 fusion.22.refs_0_
  403.1 4.5 collective-permute-done.54
  407.6 2.3 fusion.21.refs_0_
  409.9 2.3 fusion.20.refs_0_
  412.2 15.3 %grad_parts.5 = (bf16[4,72,2368]{2,1,0:T(8,128)(2,1)}, bf16[4,72,2368]{2,1,0:T(8,128)(2,1)}, bf16[4,72,2368]{2,1,0:T(8,128)(2,1)}, bf16[4,72,2368]{2,1,0:T(8,128)(2,1)}) custom-call(s32[1]{0:T(128)} %bitcast.28.tok_ref, bf16[1152,512]{1,0:T(8,128)(2,1)} %after.20.refs_0_, bf16[1152,512]{1,0:T(8,128)(2,1)} %copy-done.9, bf16[1152,512]{1,0:T(8,128)(2,1)} %bitcast.205, ...), custom_call_target="tpu_custom_call" | custom-call | flops 5980000256 | bytes 1000 | tf_op jit(solution)/shard_map/grad_parts/pallas_call | solution.py:368
  430.5 9.6 %back_through.1 = f32[512,1152]{1,0:T(8,128)S(1)} custom-call(bf16[1728,512]{1,0:T(8,128)(2,1)S(1)} %copy-done.6, bf16[1728,512]{1,0:T(8,128)(2,1)S(1)} %copy-done.4, bf16[1152,2304]{1,0:T(8,128)(2,1)} %bitcast.14.w_ref.refs_1_.w_one_ref, bf16[1152,2304]{1,0:T(8,128)(2,1)} %bitcast.18.w_ref.w_two_ref), custom_call_target="tpu_custom_call" | custom-call | flops 4140000000 | bytes 1000 | tf_op jit(solution)/shard_map/back_through/pallas_call | solution.py:282
  450.9 2.6 fusion.79
  457.1 11.5 %collective-permute-done.48 = bf16[1,1,1,1,8,3456]{5,4,3,2,1,0:T(8,128)(2,1)S(1)} collective-permute-done((bf16[1,1,1,1,8,3456]{5,4,3,2,1,0:T(8,128)(2,1)S(1)}, bf16[1,1,1,1,8,3456]{5,4,3,2,1,0:T(8,128)(2,1)S(1)}, u32[]{:S(2)}, u32[]{:S(2)}) %collective-permute-start.48) | collective-permute-done | bytes 55328 | tf_op jit(solution)/shard_map/ppermute | solution.py:87
  468.6 2.2 collective-permute-start.49
  470.8 14.2 %collective-permute-done.58 = bf16[2,72,1536]{2,1,0:T(8,128)(2,1)} collective-permute-done((bf16[2,72,1536]{2,1,0:T(8,128)(2,1)}, bf16[2,72,1536]{2,1,0:T(8,128)(2,1)}, u32[]{:S(2)}, u32[]{:S(2)}) %collective-permute-start.58) | collective-permute-done | bytes 442400 | tf_op jit(solution)/shard_map/ppermute | solution.py:87
  489.9 2.2 collective-permute-done.59
  492.8 16.3 %collective-permute-done.56 = bf16[72,3072]{1,0:T(8,128)(2,1)S(1)} collective-permute-done((bf16[72,3072]{1,0:T(8,128)(2,1)S(1)}, bf16[72,3072]{1,0:T(8,128)(2,1)S(1)}, u32[]{:S(2)}, u32[]{:S(2)}) %collective-permute-start.56) | collective-permute-done | bytes 442400 | tf_op jit(solution)/shard_map/ppermute | solution.py:87
  510.1 2.9 add_convert_fusion.4.refs_1_
  513.1 2.8 add_convert_fusion.3.refs_2_
  519.5 15.5 %collective-permute-done.43 = bf16[2,72,2368]{2,1,0:T(8,128)(2,1)S(1)} collective-permute-done((bf16[2,72,2368]{2,1,0:T(8,128)(2,1)S(1)}, bf16[2,72,2368]{2,1,0:T(8,128)(2,1)S(1)}, u32[]{:S(2)}, u32[]{:S(2)}) %collective-permute-start.43) | collective-permute-done | bytes 682016 | tf_op jit(solution)/shard_map/ppermute | solution.py:87
  538.5 13.6 %collective-permute-done.44 = bf16[2,72,2368]{2,1,0:T(8,128)(2,1)S(1)} collective-permute-done((bf16[2,72,2368]{2,1,0:T(8,128)(2,1)S(1)}, bf16[2,72,2368]{2,1,0:T(8,128)(2,1)S(1)}, u32[]{:S(2)}, u32[]{:S(2)}) %collective-permute-start.44) | collective-permute-done | bytes 682016 | tf_op jit(solution)/shard_map/ppermute | solution.py:87
  554.1 15.1 %collective-permute-done.45 = bf16[72,2368]{1,0:T(8,128)(2,1)S(1)} collective-permute-done((bf16[72,2368]{1,0:T(8,128)(2,1)S(1)}, bf16[72,2368]{1,0:T(8,128)(2,1)S(1)}, u32[]{:S(2)}, u32[]{:S(2)}) %collective-permute-start.45) | collective-permute-done | bytes 341024 | tf_op jit(solution)/shard_map/ppermute | solution.py:87
  575.9 2.5 multiply_reduce_fusion.4
  584.1 2.3 collective-permute-start.61
  588.4 2.3 collective-permute-start.62
  594.0 2.2 collective-permute-done.63
  598.3 3.1 collective-permute-done.64
  602.2 3.9 multiply_subtract_fusion.1
  (533 shorter events, 186.0 us)
Async XLA Ops:
  2.7 29.2 %collective-permute-start.3 = (bf16[72,576]{1,0:T(8,128)(2,1)}, bf16[72,576]{1,0:T(8,128)(2,1)S(1)}, u32[]{:S(2)}, u32[]{:S(2)}) collective-permute-start(bf16[72,576]{1,0:T(8,128)(2,1)} %get-tuple-element.145), channel_id=1, source_target_pairs={{0,1},{1,0},{2,3},{3,2},{4,5},{5,4},{6,7},{7,6},{8,9},{9,8},{10,11... | collective-permute-start | bytes 248840 | tf_op jit(solution)/shard_map/ppermute | solution.py:95
  4.4 17.2 %collective-permute-start = (s32[4,2]{0,1:T(2,128)}, s32[4,2]{0,1:T(2,128)}, u32[]{:S(2)}, u32[]{:S(2)}) collective-permute-start(s32[4,2]{0,1:T(2,128)} %pad_add_fusion.4), channel_id=1, source_target_pairs={{0,1},{1,0},{2,3},{3,2},{4,5},{5,4},{6,7},{7,6},{8,9},{9,8},{10,11... | collective-permute-start | bytes 104 | tf_op jit(solution)/shard_map/ppermute | solution.py:95
  5.7 25.4 %collective-permute-start.7 = (f32[216]{0:T(256)}, f32[216]{0:T(256)}, u32[]{:S(2)}, u32[]{:S(2)}) collective-permute-start(f32[216]{0:T(256)} %convert_convert_fusion.7), channel_id=1, source_target_pairs={{0,1},{1,0},{2,3},{3,2},{4,5},{5,4},{6,7},{7,6},{8,9},{9,8},{10,11... | collective-permute-start | bytes 2600 | tf_op jit(solution)/shard_map/ppermute | solution.py:95
  7.9 44.7 %collective-permute-start.14 = (bf16[1,1,1,1,72,1536]{5,4,3,2,1,0:T(8,128)(2,1)}, bf16[1,1,1,1,72,1536]{5,4,3,2,1,0:T(8,128)(2,1)}, u32[]{:S(2)}, u32[]{:S(2)}) collective-permute-start(bf16[1,1,1,1,72,1536]{5,4,3,2,1,0:T(8,128)(2,1)} %convert_bitcast_fusion), channel_id=1, source_target_pairs={{0,2},{2,0},{4,6},{6,4},{8,10},{10,8},{12,14},{14,12},{16,18},{18,... | collective-permute-start | bytes 663560 | tf_op jit(solution)/shard_map/ppermute | solution.py:87
  22.3 4.5 collective-permute-start.1
  26.8 3.6 collective-permute-start.2
  35.6 15.8 %collective-permute-start.4 = (bf16[1,1,1,1,72,2304]{5,4,3,2,1,0:T(8,128)(2,1)}, bf16[1,1,1,1,72,2304]{5,4,3,2,1,0:T(8,128)(2,1)S(1)}, u32[]{:S(2)}, u32[]{:S(2)}) collective-permute-start(bf16[1,1,1,1,72,2304]{5,4,3,2,1,0:T(8,128)(2,1)} %bitcast.201), channel_id=1, source_target_pairs={{0,16},{2,18},{4,20},{6,22},{8,24},{10,26},{12,28},{14,30},{16,0},... | collective-permute-start | bytes 995336 | tf_op jit(solution)/shard_map/ppermute | solution.py:87
  52.1 3.9 collective-permute-start.5
  56.2 3.8 collective-permute-start.6
  58.7 9.8 %collective-permute-start.15 = (bf16[1,1,1,2,72,1536]{5,4,3,2,1,0:T(8,128)(2,1)S(1)}, bf16[1,1,1,2,72,1536]{5,4,3,2,1,0:T(8,128)(2,1)}, u32[]{:S(2)}, u32[]{:S(2)}) collective-permute-start(bf16[1,1,1,2,72,1536]{5,4,3,2,1,0:T(8,128)(2,1)S(1)} %constant_dynamic-update-slice_fusion.13), channel_id=1, source_target_pairs={{0,4},{2,6},{4,0},{6,2},{8,12},{10,14},{12,8},{14,10},{16,20},{18,... | collective-permute-start | bytes 1327112 | tf_op jit(solution)/shard_map/ppermute | solution.py:87
  59.2 15.8 %collective-permute-start.9 = (bf16[2,1,1,1,72,2304]{5,4,3,2,1,0:T(8,128)(2,1)}, bf16[2,1,1,1,72,2304]{5,4,3,2,1,0:T(8,128)(2,1)}, u32[]{:S(2)}, u32[]{:S(2)}) collective-permute-start(bf16[2,1,1,1,72,2304]{5,4,3,2,1,0:T(8,128)(2,1)} %constant_dynamic-update-slice_fusion.15.refs_1_), channel_id=1, source_target_pairs={{0,8},{2,10},{4,12},{6,14},{8,0},{10,2},{12,4},{14,6},{16,24},{18,... | collective-permute-start | bytes 1990664 | tf_op jit(solution)/shard_map/ppermute | solution.py:87
  63.9 10.2 %collective-permute-start.8 = (bf16[2,2,2,1,8,3456]{5,4,3,2,1,0:T(8,128)(2,1)S(1)}, bf16[2,2,2,1,8,3456]{5,4,3,2,1,0:T(8,128)(2,1)S(1)}, u32[]{:S(2)}, u32[]{:S(2)}) collective-permute-start(bf16[2,2,2,1,8,3456]{5,4,3,2,1,0:T(8,128)(2,1)S(1)} %slice.564), channel_id=1, source_target_pairs={{0,2},{2,0},{4,6},{6,4},{8,10},{10,8},{12,14},{14,12},{16,18},{18,... | collective-permute-start | bytes 1327112 | tf_op jit(solution)/shard_map/ppermute | solution.py:87
  78.1 7.0 %collective-permute-start.10 = (bf16[2,2,1,1,8,3456]{5,4,3,2,1,0:T(8,128)(2,1)S(1)}, bf16[2,2,1,1,8,3456]{5,4,3,2,1,0:T(8,128)(2,1)S(1)}, u32[]{:S(2)}, u32[]{:S(2)}) collective-permute-start(bf16[2,2,1,1,8,3456]{5,4,3,2,1,0:T(8,128)(2,1)S(1)} %slice.565), channel_id=1, source_target_pairs={{0,4},{2,6},{4,0},{6,2},{8,12},{10,14},{12,8},{14,10},{16,20},{18,... | collective-permute-start | bytes 663560 | tf_op jit(solution)/shard_map/ppermute | solution.py:87
  79.7 22.8 %collective-permute-start.23 = (bf16[1,1,1,1,72,3072]{5,4,3,2,1,0:T(8,128)(2,1)}, bf16[1,1,1,1,72,3072]{5,4,3,2,1,0:T(8,128)(2,1)}, u32[]{:S(2)}, u32[]{:S(2)}) collective-permute-start(bf16[1,1,1,1,72,3072]{5,4,3,2,1,0:T(8,128)(2,1)} %bitcast.195), channel_id=1, source_target_pairs={{0,16},{2,18},{4,20},{6,22},{8,24},{10,26},{12,28},{14,30},{16,0},... | collective-permute-start | bytes 1327112 | tf_op jit(solution)/shard_map/ppermute | solution.py:87
  87.4 7.0 %collective-permute-start.11 = (bf16[2,1,1,1,8,3456]{5,4,3,2,1,0:T(8,128)(2,1)S(1)}, bf16[2,1,1,1,8,3456]{5,4,3,2,1,0:T(8,128)(2,1)S(1)}, u32[]{:S(2)}, u32[]{:S(2)}) collective-permute-start(bf16[2,1,1,1,8,3456]{5,4,3,2,1,0:T(8,128)(2,1)S(1)} %slice.566), channel_id=1, source_target_pairs={{0,8},{2,10},{4,12},{6,14},{8,0},{10,2},{12,4},{14,6},{16,24},{18,... | collective-permute-start | bytes 331784 | tf_op jit(solution)/shard_map/ppermute | solution.py:87
  87.9 15.7 %collective-permute-start.16 = (bf16[2,1,1,1,72,2304]{5,4,3,2,1,0:T(8,128)(2,1)S(1)}, bf16[2,1,1,1,72,2304]{5,4,3,2,1,0:T(8,128)(2,1)S(1)}, u32[]{:S(2)}, u32[]{:S(2)}) collective-permute-start(bf16[2,1,1,1,72,2304]{5,4,3,2,1,0:T(8,128)(2,1)S(1)} %get-tuple-element.128), channel_id=1, source_target_pairs={{0,2},{2,0},{4,6},{6,4},{8,10},{10,8},{12,14},{14,12},{16,18},{18,... | collective-permute-start | bytes 1990664 | tf_op jit(solution)/shard_map/ppermute | solution.py:87
  94.5 7.9 %collective-permute-start.12 = (bf16[1,1,1,1,8,3456]{5,4,3,2,1,0:T(8,128)(2,1)S(1)}, bf16[1,1,1,1,8,3456]{5,4,3,2,1,0:T(8,128)(2,1)S(1)}, u32[]{:S(2)}, u32[]{:S(2)}) collective-permute-start(bf16[1,1,1,1,8,3456]{5,4,3,2,1,0:T(8,128)(2,1)S(1)} %slice.567), channel_id=1, source_target_pairs={{0,16},{2,18},{4,20},{6,22},{8,24},{10,26},{12,28},{14,30},{16,0},... | collective-permute-start | bytes 165896 | tf_op jit(solution)/shard_map/ppermute | solution.py:87
  94.7 14.1 %collective-permute-start.17 = (bf16[2,1,1,1,72,2304]{5,4,3,2,1,0:T(8,128)(2,1)S(1)}, bf16[2,1,1,1,72,2304]{5,4,3,2,1,0:T(8,128)(2,1)S(1)}, u32[]{:S(2)}, u32[]{:S(2)}) collective-permute-start(bf16[2,1,1,1,72,2304]{5,4,3,2,1,0:T(8,128)(2,1)S(1)} %get-tuple-element.129), channel_id=1, source_target_pairs={{0,4},{2,6},{4,0},{6,2},{8,12},{10,14},{12,8},{14,10},{16,20},{18,... | collective-permute-start | bytes 1990664 | tf_op jit(solution)/shard_map/ppermute | solution.py:87
  102.4 7.5 %collective-permute-start.13 = (f32[4,3456]{1,0:T(4,128)S(1)}, f32[4,3456]{1,0:T(4,128)S(1)}, u32[]{:S(2)}, u32[]{:S(2)}) collective-permute-start(f32[4,3456]{1,0:T(4,128)S(1)} %slice_bitcast_fusion.20), channel_id=1, source_target_pairs={{0,1},{1,0},{2,3},{3,2},{4,5},{5,4},{6,7},{7,6},{8,9},{9,8},{10,11... | collective-permute-start | bytes 165896 | tf_op jit(solution)/shard_map/ppermute | solution.py:95
  103.5 48.4 %collective-permute-start.24 = (bf16[2,1,1,1,72,3072]{5,4,3,2,1,0:T(8,128)(2,1)S(1)}, bf16[2,1,1,1,72,3072]{5,4,3,2,1,0:T(8,128)(2,1)}, u32[]{:S(2)}, u32[]{:S(2)}) collective-permute-start(bf16[2,1,1,1,72,3072]{5,4,3,2,1,0:T(8,128)(2,1)S(1)} %constant_dynamic-update-slice_fusion.7), channel_id=1, source_target_pairs={{0,8},{2,10},{4,12},{6,14},{8,0},{10,2},{12,4},{14,6},{16,24},{18,... | collective-permute-start | bytes 2654216 | tf_op jit(solution)/shard_map/ppermute | solution.py:87
  103.7 32.6 %collective-permute-start.18 = (bf16[2,1,1,2,72,2304]{5,4,3,2,1,0:T(8,128)(2,1)S(1)}, bf16[2,1,1,2,72,2304]{5,4,3,2,1,0:T(8,128)(2,1)S(1)}, u32[]{:S(2)}, u32[]{:S(2)}) collective-permute-start(bf16[2,1,1,2,72,2304]{5,4,3,2,1,0:T(8,128)(2,1)S(1)} %constant_dynamic-update-slice_fusion.11), channel_id=1, source_target_pairs={{0,4},{2,6},{4,0},{6,2},{8,12},{10,14},{12,8},{14,10},{16,20},{18,... | collective-permute-start | bytes 3981320 | tf_op jit(solution)/shard_map/ppermute | solution.py:87
  108.8 28.6 %collective-permute-start.19 = (bf16[2,1,2,1,72,2304]{5,4,3,2,1,0:T(8,128)(2,1)S(1)}, bf16[2,1,2,1,72,2304]{5,4,3,2,1,0:T(8,128)(2,1)S(1)}, u32[]{:S(2)}, u32[]{:S(2)}) collective-permute-start(bf16[2,1,2,1,72,2304]{5,4,3,2,1,0:T(8,128)(2,1)S(1)} %constant_dynamic-update-slice_fusion.10), channel_id=1, source_target_pairs={{0,2},{2,0},{4,6},{6,4},{8,10},{10,8},{12,14},{14,12},{16,18},{18,... | collective-permute-start | bytes 3981320 | tf_op jit(solution)/shard_map/ppermute | solution.py:87
  138.6 64.4 %collective-permute-start.20 = (bf16[2,2,2,2,72,2304]{5,4,3,2,1,0:T(8,128)(2,1)}, bf16[2,2,2,2,72,2304]{5,4,3,2,1,0:T(8,128)(2,1)}, u32[]{:S(2)}, u32[]{:S(2)}) collective-permute-start(bf16[2,2,2,2,72,2304]{5,4,3,2,1,0:T(8,128)(2,1)} %constant_dynamic-update-slice_fusion.8), channel_id=1, source_target_pairs={{0,1},{1,0},{2,3},{3,2},{4,5},{5,4},{6,7},{7,6},{8,9},{9,8},{10,11... | collective-permute-start | bytes 15925256 | tf_op jit(solution)/shard_map/ppermute | solution.py:95
  149.9 57.0 %collective-permute-start.21 = (bf16[1152,512]{1,0:T(8,128)(2,1)}, bf16[1152,512]{1,0:T(8,128)(2,1)S(1)}, u32[]{:S(2)}, u32[]{:S(2)}) collective-permute-start(bf16[1152,512]{1,0:T(8,128)(2,1)} %after.20.refs_0_), channel_id=1, source_target_pairs={{0,1},{1,0},{2,3},{3,2},{4,5},{5,4},{6,7},{7,6},{8,9},{9,8},{10,11... | collective-permute-start | bytes 3538952 | tf_op jit(solution)/shard_map/ppermute | solution.py:95
  154.0 41.7 %collective-permute-start.29 = (bf16[1,1,2,2,72,1536]{5,4,3,2,1,0:T(8,128)(2,1)}, bf16[1,1,2,2,72,1536]{5,4,3,2,1,0:T(8,128)(2,1)}, u32[]{:S(2)}, u32[]{:S(2)}) collective-permute-start(bf16[1,1,2,2,72,1536]{5,4,3,2,1,0:T(8,128)(2,1)} %after.23), channel_id=1, source_target_pairs={{0,16},{2,18},{4,20},{6,22},{8,24},{10,26},{12,28},{14,30},{16,0},... | collective-permute-start | bytes 2654216 | tf_op jit(solution)/shard_map/ppermute | solution.py:87
  161.7 37.5 %collective-permute-start.25 = (bf16[2,1,1,1,72,3072]{5,4,3,2,1,0:T(8,128)(2,1)S(1)}, bf16[2,1,1,1,72,3072]{5,4,3,2,1,0:T(8,128)(2,1)S(1)}, u32[]{:S(2)}, u32[]{:S(2)}) collective-permute-start(bf16[2,1,1,1,72,3072]{5,4,3,2,1,0:T(8,128)(2,1)S(1)} %get-tuple-element.126), channel_id=1, source_target_pairs={{0,2},{2,0},{4,6},{6,4},{8,10},{10,8},{12,14},{14,12},{16,18},{18,... | collective-permute-start | bytes 2654216 | tf_op jit(solution)/shard_map/ppermute | solution.py:87
  169.1 31.9 %collective-permute-start.26 = (bf16[2,1,1,1,72,3072]{5,4,3,2,1,0:T(8,128)(2,1)S(1)}, bf16[2,1,1,1,72,3072]{5,4,3,2,1,0:T(8,128)(2,1)S(1)}, u32[]{:S(2)}, u32[]{:S(2)}) collective-permute-start(bf16[2,1,1,1,72,3072]{5,4,3,2,1,0:T(8,128)(2,1)S(1)} %get-tuple-element.127), channel_id=1, source_target_pairs={{0,4},{2,6},{4,0},{6,2},{8,12},{10,14},{12,8},{14,10},{16,20},{18,... | collective-permute-start | bytes 2654216 | tf_op jit(solution)/shard_map/ppermute | solution.py:87
  197.0 40.5 %collective-permute-start.30 = (bf16[2,1,2,2,72,1536]{5,4,3,2,1,0:T(8,128)(2,1)S(1)}, bf16[2,1,2,2,72,1536]{5,4,3,2,1,0:T(8,128)(2,1)}, u32[]{:S(2)}, u32[]{:S(2)}) collective-permute-start(bf16[2,1,2,2,72,1536]{5,4,3,2,1,0:T(8,128)(2,1)S(1)} %constant_dynamic-update-slice_fusion.1), channel_id=1, source_target_pairs={{0,8},{2,10},{4,12},{6,14},{8,0},{10,2},{12,4},{14,6},{16,24},{18,... | collective-permute-start | bytes 5308424 | tf_op jit(solution)/shard_map/ppermute | solution.py:87
  200.2 40.7 %collective-permute-start.27 = (bf16[2,1,1,2,72,3072]{5,4,3,2,1,0:T(8,128)(2,1)}, bf16[2,1,1,2,72,3072]{5,4,3,2,1,0:T(8,128)(2,1)}, u32[]{:S(2)}, u32[]{:S(2)}) collective-permute-start(bf16[2,1,1,2,72,3072]{5,4,3,2,1,0:T(8,128)(2,1)} %constant_dynamic-update-slice_fusion.5), channel_id=1, source_target_pairs={{0,4},{2,6},{4,0},{6,2},{8,12},{10,14},{12,8},{14,10},{16,20},{18,... | collective-permute-start | bytes 5308424 | tf_op jit(solution)/shard_map/ppermute | solution.py:87
  202.0 40.6 %collective-permute-start.28 = (bf16[2,1,2,1,72,3072]{5,4,3,2,1,0:T(8,128)(2,1)}, bf16[2,1,2,1,72,3072]{5,4,3,2,1,0:T(8,128)(2,1)}, u32[]{:S(2)}, u32[]{:S(2)}) collective-permute-start(bf16[2,1,2,1,72,3072]{5,4,3,2,1,0:T(8,128)(2,1)} %constant_dynamic-update-slice_fusion.4), channel_id=1, source_target_pairs={{0,2},{2,0},{4,6},{6,4},{8,10},{10,8},{12,14},{14,12},{16,18},{18,... | collective-permute-start | bytes 5308424 | tf_op jit(solution)/shard_map/ppermute | solution.py:87
  231.2 13.8 %collective-permute-start.22 = (bf16[512,1152]{1,0:T(8,128)(2,1)S(1)}, bf16[512,1152]{1,0:T(8,128)(2,1)S(1)}, u32[]{:S(2)}, u32[]{:S(2)}) collective-permute-start(bf16[512,1152]{1,0:T(8,128)(2,1)S(1)} %add_convert_fusion.5), channel_id=1, source_target_pairs={{0,1},{1,0},{2,3},{3,2},{4,5},{5,4},{6,7},{7,6},{8,9},{9,8},{10,11... | collective-permute-start | bytes 3538952 | tf_op jit(solution)/shard_map/ppermute | solution.py:95
  242.6 9.0 %collective-permute-start.32 = (bf16[512,1152]{1,0:T(8,128)(2,1)S(1)}, bf16[512,1152]{1,0:T(8,128)(2,1)S(1)}, u32[]{:S(2)}, u32[]{:S(2)}) collective-permute-start(bf16[512,1152]{1,0:T(8,128)(2,1)S(1)} %get-tuple-element.164), channel_id=1, source_target_pairs={{0,1},{1,0},{2,3},{3,2},{4,5},{5,4},{6,7},{7,6},{8,9},{9,8},{10,11... | collective-permute-start | bytes 3538952 | tf_op jit(solution)/shard_map/ppermute | solution.py:95
  244.4 50.3 %collective-permute-start.34 = (bf16[1152,512]{1,0:T(8,128)(2,1)S(1)}, bf16[1152,512]{1,0:T(8,128)(2,1)}, u32[]{:S(2)}, u32[]{:S(2)}) collective-permute-start(bf16[1152,512]{1,0:T(8,128)(2,1)S(1)} %bitcast.204), channel_id=1, source_target_pairs={{0,1},{1,0},{2,3},{3,2},{4,5},{5,4},{6,7},{7,6},{8,9},{9,8},{10,11... | collective-permute-start | bytes 3538952 | tf_op jit(solution)/shard_map/ppermute | solution.py:95
  280.1 48.5 %collective-permute-start.31 = (bf16[512,1152]{1,0:T(8,128)(2,1)}, bf16[512,1152]{1,0:T(8,128)(2,1)S(1)}, u32[]{:S(2)}, u32[]{:S(2)}) collective-permute-start(bf16[512,1152]{1,0:T(8,128)(2,1)} %slice.563), channel_id=1, source_target_pairs={{0,1},{1,0},{2,3},{3,2},{4,5},{5,4},{6,7},{7,6},{8,9},{9,8},{10,11... | collective-permute-start | bytes 3538952 | tf_op jit(solution)/shard_map/ppermute | solution.py:95
  292.1 36.5 %collective-permute-start.33 = (bf16[512,1152]{1,0:T(8,128)(2,1)}, bf16[512,1152]{1,0:T(8,128)(2,1)S(1)}, u32[]{:S(2)}, u32[]{:S(2)}) collective-permute-start(bf16[512,1152]{1,0:T(8,128)(2,1)} %slice.562), channel_id=1, source_target_pairs={{0,1},{1,0},{2,3},{3,2},{4,5},{5,4},{6,7},{7,6},{8,9},{9,8},{10,11... | collective-permute-start | bytes 3538952 | tf_op jit(solution)/shard_map/ppermute | solution.py:95
  304.8 44.3 %collective-permute-start.35 = (bf16[8,72,1536]{2,1,0:T(8,128)(2,1)}, bf16[8,72,1536]{2,1,0:T(8,128)(2,1)}, u32[]{:S(2)}, u32[]{:S(2)}) collective-permute-start(bf16[8,72,1536]{2,1,0:T(8,128)(2,1)} %get-tuple-element.50), channel_id=1, source_target_pairs={{0,8},{2,10},{4,12},{6,14},{8,0},{10,2},{12,4},{14,6},{16,24},{18,... | collective-permute-start | bytes 5308424 | tf_op jit(solution)/shard_map/ppermute | solution.py:87
  326.6 41.0 %collective-permute-start.36 = (bf16[4,72,3072]{2,1,0:T(8,128)(2,1)}, bf16[4,72,3072]{2,1,0:T(8,128)(2,1)}, u32[]{:S(2)}, u32[]{:S(2)}) collective-permute-start(bf16[4,72,3072]{2,1,0:T(8,128)(2,1)} %get-tuple-element.53), channel_id=1, source_target_pairs={{0,4},{2,6},{4,0},{6,2},{8,12},{10,14},{12,8},{14,10},{16,20},{18,... | collective-permute-start | bytes 5308424 | tf_op jit(solution)/shard_map/ppermute | solution.py:87
  327.6 42.3 %collective-permute-start.37 = (bf16[4,72,3072]{2,1,0:T(8,128)(2,1)}, bf16[4,72,3072]{2,1,0:T(8,128)(2,1)}, u32[]{:S(2)}, u32[]{:S(2)}) collective-permute-start(bf16[4,72,3072]{2,1,0:T(8,128)(2,1)} %get-tuple-element.55), channel_id=1, source_target_pairs={{0,2},{2,0},{4,6},{6,4},{8,10},{10,8},{12,14},{14,12},{16,18},{18,... | collective-permute-start | bytes 5308424 | tf_op jit(solution)/shard_map/ppermute | solution.py:87
  340.4 71.8 %collective-permute-start.39 = (bf16[2,2,2,2,32,576]{5,4,3,2,1,0:T(8,128)(2,1)}, bf16[2,2,2,2,32,576]{5,4,3,2,1,0:T(8,128)(2,1)}, u32[]{:S(2)}, u32[]{:S(2)}) collective-permute-start(bf16[2,2,2,2,32,576]{5,4,3,2,1,0:T(8,128)(2,1)} %bitcast.36), channel_id=1, source_target_pairs={{0,1},{1,0},{2,3},{3,2},{4,5},{5,4},{6,7},{7,6},{8,9},{9,8},{10,11... | collective-permute-start | bytes 1769480 | tf_op jit(solution)/shard_map/ppermute | solution.py:95
  352.5 57.4 %collective-permute-start.57 = (bf16[2,2,72,1536]{3,2,1,0:T(8,128)(2,1)}, bf16[2,2,72,1536]{3,2,1,0:T(8,128)(2,1)}, u32[]{:S(2)}, u32[]{:S(2)}) collective-permute-start(bf16[2,2,72,1536]{3,2,1,0:T(8,128)(2,1)} %bitcast.29.refs_1_), channel_id=1, source_target_pairs={{0,16},{2,18},{4,20},{6,22},{8,24},{10,26},{12,28},{14,30},{16,0},... | collective-permute-start | bytes 2654216 | tf_op jit(solution)/shard_map/ppermute | solution.py:87
  374.1 26.0 %collective-permute-start.53 = (bf16[2,72,3072]{2,1,0:T(8,128)(2,1)}, bf16[2,72,3072]{2,1,0:T(8,128)(2,1)}, u32[]{:S(2)}, u32[]{:S(2)}) collective-permute-start(bf16[2,72,3072]{2,1,0:T(8,128)(2,1)} %get-tuple-element.181.refs_2_), channel_id=1, source_target_pairs={{0,2},{2,0},{4,6},{6,4},{8,10},{10,8},{12,14},{14,12},{16,18},{18,... | collective-permute-start | bytes 2654216 | tf_op jit(solution)/shard_map/ppermute | solution.py:87
  385.1 27.1 %collective-permute-start.38 = (bf16[1728,512]{1,0:T(8,128)(2,1)S(1)}, bf16[1728,512]{1,0:T(8,128)(2,1)}, u32[]{:S(2)}, u32[]{:S(2)}) collective-permute-start(bf16[1728,512]{1,0:T(8,128)(2,1)S(1)} %bitcast.167), channel_id=1, source_target_pairs={{0,1},{1,0},{2,3},{3,2},{4,5},{5,4},{6,7},{7,6},{8,9},{9,8},{10,11... | collective-permute-start | bytes 5308424 | tf_op jit(solution)/shard_map/ppermute | solution.py:95
  385.2 22.4 %collective-permute-start.54 = (bf16[2,72,3072]{2,1,0:T(8,128)(2,1)}, bf16[2,72,3072]{2,1,0:T(8,128)(2,1)}, u32[]{:S(2)}, u32[]{:S(2)}) collective-permute-start(bf16[2,72,3072]{2,1,0:T(8,128)(2,1)} %get-tuple-element.180.refs_3_), channel_id=1, source_target_pairs={{0,4},{2,6},{4,0},{6,2},{8,12},{10,14},{12,8},{14,10},{16,20},{18,... | collective-permute-start | bytes 2654216 | tf_op jit(solution)/shard_map/ppermute | solution.py:87
  442.2 67.9 %collective-permute-start.40 = (bf16[4,72,2368]{2,1,0:T(8,128)(2,1)}, bf16[4,72,2368]{2,1,0:T(8,128)(2,1)}, u32[]{:S(2)}, u32[]{:S(2)}) collective-permute-start(bf16[4,72,2368]{2,1,0:T(8,128)(2,1)} %get-tuple-element.57.refs_1_), channel_id=1, source_target_pairs={{0,4},{2,6},{4,0},{6,2},{8,12},{10,14},{12,8},{14,10},{16,20},{18,... | collective-permute-start | bytes 4091912 | tf_op jit(solution)/shard_map/ppermute | solution.py:87
  443.2 69.9 %collective-permute-start.42 = (bf16[4,72,2368]{2,1,0:T(8,128)(2,1)}, bf16[4,72,2368]{2,1,0:T(8,128)(2,1)}, u32[]{:S(2)}, u32[]{:S(2)}) collective-permute-start(bf16[4,72,2368]{2,1,0:T(8,128)(2,1)} %get-tuple-element.58.refs_2_), channel_id=1, source_target_pairs={{0,2},{2,0},{4,6},{6,4},{8,10},{10,8},{12,14},{14,12},{16,18},{18,... | collective-permute-start | bytes 4091912 | tf_op jit(solution)/shard_map/ppermute | solution.py:87
  447.9 37.0 %collective-permute-start.58 = (bf16[2,72,1536]{2,1,0:T(8,128)(2,1)}, bf16[2,72,1536]{2,1,0:T(8,128)(2,1)}, u32[]{:S(2)}, u32[]{:S(2)}) collective-permute-start(bf16[2,72,1536]{2,1,0:T(8,128)(2,1)} %slice_bitcast_fusion.8), channel_id=1, source_target_pairs={{0,2},{2,0},{4,6},{6,4},{8,10},{10,8},{12,14},{14,12},{16,18},{18,... | collective-permute-start | bytes 1327112 | tf_op jit(solution)/shard_map/ppermute | solution.py:87
  449.0 38.3 %collective-permute-start.55 = (bf16[2,72,3072]{2,1,0:T(8,128)(2,1)}, bf16[2,72,3072]{2,1,0:T(8,128)(2,1)}, u32[]{:S(2)}, u32[]{:S(2)}) collective-permute-start(bf16[2,72,3072]{2,1,0:T(8,128)(2,1)} %after.30), channel_id=1, source_target_pairs={{0,8},{2,10},{4,12},{6,14},{8,0},{10,2},{12,4},{14,6},{16,24},{18,... | collective-permute-start | bytes 2654216 | tf_op jit(solution)/shard_map/ppermute | solution.py:87
  450.1 3.5 collective-permute-start.47
  453.6 14.9 %collective-permute-start.48 = (bf16[1,1,1,1,8,3456]{5,4,3,2,1,0:T(8,128)(2,1)S(1)}, bf16[1,1,1,1,8,3456]{5,4,3,2,1,0:T(8,128)(2,1)S(1)}, u32[]{:S(2)}, u32[]{:S(2)}) collective-permute-start(bf16[1,1,1,1,8,3456]{5,4,3,2,1,0:T(8,128)(2,1)S(1)} %maximum_bitcast_fusion), channel_id=1, source_target_pairs={{0,16},{2,18},{4,20},{6,22},{8,24},{10,26},{12,28},{14,30},{16,0},... | collective-permute-start | bytes 165896 | tf_op jit(solution)/shard_map/ppermute | solution.py:87
  468.6 20.6 %collective-permute-start.49 = (bf16[2,1,1,1,8,3456]{5,4,3,2,1,0:T(8,128)(2,1)S(1)}, bf16[2,1,1,1,8,3456]{5,4,3,2,1,0:T(8,128)(2,1)S(1)}, u32[]{:S(2)}, u32[]{:S(2)}) collective-permute-start(bf16[2,1,1,1,8,3456]{5,4,3,2,1,0:T(8,128)(2,1)S(1)} %pad_maximum_fusion.27), channel_id=1, source_target_pairs={{0,8},{2,10},{4,12},{6,14},{8,0},{10,2},{12,4},{14,6},{16,24},{18,... | collective-permute-start | bytes 331784 | tf_op jit(solution)/shard_map/ppermute | solution.py:87
  486.1 6.0 collective-permute-start.59
  488.7 20.4 %collective-permute-start.56 = (bf16[72,3072]{1,0:T(8,128)(2,1)S(1)}, bf16[72,3072]{1,0:T(8,128)(2,1)S(1)}, u32[]{:S(2)}, u32[]{:S(2)}) collective-permute-start(bf16[72,3072]{1,0:T(8,128)(2,1)S(1)} %slice_bitcast_fusion.12), channel_id=1, source_target_pairs={{0,16},{2,18},{4,20},{6,22},{8,24},{10,26},{12,28},{14,30},{16,0},... | collective-permute-start | bytes 1327112 | tf_op jit(solution)/shard_map/ppermute | solution.py:87
  515.9 20.3 %collective-permute-start.50 = (bf16[2,2,1,1,8,3456]{5,4,3,2,1,0:T(8,128)(2,1)}, bf16[2,2,1,1,8,3456]{5,4,3,2,1,0:T(8,128)(2,1)S(1)}, u32[]{:S(2)}, u32[]{:S(2)}) collective-permute-start(bf16[2,2,1,1,8,3456]{5,4,3,2,1,0:T(8,128)(2,1)} %after.28), channel_id=1, source_target_pairs={{0,2},{2,0},{4,6},{6,4},{8,10},{10,8},{12,14},{14,12},{16,18},{18,... | collective-permute-start | bytes 663560 | tf_op jit(solution)/shard_map/ppermute | solution.py:87
  517.3 17.7 %collective-permute-start.43 = (bf16[2,72,2368]{2,1,0:T(8,128)(2,1)S(1)}, bf16[2,72,2368]{2,1,0:T(8,128)(2,1)S(1)}, u32[]{:S(2)}, u32[]{:S(2)}) collective-permute-start(bf16[2,72,2368]{2,1,0:T(8,128)(2,1)S(1)} %slice_bitcast_fusion.4), channel_id=1, source_target_pairs={{0,4},{2,6},{4,0},{6,2},{8,12},{10,14},{12,8},{14,10},{16,20},{18,... | collective-permute-start | bytes 2045960 | tf_op jit(solution)/shard_map/ppermute | solution.py:87
  518.4 20.1 %collective-permute-start.41 = (bf16[2,72,2368]{2,1,0:T(8,128)(2,1)S(1)}, bf16[2,72,2368]{2,1,0:T(8,128)(2,1)S(1)}, u32[]{:S(2)}, u32[]{:S(2)}) collective-permute-start(bf16[2,72,2368]{2,1,0:T(8,128)(2,1)S(1)} %slice_bitcast_fusion.6), channel_id=1, source_target_pairs={{0,2},{2,0},{4,6},{6,4},{8,10},{10,8},{12,14},{14,12},{16,18},{18,... | collective-permute-start | bytes 2045960 | tf_op jit(solution)/shard_map/ppermute | solution.py:87
  535.2 16.8 %collective-permute-start.44 = (bf16[2,72,2368]{2,1,0:T(8,128)(2,1)S(1)}, bf16[2,72,2368]{2,1,0:T(8,128)(2,1)S(1)}, u32[]{:S(2)}, u32[]{:S(2)}) collective-permute-start(bf16[2,72,2368]{2,1,0:T(8,128)(2,1)S(1)} %fusion.24), channel_id=1, source_target_pairs={{0,8},{2,10},{4,12},{6,14},{8,0},{10,2},{12,4},{14,6},{16,24},{18,... | collective-permute-start | bytes 2045960 | tf_op jit(solution)/shard_map/ppermute | solution.py:87
  536.2 16.5 %collective-permute-start.51 = (bf16[2,2,1,2,8,3456]{5,4,3,2,1,0:T(8,128)(2,1)S(1)}, bf16[2,2,1,2,8,3456]{5,4,3,2,1,0:T(8,128)(2,1)S(1)}, u32[]{:S(2)}, u32[]{:S(2)}) collective-permute-start(bf16[2,2,1,2,8,3456]{5,4,3,2,1,0:T(8,128)(2,1)S(1)} %pad_maximum_fusion.21), channel_id=1, source_target_pairs={{0,4},{2,6},{4,0},{6,2},{8,12},{10,14},{12,8},{14,10},{16,20},{18,... | collective-permute-start | bytes 1327112 | tf_op jit(solution)/shard_map/ppermute | solution.py:87
  552.3 16.8 %collective-permute-start.45 = (bf16[72,2368]{1,0:T(8,128)(2,1)S(1)}, bf16[72,2368]{1,0:T(8,128)(2,1)S(1)}, u32[]{:S(2)}, u32[]{:S(2)}) collective-permute-start(bf16[72,2368]{1,0:T(8,128)(2,1)S(1)} %slice_bitcast_fusion.14), channel_id=1, source_target_pairs={{0,16},{2,18},{4,20},{6,22},{8,24},{10,26},{12,28},{14,30},{16,0},... | collective-permute-start | bytes 1022984 | tf_op jit(solution)/shard_map/ppermute | solution.py:87
  553.0 17.6 %collective-permute-start.52 = (f32[1,3456]{1,0:T(1,128)S(1)}, f32[1,3456]{1,0:T(1,128)S(1)}, u32[]{:S(2)}, u32[]{:S(2)}) collective-permute-start(f32[1,3456]{1,0:T(1,128)S(1)} %broadcast_in_dim.411), channel_id=1, source_target_pairs={{0,1},{1,0},{2,3},{3,2},{4,5},{5,4},{6,7},{7,6},{8,9},{9,8},{10,11... | collective-permute-start | bytes 41480 | tf_op jit(solution)/shard_map/ppermute | solution.py:95
  570.6 1.6 collective-permute-start.46
  584.1 3.6 collective-permute-start.61
  588.4 3.6 collective-permute-start.62
  592.6 3.6 collective-permute-start.63
  596.9 4.5 collective-permute-start.64
  (132 other events, 1263.0 us)

commit v3 on v2

--- a/solution.py
+++ b/solution.py
@@ -239,12 +239,13 @@
 
 
 def heads_kernel(x_ref, w_ref, *refs):
-    out_ref = refs[-1]
+    out_ref, turned_ref = refs[-2:]
     step = min(256, x_ref.shape[0])
     for start in range(0, x_ref.shape[0], step):
         rows = slice(start, start + step)
         product = dots(x_ref[rows, :], w_ref[:, : out_ref.shape[0]], 1, 0)
         out_ref[:, rows] = product.T
+        turned_ref[:, rows] = x_ref[rows, :].T
 
 
 def heads_of(value, weight, columns, *others):
@@ -253,7 +254,10 @@
         heads_kernel,
         in_specs=[pl.BlockSpec(memory_space=pltpu.VMEM)] * 2
         + [pl.BlockSpec(memory_space=pl.ANY)] * len(others),
-        out_shape=jax.ShapeDtypeStruct(shape, jnp.float32),
+        out_shape=[
+            jax.ShapeDtypeStruct(shape, jnp.float32),
+            jax.ShapeDtypeStruct(value.shape[::-1], value.dtype),
+        ],
         compiler_params=pltpu.CompilerParams(vmem_limit_bytes=48 << 20),
         cost_estimate=cost(5),
         name="heads_of",
@@ -381,7 +385,7 @@
     )(lax.axis_index("tok").reshape(1), *lefts, *[pair[1] for pair in flat], *others)
 
 
-def scatter_on(value, left_bits, order, count, last=jnp.bfloat16):
+def scatter_on(value, left_bits, order, count, last=jnp.bfloat16, hold=()):
     left_bits = list(left_bits)
     sent = []
     for bit in order:
@@ -390,7 +394,10 @@
         away = lax.index_in_dim(value, 1, axis, keepdims=False)
         sent.append(away)
         kept = last if bit == order[-1] else jnp.bfloat16
-        value = add(lax.index_in_dim(value, 0, axis, keepdims=False), trade(away, bit, count), kept)
+        stay = lax.index_in_dim(value, 0, axis, keepdims=False)
+        if hold and bit == order[-1]:
+            stay = after(stay, *hold)
+        value = add(stay, trade(away, bit, count), kept)
         left_bits.remove(bit)
     return value, sent
 
@@ -415,7 +422,7 @@
     bits = first[::-1] + order
     if row_size(terms, turned, count) % 8:
         half, sent = half_scatter(plain_products(terms, turned, columns), count)
-        return sent[:1], [half], lambda value: last_scatter(value[0], count)
+        return sent[:1], [half], lambda value, _: last_scatter(value[0], count)
     away, kept = grad_parts(terms, turned, columns, [{bits[0]: 1}, {bits[0]: 0}], count, *others)
     left_bits = other_bits(bits[:1], count)
     value = add(kept, trade(away, bits[0], count))
@@ -424,15 +431,15 @@
     return (
         sent[:1],
         [value],
-        lambda value: scatter_on(value[0], left_bits, order, count, jnp.float32)[0],
-    )
-
-
-def across_scatter(terms, turned, columns, count):
+        lambda value, hold: scatter_on(value[0], left_bits, order, count, jnp.float32, hold)[0],
+    )
+
+
+def across_scatter(terms, turned, columns, count, hold=()):
     first, order_a, order_b = orders(count)
     if row_size(terms, turned, count) % 8:
         half, sent = half_scatter(plain_products(terms, turned, columns), count)
-        return [half], sent, [], [], lambda value: last_scatter(value[0], count)
+        return [half], sent, [], [], lambda value, *_: value, lambda value, *_: last_scatter(value[0], count)
     half_bit = first[-1]
     parts = [
         {half_bit: half, order[-1]: away}
@@ -444,19 +451,23 @@
     for place, order in enumerate((order_a, order_b)):
         away, kept = blocks[2 * place : 2 * place + 2]
         left_bits = other_bits((order[-1], half_bit), count)
-        value = add(kept, trade(away, order[-1], count))
+        moved = trade(away, order[-1], count)
+        value = add(after(kept, *hold) if hold else kept, moved)
         firsts.append(value)
-        value, sent = scatter_on(value, left_bits, order[-2::-1], count)
-        halves.append(value)
-        mids += sent[:1]
-
-    def finish(halves):
+        halves.append((value, left_bits, order[-2::-1]))
+        mids += scatter_on(value, left_bits, order[-2::-1], count)[1][:1]
+
+    def begin(halves, before=()):
+        return [scatter_on(*half, count, hold=before)[0] for half in halves]
+
+    def finish(halves, between=()):
         kept, away = halves
+        kept = after(kept, *between[:2]) if between else kept
         value = add(kept, trade(away, half_bit, count))
         left_bits = [bit for bit in other_bits((), count) if bit in first[:-1]]
-        return scatter_on(value, left_bits, first[-2::-1], count, jnp.float32)[0]
-
-    return halves, [blocks[0], blocks[2]], firsts, mids, finish
+        return scatter_on(value, left_bits, first[-2::-1], count, jnp.float32, between[2:])[0]
+
+    return halves, [blocks[0], blocks[2]], firsts, mids, begin, finish
 
 
 def row_major(value):
@@ -503,7 +514,7 @@
     return halves
 
 
-def last_gather(halves, count):
+def last_gather(halves, count, *others):
     first, order_a, order_b = orders(count)
     axis = axis_of(first[-1], count)
     lasts = (order_a[-1], order_b[-1])
@@ -515,6 +526,7 @@
         ],
         axis=axis,
     )
+    out = after(out, *others) if others else out
     for place, (bit, value) in enumerate(zip(lasts, moved)):
         out = put(out, value, {axis: place, axis_of(bit, count): 1 - bit_of(bit)}, count)
     return out.reshape(-1, out.shape[-1])
@@ -649,7 +661,7 @@
     codes = jnp.stack([class_label, time_index], axis=1)
     first, order, _ = orders(chips)
     codes = spread(jnp.concatenate([codes, swap(codes)], axis=0), chips)
-    codes = gather_small(codes, chips, first)
+    codes = gather_small(codes, chips, order)
 
     mix_low = mix_weight.astype(half)
     mix_parts = [mix_low[:, :group], mix_low[:, group : 2 * group], mix_low[:, 2 * group :]]
@@ -660,9 +672,10 @@
         jnp.concatenate([mix_moved, mix_parts[0], mix_parts[2]], axis=1),
     )
     mix_shard = jnp.concatenate([mix_shard, proj_weight.astype(half)], axis=1)
-    mix_first = spread(after(mix_shard, codes), chips)
+    codes = gather_small(codes, chips, first)
+    mix_first = after(spread(mix_shard, chips), codes)
     mix_first = doubled(mix_first, first[0], chips)
-    codes = gather_small(after(codes, mix_first), chips, order)
+    nothing = jnp.minimum(jnp.abs(mix_first.reshape(-1)[0].astype(jnp.float32)), 0.0)
     codes = stacked(codes, chips)
     labels, times = codes[:, 0], codes[:, 1]
     for bit in first[1:]:
@@ -688,45 +701,42 @@
     )
     mod_half = split_rows(partial_mod + bias_row[None, :], chips)
     mod_half = scatter_small(mod_half, chips, order[:1])
-    mod_half = scatter_small(after(mod_half, mix_first), chips, order[1:])
-    far_down = spread(down_weight.T.astype(half), chips)
-    for bit in order:
-        far_down = doubled(far_down, bit, chips)
-    mix_halves = next_gather(after(mix_first, mod_half, far_down), chips)
-    mod_half = scatter_small(mod_half, chips, first[::-1])
+    mod_half = scatter_small(mod_half, chips, order[1:])
+    mix_halves = next_gather(mix_first, chips)
+    mod_half = scatter_small(after(mod_half, mix_first), chips, first[::-1])
     mod_half = mod_half.reshape(-1, cond_cols)
     slots = class_label.shape[0]
     modulation = joined(mod_half[:slots], swap(mod_half[slots:]))
 
-    mix_own = last_gather(mix_halves, chips)
-    far = jnp.concatenate([feed_weight[0].astype(half), feed_weight[1].astype(half)], axis=1)
-    far = first_gather(after(far, mix_first), chips)
-    far_down = after(far_down, far)
-    for bit in first:
-        far_down = doubled(far_down, bit, chips)
-    far_down = far_down.reshape(width, hidden_cols)
-    far = last_gather(next_gather(after(far, mix_own), chips), chips)
-    far_gate, far_up = far[:, :hidden_cols], far[:, hidden_cols:]
-    mix_other = swap_rows(mix_own, chips)
-    proj_full = joined(mix_own[:, mix_cols:], mix_other[:, mix_cols:])
-
-    segment, member, rows, cols = geometry(grid_height, grid_width, count)
+    later = nothing.astype(jnp.int32)
+    segment, member, rows, cols = geometry(grid_height + later, grid_width + later, count)
     tables = turn_tables(rows, cols) + (segment[None, :], segment[:, None])
     valid = (segment < SLOTS).astype(jnp.float32)[:, None]
     shift_a, scale_a, gate_a, shift_b, scale_b, gate_b = (
         pick(segment, table) for table in jnp.split(modulation, 6, axis=1)
     )
-    inputs = block_input.astype(jnp.float32)
+    inputs = block_input.astype(jnp.float32) + nothing
     first_in = modulate(inputs, shift_a, scale_a).astype(half)
-    first_turned = after(first_in.T, first_in)
+
+    mix_own = last_gather(mix_halves, chips, first_in)
+    far = jnp.concatenate(
+        [(value + nothing).astype(half) for value in (feed_weight[0], feed_weight[1], down_weight.T)],
+        axis=1,
+    )
+    far = first_gather(after(far, mix_first, mod_half), chips)
+    far = last_gather(next_gather(after(far, first_in), chips), chips)
+    far_gate, far_up, far_down = (
+        far[:, place * hidden_cols : (place + 1) * hidden_cols] for place in range(3)
+    )
+    mix_other = swap_rows(mix_own, chips)
+    proj_full = joined(mix_own[:, mix_cols:], mix_other[:, mix_cols:])
+
+    shape = (3, heads, HEAD, count)
+    raw_own, first_turned = heads_of(first_in, mix_own, mix_cols)
     first_moved = swap(first_turned)
-
-    shape = (3, heads, HEAD, count)
-    att_own, log_own, *qkv_own = attend(
-        heads_of(first_in, mix_own, mix_cols).reshape(shape), tables
-    )
+    att_own, log_own, *qkv_own = attend(raw_own.reshape(shape), tables)
     att_other, log_other, *qkv_other = attend(
-        heads_of(first_in, mix_other, mix_cols, first_moved).reshape(shape), tables
+        heads_of(first_in, mix_other, mix_cols, first_moved)[0].reshape(shape), tables
     )
     attended = joined(att_own, att_other, 0).reshape(width, count)
     attended_moved = swap(attended)
@@ -737,12 +747,7 @@
     gate_pre = jnp.dot(second_pair, far_gate, preferred_element_type=jnp.float32)
     up_pre = jnp.dot(second_pair, far_up, preferred_element_type=jnp.float32)
     hidden = (jax.nn.silu(gate_pre) * up_pre).astype(half)
-    partial_value = against(hidden, far_down)
-    result = partial_value[:count] + swap(partial_value[count:].astype(half)).astype(jnp.float32)
-    block_output = (valid * (middle + gate_b * result)).astype(half)
-
     grad_out = valid * out_grad.astype(jnp.float32)
-    d_gate_b = grad_out * result
     result_grad = (gate_b * grad_out).astype(half)
     result_pair = jnp.concatenate([result_grad, swap(result_grad)], axis=0)
     down_sent, down_half, down_finish = chain_scatter(
@@ -752,12 +757,6 @@
     sig = jax.nn.sigmoid(gate_pre)
     gate_grad = (d_hidden * up_pre * sig * (1.0 + gate_pre * (1.0 - sig))).astype(half)
     up_grad = (d_hidden * gate_pre * sig).astype(half)
-    feed_half, _, _, feed_mids, feed_finish = across_scatter(
-        [([(second_pair, gate_grad, 0)], 0), ([(second_pair, up_grad, 0)], hidden_cols)],
-        True,
-        2 * hidden_cols,
-        chips,
-    )
     second_part = against(gate_grad, far_gate) + against(up_grad, far_up)
     second_grad = second_part[:count] + swap(second_part[count:].astype(half)).astype(jnp.float32)
     pull_second = jax.vjp(modulate, middle, shift_b, scale_b)[1]
@@ -771,11 +770,18 @@
     grad_other = after(grad_other, *down_sent)
     mg_other = attend_back(*qkv_other, grad_other, log_other, tables).reshape(mix_cols, count)
     mg_moved = swap(mg_other)
-    grad_own = after(grad_own, mg_other, *feed_mids)
+    feed_half, _, _, feed_mids, feed_begin, feed_finish = across_scatter(
+        [([(second_pair, gate_grad, 0)], 0), ([(second_pair, up_grad, 0)], hidden_cols)],
+        True,
+        2 * hidden_cols,
+        chips,
+        (mg_other,),
+    )
+    grad_own = after(grad_own, *feed_mids) if feed_mids else grad_own
     mg_own = attend_back(*qkv_own, grad_own, log_own, tables).reshape(mix_cols, count)
     branch_grad_own, branch_grad_other = parted(branch_grad)
     proj_start = -(-mix_cols // 128) * 128
-    near_half, near_sent, near_firsts, _, near_finish = across_scatter(
+    near_half, near_sent, _, near_mids, near_begin, near_finish = across_scatter(
         [
             ([(first_turned, mg_own, 1), (first_moved, mg_moved, 1)], 0),
             ([(attended, branch_grad_own, 0), (attended_moved, swap_rows(branch_grad_other, chips), 0)], proj_start),
@@ -784,8 +790,10 @@
         proj_start + proj_cols,
         chips,
     )
-    down_grad = down_finish(jax.tree.map(lambda value: after(value, *near_sent), down_half)).T
-    feed_grad = feed_finish(jax.tree.map(lambda value: after(value, *near_sent), feed_half))
+    down_grad = down_finish([after(value, *near_sent) for value in down_half], near_mids).T
+    feed_half = feed_begin(feed_half, near_sent)
+    near_half = near_begin(near_half)
+    feed_grad = feed_finish(feed_half, [*near_mids, near_half[-1]])
     feed_grad = jnp.stack([feed_grad[:, :hidden_cols], feed_grad[:, hidden_cols:]])
     near_grad = near_finish(near_half)
     proj_grad = near_grad[:, proj_start:]
@@ -797,12 +805,17 @@
         jnp.concatenate([mix_parts[1], mix_moved, mix_parts[2]], axis=1),
     )
 
-    mg_own, mg_other = after(mg_own, *near_sent), after(mg_other, *near_sent)
+    partial_value = against(after(hidden, *near_sent), far_down)
+    result = partial_value[:count] + swap(partial_value[count:].astype(half)).astype(jnp.float32)
+    block_output = (valid * (middle + gate_b * result)).astype(half)
+    d_gate_b = grad_out * result
+    held = [*near_sent, feed_half[-1]]
+    mg_own, mg_other = after(mg_own, *held), after(mg_other, *held)
     first_grad = back_through(mg_own, mg_other, mix_own, mix_other)
     pull_first = jax.vjp(modulate, inputs, shift_a, scale_a)[1]
     d_inputs, d_shift_a, d_scale_a = pull_first(first_grad)
     input_grad = d_inputs + d_middle
-    member_low = member.astype(half)
+    member_low = after(member.astype(half), *near_sent)
     d_modulation = jnp.concatenate(
         [
             across(member_low, piece.astype(half))
@@ -812,8 +825,8 @@
     ).astype(half)
     mod_own, mod_other = parted(d_modulation)
     mod_all = spread(jnp.concatenate([mod_own, swap(mod_other)], axis=0), chips)
-    mod_all = after(gather_small(mod_all, chips, first), *near_firsts)
-    mod_all = stacked(gather_small(mod_all, chips, order), chips)
+    mod_all = gather_small(after(mod_all, *near_mids), chips, first + order)
+    mod_all = stacked(mod_all, chips)
     cond_grad = across(cond_low, mod_all)
     bias_half = jnp.sum(mod_all.astype(jnp.float32), axis=0)[None, :]
     bias_full = joined(bias_half, swap(bias_half))[0]
@@ -822,7 +835,7 @@
 
     grads = (mix_grad, proj_grad, cond_grad, bias_grad, feed_grad, down_grad)
     local_squares = jnp.float32(0.0)
-    for grad in grads:
+    for grad in (near_grad[:, :mix_cols], *grads[1:]):
         local_squares = local_squares + jnp.sum(grad * grad)
     grad_norm = jnp.sqrt(sum_all(local_squares, chips))
     factor = CLIP_NORM / jnp.maximum(grad_norm, CLIP_NORM)

time: 622 us -> 589 us (0.947)
  waiting for transfers between devices: 202 us -> 151 us
  local copies, waits for them, and re-layouts: 58.3 us -> 66 us
  matrix products: 59.2 us -> 66.6 us
    ppermute x48 -> x44, waiting for transfers between devices: 201 us -> 151 us  [trade(): lax.ppermute(value, 'tok', [(place, place ^ 1 << bit) for place in range(...]
    concatenate x12 -> x8, other arithmetic: 18.7 us -> 13.2 us  [doubled(): out = jnp.concatenate([value, value], axis=axis)]
    unnamed x262 -> x346, local copies, waits for them, and re-layouts: 18 us -> 20.8 us
    dynamic_update_slice x16 -> x12, local copies, waits for them, and re-layouts: 18.5 us -> 16.8 us  [put(): return lax.dynamic_update_slice(out, value, tuple(start))]
    ppermute x48 -> x44, starting transfers between devices: 55.4 us -> 56.2 us  [trade(): lax.ppermute(value, 'tok', [(place, place ^ 1 << bit) for place in range(...]
  transfers between devices with their start and end apart: 65 -> 61, of which waited for: 29 -> 28; matrix products, arithmetic and copies ran while one was open for 33% -> 39% of each run, Pallas kernels for 11% -> 17%
where the time goes in v3:
time: 589 us; the launch traced here: 581 us
  waiting for transfers between devices  151 us (26%)
  other arithmetic  128 us (22%)
  Pallas kernels  96.7 us (16%)
  matrix products  66.6 us (11%)
  local copies, waits for them, and re-layouts  66 us (11%)
  starting transfers between devices  60.2 us (10%)
  between operations  12.3 us (2%)
    ppermute x44, waiting for transfers between devices, trade(): lax.ppermute(value, 'tok', [(place, place ^ 1 << bit) for place in range(...  151 us
    ppermute x44, starting transfers between devices, trade(): lax.ppermute(value, 'tok', [(place, place ^ 1 << bit) for place in range(...  56.2 us
    pallas_call x3, Pallas kernels, grad_parts(): pl.pallas_call(kernel, grid=(4,), in_specs=[pl.BlockSpec(memory_space=plt...  42.4 us
    convert_element_type x12, other arithmetic, add(): return (one.astype(jnp.float32) + two.astype(jnp.float32)).astype(kept)  22.9 us
    unnamed x346, local copies, waits for them, and re-layouts  20.8 us
    pallas_call x2, Pallas kernels, attend_back(): pl.pallas_call(attend_back_kernel, grid=(heads,), in_specs=[block] * 4 +...  19.2 us
    dot_general x3, matrix products, against(): lax.dot_general(left, right, (((1,), (1,)), ((), ())), preferred_element_...  16.9 us
    dynamic_update_slice x12, local copies, waits for them, and re-layouts, put(): return lax.dynamic_update_slice(out, value, tuple(start))  16.8 us
  transfers between devices with their start and end apart: 61, of which 28 were waited for; matrix products, arithmetic and copies ran while one was open for 39% of the time, Pallas kernels for 17%

profile of v3, /device:TPU:0, one launch (start us, length us, event | category | flops | bytes accessed | tf_op | source)
XLA Modules:
  0.0 581.1 jit_solution(5869990404205731128)
XLA Ops:
  7.8 2.7 collective-permute-start.2
  15.6 3.1 collective-permute-start.4
  33.1 2.6 collective-permute-start.6
  36.8 9.9 %collective-permute-done.6 = bf16[1,1,1,1,72,2304]{5,4,3,2,1,0:T(8,128)(2,1)S(1)} collective-permute-done((bf16[1,1,1,1,72,2304]{5,4,3,2,1,0:T(8,128)(2,1)}, bf16[1,1,1,1,72,2304]{5,4,3,2,1,0:T(8,128)(2,1)S(1)}, u32[]{:S(2)}, u32[]{:S(2)}) %collective-permute-start.6) | collective-permute-done | bytes 331808 | tf_op jit(solution)/shard_map/ppermute | solution.py:87
  62.0 4.4 collective-permute-done.9
  75.7 3.3 collective-permute-start.12
  79.0 2.5 pad_maximum_fusion.10
  83.8 2.5 pad_maximum_fusion.11
  89.0 6.0 %add_convert_fusion.6.refs_1_.x_ref = bf16[512,1152]{1,0:T(8,128)(2,1)} fusion(bf16[512,1152]{1,0:T(8,128)(2,1)S(1)} %copy-done.34, f32[1152]{0:T(1024)S(1)} %get-tuple-element.80, f32[1152]{0:T(1024)S(1)} %get-tuple-element.81, f32[1152]{0:T(1024)S(1)} %get-tuple-element.82, f32[1152]{0:T(1024)S(1)} %get-tuple-element.83, f32[1152]{0:T(1024)S(1)} %get-tuple-element.84, ...), kind=kLoop, calls=%fused_computation.55 | loop fusion | flops 9437184 | bytes 2402308 | tf_op jit(solution)/shard_map/convert_element_type | solution.py:719
  100.5 4.5 maximum_maximum_fusion.1.refs_0_
  105.5 12.8 %collective-permute-done.21 = bf16[1,1,1,1,72,4608]{5,4,3,2,1,0:T(8,128)(2,1)S(1)} collective-permute-done((bf16[1,1,1,1,72,4608]{5,4,3,2,1,0:T(8,128)(2,1)}, bf16[1,1,1,1,72,4608]{5,4,3,2,1,0:T(8,128)(2,1)S(1)}, u32[]{:S(2)}, u32[]{:S(2)}) %collective-permute-start.21) | collective-permute-done | bytes 663584 | tf_op jit(solution)/shard_map/ppermute | solution.py:87
  119.3 3.5 pad_maximum_fusion.1
  122.8 5.0 collective-permute-done.16
  127.8 2.5 constant_dynamic-update-slice_fusion.7
  130.3 5.5 collective-permute-done.17
  135.7 2.5 constant_dynamic-update-slice_fusion.6
  138.3 6.3 %heads_of.2 = (f32[1728,512]{1,0:T(8,128)S(1)}, bf16[1152,512]{1,0:T(8,128)(2,1)}) custom-call(bf16[512,1152]{1,0:T(8,128)(2,1)S(1)} %copy-done.5, bf16[1152,2304]{1,0:T(8,128)(2,1)} %bitcast.12.w_ref.w_one_ref), custom_call_target="tpu_custom_call" | custom-call | flops 2300000000 | bytes 1000 | tf_op jit(solution)/shard_map/heads_of/pallas_call | solution.py:253
  145.0 5.4 collective-permute-done.22
  154.0 5.9 %attend.2 = (bf16[8,72,512]{2,1,0:T(8,128)(2,1)S(1)}, f32[8,1,512]{2,1,0:T(1,128)S(1)}, bf16[8,72,512]{2,1,0:T(8,128)(2,1)S(1)}, bf16[8,72,512]{2,1,0:T(8,128)(2,1)S(1)}, bf16[8,72,512]{2,1,0:T(8,128)(2,1)S(1)}) custom-call(f32[3,8,72,512]{3,2,1,0:T(8,128)S(1)} %bitcast.150, f32[3,8,72,512]{3,2,1,0:T(8,128)S(1)} %bitcast.151, ...), custom_call_target="tpu_custom_call" | custom-call | flops 2760000000 | bytes 1000 | tf_op jit(solution)/shard_map/attend/pallas_call | solution.py:176
  162.5 21.4 %collective-permute-done.23 = bf16[2,1,1,1,72,4608]{5,4,3,2,1,0:T(8,128)(2,1)S(1)} collective-permute-done((bf16[2,1,1,1,72,4608]{5,4,3,2,1,0:T(8,128)(2,1)S(1)}, bf16[2,1,1,1,72,4608]{5,4,3,2,1,0:T(8,128)(2,1)S(1)}, u32[]{:S(2)}, u32[]{:S(2)}) %collective-permute-start.23) | collective-permute-done | bytes 1327136 | tf_op jit(solution)/shard_map/ppermute | solution.py:87
  185.5 6.5 %collective-permute-done.24 = bf16[2,1,1,1,72,4608]{5,4,3,2,1,0:T(8,128)(2,1)S(1)} collective-permute-done((bf16[2,1,1,1,72,4608]{5,4,3,2,1,0:T(8,128)(2,1)S(1)}, bf16[2,1,1,1,72,4608]{5,4,3,2,1,0:T(8,128)(2,1)S(1)}, u32[]{:S(2)}, u32[]{:S(2)}) %collective-permute-start.24) | collective-permute-done | bytes 1327136 | tf_op jit(solution)/shard_map/ppermute | solution.py:87
  194.0 7.4 %maximum_maximum_fusion = bf16[2,2,2,2,72,4608]{5,4,3,2,1,0:T(8,128)(2,1)} fusion(bf16[2,1,2,1,72,4608]{5,4,3,2,1,0:T(8,128)(2,1)S(1)} %constant_dynamic-update-slice_fusion.2, bf16[2,1,1,2,72,4608]{5,4,3,2,1,0:T(8,128)(2,1)} %constant_dynamic-update-slice_fusion.3), kind=kLoop, calls=%fused_computation | loop fusion | flops 15925248 | bytes 15925248 | tf_op jit(solution)/shard_map/concatenate | solution.py:522
  201.4 7.4 %heads_of.3 = (f32[1728,512]{1,0:T(8,128)}, bf16[1152,512]{1,0:T(8,128)(2,1)}) custom-call(bf16[512,1152]{1,0:T(8,128)(2,1)S(1)} %copy-done.6, bf16[1152,2304]{1,0:T(8,128)(2,1)} %bitcast.16.w_ref.w_two_ref, bf16[1152,512]{1,0:T(8,128)(2,1)} %collective-permute-done.19.refs_0_.refs_1_), custom_call_target="tpu_custom_call" | custom-call | flops 2300000000 | bytes 1000 | tf_op jit(solution)/shard_map/heads_of/pallas_call | solution.py:253
  210.8 6.1 %attend.3 = (bf16[8,72,512]{2,1,0:T(8,128)(2,1)S(1)}, f32[8,1,512]{2,1,0:T(1,128)S(1)}, bf16[8,72,512]{2,1,0:T(8,128)(2,1)S(1)}, bf16[8,72,512]{2,1,0:T(8,128)(2,1)S(1)}, bf16[8,72,512]{2,1,0:T(8,128)(2,1)S(1)}) custom-call(f32[3,8,72,512]{3,2,1,0:T(8,128)S(1)} %bitcast.153, f32[3,8,72,512]{3,2,1,0:T(8,128)S(1)} %bitcast.154, ...), custom_call_target="tpu_custom_call" | custom-call | flops 2760000000 | bytes 1000 | tf_op jit(solution)/shard_map/attend/pallas_call | solution.py:176
  218.5 3.0 broadcast_select_fusion.1
  221.7 7.0 %fusion.72 = (f32[512]{0:T(512)S(1)}, f32[512,1152]{1,0:T(8,128)S(1)}, bf16[512,1152]{1,0:T(8,128)(2,1)S(1)}, f32[512,1152]{1,0:T(8,128)}) fusion(f32[1152]{0:T(1024)S(1)} %copy-done.148, pred[512]{0:T(512)(128)(4,1)S(1)} %copy-done.119, f32[1152]{0:T(1024)S(1)} %copy-done.149, pred[512]{0:T(512)(128)(4,1)S(1)} %copy-done.124, f32[1152]{0:T(1024)S(1)} %copy-done.150, ...), kind=kOutput, calls=%fused_computation.306 | convolution fusion | flops 1374289408 | bytes 12134404 | tf_op jit(solution)/shard_map/dot_general | solution.py:136
  229.8 4.0 add_convert_fusion.5
  233.8 13.0 %collective-permute-done.25 = bf16[2,1,1,2,72,4608]{5,4,3,2,1,0:T(8,128)(2,1)} collective-permute-done((bf16[2,1,1,2,72,4608]{5,4,3,2,1,0:T(8,128)(2,1)}, bf16[2,1,1,2,72,4608]{5,4,3,2,1,0:T(8,128)(2,1)}, u32[]{:S(2)}, u32[]{:S(2)}) %collective-permute-start.25) | collective-permute-done | bytes 2654240 | tf_op jit(solution)/shard_map/ppermute | solution.py:87
  251.7 6.3 %fusion.6 = f32[1024,1536]{1,0:T(8,128)} fusion(bf16[1152,4608]{1,0:T(8,128)(2,1)S(1)} %bitcast.173, bf16[512,1152]{1,0:T(8,128)(2,1)S(1)} %collective-permute-done.20, bf16[512,1152]{1,0:T(8,128)(2,1)S(1)} %add_convert_fusion.5), kind=kOutput, calls=%fused_computation.19 | convolution fusion | flops 3628597248 | bytes 12189696 | tf_op jit(solution)/shard_map/dot_general | solution.py:748
  259.1 6.2 %fusion.2 = f32[1024,1536]{1,0:T(8,128)} fusion(bf16[1152,4608]{1,0:T(8,128)(2,1)S(1)} %bitcast.174, bf16[512,1152]{1,0:T(8,128)(2,1)S(1)} %collective-permute-done.28, bf16[512,1152]{1,0:T(8,128)(2,1)S(1)} %get-tuple-element.175), kind=kOutput, calls=%fused_computation.15 | convolution fusion | flops 3628597248 | bytes 12189696 | tf_op jit(solution)/shard_map/dot_general | solution.py:756
  265.3 14.3 %multiply_convert_fusion.1 = (bf16[1024,1536]{1,0:T(8,128)(2,1)}, bf16[1024,1536]{1,0:T(8,128)(2,1)}, bf16[1024,1536]{1,0:T(8,128)(2,1)}) fusion(f32[1024,1536]{1,0:T(8,128)} %fusion.2, f32[1024,1536]{1,0:T(8,128)} %fusion.6, bf16[1152,4608]{1,0:T(8,128)(2,1)} %bitcast.175, bf16[512,1152]{1,0:T(8,128)(2,1)S(1)} %collective-permute-done.20, ...), kind=kOutput, calls=%fused_computation.2 | convolution fusion | flops 3653763072 | bytes 27918336 | tf_op jit(solution)/shard_map/dot_general | solution.py:747
  279.5 6.3 %fusion.4 = f32[1024,1152]{1,0:T(8,128)S(1)} fusion(bf16[1024,1536]{1,0:T(8,128)(2,1)} %get-tuple-element.123.refs_2_, bf16[1152,4608]{1,0:T(8,128)(2,1)S(1)} %bitcast.177), kind=kOutput, calls=%fused_computation.17 | convolution fusion | flops 3623878656 | bytes 11403264 | tf_op jit(solution)/shard_map/dot_general | solution.py:60
  285.8 4.3 convolution_add_fusion.1
  295.0 9.8 %grad_parts.4 = (bf16[8,72,1536]{2,1,0:T(8,128)(2,1)}, bf16[8,72,1536]{2,1,0:T(8,128)(2,1)}) custom-call(s32[1]{0:T(128)} %bitcast.25.tok_ref, bf16[1024,1152]{1,0:T(8,128)(2,1)} %pad_maximum_fusion.5.refs_0_, bf16[1024,1536]{1,0:T(8,128)(2,1)} %get-tuple-element.122.refs_1_.refs_0_, bf16[1152,512]{1,0:T(8,128)(2,1)} %collective-permute-done.27.refs_2_.refs_3_), custom_call_target="tpu_custom_call" | custom-call | flops 4140000000 | bytes 1000 | tf_op jit(solution)/shard_map/grad_parts/pallas_call | solution.py:372
  305.4 3.2 pad_maximum_fusion.4.refs_0_
  308.6 17.2 %grad_parts.3 = (bf16[4,72,3072]{2,1,0:T(8,128)(2,1)}, bf16[4,72,3072]{2,1,0:T(8,128)(2,1)}, bf16[4,72,3072]{2,1,0:T(8,128)(2,1)}, bf16[4,72,3072]{2,1,0:T(8,128)(2,1)}) custom-call(s32[1]{0:T(128)} %bitcast.25.tok_ref, bf16[1024,1152]{1,0:T(8,128)(2,1)} %pad_maximum_fusion.4.refs_0_, bf16[1024,1536]{1,0:T(8,128)(2,1)} %get-tuple-element.121.refs_1_, ...), custom_call_target="tpu_custom_call" | custom-call | flops 8280000000 | bytes 1000 | tf_op jit(solution)/shard_map/grad_parts/pallas_call | solution.py:372
  328.1 2.5 multiply_reduce_fusion.1
  330.7 3.4 fusion.71
  340.9 4.9 collective-permute-done.30
  352.3 9.5 %attend_back.2 = bf16[3,8,72,512]{3,2,1,0:T(8,128)(2,1)S(1)} custom-call(bf16[8,72,512]{2,1,0:T(8,128)(2,1)S(1)} %get-tuple-element.53.q_ref, bf16[8,72,512]{2,1,0:T(8,128)(2,1)S(1)} %copy-done.26, bf16[8,72,512]{2,1,0:T(8,128)(2,1)S(1)} %copy-done.28, bf16[8,72,512]{2,1,0:T(8,128)(2,1)S(1)} %copy-done.12, f32[8,1,512]{2,1,0:T(1,128)S(1)} %get-tuple-element.58.log_ref, ...), custom_call_target="tpu_custom_call" | custom-call | flops 4600000000 | bytes 1000 | tf_op jit(solution)/shard_map/attend_back/pallas_call | solution.py:217
  363.0 3.5 collective-permute-done.32
  366.5 2.7 add_convert_fusion
  378.6 9.7 %attend_back.3 = bf16[3,8,72,512]{3,2,1,0:T(8,128)(2,1)S(1)} custom-call(bf16[8,72,512]{2,1,0:T(8,128)(2,1)S(1)} %copy-done.20, bf16[8,72,512]{2,1,0:T(8,128)(2,1)S(1)} %copy-done.22, bf16[8,72,512]{2,1,0:T(8,128)(2,1)S(1)} %copy-done.24, bf16[8,72,512]{2,1,0:T(8,128)(2,1)S(1)} %copy-done.11, f32[8,1,512]{2,1,0:T(1,128)S(1)} %copy-done.30, ...), custom_call_target="tpu_custom_call" | custom-call | flops 4600000000 | bytes 1000 | tf_op jit(solution)/shard_map/attend_back/pallas_call | solution.py:217
  390.0 2.3 fusion.16.refs_0_
  392.3 15.3 %grad_parts.5 = (bf16[4,72,2368]{2,1,0:T(8,128)(2,1)}, bf16[4,72,2368]{2,1,0:T(8,128)(2,1)}, bf16[4,72,2368]{2,1,0:T(8,128)(2,1)}, bf16[4,72,2368]{2,1,0:T(8,128)(2,1)}) custom-call(s32[1]{0:T(128)} %bitcast.25.tok_ref, bf16[1152,512]{1,0:T(8,128)(2,1)} %get-tuple-element.46.refs_0_, bf16[1152,512]{1,0:T(8,128)(2,1)} %collective-permute-done.19.refs_0_.refs_1_, ...), custom_call_target="tpu_custom_call" | custom-call | flops 5980000256 | bytes 1000 | tf_op jit(solution)/shard_map/grad_parts/pallas_call | solution.py:372
  409.8 2.6 add_convert_fusion.9.refs_3_
  419.0 9.5 %back_through.1 = f32[512,1152]{1,0:T(8,128)S(1)} custom-call(bf16[1728,512]{1,0:T(8,128)(2,1)S(1)} %copy-done.8, bf16[1728,512]{1,0:T(8,128)(2,1)S(1)} %copy-done.4, bf16[1152,2304]{1,0:T(8,128)(2,1)} %bitcast.12.w_ref.w_one_ref, bf16[1152,2304]{1,0:T(8,128)(2,1)} %bitcast.16.w_ref.w_two_ref), custom_call_target="tpu_custom_call" | custom-call | flops 4140000000 | bytes 1000 | tf_op jit(solution)/shard_map/back_through/pallas_call | solution.py:286
  431.2 6.3 %fusion = f32[1024,1152]{1,0:T(8,128)S(1)} fusion(bf16[1024,1536]{1,0:T(8,128)(2,1)S(1)} %copy-done.67, bf16[1152,4608]{1,0:T(8,128)(2,1)} %bitcast.176), kind=kOutput, calls=%fused_computation.13 | convolution fusion | flops 3623878656 | bytes 11403264 | tf_op jit(solution)/shard_map/dot_general | solution.py:60
  437.6 3.2 convolution_convert_fusion.3
  442.6 3.5 convolution_convert_fusion.4
  446.2 2.9 fusion.70
  449.3 2.5 add_convert_fusion.8.refs_0_
  466.6 5.5 add_add_fusion.2
  483.1 2.7 collective-permute-start.51
  487.6 8.1 %collective-permute-done.46 = bf16[2,2,1,1,8,3456]{5,4,3,2,1,0:T(8,128)(2,1)S(1)} collective-permute-done((bf16[2,2,1,1,8,3456]{5,4,3,2,1,0:T(8,128)(2,1)S(1)}, bf16[2,2,1,1,8,3456]{5,4,3,2,1,0:T(8,128)(2,1)S(1)}, u32[]{:S(2)}, u32[]{:S(2)}) %collective-permute-start.46) | collective-permute-done | bytes 221216 | tf_op jit(solution)/shard_map/ppermute | solution.py:87
  501.6 2.7 collective-permute-done.51
  510.4 8.6 %collective-permute-done.41 = bf16[2,72,2368]{2,1,0:T(8,128)(2,1)S(1)} collective-permute-done((bf16[2,72,2368]{2,1,0:T(8,128)(2,1)}, bf16[2,72,2368]{2,1,0:T(8,128)(2,1)S(1)}, u32[]{:S(2)}, u32[]{:S(2)}) %collective-permute-start.41) | collective-permute-done | bytes 682016 | tf_op jit(solution)/shard_map/ppermute | solution.py:87
  521.3 16.7 %collective-permute-done.42 = bf16[72,2368]{1,0:T(8,128)(2,1)S(1)} collective-permute-done((bf16[72,2368]{1,0:T(8,128)(2,1)S(1)}, bf16[72,2368]{1,0:T(8,128)(2,1)S(1)}, u32[]{:S(2)}, u32[]{:S(2)}) %collective-permute-start.42) | collective-permute-done | bytes 341024 | tf_op jit(solution)/shard_map/ppermute | solution.py:87
  546.7 2.3 collective-permute-done.56
  555.3 2.3 collective-permute-done.58
  560.0 2.9 collective-permute-done.59
  563.6 2.3 multiply_subtract_fusion.4
  571.0 2.3 multiply_subtract_fusion.3
  576.8 2.8 multiply_subtract_fusion.2
  (604 shorter events, 191.0 us)
Async XLA Ops:
  1.5 5.5 collective-permute-start.1
  3.8 26.3 %collective-permute-start = (bf16[72,576]{1,0:T(8,128)(2,1)}, bf16[72,576]{1,0:T(8,128)(2,1)}, u32[]{:S(2)}, u32[]{:S(2)}) collective-permute-start(bf16[72,576]{1,0:T(8,128)(2,1)} %get-tuple-element.154), channel_id=1, source_target_pairs={{0,1},{1,0},{2,3},{3,2},{4,5},{5,4},{6,7},{7,6},{8,9},{9,8},{10,11... | collective-permute-start | bytes 248840 | tf_op jit(solution)/shard_map/ppermute | solution.py:95
  4.6 17.6 %collective-permute-start.7 = (f32[216]{0:T(256)S(1)}, f32[216]{0:T(256)S(1)}, u32[]{:S(2)}, u32[]{:S(2)}) collective-permute-start(f32[216]{0:T(256)S(1)} %convert_convert_fusion.1), channel_id=1, source_target_pairs={{0,1},{1,0},{2,3},{3,2},{4,5},{5,4},{6,7},{7,6},{8,9},{9,8},{10,11... | collective-permute-start | bytes 2600 | tf_op jit(solution)/shard_map/ppermute | solution.py:95
  7.8 4.2 collective-permute-start.2
  12.0 3.6 collective-permute-start.3
  15.6 4.7 collective-permute-start.4
  20.3 3.7 collective-permute-start.5
  28.3 30.9 %collective-permute-start.8 = (bf16[2,2,2,1,8,3456]{5,4,3,2,1,0:T(8,128)(2,1)}, bf16[2,2,2,1,8,3456]{5,4,3,2,1,0:T(8,128)(2,1)}, u32[]{:S(2)}, u32[]{:S(2)}) collective-permute-start(bf16[2,2,2,1,8,3456]{5,4,3,2,1,0:T(8,128)(2,1)} %slice.578), channel_id=1, source_target_pairs={{0,2},{2,0},{4,6},{6,4},{8,10},{10,8},{12,14},{14,12},{16,18},{18,... | collective-permute-start | bytes 1327112 | tf_op jit(solution)/shard_map/ppermute | solution.py:87
  33.1 13.7 %collective-permute-start.6 = (bf16[1,1,1,1,72,2304]{5,4,3,2,1,0:T(8,128)(2,1)}, bf16[1,1,1,1,72,2304]{5,4,3,2,1,0:T(8,128)(2,1)S(1)}, u32[]{:S(2)}, u32[]{:S(2)}) collective-permute-start(bf16[1,1,1,1,72,2304]{5,4,3,2,1,0:T(8,128)(2,1)} %after.20), channel_id=1, source_target_pairs={{0,16},{2,18},{4,20},{6,22},{8,24},{10,26},{12,28},{14,30},{16,0},... | collective-permute-start | bytes 995336 | tf_op jit(solution)/shard_map/ppermute | solution.py:87
  46.8 20.4 %collective-permute-start.10 = (bf16[2,1,1,1,72,2304]{5,4,3,2,1,0:T(8,128)(2,1)S(1)}, bf16[2,1,1,1,72,2304]{5,4,3,2,1,0:T(8,128)(2,1)}, u32[]{:S(2)}, u32[]{:S(2)}) collective-permute-start(bf16[2,1,1,1,72,2304]{5,4,3,2,1,0:T(8,128)(2,1)S(1)} %constant_dynamic-update-slice_fusion.11), channel_id=1, source_target_pairs={{0,8},{2,10},{4,12},{6,14},{8,0},{10,2},{12,4},{14,6},{16,24},{18,... | collective-permute-start | bytes 1990664 | tf_op jit(solution)/shard_map/ppermute | solution.py:87
  52.0 282.1 %copy-start.116 = (f32[512]{0:T(512)}, f32[512]{0:T(512)S(1)}, u32[]{:S(2)}) copy-start(f32[512]{0:T(512)S(1)} %get-tuple-element.176) | copy-start | bytes 6148
  60.4 6.0 %collective-permute-start.9 = (bf16[2,2,1,1,8,3456]{5,4,3,2,1,0:T(8,128)(2,1)S(1)}, bf16[2,2,1,1,8,3456]{5,4,3,2,1,0:T(8,128)(2,1)S(1)}, u32[]{:S(2)}, u32[]{:S(2)}) collective-permute-start(bf16[2,2,1,1,8,3456]{5,4,3,2,1,0:T(8,128)(2,1)S(1)} %slice.579), channel_id=1, source_target_pairs={{0,4},{2,6},{4,0},{6,2},{8,12},{10,14},{12,8},{14,10},{16,20},{18,... | collective-permute-start | bytes 663560 | tf_op jit(solution)/shard_map/ppermute | solution.py:87
  70.8 4.8 collective-permute-start.11
  73.6 22.2 %collective-permute-start.14 = (bf16[2,1,1,1,72,2304]{5,4,3,2,1,0:T(8,128)(2,1)}, bf16[2,1,1,1,72,2304]{5,4,3,2,1,0:T(8,128)(2,1)}, u32[]{:S(2)}, u32[]{:S(2)}) collective-permute-start(bf16[2,1,1,1,72,2304]{5,4,3,2,1,0:T(8,128)(2,1)} %get-tuple-element.134), channel_id=1, source_target_pairs={{0,2},{2,0},{4,6},{6,4},{8,10},{10,8},{12,14},{14,12},{16,18},{18,... | collective-permute-start | bytes 1990664 | tf_op jit(solution)/shard_map/ppermute | solution.py:87
  75.7 7.4 %collective-permute-start.12 = (bf16[1,1,1,1,8,3456]{5,4,3,2,1,0:T(8,128)(2,1)S(1)}, bf16[1,1,1,1,8,3456]{5,4,3,2,1,0:T(8,128)(2,1)S(1)}, u32[]{:S(2)}, u32[]{:S(2)}) collective-permute-start(bf16[1,1,1,1,8,3456]{5,4,3,2,1,0:T(8,128)(2,1)S(1)} %slice.581), channel_id=1, source_target_pairs={{0,16},{2,18},{4,20},{6,22},{8,24},{10,26},{12,28},{14,30},{16,0},... | collective-permute-start | bytes 165896 | tf_op jit(solution)/shard_map/ppermute | solution.py:87
  81.6 16.9 %collective-permute-start.15 = (bf16[2,1,1,1,72,2304]{5,4,3,2,1,0:T(8,128)(2,1)}, bf16[2,1,1,1,72,2304]{5,4,3,2,1,0:T(8,128)(2,1)}, u32[]{:S(2)}, u32[]{:S(2)}) collective-permute-start(bf16[2,1,1,1,72,2304]{5,4,3,2,1,0:T(8,128)(2,1)} %get-tuple-element.135), channel_id=1, source_target_pairs={{0,4},{2,6},{4,0},{6,2},{8,12},{10,14},{12,8},{14,10},{16,20},{18,... | collective-permute-start | bytes 1990664 | tf_op jit(solution)/shard_map/ppermute | solution.py:87
  83.1 4.1 collective-permute-start.13
  86.3 32.1 %collective-permute-start.21 = (bf16[1,1,1,1,72,4608]{5,4,3,2,1,0:T(8,128)(2,1)}, bf16[1,1,1,1,72,4608]{5,4,3,2,1,0:T(8,128)(2,1)S(1)}, u32[]{:S(2)}, u32[]{:S(2)}) collective-permute-start(bf16[1,1,1,1,72,4608]{5,4,3,2,1,0:T(8,128)(2,1)} %bitcast.182), channel_id=1, source_target_pairs={{0,16},{2,18},{4,20},{6,22},{8,24},{10,26},{12,28},{14,30},{16,0},... | collective-permute-start | bytes 1990664 | tf_op jit(solution)/shard_map/ppermute | solution.py:87
  96.9 30.9 %collective-permute-start.16 = (bf16[2,1,1,2,72,2304]{5,4,3,2,1,0:T(8,128)(2,1)S(1)}, bf16[2,1,1,2,72,2304]{5,4,3,2,1,0:T(8,128)(2,1)}, u32[]{:S(2)}, u32[]{:S(2)}) collective-permute-start(bf16[2,1,1,2,72,2304]{5,4,3,2,1,0:T(8,128)(2,1)S(1)} %constant_dynamic-update-slice_fusion.9), channel_id=1, source_target_pairs={{0,4},{2,6},{4,0},{6,2},{8,12},{10,14},{12,8},{14,10},{16,20},{18,... | collective-permute-start | bytes 3981320 | tf_op jit(solution)/shard_map/ppermute | solution.py:87
  105.0 30.8 %collective-permute-start.17 = (bf16[2,1,2,1,72,2304]{5,4,3,2,1,0:T(8,128)(2,1)}, bf16[2,1,2,1,72,2304]{5,4,3,2,1,0:T(8,128)(2,1)}, u32[]{:S(2)}, u32[]{:S(2)}) collective-permute-start(bf16[2,1,2,1,72,2304]{5,4,3,2,1,0:T(8,128)(2,1)} %constant_dynamic-update-slice_fusion.8), channel_id=1, source_target_pairs={{0,2},{2,0},{4,6},{6,4},{8,10},{10,8},{12,14},{14,12},{16,18},{18,... | collective-permute-start | bytes 3981320 | tf_op jit(solution)/shard_map/ppermute | solution.py:87
  119.3 31.2 %collective-permute-start.22 = (bf16[2,1,1,1,72,4608]{5,4,3,2,1,0:T(8,128)(2,1)}, bf16[2,1,1,1,72,4608]{5,4,3,2,1,0:T(8,128)(2,1)S(1)}, u32[]{:S(2)}, u32[]{:S(2)}) collective-permute-start(bf16[2,1,1,1,72,4608]{5,4,3,2,1,0:T(8,128)(2,1)} %constant_dynamic-update-slice_fusion.5), channel_id=1, source_target_pairs={{0,8},{2,10},{4,12},{6,14},{8,0},{10,2},{12,4},{14,6},{16,24},{18,... | collective-permute-start | bytes 3981320 | tf_op jit(solution)/shard_map/ppermute | solution.py:87
  138.3 63.2 %collective-permute-start.18 = (bf16[2,2,2,2,72,2304]{5,4,3,2,1,0:T(8,128)(2,1)}, bf16[2,2,2,2,72,2304]{5,4,3,2,1,0:T(8,128)(2,1)}, u32[]{:S(2)}, u32[]{:S(2)}) collective-permute-start(bf16[2,2,2,2,72,2304]{5,4,3,2,1,0:T(8,128)(2,1)} %constant_dynamic-update-slice_fusion.6), channel_id=1, source_target_pairs={{0,1},{1,0},{2,3},{3,2},{4,5},{5,4},{6,7},{7,6},{8,9},{9,8},{10,11... | collective-permute-start | bytes 15925256 | tf_op jit(solution)/shard_map/ppermute | solution.py:95
  144.5 56.9 %collective-permute-start.19 = (bf16[1152,512]{1,0:T(8,128)(2,1)}, bf16[1152,512]{1,0:T(8,128)(2,1)}, u32[]{:S(2)}, u32[]{:S(2)}) collective-permute-start(bf16[1152,512]{1,0:T(8,128)(2,1)} %get-tuple-element.46.refs_0_), channel_id=1, source_target_pairs={{0,1},{1,0},{2,3},{3,2},{4,5},{5,4},{6,7},{7,6},{8,9},{9,8},{10,11... | collective-permute-start | bytes 3538952 | tf_op jit(solution)/shard_map/ppermute | solution.py:95
  153.6 30.2 %collective-permute-start.23 = (bf16[2,1,1,1,72,4608]{5,4,3,2,1,0:T(8,128)(2,1)S(1)}, bf16[2,1,1,1,72,4608]{5,4,3,2,1,0:T(8,128)(2,1)S(1)}, u32[]{:S(2)}, u32[]{:S(2)}) collective-permute-start(bf16[2,1,1,1,72,4608]{5,4,3,2,1,0:T(8,128)(2,1)S(1)} %get-tuple-element.126), channel_id=1, source_target_pairs={{0,2},{2,0},{4,6},{6,4},{8,10},{10,8},{12,14},{14,12},{16,18},{18,... | collective-permute-start | bytes 3981320 | tf_op jit(solution)/shard_map/ppermute | solution.py:87
  159.9 32.1 %collective-permute-start.24 = (bf16[2,1,1,1,72,4608]{5,4,3,2,1,0:T(8,128)(2,1)S(1)}, bf16[2,1,1,1,72,4608]{5,4,3,2,1,0:T(8,128)(2,1)S(1)}, u32[]{:S(2)}, u32[]{:S(2)}) collective-permute-start(bf16[2,1,1,1,72,4608]{5,4,3,2,1,0:T(8,128)(2,1)S(1)} %get-tuple-element.127), channel_id=1, source_target_pairs={{0,4},{2,6},{4,0},{6,2},{8,12},{10,14},{12,8},{14,10},{16,20},{18,... | collective-permute-start | bytes 3981320 | tf_op jit(solution)/shard_map/ppermute | solution.py:87
  185.0 61.9 %collective-permute-start.25 = (bf16[2,1,1,2,72,4608]{5,4,3,2,1,0:T(8,128)(2,1)}, bf16[2,1,1,2,72,4608]{5,4,3,2,1,0:T(8,128)(2,1)}, u32[]{:S(2)}, u32[]{:S(2)}) collective-permute-start(bf16[2,1,1,2,72,4608]{5,4,3,2,1,0:T(8,128)(2,1)} %constant_dynamic-update-slice_fusion.3), channel_id=1, source_target_pairs={{0,4},{2,6},{4,0},{6,2},{8,12},{10,14},{12,8},{14,10},{16,20},{18,... | collective-permute-start | bytes 7962632 | tf_op jit(solution)/shard_map/ppermute | solution.py:87
  192.2 56.9 %collective-permute-start.26 = (bf16[2,1,2,1,72,4608]{5,4,3,2,1,0:T(8,128)(2,1)S(1)}, bf16[2,1,2,1,72,4608]{5,4,3,2,1,0:T(8,128)(2,1)}, u32[]{:S(2)}, u32[]{:S(2)}) collective-permute-start(bf16[2,1,2,1,72,4608]{5,4,3,2,1,0:T(8,128)(2,1)S(1)} %constant_dynamic-update-slice_fusion.2), channel_id=1, source_target_pairs={{0,2},{2,0},{4,6},{6,4},{8,10},{10,8},{12,14},{14,12},{16,18},{18,... | collective-permute-start | bytes 7962632 | tf_op jit(solution)/shard_map/ppermute | solution.py:87
  228.7 101.9 %copy-start.31 = (f32[512,1152]{1,0:T(8,128)}, f32[512,1152]{1,0:T(8,128)S(1)}, u32[]{:S(2)}) copy-start(f32[512,1152]{1,0:T(8,128)S(1)} %get-tuple-element.120) | copy-start | bytes 7077892
  228.8 101.8 %copy-start.114 = (f32[512]{0:T(512)}, f32[512]{0:T(512)S(1)}, u32[]{:S(2)}) copy-start(f32[512]{0:T(512)S(1)} %broadcast_multiply_fusion) | copy-start | bytes 6148
  233.8 18.0 %collective-permute-start.20 = (bf16[512,1152]{1,0:T(8,128)(2,1)S(1)}, bf16[512,1152]{1,0:T(8,128)(2,1)S(1)}, u32[]{:S(2)}, u32[]{:S(2)}) collective-permute-start(bf16[512,1152]{1,0:T(8,128)(2,1)S(1)} %add_convert_fusion.5), channel_id=1, source_target_pairs={{0,1},{1,0},{2,3},{3,2},{4,5},{5,4},{6,7},{7,6},{8,9},{9,8},{10,11... | collective-permute-start | bytes 3538952 | tf_op jit(solution)/shard_map/ppermute | solution.py:95
  249.0 9.1 %collective-permute-start.28 = (bf16[512,1152]{1,0:T(8,128)(2,1)S(1)}, bf16[512,1152]{1,0:T(8,128)(2,1)S(1)}, u32[]{:S(2)}, u32[]{:S(2)}) collective-permute-start(bf16[512,1152]{1,0:T(8,128)(2,1)S(1)} %get-tuple-element.175), channel_id=1, source_target_pairs={{0,1},{1,0},{2,3},{3,2},{4,5},{5,4},{6,7},{7,6},{8,9},{9,8},{10,11... | collective-permute-start | bytes 3538952 | tf_op jit(solution)/shard_map/ppermute | solution.py:95
  251.2 43.9 %collective-permute-start.27 = (bf16[1152,512]{1,0:T(8,128)(2,1)}, bf16[1152,512]{1,0:T(8,128)(2,1)}, u32[]{:S(2)}, u32[]{:S(2)}) collective-permute-start(bf16[1152,512]{1,0:T(8,128)(2,1)} %bitcast.18.refs_2_), channel_id=1, source_target_pairs={{0,1},{1,0},{2,3},{3,2},{4,5},{5,4},{6,7},{7,6},{8,9},{9,8},{10,11... | collective-permute-start | bytes 3538952 | tf_op jit(solution)/shard_map/ppermute | solution.py:95
  291.3 36.8 %collective-permute-start.29 = (bf16[512,1152]{1,0:T(8,128)(2,1)}, bf16[512,1152]{1,0:T(8,128)(2,1)}, u32[]{:S(2)}, u32[]{:S(2)}) collective-permute-start(bf16[512,1152]{1,0:T(8,128)(2,1)} %slice.577), channel_id=1, source_target_pairs={{0,1},{1,0},{2,3},{3,2},{4,5},{5,4},{6,7},{7,6},{8,9},{9,8},{10,11... | collective-permute-start | bytes 3538952 | tf_op jit(solution)/shard_map/ppermute | solution.py:95
  304.9 40.9 %collective-permute-start.30 = (bf16[8,72,1536]{2,1,0:T(8,128)(2,1)}, bf16[8,72,1536]{2,1,0:T(8,128)(2,1)}, u32[]{:S(2)}, u32[]{:S(2)}) collective-permute-start(bf16[8,72,1536]{2,1,0:T(8,128)(2,1)} %get-tuple-element.57), channel_id=1, source_target_pairs={{0,8},{2,10},{4,12},{6,14},{8,0},{10,2},{12,4},{14,6},{16,24},{18,... | collective-permute-start | bytes 5308424 | tf_op jit(solution)/shard_map/ppermute | solution.py:87
  325.9 40.6 %collective-permute-start.32 = (bf16[4,72,3072]{2,1,0:T(8,128)(2,1)}, bf16[4,72,3072]{2,1,0:T(8,128)(2,1)}, u32[]{:S(2)}, u32[]{:S(2)}) collective-permute-start(bf16[4,72,3072]{2,1,0:T(8,128)(2,1)} %get-tuple-element.61), channel_id=1, source_target_pairs={{0,2},{2,0},{4,6},{6,4},{8,10},{10,8},{12,14},{14,12},{16,18},{18,... | collective-permute-start | bytes 5308424 | tf_op jit(solution)/shard_map/ppermute | solution.py:87
  327.6 41.6 %collective-permute-start.31 = (bf16[4,72,3072]{2,1,0:T(8,128)(2,1)}, bf16[4,72,3072]{2,1,0:T(8,128)(2,1)}, u32[]{:S(2)}, u32[]{:S(2)}) collective-permute-start(bf16[4,72,3072]{2,1,0:T(8,128)(2,1)} %get-tuple-element.59), channel_id=1, source_target_pairs={{0,4},{2,6},{4,0},{6,2},{8,12},{10,14},{12,8},{14,10},{16,20},{18,... | collective-permute-start | bytes 5308424 | tf_op jit(solution)/shard_map/ppermute | solution.py:87
  337.7 54.6 %collective-permute-start.34 = (bf16[2,2,2,2,32,576]{5,4,3,2,1,0:T(8,128)(2,1)}, bf16[2,2,2,2,32,576]{5,4,3,2,1,0:T(8,128)(2,1)}, u32[]{:S(2)}, u32[]{:S(2)}) collective-permute-start(bf16[2,2,2,2,32,576]{5,4,3,2,1,0:T(8,128)(2,1)} %bitcast.34), channel_id=1, source_target_pairs={{0,1},{1,0},{2,3},{3,2},{4,5},{5,4},{6,7},{7,6},{8,9},{9,8},{10,11... | collective-permute-start | bytes 1769480 | tf_op jit(solution)/shard_map/ppermute | solution.py:95
  349.1 40.9 %collective-permute-start.52 = (bf16[2,2,72,1536]{3,2,1,0:T(8,128)(2,1)}, bf16[2,2,72,1536]{3,2,1,0:T(8,128)(2,1)}, u32[]{:S(2)}, u32[]{:S(2)}) collective-permute-start(bf16[2,2,72,1536]{3,2,1,0:T(8,128)(2,1)} %bitcast.27.refs_1_), channel_id=1, source_target_pairs={{0,16},{2,18},{4,20},{6,22},{8,24},{10,26},{12,28},{14,30},{16,0},... | collective-permute-start | bytes 2654216 | tf_op jit(solution)/shard_map/ppermute | solution.py:87
  361.8 30.5 %collective-permute-start.33 = (bf16[1728,512]{1,0:T(8,128)(2,1)S(1)}, bf16[1728,512]{1,0:T(8,128)(2,1)}, u32[]{:S(2)}, u32[]{:S(2)}) collective-permute-start(bf16[1728,512]{1,0:T(8,128)(2,1)S(1)} %bitcast.156), channel_id=1, source_target_pairs={{0,1},{1,0},{2,3},{3,2},{4,5},{5,4},{6,7},{7,6},{8,9},{9,8},{10,11... | collective-permute-start | bytes 5308424 | tf_op jit(solution)/shard_map/ppermute | solution.py:95
  373.2 76.0 %collective-permute-start.49 = (bf16[2,72,3072]{2,1,0:T(8,128)(2,1)}, bf16[2,72,3072]{2,1,0:T(8,128)(2,1)}, u32[]{:S(2)}, u32[]{:S(2)}) collective-permute-start(bf16[2,72,3072]{2,1,0:T(8,128)(2,1)} %get-tuple-element.131.refs_1_), channel_id=1, source_target_pairs={{0,2},{2,0},{4,6},{6,4},{8,10},{10,8},{12,14},{14,12},{16,18},{18,... | collective-permute-start | bytes 2654216 | tf_op jit(solution)/shard_map/ppermute | solution.py:87
  374.9 34.9 %collective-permute-start.36 = (bf16[2,72,3072]{2,1,0:T(8,128)(2,1)}, bf16[2,72,3072]{2,1,0:T(8,128)(2,1)}, u32[]{:S(2)}, u32[]{:S(2)}) collective-permute-start(bf16[2,72,3072]{2,1,0:T(8,128)(2,1)} %get-tuple-element.193.refs_2_), channel_id=1, source_target_pairs={{0,4},{2,6},{4,0},{6,2},{8,12},{10,14},{12,8},{14,10},{16,20},{18,... | collective-permute-start | bytes 2654216 | tf_op jit(solution)/shard_map/ppermute | solution.py:87
  407.6 52.0 %collective-permute-start.37 = (bf16[4,72,2368]{2,1,0:T(8,128)(2,1)}, bf16[4,72,2368]{2,1,0:T(8,128)(2,1)}, u32[]{:S(2)}, u32[]{:S(2)}) collective-permute-start(bf16[4,72,2368]{2,1,0:T(8,128)(2,1)} %get-tuple-element.63.refs_1_), channel_id=1, source_target_pairs={{0,4},{2,6},{4,0},{6,2},{8,12},{10,14},{12,8},{14,10},{16,20},{18,... | collective-permute-start | bytes 4091912 | tf_op jit(solution)/shard_map/ppermute | solution.py:87
  408.1 54.3 %collective-permute-start.39 = (bf16[4,72,2368]{2,1,0:T(8,128)(2,1)}, bf16[4,72,2368]{2,1,0:T(8,128)(2,1)}, u32[]{:S(2)}, u32[]{:S(2)}) collective-permute-start(bf16[4,72,2368]{2,1,0:T(8,128)(2,1)} %get-tuple-element.64.refs_2_), channel_id=1, source_target_pairs={{0,2},{2,0},{4,6},{6,4},{8,10},{10,8},{12,14},{14,12},{16,18},{18,... | collective-permute-start | bytes 4091912 | tf_op jit(solution)/shard_map/ppermute | solution.py:87
  412.4 64.4 %collective-permute-start.50 = (bf16[2,72,3072]{2,1,0:T(8,128)(2,1)}, bf16[2,72,3072]{2,1,0:T(8,128)(2,1)}, u32[]{:S(2)}, u32[]{:S(2)}) collective-permute-start(bf16[2,72,3072]{2,1,0:T(8,128)(2,1)} %add_convert_fusion.9.refs_3_), channel_id=1, source_target_pairs={{0,8},{2,10},{4,12},{6,14},{8,0},{10,2},{12,4},{14,6},{16,24},{18,... | collective-permute-start | bytes 2654216 | tf_op jit(solution)/shard_map/ppermute | solution.py:87
  414.3 40.6 %collective-permute-start.53 = (bf16[2,72,1536]{2,1,0:T(8,128)(2,1)}, bf16[2,72,1536]{2,1,0:T(8,128)(2,1)}, u32[]{:S(2)}, u32[]{:S(2)}) collective-permute-start(bf16[2,72,1536]{2,1,0:T(8,128)(2,1)} %slice_bitcast_fusion.8), channel_id=1, source_target_pairs={{0,2},{2,0},{4,6},{6,4},{8,10},{10,8},{12,14},{14,12},{16,18},{18,... | collective-permute-start | bytes 1327112 | tf_op jit(solution)/shard_map/ppermute | solution.py:87
  449.2 7.0 %collective-permute-start.35 = (bf16[512,1152]{1,0:T(8,128)(2,1)S(1)}, bf16[512,1152]{1,0:T(8,128)(2,1)S(1)}, u32[]{:S(2)}, u32[]{:S(2)}) collective-permute-start(bf16[512,1152]{1,0:T(8,128)(2,1)S(1)} %copy-done.80), channel_id=1, source_target_pairs={{0,1},{1,0},{2,3},{3,2},{4,5},{5,4},{6,7},{7,6},{8,9},{9,8},{10,11... | collective-permute-start | bytes 3538952 | tf_op jit(solution)/shard_map/ppermute | solution.py:95
  457.3 1.7 collective-permute-start.43
  458.5 27.3 %collective-permute-start.54 = (bf16[72,1536]{1,0:T(8,128)(2,1)}, bf16[72,1536]{1,0:T(8,128)(2,1)}, u32[]{:S(2)}, u32[]{:S(2)}) collective-permute-start(bf16[72,1536]{1,0:T(8,128)(2,1)} %get-tuple-element.153), channel_id=1, source_target_pairs={{0,4},{2,6},{4,0},{6,2},{8,12},{10,14},{12,8},{14,10},{16,20},{18,... | collective-permute-start | bytes 663560 | tf_op jit(solution)/shard_map/ppermute | solution.py:87
  466.2 8.2 %collective-permute-start.44 = (bf16[1,1,1,1,8,3456]{5,4,3,2,1,0:T(8,128)(2,1)}, bf16[1,1,1,1,8,3456]{5,4,3,2,1,0:T(8,128)(2,1)}, u32[]{:S(2)}, u32[]{:S(2)}) collective-permute-start(bf16[1,1,1,1,8,3456]{5,4,3,2,1,0:T(8,128)(2,1)} %after.34), channel_id=1, source_target_pairs={{0,16},{2,18},{4,20},{6,22},{8,24},{10,26},{12,28},{14,30},{16,0},... | collective-permute-start | bytes 165896 | tf_op jit(solution)/shard_map/ppermute | solution.py:87
  472.2 25.7 %collective-permute-start.40 = (bf16[2,72,2368]{2,1,0:T(8,128)(2,1)}, bf16[2,72,2368]{2,1,0:T(8,128)(2,1)}, u32[]{:S(2)}, u32[]{:S(2)}) collective-permute-start(bf16[2,72,2368]{2,1,0:T(8,128)(2,1)} %slice_bitcast_fusion.4.refs_2_), channel_id=1, source_target_pairs={{0,4},{2,6},{4,0},{6,2},{8,12},{10,14},{12,8},{14,10},{16,20},{18,... | collective-permute-start | bytes 2045960 | tf_op jit(solution)/shard_map/ppermute | solution.py:87
  473.5 36.9 %collective-permute-start.38 = (bf16[2,72,2368]{2,1,0:T(8,128)(2,1)}, bf16[2,72,2368]{2,1,0:T(8,128)(2,1)S(1)}, u32[]{:S(2)}, u32[]{:S(2)}) collective-permute-start(bf16[2,72,2368]{2,1,0:T(8,128)(2,1)} %slice_bitcast_fusion.6.refs_1_), channel_id=1, source_target_pairs={{0,2},{2,0},{4,6},{6,4},{8,10},{10,8},{12,14},{14,12},{16,18},{18,... | collective-permute-start | bytes 2045960 | tf_op jit(solution)/shard_map/ppermute | solution.py:87
  475.3 4.8 collective-permute-start.45
  481.0 14.8 %collective-permute-start.46 = (bf16[2,2,1,1,8,3456]{5,4,3,2,1,0:T(8,128)(2,1)S(1)}, bf16[2,2,1,1,8,3456]{5,4,3,2,1,0:T(8,128)(2,1)S(1)}, u32[]{:S(2)}, u32[]{:S(2)}) collective-permute-start(bf16[2,2,1,1,8,3456]{5,4,3,2,1,0:T(8,128)(2,1)S(1)} %pad_maximum_fusion.18), channel_id=1, source_target_pairs={{0,2},{2,0},{4,6},{6,4},{8,10},{10,8},{12,14},{14,12},{16,18},{18,... | collective-permute-start | bytes 663560 | tf_op jit(solution)/shard_map/ppermute | solution.py:87
  483.1 21.2 %collective-permute-start.51 = (bf16[72,3072]{1,0:T(8,128)(2,1)}, bf16[72,3072]{1,0:T(8,128)(2,1)}, u32[]{:S(2)}, u32[]{:S(2)}) collective-permute-start(bf16[72,3072]{1,0:T(8,128)(2,1)} %get-tuple-element.145), channel_id=1, source_target_pairs={{0,16},{2,18},{4,20},{6,22},{8,24},{10,26},{12,28},{14,30},{16,0},... | collective-permute-start | bytes 1327112 | tf_op jit(solution)/shard_map/ppermute | solution.py:87
  497.3 11.0 %collective-permute-start.47 = (bf16[2,2,1,2,8,3456]{5,4,3,2,1,0:T(8,128)(2,1)}, bf16[2,2,1,2,8,3456]{5,4,3,2,1,0:T(8,128)(2,1)S(1)}, u32[]{:S(2)}, u32[]{:S(2)}) collective-permute-start(bf16[2,2,1,2,8,3456]{5,4,3,2,1,0:T(8,128)(2,1)} %pad_maximum_fusion.17), channel_id=1, source_target_pairs={{0,4},{2,6},{4,0},{6,2},{8,12},{10,14},{12,8},{14,10},{16,20},{18,... | collective-permute-start | bytes 1327112 | tf_op jit(solution)/shard_map/ppermute | solution.py:87
  500.0 19.1 %collective-permute-start.41 = (bf16[2,72,2368]{2,1,0:T(8,128)(2,1)}, bf16[2,72,2368]{2,1,0:T(8,128)(2,1)S(1)}, u32[]{:S(2)}, u32[]{:S(2)}) collective-permute-start(bf16[2,72,2368]{2,1,0:T(8,128)(2,1)} %fusion.18.refs_1_), channel_id=1, source_target_pairs={{0,8},{2,10},{4,12},{6,14},{8,0},{10,2},{12,4},{14,6},{16,24},{18,... | collective-permute-start | bytes 2045960 | tf_op jit(solution)/shard_map/ppermute | solution.py:87
  509.3 11.2 %collective-permute-start.48 = (f32[1,3456]{1,0:T(1,128)S(1)}, f32[1,3456]{1,0:T(1,128)S(1)}, u32[]{:S(2)}, u32[]{:S(2)}) collective-permute-start(f32[1,3456]{1,0:T(1,128)S(1)} %broadcast_in_dim.411), channel_id=1, source_target_pairs={{0,1},{1,0},{2,3},{3,2},{4,5},{5,4},{6,7},{7,6},{8,9},{9,8},{10,11... | collective-permute-start | bytes 41480 | tf_op jit(solution)/shard_map/ppermute | solution.py:95
  519.4 18.6 %collective-permute-start.42 = (bf16[72,2368]{1,0:T(8,128)(2,1)S(1)}, bf16[72,2368]{1,0:T(8,128)(2,1)S(1)}, u32[]{:S(2)}, u32[]{:S(2)}) collective-permute-start(bf16[72,2368]{1,0:T(8,128)(2,1)S(1)} %slice_bitcast_fusion.14), channel_id=1, source_target_pairs={{0,16},{2,18},{4,20},{6,22},{8,24},{10,26},{12,28},{14,30},{16,0},... | collective-permute-start | bytes 1022984 | tf_op jit(solution)/shard_map/ppermute | solution.py:87
  543.4 1.3 collective-permute-start.55
  545.3 3.7 collective-permute-start.56
  549.6 3.7 collective-permute-start.57
  554.0 3.7 collective-permute-start.58
  558.3 4.6 collective-permute-start.59
  565.9 8.0 %collective-permute-start.60 = (f32[72,576]{1,0:T(8,128)S(1)}, f32[72,576]{1,0:T(8,128)S(1)}, u32[]{:S(2)}, u32[]{:S(2)}) collective-permute-start(f32[72,576]{1,0:T(8,128)S(1)} %get-tuple-element.148), channel_id=1, source_target_pairs={{0,1},{1,0},{2,3},{3,2},{4,5},{5,4},{6,7},{7,6},{8,9},{9,8},{10,11... | collective-permute-start | bytes 497672 | tf_op jit(solution)/shard_map/ppermute | solution.py:95
  (170 other events, 1178.2 us)

commit v4 on v3

--- a/solution.py
+++ b/solution.py
@@ -119,6 +119,11 @@
 
 
 SCORE_SCALE = HEAD ** (-0.5)
+FEED_BLOCK = 512
+FEED_ROWS = 512
+TURN_BLOCK = 768
+TURN_CHUNKS = 1
+NEAR_CHUNKS = 2
 
 
 def cost(micros):
@@ -296,6 +301,142 @@
     )(one, two, weight_one, weight_two)
 
 
+def feed_kernel(
+    x_one, x_two, r_one, r_two, gate_ref, up_ref, down_ref,
+    hidden_ref, gate_out, up_out, own_ref, sent_ref, total_ref,
+):
+    step = pl.program_id(0)
+    count = x_one.shape[0]
+    rows = min(FEED_ROWS, count)
+    low = jnp.bfloat16
+
+    @pl.when(step == 0)
+    def _():
+        total_ref[...] = jnp.zeros_like(total_ref)
+
+    for half, (x_ref, r_ref) in enumerate(((x_one, r_one), (x_two, r_two))):
+        for start in range(0, count, rows):
+            here = slice(start, start + rows)
+            place = slice(half * count + start, half * count + start + rows)
+            gate = dots(x_ref[here, :], gate_ref[...], 1, 0)
+            up = dots(x_ref[here, :], up_ref[...], 1, 0)
+            d_hidden = dots(r_ref[here, :], down_ref[...], 1, 0)
+            sig = 1.0 / (1.0 + jnp.exp(-gate))
+            active = gate * sig
+            hidden_ref[place, :] = (active * up).astype(low)
+            d_gate = (d_hidden * up * sig * (1.0 + gate * (1.0 - sig))).astype(low)
+            d_up = (d_hidden * active).astype(low)
+            gate_out[place, :] = d_gate
+            up_out[place, :] = d_up
+            total_ref[place, :] += dots(d_gate, gate_ref[...], 1, 1) + dots(
+                d_up, up_ref[...], 1, 1
+            )
+
+    @pl.when(step == pl.num_programs(0) - 1)
+    def _():
+        own_ref[...] = total_ref[:count, :]
+        sent_ref[...] = total_ref[count:, :].astype(low)
+
+
+def feed_both_ways(x_one, x_two, r_one, r_two, far):
+    count, width = x_one.shape
+    size = far.shape[1] // 3
+    block = FEED_BLOCK
+    steps = size // block
+    fixed = pl.BlockSpec((count, width), lambda i: (0, 0))
+
+    def weight(place):
+        return pl.BlockSpec((width, block), lambda i: (0, place * steps + i))
+
+    moving = pl.BlockSpec((2 * count, block), lambda i: (0, i))
+    wide = jax.ShapeDtypeStruct((2 * count, size), jnp.bfloat16)
+    return pl.pallas_call(
+        feed_kernel,
+        grid=(steps,),
+        in_specs=[fixed] * 4 + [weight(place) for place in range(3)],
+        out_specs=[moving] * 3 + [fixed] * 2,
+        out_shape=[wide] * 3
+        + [
+            jax.ShapeDtypeStruct((count, width), jnp.float32),
+            jax.ShapeDtypeStruct((count, width), jnp.bfloat16),
+        ],
+        scratch_shapes=[pltpu.VMEM((2 * count, width), jnp.float32)],
+        compiler_params=pltpu.CompilerParams(vmem_limit_bytes=56 << 20),
+        cost_estimate=cost(22),
+        name="feed_both_ways",
+    )(x_one, x_two, r_one, r_two, far, far, far)
+
+
+def hand_out(block_ref, outs, parts, count):
+    for out, fixed_bits in zip(outs, parts):
+        rest = other_bits(fixed_bits, count)
+        for chip in range(count):
+            if all((chip >> bit) & 1 == wanted for bit, wanted in fixed_bits.items()):
+                out[block_index(chip, rest)] = block_ref[chip]
+
+
+def turned_parts(lefts, rights, parts, count, *others):
+    tokens, rows = lefts[0].shape
+    columns = rights[0].shape[1]
+    size = rows // count
+    chunk = rows // TURN_CHUNKS
+    block = TURN_BLOCK
+    steps = columns // block
+
+    def kernel(tok_ref, one_ref, two_ref, *refs):
+        right_refs = refs[: len(rights)]
+        outs = refs[len(rights) + len(others) :]
+        outs, (turn_ref, block_ref) = outs[: len(parts)], outs[len(parts) :]
+        step = pl.program_id(0)
+        tok = tok_ref[0]
+
+        @pl.when(step == 0)
+        def _():
+            for half, ref in enumerate((one_ref, two_ref)):
+                for start in range(0, rows, 128):
+                    turn_ref[start : start + 128, half * tokens : (half + 1) * tokens] = ref[
+                        :, start : start + 128
+                    ].T
+
+        for place, right_ref in enumerate(right_refs):
+
+            @pl.when(step // steps == place)
+            def _():
+                for piece in range(rows // chunk):
+                    total = dots(turn_ref[piece * chunk : (piece + 1) * chunk, :], right_ref[...], 1, 0)
+                    for inner in range(chunk // size):
+                        value = total[inner * size : (inner + 1) * size, :].astype(jnp.bfloat16)
+                        block_ref[(piece * (chunk // size) + inner) ^ tok] = value
+                hand_out(block_ref, outs, parts, count)
+
+    fixed = pl.BlockSpec((tokens, rows), lambda i: (0, 0))
+
+    def moving(place):
+        return pl.BlockSpec(
+            (2 * tokens, block), lambda i: (0, jnp.clip(i - place * steps, 0, steps - 1))
+        )
+
+    shapes = [(count >> len(part), size) for part in parts]
+    return pl.pallas_call(
+        kernel,
+        grid=(steps * len(rights),),
+        in_specs=[pl.BlockSpec(memory_space=pltpu.SMEM), fixed, fixed]
+        + [moving(place) for place in range(len(rights))]
+        + [pl.BlockSpec(memory_space=pl.ANY)] * len(others),
+        out_specs=[pl.BlockSpec(shape + (block,), lambda i: (0, 0, i)) for shape in shapes],
+        out_shape=[
+            jax.ShapeDtypeStruct(shape + (columns * len(rights),), jnp.bfloat16) for shape in shapes
+        ],
+        scratch_shapes=[
+            pltpu.VMEM((rows, 2 * tokens), jnp.bfloat16),
+            pltpu.VMEM((count, size, block), jnp.bfloat16),
+        ],
+        compiler_params=pltpu.CompilerParams(vmem_limit_bytes=48 << 20),
+        cost_estimate=cost(6 * len(rights)),
+        name="turned_parts",
+    )(lax.axis_index("tok").reshape(1), *lefts, *rights, *others)
+
+
 def block_index(chip, bits):
     place = 0
     for bit in bits:
@@ -307,11 +448,11 @@
     return [bit for bit in range(count.bit_length() - 2, -1, -1) if bit not in bits]
 
 
-def grad_parts(terms, turned, columns, parts, count, *others):
+def grad_parts(terms, columns, parts, count):
     left = terms[0][0][0][0]
-    rows = left.shape[1] if turned else left.shape[0]
+    rows = left.shape[0]
     size = rows // count
-    chunk = rows // 4
+    chunk = rows // NEAR_CHUNKS
     flat = [pair for term, _ in terms for pair in term]
     lefts = []
     for pair in flat:
@@ -321,28 +462,15 @@
     def kernel(tok_ref, *refs):
         left_refs = refs[: len(lefts)]
         right_refs = refs[len(lefts) : len(lefts) + len(flat)]
-        outs = refs[len(lefts) + len(flat) + len(others) :]
-        outs, scratch = outs[: len(parts)], outs[len(parts) :]
+        outs = refs[len(lefts) + len(flat) :]
         step = pl.program_id(0)
         tok = tok_ref[0]
-        if turned:
-
-            @pl.when(step == 0)
-            def _():
-                for left_ref, turn_ref in zip(left_refs, scratch):
-                    for start in range(0, rows, 128):
-                        turn_ref[start : start + 128, :] = left_ref[:, start : start + 128].T
-
         place = 0
         for term, start in terms:
             total = None
             for left, right, axis in term:
                 which = [left is other for other in lefts].index(True)
-                if turned:
-                    part = scratch[which][pl.ds(pl.multiple_of(step * chunk, chunk), chunk), :]
-                else:
-                    part = left_refs[which][...]
-                product = dots(part, right_refs[place][...], 1, axis)
+                product = dots(left_refs[which][...], right_refs[place][...], 1, axis)
                 total = product if total is None else total + product
                 place += 1
             width = total.shape[1]
@@ -362,27 +490,20 @@
     def fixed(value):
         return pl.BlockSpec(value.shape, lambda i: (0,) * value.ndim)
 
-    if turned:
-        left_specs = [fixed(value) for value in lefts]
-        scratch = [pltpu.VMEM(value.shape[::-1], value.dtype) for value in lefts]
-    else:
-        left_specs = [pl.BlockSpec((chunk, value.shape[1]), lambda i: (i, 0)) for value in lefts]
-        scratch = []
+    left_specs = [pl.BlockSpec((chunk, value.shape[1]), lambda i: (i, 0)) for value in lefts]
     shapes = [(count >> len(part), size, columns) for part in parts]
     return pl.pallas_call(
         kernel,
-        grid=(4,),
+        grid=(rows // chunk,),
         in_specs=[pl.BlockSpec(memory_space=pltpu.SMEM)]
         + left_specs
-        + [fixed(pair[1]) for pair in flat]
-        + [pl.BlockSpec(memory_space=pl.ANY)] * len(others),
+        + [fixed(pair[1]) for pair in flat],
         out_specs=[pl.BlockSpec(shape, lambda i: (0, 0, 0)) for shape in shapes],
         out_shape=[jax.ShapeDtypeStruct(shape, jnp.bfloat16) for shape in shapes],
-        scratch_shapes=scratch,
         compiler_params=pltpu.CompilerParams(vmem_limit_bytes=56 << 20),
         cost_estimate=cost(6 * columns // 1024),
         name="grad_parts",
-    )(lax.axis_index("tok").reshape(1), *lefts, *[pair[1] for pair in flat], *others)
+    )(lax.axis_index("tok").reshape(1), *lefts, *[pair[1] for pair in flat])
 
 
 def scatter_on(value, left_bits, order, count, last=jnp.bfloat16, hold=()):
@@ -402,58 +523,82 @@
     return value, sent
 
 
-def plain_products(terms, turned, columns):
+def plain_products(terms, columns):
     pieces = []
     for place, (term, start) in enumerate(terms):
-        total = sum(dots(one, two, 0 if turned else 1, axis) for one, two, axis in term)
+        total = sum(dots(one, two, 1, axis) for one, two, axis in term)
         end = terms[place + 1][1] if place + 1 < len(terms) else columns
         total = jnp.pad(total, ((0, 0), (0, end - start - total.shape[1])))
         pieces.append(total.astype(jnp.bfloat16))
     return pieces
 
 
-def row_size(terms, turned, count):
-    left = terms[0][0][0][0]
-    return (left.shape[1] if turned else left.shape[0]) // count
-
-
-def chain_scatter(terms, turned, columns, count, *others):
+def near_scatter(terms, columns, count, hold=()):
+    return across_scatter(
+        lambda parts: grad_parts(terms, columns, parts, count),
+        lambda: plain_products(terms, columns),
+        terms[0][0][0][0].shape[0],
+        count,
+        hold,
+    )
+
+
+def turned_products(lefts, rights):
+    left = jnp.concatenate(lefts, axis=0)
+    return [across(left, right).astype(jnp.bfloat16) for right in rights]
+
+
+def feed_scatter(lefts, rights, count, hold=()):
+    return across_scatter(
+        lambda parts: turned_parts(lefts, rights, parts, count),
+        lambda: turned_products(lefts, rights),
+        lefts[0].shape[1],
+        count,
+        hold,
+    )
+
+
+def chain_scatter(lefts, rights, count, *others):
     first, order, _ = orders(count)
     bits = first[::-1] + order
-    if row_size(terms, turned, count) % 8:
-        half, sent = half_scatter(plain_products(terms, turned, columns), count)
-        return sent[:1], [half], lambda value, _: last_scatter(value[0], count)
-    away, kept = grad_parts(terms, turned, columns, [{bits[0]: 1}, {bits[0]: 0}], count, *others)
+    if (lefts[0].shape[1] // count) % 8:
+        half, sent = half_scatter(turned_products(lefts, rights), count)
+        return sent[:1], [half], lambda value, *_: last_scatter(value[0], count)
+    away, kept = turned_parts(lefts, rights, [{bits[0]: 1}, {bits[0]: 0}], count, *others)
     left_bits = other_bits(bits[:1], count)
     value = add(kept, trade(away, bits[0], count))
-    value, sent = scatter_on(value, left_bits, bits[1 : len(first)], count)
-    left_bits = [bit for bit in left_bits if bit in order]
-    return (
-        sent[:1],
-        [value],
-        lambda value, hold: scatter_on(value[0], left_bits, order, count, jnp.float32, hold)[0],
-    )
-
-
-def across_scatter(terms, turned, columns, count, hold=()):
+    value = value.reshape((2,) * len(left_bits) + value.shape[-2:])
+    axis = left_bits.index(bits[1])
+    away = lax.index_in_dim(value, 1, axis, keepdims=False)
+    stay = lax.index_in_dim(value, 0, axis, keepdims=False)
+    moved = trade(away, bits[1], count)
+    left_bits.remove(bits[1])
+
+    def finish(_, before, hold):
+        value = add(after(stay, *before), moved)
+        return scatter_on(value, left_bits, bits[2:], count, jnp.float32, hold)[0]
+
+    return [away], [], finish
+
+
+def across_scatter(make_parts, make_plain, rows, count, hold=()):
     first, order_a, order_b = orders(count)
-    if row_size(terms, turned, count) % 8:
-        half, sent = half_scatter(plain_products(terms, turned, columns), count)
-        return [half], sent, [], [], lambda value, *_: value, lambda value, *_: last_scatter(value[0], count)
+    if (rows // count) % 8:
+        half, sent = half_scatter(make_plain(), count)
+        return [half], sent, [], lambda value, *_: value, lambda value, *_: last_scatter(value[0], count)
     half_bit = first[-1]
     parts = [
         {half_bit: half, order[-1]: away}
         for half, order in enumerate((order_a, order_b))
         for away in (1, 0)
     ]
-    blocks = grad_parts(terms, turned, columns, parts, count)
-    halves, firsts, mids = [], [], []
+    blocks = make_parts(parts)
+    halves, mids = [], []
     for place, order in enumerate((order_a, order_b)):
         away, kept = blocks[2 * place : 2 * place + 2]
         left_bits = other_bits((order[-1], half_bit), count)
         moved = trade(away, order[-1], count)
         value = add(after(kept, *hold) if hold else kept, moved)
-        firsts.append(value)
         halves.append((value, left_bits, order[-2::-1]))
         mids += scatter_on(value, left_bits, order[-2::-1], count)[1][:1]
 
@@ -467,7 +612,7 @@
         left_bits = [bit for bit in other_bits((), count) if bit in first[:-1]]
         return scatter_on(value, left_bits, first[-2::-1], count, jnp.float32, between[2:])[0]
 
-    return halves, [blocks[0], blocks[2]], firsts, mids, begin, finish
+    return halves, [blocks[0], blocks[2]], mids, begin, finish
 
 
 def row_major(value):
@@ -703,7 +848,7 @@
     mod_half = scatter_small(mod_half, chips, order[:1])
     mod_half = scatter_small(mod_half, chips, order[1:])
     mix_halves = next_gather(mix_first, chips)
-    mod_half = scatter_small(after(mod_half, mix_first), chips, first[::-1])
+    mod_half = scatter_small(after(mod_half, *mix_halves), chips, first[::-1])
     mod_half = mod_half.reshape(-1, cond_cols)
     slots = class_label.shape[0]
     modulation = joined(mod_half[:slots], swap(mod_half[slots:]))
@@ -723,11 +868,11 @@
         [(value + nothing).astype(half) for value in (feed_weight[0], feed_weight[1], down_weight.T)],
         axis=1,
     )
-    far = first_gather(after(far, mix_first, mod_half), chips)
+    far = doubled(spread(after(far, mix_first), chips), first[0], chips)
+    far = after(far, mod_half)
+    for bit in first[1:]:
+        far = doubled(far, bit, chips)
     far = last_gather(next_gather(after(far, first_in), chips), chips)
-    far_gate, far_up, far_down = (
-        far[:, place * hidden_cols : (place + 1) * hidden_cols] for place in range(3)
-    )
     mix_other = swap_rows(mix_own, chips)
     proj_full = joined(mix_own[:, mix_cols:], mix_other[:, mix_cols:])
 
@@ -743,22 +888,16 @@
     branch = dots(attended, proj_full, 0, 0)
     middle = inputs + gate_a * branch
     second_in = modulate(middle, shift_b, scale_b).astype(half)
-    second_pair = jnp.concatenate([second_in, swap(second_in)], axis=0)
-    gate_pre = jnp.dot(second_pair, far_gate, preferred_element_type=jnp.float32)
-    up_pre = jnp.dot(second_pair, far_up, preferred_element_type=jnp.float32)
-    hidden = (jax.nn.silu(gate_pre) * up_pre).astype(half)
     grad_out = valid * out_grad.astype(jnp.float32)
     result_grad = (gate_b * grad_out).astype(half)
-    result_pair = jnp.concatenate([result_grad, swap(result_grad)], axis=0)
+    second_other, result_other = swap(second_in), swap(result_grad)
+    hidden, gate_grad, up_grad, second_own, second_sent = feed_both_ways(
+        second_in, second_other, result_grad, result_other, far
+    )
     down_sent, down_half, down_finish = chain_scatter(
-        [([(result_pair, hidden, 0)], 0)], True, hidden_cols, chips, attended_moved
-    )
-    d_hidden = jnp.dot(result_pair, far_down, preferred_element_type=jnp.float32)
-    sig = jax.nn.sigmoid(gate_pre)
-    gate_grad = (d_hidden * up_pre * sig * (1.0 + gate_pre * (1.0 - sig))).astype(half)
-    up_grad = (d_hidden * gate_pre * sig).astype(half)
-    second_part = against(gate_grad, far_gate) + against(up_grad, far_up)
-    second_grad = second_part[:count] + swap(second_part[count:].astype(half)).astype(jnp.float32)
+        (result_grad, result_other), [hidden], chips, attended_moved
+    )
+    second_grad = second_own + swap(second_sent).astype(jnp.float32)
     pull_second = jax.vjp(modulate, middle, shift_b, scale_b)[1]
     d_middle, d_shift_b, d_scale_b = pull_second(second_grad)
     d_middle = d_middle + grad_out
@@ -767,30 +906,25 @@
     attended_grad = dots(proj_full, branch_grad, 1, 1).astype(half).reshape(HEADS, HEAD, count)
     grad_own = lax.dynamic_slice_in_dim(attended_grad, side * heads, heads, 0)
     grad_other = lax.dynamic_slice_in_dim(attended_grad, (1 - side) * heads, heads, 0)
-    grad_other = after(grad_other, *down_sent)
     mg_other = attend_back(*qkv_other, grad_other, log_other, tables).reshape(mix_cols, count)
     mg_moved = swap(mg_other)
-    feed_half, _, _, feed_mids, feed_begin, feed_finish = across_scatter(
-        [([(second_pair, gate_grad, 0)], 0), ([(second_pair, up_grad, 0)], hidden_cols)],
-        True,
-        2 * hidden_cols,
-        chips,
-        (mg_other,),
-    )
-    grad_own = after(grad_own, *feed_mids) if feed_mids else grad_own
+    grad_own = after(grad_own, mg_other, *down_sent)
     mg_own = attend_back(*qkv_own, grad_own, log_own, tables).reshape(mix_cols, count)
+    feed_half, _, feed_mids, feed_begin, feed_finish = feed_scatter(
+        (second_in, second_other), [gate_grad, up_grad], chips, (mg_own,)
+    )
+    mg_moved = after(mg_moved, *feed_mids) if feed_mids else mg_moved
     branch_grad_own, branch_grad_other = parted(branch_grad)
     proj_start = -(-mix_cols // 128) * 128
-    near_half, near_sent, _, near_mids, near_begin, near_finish = across_scatter(
+    near_half, near_sent, near_mids, near_begin, near_finish = near_scatter(
         [
             ([(first_turned, mg_own, 1), (first_moved, mg_moved, 1)], 0),
             ([(attended, branch_grad_own, 0), (attended_moved, swap_rows(branch_grad_other, chips), 0)], proj_start),
         ],
-        False,
         proj_start + proj_cols,
         chips,
     )
-    down_grad = down_finish([after(value, *near_sent) for value in down_half], near_mids).T
+    down_grad = down_finish(down_half, near_mids, near_mids).T
     feed_half = feed_begin(feed_half, near_sent)
     near_half = near_begin(near_half)
     feed_grad = feed_finish(feed_half, [*near_mids, near_half[-1]])
@@ -805,7 +939,7 @@
         jnp.concatenate([mix_parts[1], mix_moved, mix_parts[2]], axis=1),
     )
 
-    partial_value = against(after(hidden, *near_sent), far_down)
+    partial_value = against(after(hidden, *near_sent, *near_mids), far[:, 2 * hidden_cols :])
     result = partial_value[:count] + swap(partial_value[count:].astype(half)).astype(jnp.float32)
     block_output = (valid * (middle + gate_b * result)).astype(half)
     d_gate_b = grad_out * result
@@ -815,7 +949,7 @@
     pull_first = jax.vjp(modulate, inputs, shift_a, scale_a)[1]
     d_inputs, d_shift_a, d_scale_a = pull_first(first_grad)
     input_grad = d_inputs + d_middle
-    member_low = after(member.astype(half), *near_sent)
+    member_low = after(member.astype(half), *near_sent, *near_mids)
     d_modulation = jnp.concatenate(
         [
             across(member_low, piece.astype(half))

time: 589 us -> 553 us (0.939)
  matrix products: 66.6 us -> 32 us
  waiting for transfers between devices: 151 us -> 127 us
  Pallas kernels: 96.7 us -> 120 us
  other arithmetic: 128 us -> 116 us
  starting transfers between devices: 60.2 us -> 66.1 us
    dot_general x3 -> x0, matrix products: 26.7 us -> none  [the longest x1 14.3 us: body(): jnp.dot(second_pair, far_gate, preferred_element_type=jnp.float32)]
    pallas_call x3 -> x4, Pallas kernels: 42.4 us -> 66.3 us  [the longest x1 30.5 us: feed_both_ways(): pl.pallas_call(feed_kernel, grid=(steps,), in_specs=[fixed] * 4 + [weight...]
    ppermute x44, waiting for transfers between devices: 151 us -> 127 us  [trade(): lax.ppermute(value, 'tok', [(place, place ^ 1 << bit) for place in range(...]
    dot_general x3 -> x1, matrix products: 16.9 us -> 6.25 us  [against(): lax.dot_general(left, right, (((1,), (1,)), ((), ())), preferred_element_...]
    unnamed x346 -> x394, local copies, waits for them, and re-layouts: 20.8 us -> 26.2 us
  transfers between devices with their start and end apart: 61 -> 61, of which waited for: 28 -> 26; matrix products, arithmetic and copies ran while one was open for 39% -> 33% of each run, Pallas kernels for 17% -> 22%
where the time goes in v4:
time: 553 us; the launch traced here: 545 us
  waiting for transfers between devices  127 us (23%)
  Pallas kernels  120 us (22%)
  other arithmetic  116 us (21%)
  local copies, waits for them, and re-layouts  71.4 us (13%)
  starting transfers between devices  66.1 us (12%)
  matrix products  32 us (6%)
  between operations  11.9 us (2%)
    ppermute x44, waiting for transfers between devices, trade(): lax.ppermute(value, 'tok', [(place, place ^ 1 << bit) for place in range(...  127 us
    ppermute x44, starting transfers between devices, trade(): lax.ppermute(value, 'tok', [(place, place ^ 1 << bit) for place in range(...  61.2 us
    pallas_call x1, Pallas kernels, feed_both_ways(): pl.pallas_call(feed_kernel, grid=(steps,), in_specs=[fixed] * 4 + [weight...  30.5 us
    unnamed x394, local copies, waits for them, and re-layouts  26.2 us
    convert_element_type x12, other arithmetic, add(): return (one.astype(jnp.float32) + two.astype(jnp.float32)).astype(kept)  23 us
    pallas_call x2, Pallas kernels, turned_parts(): pl.pallas_call(kernel, grid=(steps * len(rights),), in_specs=[pl.BlockSpe...  20.8 us
    dynamic_update_slice x12, local copies, waits for them, and re-layouts, put(): return lax.dynamic_update_slice(out, value, tuple(start))  19.8 us
    pallas_call x2, Pallas kernels, attend_back(): pl.pallas_call(attend_back_kernel, grid=(heads,), in_specs=[block] * 4 +...  19.1 us
  transfers between devices with their start and end apart: 61, of which 26 were waited for; matrix products, arithmetic and copies ran while one was open for 33% of the time, Pallas kernels for 22%

profile of v4, /device:TPU:0, one launch (start us, length us, event | category | flops | bytes accessed | tf_op | source)
XLA Modules:
  0.0 545.0 jit_solution(15759915812966855651)
XLA Ops:
  7.8 2.7 collective-permute-start.2
  15.6 3.1 collective-permute-start.4
  33.0 2.7 collective-permute-start.6
  36.9 9.9 %collective-permute-done.6 = bf16[1,1,1,1,72,2304]{5,4,3,2,1,0:T(8,128)(2,1)S(1)} collective-permute-done((bf16[1,1,1,1,72,2304]{5,4,3,2,1,0:T(8,128)(2,1)}, bf16[1,1,1,1,72,2304]{5,4,3,2,1,0:T(8,128)(2,1)S(1)}, u32[]{:S(2)}, u32[]{:S(2)}) %collective-permute-start.6) | collective-permute-done | bytes 331808 | tf_op jit(solution)/shard_map/ppermute | solution.py:87
  60.5 4.4 collective-permute-done.9
  67.9 2.6 pad_maximum_fusion.9
  70.5 3.3 collective-permute-start.22
  77.2 10.5 %collective-permute-done.12 = bf16[2,1,1,1,72,2304]{5,4,3,2,1,0:T(8,128)(2,1)S(1)} collective-permute-done((bf16[2,1,1,1,72,2304]{5,4,3,2,1,0:T(8,128)(2,1)S(1)}, bf16[2,1,1,1,72,2304]{5,4,3,2,1,0:T(8,128)(2,1)S(1)}, u32[]{:S(2)}, u32[]{:S(2)}) %collective-permute-start.12) | collective-permute-done | bytes 663584 | tf_op jit(solution)/shard_map/ppermute | solution.py:87
  91.3 6.3 %maximum_maximum_fusion.1.refs_0_ = bf16[2,2,2,2,72,2304]{5,4,3,2,1,0:T(8,128)(2,1)} fusion(bf16[2,1,2,1,72,2304]{5,4,3,2,1,0:T(8,128)(2,1)} %copy-done.62, bf16[2,1,1,2,72,2304]{5,4,3,2,1,0:T(8,128)(2,1)} %constant_dynamic-update-slice_fusion.9.refs_1_), kind=kLoop, calls=%fused_computation.1 | loop fusion | flops 7962624 | bytes 7962624 | tf_op jit(solution)/shard_map/concatenate | solution.py:667
  98.7 4.2 collective-permute-done.13
  105.3 3.2 collective-permute-done.14
  109.1 3.5 pad_maximum_fusion.1
  113.5 5.8 %add_convert_fusion.6.refs_1_.x_ref = bf16[512,1152]{1,0:T(8,128)(2,1)} fusion(bf16[512,1152]{1,0:T(8,128)(2,1)S(1)} %copy-done.49, f32[1152]{0:T(1024)S(1)} %get-tuple-element.90, f32[1152]{0:T(1024)S(1)} %get-tuple-element.91, f32[1152]{0:T(1024)S(1)} %get-tuple-element.92, f32[1152]{0:T(1024)S(1)} %get-tuple-element.93, f32[1152]{0:T(1024)S(1)} %get-tuple-element.94, ...), kind=kLoop, calls=%fused_computation.38 | loop fusion | flops 9437184 | bytes 2402308 | tf_op jit(solution)/shard_map/convert_element_type | solution.py:864
  120.1 4.8 collective-permute-done.16
  124.8 2.5 constant_dynamic-update-slice_fusion.7
  127.3 2.6 constant_dynamic-update-slice_fusion.6
  129.9 6.2 %heads_of.2 = (f32[1728,512]{1,0:T(8,128)S(1)}, bf16[1152,512]{1,0:T(8,128)(2,1)}) custom-call(bf16[512,1152]{1,0:T(8,128)(2,1)S(1)} %copy-done.7, bf16[1152,2304]{1,0:T(8,128)(2,1)} %bitcast.161), custom_call_target="tpu_custom_call" | custom-call | flops 2300000000 | bytes 1000 | tf_op jit(solution)/shard_map/heads_of/pallas_call | solution.py:258
  136.6 7.3 %collective-permute-done.23 = bf16[2,1,1,1,72,4608]{5,4,3,2,1,0:T(8,128)(2,1)} collective-permute-done((bf16[2,1,1,1,72,4608]{5,4,3,2,1,0:T(8,128)(2,1)}, bf16[2,1,1,1,72,4608]{5,4,3,2,1,0:T(8,128)(2,1)}, u32[]{:S(2)}, u32[]{:S(2)}) %collective-permute-start.23) | collective-permute-done | bytes 1327136 | tf_op jit(solution)/shard_map/ppermute | solution.py:87
  143.9 2.5 constant_dynamic-update-slice_fusion.4.refs_0_
  148.9 5.9 %attend.2 = (bf16[8,72,512]{2,1,0:T(8,128)(2,1)S(1)}, f32[8,1,512]{2,1,0:T(1,128)S(1)}, bf16[8,72,512]{2,1,0:T(8,128)(2,1)S(1)}, bf16[8,72,512]{2,1,0:T(8,128)(2,1)S(1)}, bf16[8,72,512]{2,1,0:T(8,128)(2,1)S(1)}) custom-call(f32[3,8,72,512]{3,2,1,0:T(8,128)S(1)} %bitcast.143, f32[3,8,72,512]{3,2,1,0:T(8,128)S(1)} %bitcast.144, ...), custom_call_target="tpu_custom_call" | custom-call | flops 2760000000 | bytes 1000 | tf_op jit(solution)/shard_map/attend/pallas_call | solution.py:181
  158.3 20.3 %collective-permute-done.24 = bf16[2,1,1,1,72,4608]{5,4,3,2,1,0:T(8,128)(2,1)S(1)} collective-permute-done((bf16[2,1,1,1,72,4608]{5,4,3,2,1,0:T(8,128)(2,1)S(1)}, bf16[2,1,1,1,72,4608]{5,4,3,2,1,0:T(8,128)(2,1)S(1)}, u32[]{:S(2)}, u32[]{:S(2)}) %collective-permute-start.24) | collective-permute-done | bytes 1327136 | tf_op jit(solution)/shard_map/ppermute | solution.py:87
  181.1 5.9 %collective-permute-done.25 = bf16[2,1,1,1,72,4608]{5,4,3,2,1,0:T(8,128)(2,1)S(1)} collective-permute-done((bf16[2,1,1,1,72,4608]{5,4,3,2,1,0:T(8,128)(2,1)S(1)}, bf16[2,1,1,1,72,4608]{5,4,3,2,1,0:T(8,128)(2,1)S(1)}, u32[]{:S(2)}, u32[]{:S(2)}) %collective-permute-start.25) | collective-permute-done | bytes 1327136 | tf_op jit(solution)/shard_map/ppermute | solution.py:87
  188.8 7.4 %maximum_maximum_fusion = bf16[2,2,2,2,72,4608]{5,4,3,2,1,0:T(8,128)(2,1)} fusion(bf16[2,1,2,1,72,4608]{5,4,3,2,1,0:T(8,128)(2,1)S(1)} %constant_dynamic-update-slice_fusion.2, bf16[2,1,1,2,72,4608]{5,4,3,2,1,0:T(8,128)(2,1)} %constant_dynamic-update-slice_fusion.3), kind=kLoop, calls=%fused_computation | loop fusion | flops 15925248 | bytes 15925248 | tf_op jit(solution)/shard_map/concatenate | solution.py:667
  196.2 7.4 %heads_of.3 = (f32[1728,512]{1,0:T(8,128)}, bf16[1152,512]{1,0:T(8,128)(2,1)}) custom-call(bf16[512,1152]{1,0:T(8,128)(2,1)S(1)} %copy-done.8, bf16[1152,2304]{1,0:T(8,128)(2,1)} %bitcast.16.w_ref.w_two_ref, bf16[1152,512]{1,0:T(8,128)(2,1)} %collective-permute-done.19.refs_0_.refs_1_), custom_call_target="tpu_custom_call" | custom-call | flops 2300000000 | bytes 1000 | tf_op jit(solution)/shard_map/heads_of/pallas_call | solution.py:258
  205.5 6.1 %attend.3 = (bf16[8,72,512]{2,1,0:T(8,128)(2,1)S(1)}, f32[8,1,512]{2,1,0:T(1,128)S(1)}, bf16[8,72,512]{2,1,0:T(8,128)(2,1)S(1)}, bf16[8,72,512]{2,1,0:T(8,128)(2,1)S(1)}, bf16[8,72,512]{2,1,0:T(8,128)(2,1)S(1)}) custom-call(f32[3,8,72,512]{3,2,1,0:T(8,128)S(1)} %bitcast.146, f32[3,8,72,512]{3,2,1,0:T(8,128)S(1)} %bitcast.147, ...), custom_call_target="tpu_custom_call" | custom-call | flops 2760000000 | bytes 1000 | tf_op jit(solution)/shard_map/attend/pallas_call | solution.py:181
  213.4 3.0 broadcast_select_fusion.1
  216.6 6.8 %fusion.62 = (f32[512]{0:T(512)S(1)}, f32[512,1152]{1,0:T(8,128)S(1)}, bf16[512,1152]{1,0:T(8,128)(2,1)S(1)}, f32[512,1152]{1,0:T(8,128)}) fusion(f32[1152]{0:T(1024)S(1)} %copy-done.174, pred[512]{0:T(512)(128)(4,1)S(1)} %copy-done.140, f32[1152]{0:T(1024)S(1)} %copy-done.176, pred[512]{0:T(512)(128)(4,1)S(1)} %copy-done.145, f32[1152]{0:T(1024)S(1)} %copy-done.178, ...), kind=kOutput, calls=%fused_computation.288 | convolution fusion | flops 1374289408 | bytes 12134404 | tf_op jit(solution)/shard_map/dot_general | solution.py:141
  224.5 4.0 add_convert_fusion.5.x_one.one_ref
  229.1 12.7 %collective-permute-done.26 = bf16[2,1,1,2,72,4608]{5,4,3,2,1,0:T(8,128)(2,1)} collective-permute-done((bf16[2,1,1,2,72,4608]{5,4,3,2,1,0:T(8,128)(2,1)}, bf16[2,1,1,2,72,4608]{5,4,3,2,1,0:T(8,128)(2,1)}, u32[]{:S(2)}, u32[]{:S(2)}) %collective-permute-start.26) | collective-permute-done | bytes 2654240 | tf_op jit(solution)/shard_map/ppermute | solution.py:87
  241.8 3.5 constant_dynamic-update-slice_fusion.1
  245.3 3.4 constant_dynamic-update-slice_fusion
  250.2 30.5 %feed_both_ways.1 = (bf16[1024,1536]{1,0:T(8,128)(2,1)}, bf16[1024,1536]{1,0:T(8,128)(2,1)}, bf16[1024,1536]{1,0:T(8,128)(2,1)}, f32[512,1152]{1,0:T(8,128)}, bf16[512,1152]{1,0:T(8,128)(2,1)}) custom-call(bf16[512,1152]{1,0:T(8,128)(2,1)} %copy-done.20, bf16[512,1152]{1,0:T(8,128)(2,1)} %copy-done.25, bf16[512,1152]{1,0:T(8,128)(2,1)} %copy-done.23, ...), custom_call_target="tpu_custom_call" | custom-call | flops 10119999488 | bytes 1000 | tf_op jit(solution)/shard_map/feed_both_ways/pallas_call | solution.py:353
  282.9 7.6 %turned_parts.2 = (bf16[8,72,1536]{2,1,0:T(8,128)(2,1)S(1)}, bf16[8,72,1536]{2,1,0:T(8,128)(2,1)}) custom-call(s32[1]{0:T(128)} %bitcast.25.tok_ref, bf16[512,1152]{1,0:T(8,128)(2,1)S(1)} %copy-done.24, bf16[512,1152]{1,0:T(8,128)(2,1)S(1)} %copy-done.28, bf16[1024,1536]{1,0:T(8,128)(2,1)} %get-tuple-element.54.refs_0_, ...), custom_call_target="tpu_custom_call" | custom-call | flops 2760000000 | bytes 1000 | tf_op jit(solution)/shard_map/turned_parts/pallas_call | solution.py:420
  291.2 13.2 %turned_parts.3 = (bf16[4,72,3072]{2,1,0:T(8,128)(2,1)}, bf16[4,72,3072]{2,1,0:T(8,128)(2,1)S(1)}, bf16[4,72,3072]{2,1,0:T(8,128)(2,1)}, bf16[4,72,3072]{2,1,0:T(8,128)(2,1)}) custom-call(s32[1]{0:T(128)} %bitcast.25.tok_ref, bf16[512,1152]{1,0:T(8,128)(2,1)S(1)} %copy-done.21, bf16[512,1152]{1,0:T(8,128)(2,1)S(1)} %copy-done.26, ...), custom_call_target="tpu_custom_call" | custom-call | flops 5520000000 | bytes 1000 | tf_op jit(solution)/shard_map/turned_parts/pallas_call | solution.py:420
  307.3 2.6 multiply_reduce_fusion.1
  310.0 2.9 fusion.61
  319.1 9.5 %attend_back.2 = bf16[3,8,72,512]{3,2,1,0:T(8,128)(2,1)S(1)} custom-call(bf16[8,72,512]{2,1,0:T(8,128)(2,1)S(1)} %copy-done.36, bf16[8,72,512]{2,1,0:T(8,128)(2,1)S(1)} %copy-done.38, bf16[8,72,512]{2,1,0:T(8,128)(2,1)S(1)} %copy-done.40, bf16[8,72,512]{2,1,0:T(8,128)(2,1)S(1)} %get-tuple-element.145.g_ref, f32[8,1,512]{2,1,0:T(1,128)S(1)} %copy-done.44, ...), custom_call_target="tpu_custom_call" | custom-call | flops 4600000000 | bytes 1000 | tf_op jit(solution)/shard_map/attend_back/pallas_call | solution.py:222
  338.7 9.6 %attend_back.3 = bf16[3,8,72,512]{3,2,1,0:T(8,128)(2,1)S(1)} custom-call(bf16[8,72,512]{2,1,0:T(8,128)(2,1)S(1)} %copy-done.30, bf16[8,72,512]{2,1,0:T(8,128)(2,1)S(1)} %copy-done.32, bf16[8,72,512]{2,1,0:T(8,128)(2,1)S(1)} %copy-done.34, bf16[8,72,512]{2,1,0:T(8,128)(2,1)S(1)} %copy-done.13, f32[8,1,512]{2,1,0:T(1,128)S(1)} %copy-done.42, ...), custom_call_target="tpu_custom_call" | custom-call | flops 4600000000 | bytes 1000 | tf_op jit(solution)/shard_map/attend_back/pallas_call | solution.py:222
  362.4 15.0 %grad_parts.1 = (bf16[4,72,2368]{2,1,0:T(8,128)(2,1)}, bf16[4,72,2368]{2,1,0:T(8,128)(2,1)}, bf16[4,72,2368]{2,1,0:T(8,128)(2,1)}, bf16[4,72,2368]{2,1,0:T(8,128)(2,1)}) custom-call(s32[1]{0:T(128)} %bitcast.25.tok_ref, bf16[1152,512]{1,0:T(8,128)(2,1)} %get-tuple-element.51.refs_0_, bf16[1152,512]{1,0:T(8,128)(2,1)} %collective-permute-done.19.refs_0_.refs_1_, ...), custom_call_target="tpu_custom_call" | custom-call | flops 5980000256 | bytes 1000 | tf_op jit(solution)/shard_map/grad_parts/pallas_call | solution.py:495
  379.5 2.6 add_convert_fusion.10.refs_3_
  386.0 9.5 %back_through.1 = f32[512,1152]{1,0:T(8,128)S(1)} custom-call(bf16[1728,512]{1,0:T(8,128)(2,1)S(1)} %copy-done.4, bf16[1728,512]{1,0:T(8,128)(2,1)S(1)} %copy-done.6, bf16[1152,2304]{1,0:T(8,128)(2,1)} %bitcast.163, bf16[1152,2304]{1,0:T(8,128)(2,1)} %bitcast.16.w_ref.w_two_ref), custom_call_target="tpu_custom_call" | custom-call | flops 4140000000 | bytes 1000 | tf_op jit(solution)/shard_map/back_through/pallas_call | solution.py:291
  397.1 2.9 fusion.60
  400.6 2.3 add_convert_fusion.9.refs_0_
  402.9 9.3 %collective-permute-done.36 = bf16[4,72,2368]{2,1,0:T(8,128)(2,1)} collective-permute-done((bf16[4,72,2368]{2,1,0:T(8,128)(2,1)}, bf16[4,72,2368]{2,1,0:T(8,128)(2,1)}, u32[]{:S(2)}, u32[]{:S(2)}) %collective-permute-start.36) | collective-permute-done | bytes 1364000 | tf_op jit(solution)/shard_map/ppermute | solution.py:87
  429.0 2.2 convolution_convert_fusion.5
  431.2 3.1 convolution_convert_fusion.4
  434.4 6.3 %fusion = f32[1024,1152]{1,0:T(8,128)S(1)} fusion(bf16[1024,1536]{1,0:T(8,128)(2,1)S(1)} %copy-done.88, bf16[1152,4608]{1,0:T(8,128)(2,1)} %bitcast.167), kind=kOutput, calls=%fused_computation.3 | convolution fusion | flops 3623878656 | bytes 11403264 | tf_op jit(solution)/shard_map/dot_general | solution.py:60
  441.8 2.2 copy-done.55
  444.0 2.4 convolution_convert_fusion.3
  446.4 2.6 convolution_convert_fusion.2
  452.9 3.9 collective-permute-done.54
  459.2 2.4 fusion.8.refs_1_
  464.4 2.6 convolution_convert_fusion.1
  470.6 5.8 %add_add_fusion.2 = (f32[512,1152]{1,0:T(8,128)}, bf16[512,1152]{1,0:T(8,128)(2,1)}) fusion(f32[512,1152]{1,0:T(8,128)} %get-tuple-element.126, f32[512]{0:T(512)} %negate_multiply_fusion, bf16[512,1152]{1,0:T(8,128)(2,1)S(1)} %copy-done.59, f32[512]{0:T(512)S(1)} %copy-done.138, f32[512,1152]{1,0:T(8,128)} %copy-done.52, f32[512]{0:T(512)} %copy-done.170, ...), kind=kLoop, calls=%fused_computation.23 | loop fusion | flops 9437184 | bytes 15362048 | tf_op jit(solution)/shard_map/add | solution.py:951
  476.7 2.6 collective-permute-start.45
  483.3 2.2 collective-permute-start.42
  485.6 2.5 collective-permute-done.46
  489.4 10.9 %collective-permute-done.42 = bf16[72,2368]{1,0:T(8,128)(2,1)S(1)} collective-permute-done((bf16[72,2368]{1,0:T(8,128)(2,1)S(1)}, bf16[72,2368]{1,0:T(8,128)(2,1)S(1)}, u32[]{:S(2)}, u32[]{:S(2)}) %collective-permute-start.42) | collective-permute-done | bytes 341024 | tf_op jit(solution)/shard_map/ppermute | solution.py:87
  514.8 2.3 collective-permute-start.57
  520.5 2.3 collective-permute-done.58
  525.1 2.9 collective-permute-done.59
  528.7 2.3 multiply_subtract_fusion.4
  533.7 2.2 multiply_subtract_fusion
  540.8 2.8 multiply_subtract_fusion.2
  (644 shorter events, 174.6 us)
Async XLA Ops:
  1.5 5.5 %collective-permute-start.1 = (s32[4,2]{0,1:T(2,128)S(1)}, s32[4,2]{0,1:T(2,128)S(1)}, u32[]{:S(2)}, u32[]{:S(2)}) collective-permute-start(s32[4,2]{0,1:T(2,128)S(1)} %pad_add_fusion.4), channel_id=1, source_target_pairs={{0,1},{1,0},{2,3},{3,2},{4,5},{5,4},{6,7},{7,6},{8,9},{9,8},{10,11... | collective-permute-start | bytes 104 | tf_op jit(solution)/shard_map/ppermute | solution.py:95
  3.8 26.3 %collective-permute-start = (bf16[72,576]{1,0:T(8,128)(2,1)}, bf16[72,576]{1,0:T(8,128)(2,1)}, u32[]{:S(2)}, u32[]{:S(2)}) collective-permute-start(bf16[72,576]{1,0:T(8,128)(2,1)} %get-tuple-element.161), channel_id=1, source_target_pairs={{0,1},{1,0},{2,3},{3,2},{4,5},{5,4},{6,7},{7,6},{8,9},{9,8},{10,11... | collective-permute-start | bytes 248840 | tf_op jit(solution)/shard_map/ppermute | solution.py:95
  4.6 17.6 %collective-permute-start.7 = (f32[216]{0:T(256)S(1)}, f32[216]{0:T(256)S(1)}, u32[]{:S(2)}, u32[]{:S(2)}) collective-permute-start(f32[216]{0:T(256)S(1)} %convert_convert_fusion.1), channel_id=1, source_target_pairs={{0,1},{1,0},{2,3},{3,2},{4,5},{5,4},{6,7},{7,6},{8,9},{9,8},{10,11... | collective-permute-start | bytes 2600 | tf_op jit(solution)/shard_map/ppermute | solution.py:95
  7.8 4.2 collective-permute-start.2
  12.0 3.6 collective-permute-start.3
  15.6 4.7 collective-permute-start.4
  20.3 3.7 collective-permute-start.5
  28.3 29.4 %collective-permute-start.8 = (bf16[2,2,2,1,8,3456]{5,4,3,2,1,0:T(8,128)(2,1)}, bf16[2,2,2,1,8,3456]{5,4,3,2,1,0:T(8,128)(2,1)}, u32[]{:S(2)}, u32[]{:S(2)}) collective-permute-start(bf16[2,2,2,1,8,3456]{5,4,3,2,1,0:T(8,128)(2,1)} %slice.534), channel_id=1, source_target_pairs={{0,2},{2,0},{4,6},{6,4},{8,10},{10,8},{12,14},{14,12},{16,18},{18,... | collective-permute-start | bytes 1327112 | tf_op jit(solution)/shard_map/ppermute | solution.py:87
  33.0 13.7 %collective-permute-start.6 = (bf16[1,1,1,1,72,2304]{5,4,3,2,1,0:T(8,128)(2,1)}, bf16[1,1,1,1,72,2304]{5,4,3,2,1,0:T(8,128)(2,1)S(1)}, u32[]{:S(2)}, u32[]{:S(2)}) collective-permute-start(bf16[1,1,1,1,72,2304]{5,4,3,2,1,0:T(8,128)(2,1)} %after.21), channel_id=1, source_target_pairs={{0,16},{2,18},{4,20},{6,22},{8,24},{10,26},{12,28},{14,30},{16,0},... | collective-permute-start | bytes 995336 | tf_op jit(solution)/shard_map/ppermute | solution.py:87
  48.4 17.2 %collective-permute-start.10 = (bf16[2,1,1,1,72,2304]{5,4,3,2,1,0:T(8,128)(2,1)S(1)}, bf16[2,1,1,1,72,2304]{5,4,3,2,1,0:T(8,128)(2,1)}, u32[]{:S(2)}, u32[]{:S(2)}) collective-permute-start(bf16[2,1,1,1,72,2304]{5,4,3,2,1,0:T(8,128)(2,1)S(1)} %constant_dynamic-update-slice_fusion.11), channel_id=1, source_target_pairs={{0,8},{2,10},{4,12},{6,14},{8,0},{10,2},{12,4},{14,6},{16,24},{18,... | collective-permute-start | bytes 1990664 | tf_op jit(solution)/shard_map/ppermute | solution.py:87
  53.5 59.9 %copy-start.144 = (pred[512]{0:T(512)(128)(4,1)}, pred[512]{0:T(512)(128)(4,1)S(1)}, u32[]{:S(2)}) copy-start(pred[512]{0:T(512)(128)(4,1)S(1)} %get-tuple-element.185) | copy-start | bytes 1540
  53.5 59.9 %copy-start.149 = (pred[512]{0:T(512)(128)(4,1)}, pred[512]{0:T(512)(128)(4,1)S(1)}, u32[]{:S(2)}) copy-start(pred[512]{0:T(512)(128)(4,1)S(1)} %get-tuple-element.186) | copy-start | bytes 1540
  53.5 59.9 %copy-start.154 = (pred[512]{0:T(512)(128)(4,1)}, pred[512]{0:T(512)(128)(4,1)S(1)}, u32[]{:S(2)}) copy-start(pred[512]{0:T(512)(128)(4,1)S(1)} %get-tuple-element.187) | copy-start | bytes 1540
  58.9 6.0 %collective-permute-start.9 = (bf16[2,2,1,1,8,3456]{5,4,3,2,1,0:T(8,128)(2,1)S(1)}, bf16[2,2,1,1,8,3456]{5,4,3,2,1,0:T(8,128)(2,1)S(1)}, u32[]{:S(2)}, u32[]{:S(2)}) collective-permute-start(bf16[2,2,1,1,8,3456]{5,4,3,2,1,0:T(8,128)(2,1)S(1)} %slice.535), channel_id=1, source_target_pairs={{0,4},{2,6},{4,0},{6,2},{8,12},{10,14},{12,8},{14,10},{16,20},{18,... | collective-permute-start | bytes 663560 | tf_op jit(solution)/shard_map/ppermute | solution.py:87
  70.5 32.9 %collective-permute-start.22 = (bf16[1,1,1,1,72,4608]{5,4,3,2,1,0:T(8,128)(2,1)}, bf16[1,1,1,1,72,4608]{5,4,3,2,1,0:T(8,128)(2,1)}, u32[]{:S(2)}, u32[]{:S(2)}) collective-permute-start(bf16[1,1,1,1,72,4608]{5,4,3,2,1,0:T(8,128)(2,1)} %bitcast.174), channel_id=1, source_target_pairs={{0,16},{2,18},{4,20},{6,22},{8,24},{10,26},{12,28},{14,30},{16,0},... | collective-permute-start | bytes 1990664 | tf_op jit(solution)/shard_map/ppermute | solution.py:87
  73.8 13.9 %collective-permute-start.12 = (bf16[2,1,1,1,72,2304]{5,4,3,2,1,0:T(8,128)(2,1)S(1)}, bf16[2,1,1,1,72,2304]{5,4,3,2,1,0:T(8,128)(2,1)S(1)}, u32[]{:S(2)}, u32[]{:S(2)}) collective-permute-start(bf16[2,1,1,1,72,2304]{5,4,3,2,1,0:T(8,128)(2,1)S(1)} %get-tuple-element.141), channel_id=1, source_target_pairs={{0,4},{2,6},{4,0},{6,2},{8,12},{10,14},{12,8},{14,10},{16,20},{18,... | collective-permute-start | bytes 1990664 | tf_op jit(solution)/shard_map/ppermute | solution.py:87
  75.4 13.6 %collective-permute-start.11 = (bf16[2,1,1,1,72,2304]{5,4,3,2,1,0:T(8,128)(2,1)S(1)}, bf16[2,1,1,1,72,2304]{5,4,3,2,1,0:T(8,128)(2,1)S(1)}, u32[]{:S(2)}, u32[]{:S(2)}) collective-permute-start(bf16[2,1,1,1,72,2304]{5,4,3,2,1,0:T(8,128)(2,1)S(1)} %get-tuple-element.142), channel_id=1, source_target_pairs={{0,2},{2,0},{4,6},{6,4},{8,10},{10,8},{12,14},{14,12},{16,18},{18,... | collective-permute-start | bytes 1990664 | tf_op jit(solution)/shard_map/ppermute | solution.py:87
  90.9 12.0 %collective-permute-start.13 = (bf16[2,1,1,1,8,3456]{5,4,3,2,1,0:T(8,128)(2,1)S(1)}, bf16[2,1,1,1,8,3456]{5,4,3,2,1,0:T(8,128)(2,1)S(1)}, u32[]{:S(2)}, u32[]{:S(2)}) collective-permute-start(bf16[2,1,1,1,8,3456]{5,4,3,2,1,0:T(8,128)(2,1)S(1)} %slice.536), channel_id=1, source_target_pairs={{0,8},{2,10},{4,12},{6,14},{8,0},{10,2},{12,4},{14,6},{16,24},{18,... | collective-permute-start | bytes 331784 | tf_op jit(solution)/shard_map/ppermute | solution.py:87
  97.5 27.3 %collective-permute-start.16 = (bf16[2,1,1,2,72,2304]{5,4,3,2,1,0:T(8,128)(2,1)}, bf16[2,1,1,2,72,2304]{5,4,3,2,1,0:T(8,128)(2,1)}, u32[]{:S(2)}, u32[]{:S(2)}) collective-permute-start(bf16[2,1,1,2,72,2304]{5,4,3,2,1,0:T(8,128)(2,1)} %constant_dynamic-update-slice_fusion.9.refs_1_), channel_id=1, source_target_pairs={{0,4},{2,6},{4,0},{6,2},{8,12},{10,14},{12,8},{14,10},{16,20},{18,... | collective-permute-start | bytes 3981320 | tf_op jit(solution)/shard_map/ppermute | solution.py:87
  98.3 29.1 %collective-permute-start.17 = (bf16[2,1,2,1,72,2304]{5,4,3,2,1,0:T(8,128)(2,1)S(1)}, bf16[2,1,2,1,72,2304]{5,4,3,2,1,0:T(8,128)(2,1)}, u32[]{:S(2)}, u32[]{:S(2)}) collective-permute-start(bf16[2,1,2,1,72,2304]{5,4,3,2,1,0:T(8,128)(2,1)S(1)} %copy-done.63), channel_id=1, source_target_pairs={{0,2},{2,0},{4,6},{6,4},{8,10},{10,8},{12,14},{14,12},{16,18},{18,... | collective-permute-start | bytes 3981320 | tf_op jit(solution)/shard_map/ppermute | solution.py:87
  102.9 5.5 %collective-permute-start.14 = (bf16[1,1,1,1,8,3456]{5,4,3,2,1,0:T(8,128)(2,1)S(1)}, bf16[1,1,1,1,8,3456]{5,4,3,2,1,0:T(8,128)(2,1)S(1)}, u32[]{:S(2)}, u32[]{:S(2)}) collective-permute-start(bf16[1,1,1,1,8,3456]{5,4,3,2,1,0:T(8,128)(2,1)S(1)} %slice.537), channel_id=1, source_target_pairs={{0,16},{2,18},{4,20},{6,22},{8,24},{10,26},{12,28},{14,30},{16,0},... | collective-permute-start | bytes 165896 | tf_op jit(solution)/shard_map/ppermute | solution.py:87
  108.5 4.1 collective-permute-start.15
  112.6 31.3 %collective-permute-start.23 = (bf16[2,1,1,1,72,4608]{5,4,3,2,1,0:T(8,128)(2,1)}, bf16[2,1,1,1,72,4608]{5,4,3,2,1,0:T(8,128)(2,1)}, u32[]{:S(2)}, u32[]{:S(2)}) collective-permute-start(bf16[2,1,1,1,72,4608]{5,4,3,2,1,0:T(8,128)(2,1)} %after.25), channel_id=1, source_target_pairs={{0,8},{2,10},{4,12},{6,14},{8,0},{10,2},{12,4},{14,6},{16,24},{18,... | collective-permute-start | bytes 3981320 | tf_op jit(solution)/shard_map/ppermute | solution.py:87
  129.9 66.3 %collective-permute-start.18 = (bf16[2,2,2,2,72,2304]{5,4,3,2,1,0:T(8,128)(2,1)}, bf16[2,2,2,2,72,2304]{5,4,3,2,1,0:T(8,128)(2,1)}, u32[]{:S(2)}, u32[]{:S(2)}) collective-permute-start(bf16[2,2,2,2,72,2304]{5,4,3,2,1,0:T(8,128)(2,1)} %constant_dynamic-update-slice_fusion.6), channel_id=1, source_target_pairs={{0,1},{1,0},{2,3},{3,2},{4,5},{5,4},{6,7},{7,6},{8,9},{9,8},{10,11... | collective-permute-start | bytes 15925256 | tf_op jit(solution)/shard_map/ppermute | solution.py:95
  136.1 60.1 %collective-permute-start.19 = (bf16[1152,512]{1,0:T(8,128)(2,1)}, bf16[1152,512]{1,0:T(8,128)(2,1)}, u32[]{:S(2)}, u32[]{:S(2)}) collective-permute-start(bf16[1152,512]{1,0:T(8,128)(2,1)} %get-tuple-element.51.refs_0_), channel_id=1, source_target_pairs={{0,1},{1,0},{2,3},{3,2},{4,5},{5,4},{6,7},{7,6},{8,9},{9,8},{10,11... | collective-permute-start | bytes 3538952 | tf_op jit(solution)/shard_map/ppermute | solution.py:95
  148.4 30.2 %collective-permute-start.24 = (bf16[2,1,1,1,72,4608]{5,4,3,2,1,0:T(8,128)(2,1)S(1)}, bf16[2,1,1,1,72,4608]{5,4,3,2,1,0:T(8,128)(2,1)S(1)}, u32[]{:S(2)}, u32[]{:S(2)}) collective-permute-start(bf16[2,1,1,1,72,4608]{5,4,3,2,1,0:T(8,128)(2,1)S(1)} %get-tuple-element.133), channel_id=1, source_target_pairs={{0,2},{2,0},{4,6},{6,4},{8,10},{10,8},{12,14},{14,12},{16,18},{18,... | collective-permute-start | bytes 3981320 | tf_op jit(solution)/shard_map/ppermute | solution.py:87
  154.9 32.1 %collective-permute-start.25 = (bf16[2,1,1,1,72,4608]{5,4,3,2,1,0:T(8,128)(2,1)S(1)}, bf16[2,1,1,1,72,4608]{5,4,3,2,1,0:T(8,128)(2,1)S(1)}, u32[]{:S(2)}, u32[]{:S(2)}) collective-permute-start(bf16[2,1,1,1,72,4608]{5,4,3,2,1,0:T(8,128)(2,1)S(1)} %get-tuple-element.134), channel_id=1, source_target_pairs={{0,4},{2,6},{4,0},{6,2},{8,12},{10,14},{12,8},{14,10},{16,20},{18,... | collective-permute-start | bytes 3981320 | tf_op jit(solution)/shard_map/ppermute | solution.py:87
  179.8 62.0 %collective-permute-start.26 = (bf16[2,1,1,2,72,4608]{5,4,3,2,1,0:T(8,128)(2,1)}, bf16[2,1,1,2,72,4608]{5,4,3,2,1,0:T(8,128)(2,1)}, u32[]{:S(2)}, u32[]{:S(2)}) collective-permute-start(bf16[2,1,1,2,72,4608]{5,4,3,2,1,0:T(8,128)(2,1)} %constant_dynamic-update-slice_fusion.3), channel_id=1, source_target_pairs={{0,4},{2,6},{4,0},{6,2},{8,12},{10,14},{12,8},{14,10},{16,20},{18,... | collective-permute-start | bytes 7962632 | tf_op jit(solution)/shard_map/ppermute | solution.py:87
  187.2 58.2 %collective-permute-start.27 = (bf16[2,1,2,1,72,4608]{5,4,3,2,1,0:T(8,128)(2,1)S(1)}, bf16[2,1,2,1,72,4608]{5,4,3,2,1,0:T(8,128)(2,1)}, u32[]{:S(2)}, u32[]{:S(2)}) collective-permute-start(bf16[2,1,2,1,72,4608]{5,4,3,2,1,0:T(8,128)(2,1)S(1)} %constant_dynamic-update-slice_fusion.2), channel_id=1, source_target_pairs={{0,2},{2,0},{4,6},{6,4},{8,10},{10,8},{12,14},{14,12},{16,18},{18,... | collective-permute-start | bytes 7962632 | tf_op jit(solution)/shard_map/ppermute | solution.py:87
  228.5 20.3 %collective-permute-start.20 = (bf16[512,1152]{1,0:T(8,128)(2,1)S(1)}, bf16[512,1152]{1,0:T(8,128)(2,1)S(1)}, u32[]{:S(2)}, u32[]{:S(2)}) collective-permute-start(bf16[512,1152]{1,0:T(8,128)(2,1)S(1)} %add_convert_fusion.5.x_one.one_ref), channel_id=1, source_target_pairs={{0,1},{1,0},{2,3},{3,2},{4,5},{5,4},{6,7},{7,6},{8,9},{9,8},{10,11... | collective-permute-start | bytes 3538952 | tf_op jit(solution)/shard_map/ppermute | solution.py:95
  228.6 20.2 %collective-permute-start.21 = (bf16[512,1152]{1,0:T(8,128)(2,1)S(1)}, bf16[512,1152]{1,0:T(8,128)(2,1)S(1)}, u32[]{:S(2)}, u32[]{:S(2)}) collective-permute-start(bf16[512,1152]{1,0:T(8,128)(2,1)S(1)} %get-tuple-element.182.r_one.one_ref), channel_id=1, source_target_pairs={{0,1},{1,0},{2,3},{3,2},{4,5},{5,4},{6,7},{7,6},{8,9},{9,8},{10,11... | collective-permute-start | bytes 3538952 | tf_op jit(solution)/shard_map/ppermute | solution.py:95
  248.8 32.4 %collective-permute-start.28 = (bf16[1152,512]{1,0:T(8,128)(2,1)}, bf16[1152,512]{1,0:T(8,128)(2,1)S(1)}, u32[]{:S(2)}, u32[]{:S(2)}) collective-permute-start(bf16[1152,512]{1,0:T(8,128)(2,1)} %bitcast.18.refs_2_), channel_id=1, source_target_pairs={{0,1},{1,0},{2,3},{3,2},{4,5},{5,4},{6,7},{7,6},{8,9},{9,8},{10,11... | collective-permute-start | bytes 3538952 | tf_op jit(solution)/shard_map/ppermute | solution.py:95
  280.7 26.5 %collective-permute-start.29 = (bf16[512,1152]{1,0:T(8,128)(2,1)}, bf16[512,1152]{1,0:T(8,128)(2,1)}, u32[]{:S(2)}, u32[]{:S(2)}) collective-permute-start(bf16[512,1152]{1,0:T(8,128)(2,1)} %get-tuple-element.59), channel_id=1, source_target_pairs={{0,1},{1,0},{2,3},{3,2},{4,5},{5,4},{6,7},{7,6},{8,9},{9,8},{10,11... | collective-permute-start | bytes 3538952 | tf_op jit(solution)/shard_map/ppermute | solution.py:95
  290.5 40.7 %collective-permute-start.30 = (bf16[8,72,1536]{2,1,0:T(8,128)(2,1)S(1)}, bf16[8,72,1536]{2,1,0:T(8,128)(2,1)}, u32[]{:S(2)}, u32[]{:S(2)}) collective-permute-start(bf16[8,72,1536]{2,1,0:T(8,128)(2,1)S(1)} %get-tuple-element.65), channel_id=1, source_target_pairs={{0,8},{2,10},{4,12},{6,14},{8,0},{10,2},{12,4},{14,6},{16,24},{18,... | collective-permute-start | bytes 5308424 | tf_op jit(solution)/shard_map/ppermute | solution.py:87
  304.4 45.2 %collective-permute-start.33 = (bf16[4,72,3072]{2,1,0:T(8,128)(2,1)}, bf16[4,72,3072]{2,1,0:T(8,128)(2,1)}, u32[]{:S(2)}, u32[]{:S(2)}) collective-permute-start(bf16[4,72,3072]{2,1,0:T(8,128)(2,1)} %get-tuple-element.72), channel_id=1, source_target_pairs={{0,2},{2,0},{4,6},{6,4},{8,10},{10,8},{12,14},{14,12},{16,18},{18,... | collective-permute-start | bytes 5308424 | tf_op jit(solution)/shard_map/ppermute | solution.py:87
  306.0 47.3 %collective-permute-start.32 = (bf16[4,72,3072]{2,1,0:T(8,128)(2,1)}, bf16[4,72,3072]{2,1,0:T(8,128)(2,1)}, u32[]{:S(2)}, u32[]{:S(2)}) collective-permute-start(bf16[4,72,3072]{2,1,0:T(8,128)(2,1)} %get-tuple-element.70), channel_id=1, source_target_pairs={{0,4},{2,6},{4,0},{6,2},{8,12},{10,14},{12,8},{14,10},{16,20},{18,... | collective-permute-start | bytes 5308424 | tf_op jit(solution)/shard_map/ppermute | solution.py:87
  330.0 32.4 %collective-permute-start.31 = (bf16[1728,512]{1,0:T(8,128)(2,1)S(1)}, bf16[1728,512]{1,0:T(8,128)(2,1)}, u32[]{:S(2)}, u32[]{:S(2)}) collective-permute-start(bf16[1728,512]{1,0:T(8,128)(2,1)S(1)} %bitcast.153), channel_id=1, source_target_pairs={{0,1},{1,0},{2,3},{3,2},{4,5},{5,4},{6,7},{7,6},{8,9},{9,8},{10,11... | collective-permute-start | bytes 5308424 | tf_op jit(solution)/shard_map/ppermute | solution.py:95
  330.0 32.4 %collective-permute-start.34 = (bf16[2,2,2,2,32,576]{5,4,3,2,1,0:T(8,128)(2,1)}, bf16[2,2,2,2,32,576]{5,4,3,2,1,0:T(8,128)(2,1)}, u32[]{:S(2)}, u32[]{:S(2)}) collective-permute-start(bf16[2,2,2,2,32,576]{5,4,3,2,1,0:T(8,128)(2,1)} %bitcast.34), channel_id=1, source_target_pairs={{0,1},{1,0},{2,3},{3,2},{4,5},{5,4},{6,7},{7,6},{8,9},{9,8},{10,11... | collective-permute-start | bytes 1769480 | tf_op jit(solution)/shard_map/ppermute | solution.py:95
  357.0 22.5 %collective-permute-start.38 = (bf16[2,72,3072]{2,1,0:T(8,128)(2,1)S(1)}, bf16[2,72,3072]{2,1,0:T(8,128)(2,1)}, u32[]{:S(2)}, u32[]{:S(2)}) collective-permute-start(bf16[2,72,3072]{2,1,0:T(8,128)(2,1)S(1)} %get-tuple-element.200.refs_2_), channel_id=1, source_target_pairs={{0,4},{2,6},{4,0},{6,2},{8,12},{10,14},{12,8},{14,10},{16,20},{18,... | collective-permute-start | bytes 2654216 | tf_op jit(solution)/shard_map/ppermute | solution.py:87
  360.0 60.5 %collective-permute-start.52 = (bf16[2,2,72,1536]{3,2,0,1:T(8,128)(2,1)}, bf16[2,2,72,1536]{3,2,0,1:T(8,128)(2,1)}, u32[]{:S(2)}, u32[]{:S(2)}) collective-permute-start(bf16[2,2,72,1536]{3,2,0,1:T(8,128)(2,1)} %copy.138), channel_id=1, source_target_pairs={{0,16},{2,18},{4,20},{6,22},{8,24},{10,26},{12,28},{14,30},{16,0},... | collective-permute-start | bytes 2654216 | tf_op jit(solution)/shard_map/ppermute | solution.py:87
  361.6 39.0 %collective-permute-start.49 = (bf16[2,72,3072]{2,1,0:T(8,128)(2,1)}, bf16[2,72,3072]{2,1,0:T(8,128)(2,1)}, u32[]{:S(2)}, u32[]{:S(2)}) collective-permute-start(bf16[2,72,3072]{2,1,0:T(8,128)(2,1)} %get-tuple-element.138.refs_1_), channel_id=1, source_target_pairs={{0,2},{2,0},{4,6},{6,4},{8,10},{10,8},{12,14},{14,12},{16,18},{18,... | collective-permute-start | bytes 2654216 | tf_op jit(solution)/shard_map/ppermute | solution.py:87
  377.4 34.8 %collective-permute-start.36 = (bf16[4,72,2368]{2,1,0:T(8,128)(2,1)}, bf16[4,72,2368]{2,1,0:T(8,128)(2,1)}, u32[]{:S(2)}, u32[]{:S(2)}) collective-permute-start(bf16[4,72,2368]{2,1,0:T(8,128)(2,1)} %get-tuple-element.74.refs_2_), channel_id=1, source_target_pairs={{0,2},{2,0},{4,6},{6,4},{8,10},{10,8},{12,14},{14,12},{16,18},{18,... | collective-permute-start | bytes 4091912 | tf_op jit(solution)/shard_map/ppermute | solution.py:87
  378.6 37.3 %collective-permute-start.35 = (bf16[4,72,2368]{2,1,0:T(8,128)(2,1)}, bf16[4,72,2368]{2,1,0:T(8,128)(2,1)}, u32[]{:S(2)}, u32[]{:S(2)}) collective-permute-start(bf16[4,72,2368]{2,1,0:T(8,128)(2,1)} %get-tuple-element.73.refs_1_), channel_id=1, source_target_pairs={{0,4},{2,6},{4,0},{6,2},{8,12},{10,14},{12,8},{14,10},{16,20},{18,... | collective-permute-start | bytes 4091912 | tf_op jit(solution)/shard_map/ppermute | solution.py:87
  382.1 42.9 %collective-permute-start.50 = (bf16[2,72,3072]{2,1,0:T(8,128)(2,1)}, bf16[2,72,3072]{2,1,0:T(8,128)(2,1)}, u32[]{:S(2)}, u32[]{:S(2)}) collective-permute-start(bf16[2,72,3072]{2,1,0:T(8,128)(2,1)} %add_convert_fusion.10.refs_3_), channel_id=1, source_target_pairs={{0,8},{2,10},{4,12},{6,14},{8,0},{10,2},{12,4},{14,6},{16,24},{18,... | collective-permute-start | bytes 2654216 | tf_op jit(solution)/shard_map/ppermute | solution.py:87
  415.0 44.2 %collective-permute-start.40 = (bf16[2,72,2368]{2,1,0:T(8,128)(2,1)}, bf16[2,72,2368]{2,1,0:T(8,128)(2,1)}, u32[]{:S(2)}, u32[]{:S(2)}) collective-permute-start(bf16[2,72,2368]{2,1,0:T(8,128)(2,1)} %slice_bitcast_fusion.6.refs_4_.refs_2_), channel_id=1, source_target_pairs={{0,4},{2,6},{4,0},{6,2},{8,12},{10,14},{12,8},{14,10},{16,20},{18,... | collective-permute-start | bytes 2045960 | tf_op jit(solution)/shard_map/ppermute | solution.py:87
  419.6 59.8 %collective-permute-start.39 = (bf16[2,72,2368]{2,1,0:T(8,128)(2,1)}, bf16[2,72,2368]{2,1,0:T(8,128)(2,1)}, u32[]{:S(2)}, u32[]{:S(2)}) collective-permute-start(bf16[2,72,2368]{2,1,0:T(8,128)(2,1)} %slice_bitcast_fusion.7.refs_3_.refs_1_), channel_id=1, source_target_pairs={{0,2},{2,0},{4,6},{6,4},{8,10},{10,8},{12,14},{14,12},{16,18},{18,... | collective-permute-start | bytes 2045960 | tf_op jit(solution)/shard_map/ppermute | solution.py:87
  423.9 25.2 %collective-permute-start.53 = (bf16[2,72,1536]{2,1,0:T(8,128)(2,1)}, bf16[2,72,1536]{2,1,0:T(8,128)(2,1)}, u32[]{:S(2)}, u32[]{:S(2)}) collective-permute-start(bf16[2,72,1536]{2,1,0:T(8,128)(2,1)} %slice_bitcast_fusion.8), channel_id=1, source_target_pairs={{0,2},{2,0},{4,6},{6,4},{8,10},{10,8},{12,14},{14,12},{16,18},{18,... | collective-permute-start | bytes 1327112 | tf_op jit(solution)/shard_map/ppermute | solution.py:87
  427.6 35.5 %collective-permute-start.51 = (bf16[72,3072]{1,0:T(8,128)(2,1)}, bf16[72,3072]{1,0:T(8,128)(2,1)}, u32[]{:S(2)}, u32[]{:S(2)}) collective-permute-start(bf16[72,3072]{1,0:T(8,128)(2,1)} %get-tuple-element.152), channel_id=1, source_target_pairs={{0,16},{2,18},{4,20},{6,22},{8,24},{10,26},{12,28},{14,30},{16,0},... | collective-permute-start | bytes 1327112 | tf_op jit(solution)/shard_map/ppermute | solution.py:87
  441.8 22.6 %collective-permute-start.37 = (bf16[512,1152]{1,0:T(8,128)(2,1)}, bf16[512,1152]{1,0:T(8,128)(2,1)}, u32[]{:S(2)}, u32[]{:S(2)}) collective-permute-start(bf16[512,1152]{1,0:T(8,128)(2,1)} %slice.533), channel_id=1, source_target_pairs={{0,1},{1,0},{2,3},{3,2},{4,5},{5,4},{6,7},{7,6},{8,9},{9,8},{10,11... | collective-permute-start | bytes 3538952 | tf_op jit(solution)/shard_map/ppermute | solution.py:95
  450.9 5.9 %collective-permute-start.54 = (bf16[72,1536]{1,0:T(8,128)(2,1)S(1)}, bf16[72,1536]{1,0:T(8,128)(2,1)S(1)}, u32[]{:S(2)}, u32[]{:S(2)}) collective-permute-start(bf16[72,1536]{1,0:T(8,128)(2,1)S(1)} %get-tuple-element.160), channel_id=1, source_target_pairs={{0,4},{2,6},{4,0},{6,2},{8,12},{10,14},{12,8},{14,10},{16,20},{18,... | collective-permute-start | bytes 663560 | tf_op jit(solution)/shard_map/ppermute | solution.py:87
  461.6 17.7 %collective-permute-start.41 = (bf16[2,72,2368]{2,1,0:T(8,128)(2,1)}, bf16[2,72,2368]{2,1,0:T(8,128)(2,1)}, u32[]{:S(2)}, u32[]{:S(2)}) collective-permute-start(bf16[2,72,2368]{2,1,0:T(8,128)(2,1)} %fusion.8.refs_1_), channel_id=1, source_target_pairs={{0,8},{2,10},{4,12},{6,14},{8,0},{10,2},{12,4},{14,6},{16,24},{18,... | collective-permute-start | bytes 2045960 | tf_op jit(solution)/shard_map/ppermute | solution.py:87
  467.2 1.7 collective-permute-start.43
  469.6 7.1 %collective-permute-start.44 = (bf16[1,1,1,1,8,3456]{5,4,3,2,1,0:T(8,128)(2,1)}, bf16[1,1,1,1,8,3456]{5,4,3,2,1,0:T(8,128)(2,1)S(1)}, u32[]{:S(2)}, u32[]{:S(2)}) collective-permute-start(bf16[1,1,1,1,8,3456]{5,4,3,2,1,0:T(8,128)(2,1)} %after.36), channel_id=1, source_target_pairs={{0,16},{2,18},{4,20},{6,22},{8,24},{10,26},{12,28},{14,30},{16,0},... | collective-permute-start | bytes 165896 | tf_op jit(solution)/shard_map/ppermute | solution.py:87
  476.7 5.3 collective-permute-start.45
  482.1 6.0 %collective-permute-start.46 = (bf16[2,2,1,1,8,3456]{5,4,3,2,1,0:T(8,128)(2,1)S(1)}, bf16[2,2,1,1,8,3456]{5,4,3,2,1,0:T(8,128)(2,1)S(1)}, u32[]{:S(2)}, u32[]{:S(2)}) collective-permute-start(bf16[2,2,1,1,8,3456]{5,4,3,2,1,0:T(8,128)(2,1)S(1)} %pad_maximum_fusion.16), channel_id=1, source_target_pairs={{0,2},{2,0},{4,6},{6,4},{8,10},{10,8},{12,14},{14,12},{16,18},{18,... | collective-permute-start | bytes 663560 | tf_op jit(solution)/shard_map/ppermute | solution.py:87
  483.3 17.0 %collective-permute-start.42 = (bf16[72,2368]{1,0:T(8,128)(2,1)S(1)}, bf16[72,2368]{1,0:T(8,128)(2,1)S(1)}, u32[]{:S(2)}, u32[]{:S(2)}) collective-permute-start(bf16[72,2368]{1,0:T(8,128)(2,1)S(1)} %slice_bitcast_fusion.14), channel_id=1, source_target_pairs={{0,16},{2,18},{4,20},{6,22},{8,24},{10,26},{12,28},{14,30},{16,0},... | collective-permute-start | bytes 1022984 | tf_op jit(solution)/shard_map/ppermute | solution.py:87
  488.2 14.9 %collective-permute-start.47 = (bf16[2,2,1,2,8,3456]{5,4,3,2,1,0:T(8,128)(2,1)S(1)}, bf16[2,2,1,2,8,3456]{5,4,3,2,1,0:T(8,128)(2,1)S(1)}, u32[]{:S(2)}, u32[]{:S(2)}) collective-permute-start(bf16[2,2,1,2,8,3456]{5,4,3,2,1,0:T(8,128)(2,1)S(1)} %pad_maximum_fusion.15), channel_id=1, source_target_pairs={{0,4},{2,6},{4,0},{6,2},{8,12},{10,14},{12,8},{14,10},{16,20},{18,... | collective-permute-start | bytes 1327112 | tf_op jit(solution)/shard_map/ppermute | solution.py:87
  504.1 1.8 collective-permute-start.48
  508.5 1.5 collective-permute-start.55
  510.5 3.7 collective-permute-start.56
  514.8 3.7 collective-permute-start.57
  519.1 3.7 collective-permute-start.58
  523.4 4.6 collective-permute-start.59
  531.0 7.0 %collective-permute-start.60 = (f32[72,576]{1,0:T(8,128)S(1)}, f32[72,576]{1,0:T(8,128)S(1)}, u32[]{:S(2)}, u32[]{:S(2)}) collective-permute-start(f32[72,576]{1,0:T(8,128)S(1)} %get-tuple-element.155), channel_id=1, source_target_pairs={{0,1},{1,0},{2,3},{3,2},{4,5},{5,4},{6,7},{7,6},{8,9},{9,8},{10,11... | collective-permute-start | bytes 497672 | tf_op jit(solution)/shard_map/ppermute | solution.py:95
  (194 other events, 1203.7 us)

commit v5 on v4

--- a/solution.py
+++ b/solution.py
@@ -817,7 +817,7 @@
         jnp.concatenate([mix_moved, mix_parts[0], mix_parts[2]], axis=1),
     )
     mix_shard = jnp.concatenate([mix_shard, proj_weight.astype(half)], axis=1)
-    codes = gather_small(codes, chips, first)
+    codes = gather_small(after(codes, mix_shard), chips, first)
     mix_first = after(spread(mix_shard, chips), codes)
     mix_first = doubled(mix_first, first[0], chips)
     nothing = jnp.minimum(jnp.abs(mix_first.reshape(-1)[0].astype(jnp.float32)), 0.0)
@@ -924,9 +924,9 @@
         proj_start + proj_cols,
         chips,
     )
-    down_grad = down_finish(down_half, near_mids, near_mids).T
     feed_half = feed_begin(feed_half, near_sent)
     near_half = near_begin(near_half)
+    down_grad = down_finish(down_half, near_half[-1:], near_half[-1:]).T
     feed_grad = feed_finish(feed_half, [*near_mids, near_half[-1]])
     feed_grad = jnp.stack([feed_grad[:, :hidden_cols], feed_grad[:, hidden_cols:]])
     near_grad = near_finish(near_half)
@@ -939,7 +939,7 @@
         jnp.concatenate([mix_parts[1], mix_moved, mix_parts[2]], axis=1),
     )
 
-    partial_value = against(after(hidden, *near_sent, *near_mids), far[:, 2 * hidden_cols :])
+    partial_value = against(after(hidden, *near_sent), far[:, 2 * hidden_cols :])
     result = partial_value[:count] + swap(partial_value[count:].astype(half)).astype(jnp.float32)
     block_output = (valid * (middle + gate_b * result)).astype(half)
     d_gate_b = grad_out * result
@@ -949,7 +949,7 @@
     pull_first = jax.vjp(modulate, inputs, shift_a, scale_a)[1]
     d_inputs, d_shift_a, d_scale_a = pull_first(first_grad)
     input_grad = d_inputs + d_middle
-    member_low = after(member.astype(half), *near_sent, *near_mids)
+    member_low = after(member.astype(half), *near_sent, *near_mids, near_half[-1])
     d_modulation = jnp.concatenate(
         [
             across(member_low, piece.astype(half))

time: 553 us -> 547 us (0.989)
    unnamed x394 -> x378, local copies, waits for them, and re-layouts: 26.2 us -> 22.5 us
  transfers between devices with their start and end apart: 61 -> 61, of which waited for: 26 -> 30; matrix products, arithmetic and copies ran while one was open for 33% -> 33% of each run, Pallas kernels for 22% -> 22%
where the time goes in v5:
time: 547 us; the launch traced here: 540 us
  waiting for transfers between devices  129 us (24%)
  Pallas kernels  120 us (22%)
  other arithmetic  119 us (22%)
  local copies, waits for them, and re-layouts  67.7 us (12%)
  starting transfers between devices  63.4 us (12%)
  matrix products  28.1 us (5%)
  between operations  11.9 us (2%)
    ppermute x44, waiting for transfers between devices, trade(): lax.ppermute(value, 'tok', [(place, place ^ 1 << bit) for place in range(...  127 us
    ppermute x44, starting transfers between devices, trade(): lax.ppermute(value, 'tok', [(place, place ^ 1 << bit) for place in range(...  58.8 us
    pallas_call x1, Pallas kernels, feed_both_ways(): pl.pallas_call(feed_kernel, grid=(steps,), in_specs=[fixed] * 4 + [weight...  30.4 us
    convert_element_type x12, other arithmetic, add(): return (one.astype(jnp.float32) + two.astype(jnp.float32)).astype(kept)  23.2 us
    unnamed x378, local copies, waits for them, and re-layouts  22.5 us
    dynamic_update_slice x12, local copies, waits for them, and re-layouts, put(): return lax.dynamic_update_slice(out, value, tuple(start))  20.7 us
    pallas_call x2, Pallas kernels, turned_parts(): pl.pallas_call(kernel, grid=(steps * len(rights),), in_specs=[pl.BlockSpe...  20.4 us
    pallas_call x2, Pallas kernels, attend_back(): pl.pallas_call(attend_back_kernel, grid=(heads,), in_specs=[block] * 4 +...  19.4 us
  transfers between devices with their start and end apart: 61, of which 30 were waited for; matrix products, arithmetic and copies ran while one was open for 33% of the time, Pallas kernels for 22%

profile of v5, /device:TPU:0, one launch (start us, length us, event | category | flops | bytes accessed | tf_op | source)
XLA Modules:
  0.0 539.7 jit_solution(10655075004134358429)
XLA Ops:
  6.6 2.5 collective-permute-start.2
  17.5 3.1 collective-permute-start.4
  27.2 3.0 collective-permute-start.6
  35.2 6.9 %collective-permute-done.6 = bf16[1,1,1,1,72,2304]{5,4,3,2,1,0:T(8,128)(2,1)} collective-permute-done((bf16[1,1,1,1,72,2304]{5,4,3,2,1,0:T(8,128)(2,1)}, bf16[1,1,1,1,72,2304]{5,4,3,2,1,0:T(8,128)(2,1)}, u32[]{:S(2)}, u32[]{:S(2)}) %collective-permute-start.6) | collective-permute-done | bytes 331808 | tf_op jit(solution)/shard_map/ppermute | solution.py:87
  56.6 4.4 collective-permute-done.9
  64.0 2.6 pad_maximum_fusion.9
  66.6 3.3 collective-permute-start.22
  74.4 10.1 %collective-permute-done.12 = bf16[2,1,1,1,72,2304]{5,4,3,2,1,0:T(8,128)(2,1)S(1)} collective-permute-done((bf16[2,1,1,1,72,2304]{5,4,3,2,1,0:T(8,128)(2,1)S(1)}, bf16[2,1,1,1,72,2304]{5,4,3,2,1,0:T(8,128)(2,1)S(1)}, u32[]{:S(2)}, u32[]{:S(2)}) %collective-permute-start.12) | collective-permute-done | bytes 663584 | tf_op jit(solution)/shard_map/ppermute | solution.py:87
  88.1 5.9 %maximum_maximum_fusion.1.refs_0_ = bf16[2,2,2,2,72,2304]{5,4,3,2,1,0:T(8,128)(2,1)} fusion(bf16[2,1,2,1,72,2304]{5,4,3,2,1,0:T(8,128)(2,1)} %copy-done.61, bf16[2,1,1,2,72,2304]{5,4,3,2,1,0:T(8,128)(2,1)} %constant_dynamic-update-slice_fusion.9.refs_1_), kind=kLoop, calls=%fused_computation.1 | loop fusion | flops 7962624 | bytes 7962624 | tf_op jit(solution)/shard_map/concatenate | solution.py:667
  96.3 3.4 collective-permute-done.13
  102.3 3.3 collective-permute-done.14
  106.3 3.5 pad_maximum_fusion.1
  110.7 5.8 %add_convert_fusion.6.refs_1_.x_ref = bf16[512,1152]{1,0:T(8,128)(2,1)} fusion(bf16[512,1152]{1,0:T(8,128)(2,1)S(1)} %copy-done.49, f32[1152]{0:T(1024)S(1)} %get-tuple-element.90, f32[1152]{0:T(1024)S(1)} %get-tuple-element.91, f32[1152]{0:T(1024)S(1)} %get-tuple-element.92, f32[1152]{0:T(1024)S(1)} %get-tuple-element.93, f32[1152]{0:T(1024)S(1)} %get-tuple-element.94, ...), kind=kLoop, calls=%fused_computation.38 | loop fusion | flops 9437184 | bytes 2402308 | tf_op jit(solution)/shard_map/convert_element_type | solution.py:864
  117.2 4.5 collective-permute-done.16
  121.7 2.5 constant_dynamic-update-slice_fusion.7
  124.2 2.5 constant_dynamic-update-slice_fusion.6
  126.7 6.2 %heads_of.2 = (f32[1728,512]{1,0:T(8,128)S(1)}, bf16[1152,512]{1,0:T(8,128)(2,1)}) custom-call(bf16[512,1152]{1,0:T(8,128)(2,1)S(1)} %copy-done.7, bf16[1152,2304]{1,0:T(8,128)(2,1)} %bitcast.161), custom_call_target="tpu_custom_call" | custom-call | flops 2300000000 | bytes 1000 | tf_op jit(solution)/shard_map/heads_of/pallas_call | solution.py:258
  133.4 7.8 %collective-permute-done.23 = bf16[2,1,1,1,72,4608]{5,4,3,2,1,0:T(8,128)(2,1)} collective-permute-done((bf16[2,1,1,1,72,4608]{5,4,3,2,1,0:T(8,128)(2,1)}, bf16[2,1,1,1,72,4608]{5,4,3,2,1,0:T(8,128)(2,1)}, u32[]{:S(2)}, u32[]{:S(2)}) %collective-permute-start.23) | collective-permute-done | bytes 1327136 | tf_op jit(solution)/shard_map/ppermute | solution.py:87
  141.2 2.5 constant_dynamic-update-slice_fusion.4.refs_0_
  147.2 5.9 %attend.2 = (bf16[8,72,512]{2,1,0:T(8,128)(2,1)S(1)}, f32[8,1,512]{2,1,0:T(1,128)S(1)}, bf16[8,72,512]{2,1,0:T(8,128)(2,1)S(1)}, bf16[8,72,512]{2,1,0:T(8,128)(2,1)S(1)}, bf16[8,72,512]{2,1,0:T(8,128)(2,1)S(1)}) custom-call(f32[3,8,72,512]{3,2,1,0:T(8,128)S(1)} %bitcast.143, f32[3,8,72,512]{3,2,1,0:T(8,128)S(1)} %bitcast.144, ...), custom_call_target="tpu_custom_call" | custom-call | flops 2760000000 | bytes 1000 | tf_op jit(solution)/shard_map/attend/pallas_call | solution.py:181
  156.7 19.2 %collective-permute-done.24 = bf16[2,1,1,1,72,4608]{5,4,3,2,1,0:T(8,128)(2,1)S(1)} collective-permute-done((bf16[2,1,1,1,72,4608]{5,4,3,2,1,0:T(8,128)(2,1)S(1)}, bf16[2,1,1,1,72,4608]{5,4,3,2,1,0:T(8,128)(2,1)S(1)}, u32[]{:S(2)}, u32[]{:S(2)}) %collective-permute-start.24) | collective-permute-done | bytes 1327136 | tf_op jit(solution)/shard_map/ppermute | solution.py:87
  178.7 6.7 %collective-permute-done.25 = bf16[2,1,1,1,72,4608]{5,4,3,2,1,0:T(8,128)(2,1)S(1)} collective-permute-done((bf16[2,1,1,1,72,4608]{5,4,3,2,1,0:T(8,128)(2,1)S(1)}, bf16[2,1,1,1,72,4608]{5,4,3,2,1,0:T(8,128)(2,1)S(1)}, u32[]{:S(2)}, u32[]{:S(2)}) %collective-permute-start.25) | collective-permute-done | bytes 1327136 | tf_op jit(solution)/shard_map/ppermute | solution.py:87
  186.1 7.4 %maximum_maximum_fusion = bf16[2,2,2,2,72,4608]{5,4,3,2,1,0:T(8,128)(2,1)} fusion(bf16[2,1,2,1,72,4608]{5,4,3,2,1,0:T(8,128)(2,1)S(1)} %constant_dynamic-update-slice_fusion.2, bf16[2,1,1,2,72,4608]{5,4,3,2,1,0:T(8,128)(2,1)} %constant_dynamic-update-slice_fusion.3), kind=kLoop, calls=%fused_computation | loop fusion | flops 15925248 | bytes 15925248 | tf_op jit(solution)/shard_map/concatenate | solution.py:667
  193.5 7.4 %heads_of.3 = (f32[1728,512]{1,0:T(8,128)}, bf16[1152,512]{1,0:T(8,128)(2,1)}) custom-call(bf16[512,1152]{1,0:T(8,128)(2,1)S(1)} %copy-done.8, bf16[1152,2304]{1,0:T(8,128)(2,1)} %bitcast.16.w_ref.w_two_ref, bf16[1152,512]{1,0:T(8,128)(2,1)} %collective-permute-done.19.refs_0_.refs_1_), custom_call_target="tpu_custom_call" | custom-call | flops 2300000000 | bytes 1000 | tf_op jit(solution)/shard_map/heads_of/pallas_call | solution.py:258
  202.9 6.1 %attend.3 = (bf16[8,72,512]{2,1,0:T(8,128)(2,1)S(1)}, f32[8,1,512]{2,1,0:T(1,128)S(1)}, bf16[8,72,512]{2,1,0:T(8,128)(2,1)S(1)}, bf16[8,72,512]{2,1,0:T(8,128)(2,1)S(1)}, bf16[8,72,512]{2,1,0:T(8,128)(2,1)S(1)}) custom-call(f32[3,8,72,512]{3,2,1,0:T(8,128)S(1)} %bitcast.146, f32[3,8,72,512]{3,2,1,0:T(8,128)S(1)} %bitcast.147, ...), custom_call_target="tpu_custom_call" | custom-call | flops 2760000000 | bytes 1000 | tf_op jit(solution)/shard_map/attend/pallas_call | solution.py:181
  210.7 3.0 broadcast_select_fusion.1
  213.9 6.8 %fusion.62 = (f32[512]{0:T(512)S(1)}, f32[512,1152]{1,0:T(8,128)S(1)}, bf16[512,1152]{1,0:T(8,128)(2,1)S(1)}, f32[512,1152]{1,0:T(8,128)}) fusion(f32[1152]{0:T(1024)S(1)} %copy-done.165, pred[512]{0:T(512)(128)(4,1)S(1)} %copy-done.130, f32[1152]{0:T(1024)S(1)} %copy-done.167, pred[512]{0:T(512)(128)(4,1)S(1)} %copy-done.135, f32[1152]{0:T(1024)S(1)} %copy-done.169, ...), kind=kOutput, calls=%fused_computation.288 | convolution fusion | flops 1374289408 | bytes 12134404 | tf_op jit(solution)/shard_map/dot_general | solution.py:141
  221.8 4.0 add_convert_fusion.5.x_one.one_ref
  226.4 13.8 %collective-permute-done.26 = bf16[2,1,1,2,72,4608]{5,4,3,2,1,0:T(8,128)(2,1)} collective-permute-done((bf16[2,1,1,2,72,4608]{5,4,3,2,1,0:T(8,128)(2,1)}, bf16[2,1,1,2,72,4608]{5,4,3,2,1,0:T(8,128)(2,1)}, u32[]{:S(2)}, u32[]{:S(2)}) %collective-permute-start.26) | collective-permute-done | bytes 2654240 | tf_op jit(solution)/shard_map/ppermute | solution.py:87
  240.2 3.4 constant_dynamic-update-slice_fusion.1
  243.6 3.5 constant_dynamic-update-slice_fusion
  248.5 30.4 %feed_both_ways.1 = (bf16[1024,1536]{1,0:T(8,128)(2,1)}, bf16[1024,1536]{1,0:T(8,128)(2,1)}, bf16[1024,1536]{1,0:T(8,128)(2,1)}, f32[512,1152]{1,0:T(8,128)}, bf16[512,1152]{1,0:T(8,128)(2,1)}) custom-call(bf16[512,1152]{1,0:T(8,128)(2,1)} %copy-done.20, bf16[512,1152]{1,0:T(8,128)(2,1)} %copy-done.25, bf16[512,1152]{1,0:T(8,128)(2,1)} %copy-done.23, ...), custom_call_target="tpu_custom_call" | custom-call | flops 10119999488 | bytes 1000 | tf_op jit(solution)/shard_map/feed_both_ways/pallas_call | solution.py:353
  281.2 7.6 %turned_parts.2 = (bf16[8,72,1536]{2,1,0:T(8,128)(2,1)S(1)}, bf16[8,72,1536]{2,1,0:T(8,128)(2,1)}) custom-call(s32[1]{0:T(128)} %bitcast.25.tok_ref, bf16[512,1152]{1,0:T(8,128)(2,1)S(1)} %copy-done.24, bf16[512,1152]{1,0:T(8,128)(2,1)S(1)} %copy-done.28, bf16[1024,1536]{1,0:T(8,128)(2,1)} %get-tuple-element.54.refs_0_, ...), custom_call_target="tpu_custom_call" | custom-call | flops 2760000000 | bytes 1000 | tf_op jit(solution)/shard_map/turned_parts/pallas_call | solution.py:420
  289.5 12.9 %turned_parts.3 = (bf16[4,72,3072]{2,1,0:T(8,128)(2,1)}, bf16[4,72,3072]{2,1,0:T(8,128)(2,1)S(1)}, bf16[4,72,3072]{2,1,0:T(8,128)(2,1)}, bf16[4,72,3072]{2,1,0:T(8,128)(2,1)}) custom-call(s32[1]{0:T(128)} %bitcast.25.tok_ref, bf16[512,1152]{1,0:T(8,128)(2,1)S(1)} %copy-done.21, bf16[512,1152]{1,0:T(8,128)(2,1)S(1)} %copy-done.26, ...), custom_call_target="tpu_custom_call" | custom-call | flops 5520000000 | bytes 1000 | tf_op jit(solution)/shard_map/turned_parts/pallas_call | solution.py:420
  304.6 2.6 multiply_reduce_fusion.1
  307.3 2.9 fusion.61
  310.4 2.2 multiply_convert_fusion.5
  316.4 9.5 %attend_back.2 = bf16[3,8,72,512]{3,2,1,0:T(8,128)(2,1)S(1)} custom-call(bf16[8,72,512]{2,1,0:T(8,128)(2,1)S(1)} %copy-done.36, bf16[8,72,512]{2,1,0:T(8,128)(2,1)S(1)} %copy-done.38, bf16[8,72,512]{2,1,0:T(8,128)(2,1)S(1)} %copy-done.40, bf16[8,72,512]{2,1,0:T(8,128)(2,1)S(1)} %get-tuple-element.145.g_ref, f32[8,1,512]{2,1,0:T(1,128)S(1)} %copy-done.44, ...), custom_call_target="tpu_custom_call" | custom-call | flops 4600000000 | bytes 1000 | tf_op jit(solution)/shard_map/attend_back/pallas_call | solution.py:222
  337.0 9.9 %attend_back.3 = bf16[3,8,72,512]{3,2,1,0:T(8,128)(2,1)S(1)} custom-call(bf16[8,72,512]{2,1,0:T(8,128)(2,1)S(1)} %copy-done.30, bf16[8,72,512]{2,1,0:T(8,128)(2,1)S(1)} %copy-done.32, bf16[8,72,512]{2,1,0:T(8,128)(2,1)S(1)} %copy-done.34, bf16[8,72,512]{2,1,0:T(8,128)(2,1)S(1)} %copy-done.13, f32[8,1,512]{2,1,0:T(1,128)S(1)} %copy-done.42, ...), custom_call_target="tpu_custom_call" | custom-call | flops 4600000000 | bytes 1000 | tf_op jit(solution)/shard_map/attend_back/pallas_call | solution.py:222
  349.6 2.1 add_convert_fusion
  351.8 2.1 add_convert_fusion.1
  360.3 15.1 %grad_parts.1 = (bf16[4,72,2368]{2,1,0:T(8,128)(2,1)}, bf16[4,72,2368]{2,1,0:T(8,128)(2,1)}, bf16[4,72,2368]{2,1,0:T(8,128)(2,1)}, bf16[4,72,2368]{2,1,0:T(8,128)(2,1)}) custom-call(s32[1]{0:T(128)} %bitcast.25.tok_ref, bf16[1152,512]{1,0:T(8,128)(2,1)} %get-tuple-element.51.refs_0_, bf16[1152,512]{1,0:T(8,128)(2,1)} %collective-permute-done.19.refs_0_.refs_1_, ...), custom_call_target="tpu_custom_call" | custom-call | flops 5980000256 | bytes 1000 | tf_op jit(solution)/shard_map/grad_parts/pallas_call | solution.py:495
  377.3 2.6 add_convert_fusion.10.refs_3_
  379.9 7.3 %fusion = f32[1024,1152]{1,0:T(8,128)S(1)} fusion(bf16[1024,1536]{1,0:T(8,128)(2,1)} %after.33, bf16[1152,4608]{1,0:T(8,128)(2,1)} %bitcast.167), kind=kOutput, calls=%fused_computation.3 | convolution fusion | flops 3623878656 | bytes 11403264 | tf_op jit(solution)/shard_map/dot_general | solution.py:60
  390.0 9.5 %back_through.1 = f32[512,1152]{1,0:T(8,128)S(1)} custom-call(bf16[1728,512]{1,0:T(8,128)(2,1)S(1)} %copy-done.4, bf16[1728,512]{1,0:T(8,128)(2,1)S(1)} %copy-done.6, bf16[1152,2304]{1,0:T(8,128)(2,1)} %bitcast.163, bf16[1152,2304]{1,0:T(8,128)(2,1)} %bitcast.16.w_ref.w_two_ref), custom_call_target="tpu_custom_call" | custom-call | flops 4140000000 | bytes 1000 | tf_op jit(solution)/shard_map/back_through/pallas_call | solution.py:291
  401.0 3.4 fusion.60
  406.0 2.6 add_convert_fusion.9.refs_0_
  408.7 7.0 %add_add_fusion.2 = (f32[512,1152]{1,0:T(8,128)}, bf16[512,1152]{1,0:T(8,128)(2,1)}) fusion(f32[512,1152]{1,0:T(8,128)} %get-tuple-element.126, f32[512]{0:T(512)S(1)} %negate_multiply_fusion, bf16[512,1152]{1,0:T(8,128)(2,1)} %param.27, f32[512]{0:T(512)S(1)} %copy-done.128, f32[512,1152]{1,0:T(8,128)} %copy-done.52, f32[512]{0:T(512)S(1)} %copy-done.161, ...), kind=kLoop, calls=%fused_computation.23 | loop fusion | flops 9437184 | bytes 15362048 | tf_op jit(solution)/shard_map/add | solution.py:951
  424.3 2.5 collective-permute-done.50
  431.5 5.0 collective-permute-done.40
  436.5 2.1 fusion.8.refs_5_.refs_1_
  451.5 2.7 convolution_convert_fusion.1
  458.9 3.6 collective-permute-done.44
  464.3 3.8 collective-permute-done.45
  476.9 2.5 collective-permute-done.54
  482.9 4.5 collective-permute-done.47
  489.6 7.7 %collective-permute-done.42 = bf16[72,2368]{1,0:T(8,128)(2,1)S(1)} collective-permute-done((bf16[72,2368]{1,0:T(8,128)(2,1)S(1)}, bf16[72,2368]{1,0:T(8,128)(2,1)S(1)}, u32[]{:S(2)}, u32[]{:S(2)}) %collective-permute-start.42) | collective-permute-done | bytes 341024 | tf_op jit(solution)/shard_map/ppermute | solution.py:87
  510.4 2.1 collective-permute-done.57
  514.4 2.3 collective-permute-done.58
  518.9 3.0 collective-permute-done.59
  524.7 3.8 multiply_subtract_fusion.1
  528.6 2.1 multiply_subtract_fusion
  533.5 2.1 concatenate.159
  535.6 2.8 multiply_subtract_fusion.2
  (633 shorter events, 174.6 us)
Async XLA Ops:
  2.0 13.7 %collective-permute-start = (bf16[72,576]{1,0:T(8,128)(2,1)S(1)}, bf16[72,576]{1,0:T(8,128)(2,1)S(1)}, u32[]{:S(2)}, u32[]{:S(2)}) collective-permute-start(bf16[72,576]{1,0:T(8,128)(2,1)S(1)} %get-tuple-element.161), channel_id=1, source_target_pairs={{0,1},{1,0},{2,3},{3,2},{4,5},{5,4},{6,7},{7,6},{8,9},{9,8},{10,11... | collective-permute-start | bytes 248840 | tf_op jit(solution)/shard_map/ppermute | solution.py:95
  3.2 2.7 collective-permute-start.1
  3.9 11.1 %collective-permute-start.7 = (f32[216]{0:T(256)S(1)}, f32[216]{0:T(256)S(1)}, u32[]{:S(2)}, u32[]{:S(2)}) collective-permute-start(f32[216]{0:T(256)S(1)} %convert_convert_fusion.1), channel_id=1, source_target_pairs={{0,1},{1,0},{2,3},{3,2},{4,5},{5,4},{6,7},{7,6},{8,9},{9,8},{10,11... | collective-permute-start | bytes 2600 | tf_op jit(solution)/shard_map/ppermute | solution.py:95
  6.6 4.0 collective-permute-start.2
  10.7 3.6 collective-permute-start.3
  17.5 5.0 collective-permute-start.4
  22.6 3.7 collective-permute-start.5
  27.2 14.9 %collective-permute-start.6 = (bf16[1,1,1,1,72,2304]{5,4,3,2,1,0:T(8,128)(2,1)}, bf16[1,1,1,1,72,2304]{5,4,3,2,1,0:T(8,128)(2,1)}, u32[]{:S(2)}, u32[]{:S(2)}) collective-permute-start(bf16[1,1,1,1,72,2304]{5,4,3,2,1,0:T(8,128)(2,1)} %after.23), channel_id=1, source_target_pairs={{0,16},{2,18},{4,20},{6,22},{8,24},{10,26},{12,28},{14,30},{16,0},... | collective-permute-start | bytes 995336 | tf_op jit(solution)/shard_map/ppermute | solution.py:87
  33.6 20.2 %collective-permute-start.8 = (bf16[2,2,2,1,8,3456]{5,4,3,2,1,0:T(8,128)(2,1)}, bf16[2,2,2,1,8,3456]{5,4,3,2,1,0:T(8,128)(2,1)}, u32[]{:S(2)}, u32[]{:S(2)}) collective-permute-start(bf16[2,2,2,1,8,3456]{5,4,3,2,1,0:T(8,128)(2,1)} %slice.534), channel_id=1, source_target_pairs={{0,2},{2,0},{4,6},{6,4},{8,10},{10,8},{12,14},{14,12},{16,18},{18,... | collective-permute-start | bytes 1327112 | tf_op jit(solution)/shard_map/ppermute | solution.py:87
  44.7 17.1 %collective-permute-start.10 = (bf16[2,1,1,1,72,2304]{5,4,3,2,1,0:T(8,128)(2,1)S(1)}, bf16[2,1,1,1,72,2304]{5,4,3,2,1,0:T(8,128)(2,1)}, u32[]{:S(2)}, u32[]{:S(2)}) collective-permute-start(bf16[2,1,1,1,72,2304]{5,4,3,2,1,0:T(8,128)(2,1)S(1)} %constant_dynamic-update-slice_fusion.11), channel_id=1, source_target_pairs={{0,8},{2,10},{4,12},{6,14},{8,0},{10,2},{12,4},{14,6},{16,24},{18,... | collective-permute-start | bytes 1990664 | tf_op jit(solution)/shard_map/ppermute | solution.py:87
  49.6 61.0 %copy-start.134 = (pred[512]{0:T(512)(128)(4,1)}, pred[512]{0:T(512)(128)(4,1)S(1)}, u32[]{:S(2)}) copy-start(pred[512]{0:T(512)(128)(4,1)S(1)} %get-tuple-element.185) | copy-start | bytes 1540
  49.6 61.0 %copy-start.139 = (pred[512]{0:T(512)(128)(4,1)}, pred[512]{0:T(512)(128)(4,1)S(1)}, u32[]{:S(2)}) copy-start(pred[512]{0:T(512)(128)(4,1)S(1)} %get-tuple-element.186) | copy-start | bytes 1540
  49.6 61.0 %copy-start.144 = (pred[512]{0:T(512)(128)(4,1)}, pred[512]{0:T(512)(128)(4,1)S(1)}, u32[]{:S(2)}) copy-start(pred[512]{0:T(512)(128)(4,1)S(1)} %get-tuple-element.187) | copy-start | bytes 1540
  55.0 6.0 %collective-permute-start.9 = (bf16[2,2,1,1,8,3456]{5,4,3,2,1,0:T(8,128)(2,1)S(1)}, bf16[2,2,1,1,8,3456]{5,4,3,2,1,0:T(8,128)(2,1)S(1)}, u32[]{:S(2)}, u32[]{:S(2)}) collective-permute-start(bf16[2,2,1,1,8,3456]{5,4,3,2,1,0:T(8,128)(2,1)S(1)} %slice.535), channel_id=1, source_target_pairs={{0,4},{2,6},{4,0},{6,2},{8,12},{10,14},{12,8},{14,10},{16,20},{18,... | collective-permute-start | bytes 663560 | tf_op jit(solution)/shard_map/ppermute | solution.py:87
  66.6 33.7 %collective-permute-start.22 = (bf16[1,1,1,1,72,4608]{5,4,3,2,1,0:T(8,128)(2,1)}, bf16[1,1,1,1,72,4608]{5,4,3,2,1,0:T(8,128)(2,1)}, u32[]{:S(2)}, u32[]{:S(2)}) collective-permute-start(bf16[1,1,1,1,72,4608]{5,4,3,2,1,0:T(8,128)(2,1)} %bitcast.174), channel_id=1, source_target_pairs={{0,16},{2,18},{4,20},{6,22},{8,24},{10,26},{12,28},{14,30},{16,0},... | collective-permute-start | bytes 1990664 | tf_op jit(solution)/shard_map/ppermute | solution.py:87
  70.1 14.4 %collective-permute-start.12 = (bf16[2,1,1,1,72,2304]{5,4,3,2,1,0:T(8,128)(2,1)S(1)}, bf16[2,1,1,1,72,2304]{5,4,3,2,1,0:T(8,128)(2,1)S(1)}, u32[]{:S(2)}, u32[]{:S(2)}) collective-permute-start(bf16[2,1,1,1,72,2304]{5,4,3,2,1,0:T(8,128)(2,1)S(1)} %get-tuple-element.141), channel_id=1, source_target_pairs={{0,4},{2,6},{4,0},{6,2},{8,12},{10,14},{12,8},{14,10},{16,20},{18,... | collective-permute-start | bytes 1990664 | tf_op jit(solution)/shard_map/ppermute | solution.py:87
  71.6 14.1 %collective-permute-start.11 = (bf16[2,1,1,1,72,2304]{5,4,3,2,1,0:T(8,128)(2,1)S(1)}, bf16[2,1,1,1,72,2304]{5,4,3,2,1,0:T(8,128)(2,1)S(1)}, u32[]{:S(2)}, u32[]{:S(2)}) collective-permute-start(bf16[2,1,1,1,72,2304]{5,4,3,2,1,0:T(8,128)(2,1)S(1)} %get-tuple-element.142), channel_id=1, source_target_pairs={{0,2},{2,0},{4,6},{6,4},{8,10},{10,8},{12,14},{14,12},{16,18},{18,... | collective-permute-start | bytes 1990664 | tf_op jit(solution)/shard_map/ppermute | solution.py:87
  87.5 12.1 %collective-permute-start.13 = (bf16[2,1,1,1,8,3456]{5,4,3,2,1,0:T(8,128)(2,1)S(1)}, bf16[2,1,1,1,8,3456]{5,4,3,2,1,0:T(8,128)(2,1)S(1)}, u32[]{:S(2)}, u32[]{:S(2)}) collective-permute-start(bf16[2,1,1,1,8,3456]{5,4,3,2,1,0:T(8,128)(2,1)S(1)} %slice.536), channel_id=1, source_target_pairs={{0,8},{2,10},{4,12},{6,14},{8,0},{10,2},{12,4},{14,6},{16,24},{18,... | collective-permute-start | bytes 331784 | tf_op jit(solution)/shard_map/ppermute | solution.py:87
  94.0 27.7 %collective-permute-start.16 = (bf16[2,1,1,2,72,2304]{5,4,3,2,1,0:T(8,128)(2,1)}, bf16[2,1,1,2,72,2304]{5,4,3,2,1,0:T(8,128)(2,1)}, u32[]{:S(2)}, u32[]{:S(2)}) collective-permute-start(bf16[2,1,1,2,72,2304]{5,4,3,2,1,0:T(8,128)(2,1)} %constant_dynamic-update-slice_fusion.9.refs_1_), channel_id=1, source_target_pairs={{0,4},{2,6},{4,0},{6,2},{8,12},{10,14},{12,8},{14,10},{16,20},{18,... | collective-permute-start | bytes 3981320 | tf_op jit(solution)/shard_map/ppermute | solution.py:87
  94.8 29.4 %collective-permute-start.17 = (bf16[2,1,2,1,72,2304]{5,4,3,2,1,0:T(8,128)(2,1)S(1)}, bf16[2,1,2,1,72,2304]{5,4,3,2,1,0:T(8,128)(2,1)}, u32[]{:S(2)}, u32[]{:S(2)}) collective-permute-start(bf16[2,1,2,1,72,2304]{5,4,3,2,1,0:T(8,128)(2,1)S(1)} %copy-done.62), channel_id=1, source_target_pairs={{0,2},{2,0},{4,6},{6,4},{8,10},{10,8},{12,14},{14,12},{16,18},{18,... | collective-permute-start | bytes 3981320 | tf_op jit(solution)/shard_map/ppermute | solution.py:87
  99.7 6.0 %collective-permute-start.14 = (bf16[1,1,1,1,8,3456]{5,4,3,2,1,0:T(8,128)(2,1)S(1)}, bf16[1,1,1,1,8,3456]{5,4,3,2,1,0:T(8,128)(2,1)S(1)}, u32[]{:S(2)}, u32[]{:S(2)}) collective-permute-start(bf16[1,1,1,1,8,3456]{5,4,3,2,1,0:T(8,128)(2,1)S(1)} %slice.537), channel_id=1, source_target_pairs={{0,16},{2,18},{4,20},{6,22},{8,24},{10,26},{12,28},{14,30},{16,0},... | collective-permute-start | bytes 165896 | tf_op jit(solution)/shard_map/ppermute | solution.py:87
  105.7 4.1 collective-permute-start.15
  109.8 31.4 %collective-permute-start.23 = (bf16[2,1,1,1,72,4608]{5,4,3,2,1,0:T(8,128)(2,1)}, bf16[2,1,1,1,72,4608]{5,4,3,2,1,0:T(8,128)(2,1)}, u32[]{:S(2)}, u32[]{:S(2)}) collective-permute-start(bf16[2,1,1,1,72,4608]{5,4,3,2,1,0:T(8,128)(2,1)} %after.27), channel_id=1, source_target_pairs={{0,8},{2,10},{4,12},{6,14},{8,0},{10,2},{12,4},{14,6},{16,24},{18,... | collective-permute-start | bytes 3981320 | tf_op jit(solution)/shard_map/ppermute | solution.py:87
  126.7 66.8 %collective-permute-start.18 = (bf16[2,2,2,2,72,2304]{5,4,3,2,1,0:T(8,128)(2,1)}, bf16[2,2,2,2,72,2304]{5,4,3,2,1,0:T(8,128)(2,1)}, u32[]{:S(2)}, u32[]{:S(2)}) collective-permute-start(bf16[2,2,2,2,72,2304]{5,4,3,2,1,0:T(8,128)(2,1)} %constant_dynamic-update-slice_fusion.6), channel_id=1, source_target_pairs={{0,1},{1,0},{2,3},{3,2},{4,5},{5,4},{6,7},{7,6},{8,9},{9,8},{10,11... | collective-permute-start | bytes 15925256 | tf_op jit(solution)/shard_map/ppermute | solution.py:95
  132.9 60.5 %collective-permute-start.19 = (bf16[1152,512]{1,0:T(8,128)(2,1)}, bf16[1152,512]{1,0:T(8,128)(2,1)}, u32[]{:S(2)}, u32[]{:S(2)}) collective-permute-start(bf16[1152,512]{1,0:T(8,128)(2,1)} %get-tuple-element.51.refs_0_), channel_id=1, source_target_pairs={{0,1},{1,0},{2,3},{3,2},{4,5},{5,4},{6,7},{7,6},{8,9},{9,8},{10,11... | collective-permute-start | bytes 3538952 | tf_op jit(solution)/shard_map/ppermute | solution.py:95
  145.7 30.3 %collective-permute-start.24 = (bf16[2,1,1,1,72,4608]{5,4,3,2,1,0:T(8,128)(2,1)S(1)}, bf16[2,1,1,1,72,4608]{5,4,3,2,1,0:T(8,128)(2,1)S(1)}, u32[]{:S(2)}, u32[]{:S(2)}) collective-permute-start(bf16[2,1,1,1,72,4608]{5,4,3,2,1,0:T(8,128)(2,1)S(1)} %get-tuple-element.133), channel_id=1, source_target_pairs={{0,2},{2,0},{4,6},{6,4},{8,10},{10,8},{12,14},{14,12},{16,18},{18,... | collective-permute-start | bytes 3981320 | tf_op jit(solution)/shard_map/ppermute | solution.py:87
  153.2 32.1 %collective-permute-start.25 = (bf16[2,1,1,1,72,4608]{5,4,3,2,1,0:T(8,128)(2,1)S(1)}, bf16[2,1,1,1,72,4608]{5,4,3,2,1,0:T(8,128)(2,1)S(1)}, u32[]{:S(2)}, u32[]{:S(2)}) collective-permute-start(bf16[2,1,1,1,72,4608]{5,4,3,2,1,0:T(8,128)(2,1)S(1)} %get-tuple-element.134), channel_id=1, source_target_pairs={{0,4},{2,6},{4,0},{6,2},{8,12},{10,14},{12,8},{14,10},{16,20},{18,... | collective-permute-start | bytes 3981320 | tf_op jit(solution)/shard_map/ppermute | solution.py:87
  177.1 63.0 %collective-permute-start.26 = (bf16[2,1,1,2,72,4608]{5,4,3,2,1,0:T(8,128)(2,1)}, bf16[2,1,1,2,72,4608]{5,4,3,2,1,0:T(8,128)(2,1)}, u32[]{:S(2)}, u32[]{:S(2)}) collective-permute-start(bf16[2,1,1,2,72,4608]{5,4,3,2,1,0:T(8,128)(2,1)} %constant_dynamic-update-slice_fusion.3), channel_id=1, source_target_pairs={{0,4},{2,6},{4,0},{6,2},{8,12},{10,14},{12,8},{14,10},{16,20},{18,... | collective-permute-start | bytes 7962632 | tf_op jit(solution)/shard_map/ppermute | solution.py:87
  185.5 58.1 %collective-permute-start.27 = (bf16[2,1,2,1,72,4608]{5,4,3,2,1,0:T(8,128)(2,1)S(1)}, bf16[2,1,2,1,72,4608]{5,4,3,2,1,0:T(8,128)(2,1)}, u32[]{:S(2)}, u32[]{:S(2)}) collective-permute-start(bf16[2,1,2,1,72,4608]{5,4,3,2,1,0:T(8,128)(2,1)S(1)} %constant_dynamic-update-slice_fusion.2), channel_id=1, source_target_pairs={{0,2},{2,0},{4,6},{6,4},{8,10},{10,8},{12,14},{14,12},{16,18},{18,... | collective-permute-start | bytes 7962632 | tf_op jit(solution)/shard_map/ppermute | solution.py:87
  225.8 21.3 %collective-permute-start.20 = (bf16[512,1152]{1,0:T(8,128)(2,1)S(1)}, bf16[512,1152]{1,0:T(8,128)(2,1)S(1)}, u32[]{:S(2)}, u32[]{:S(2)}) collective-permute-start(bf16[512,1152]{1,0:T(8,128)(2,1)S(1)} %add_convert_fusion.5.x_one.one_ref), channel_id=1, source_target_pairs={{0,1},{1,0},{2,3},{3,2},{4,5},{5,4},{6,7},{7,6},{8,9},{9,8},{10,11... | collective-permute-start | bytes 3538952 | tf_op jit(solution)/shard_map/ppermute | solution.py:95
  225.9 21.2 %collective-permute-start.21 = (bf16[512,1152]{1,0:T(8,128)(2,1)S(1)}, bf16[512,1152]{1,0:T(8,128)(2,1)S(1)}, u32[]{:S(2)}, u32[]{:S(2)}) collective-permute-start(bf16[512,1152]{1,0:T(8,128)(2,1)S(1)} %get-tuple-element.182.r_one.one_ref), channel_id=1, source_target_pairs={{0,1},{1,0},{2,3},{3,2},{4,5},{5,4},{6,7},{7,6},{8,9},{9,8},{10,11... | collective-permute-start | bytes 3538952 | tf_op jit(solution)/shard_map/ppermute | solution.py:95
  247.1 32.4 %collective-permute-start.28 = (bf16[1152,512]{1,0:T(8,128)(2,1)}, bf16[1152,512]{1,0:T(8,128)(2,1)S(1)}, u32[]{:S(2)}, u32[]{:S(2)}) collective-permute-start(bf16[1152,512]{1,0:T(8,128)(2,1)} %bitcast.18.refs_2_), channel_id=1, source_target_pairs={{0,1},{1,0},{2,3},{3,2},{4,5},{5,4},{6,7},{7,6},{8,9},{9,8},{10,11... | collective-permute-start | bytes 3538952 | tf_op jit(solution)/shard_map/ppermute | solution.py:95
  278.9 25.6 %collective-permute-start.29 = (bf16[512,1152]{1,0:T(8,128)(2,1)}, bf16[512,1152]{1,0:T(8,128)(2,1)}, u32[]{:S(2)}, u32[]{:S(2)}) collective-permute-start(bf16[512,1152]{1,0:T(8,128)(2,1)} %get-tuple-element.59), channel_id=1, source_target_pairs={{0,1},{1,0},{2,3},{3,2},{4,5},{5,4},{6,7},{7,6},{8,9},{9,8},{10,11... | collective-permute-start | bytes 3538952 | tf_op jit(solution)/shard_map/ppermute | solution.py:95
  288.8 40.7 %collective-permute-start.30 = (bf16[8,72,1536]{2,1,0:T(8,128)(2,1)S(1)}, bf16[8,72,1536]{2,1,0:T(8,128)(2,1)}, u32[]{:S(2)}, u32[]{:S(2)}) collective-permute-start(bf16[8,72,1536]{2,1,0:T(8,128)(2,1)S(1)} %get-tuple-element.65), channel_id=1, source_target_pairs={{0,8},{2,10},{4,12},{6,14},{8,0},{10,2},{12,4},{14,6},{16,24},{18,... | collective-permute-start | bytes 5308424 | tf_op jit(solution)/shard_map/ppermute | solution.py:87
  302.4 45.8 %collective-permute-start.33 = (bf16[4,72,3072]{2,1,0:T(8,128)(2,1)}, bf16[4,72,3072]{2,1,0:T(8,128)(2,1)}, u32[]{:S(2)}, u32[]{:S(2)}) collective-permute-start(bf16[4,72,3072]{2,1,0:T(8,128)(2,1)} %get-tuple-element.72), channel_id=1, source_target_pairs={{0,2},{2,0},{4,6},{6,4},{8,10},{10,8},{12,14},{14,12},{16,18},{18,... | collective-permute-start | bytes 5308424 | tf_op jit(solution)/shard_map/ppermute | solution.py:87
  302.9 48.9 %collective-permute-start.32 = (bf16[4,72,3072]{2,1,0:T(8,128)(2,1)}, bf16[4,72,3072]{2,1,0:T(8,128)(2,1)}, u32[]{:S(2)}, u32[]{:S(2)}) collective-permute-start(bf16[4,72,3072]{2,1,0:T(8,128)(2,1)} %get-tuple-element.70), channel_id=1, source_target_pairs={{0,4},{2,6},{4,0},{6,2},{8,12},{10,14},{12,8},{14,10},{16,20},{18,... | collective-permute-start | bytes 5308424 | tf_op jit(solution)/shard_map/ppermute | solution.py:87
  327.3 33.0 %collective-permute-start.31 = (bf16[1728,512]{1,0:T(8,128)(2,1)S(1)}, bf16[1728,512]{1,0:T(8,128)(2,1)}, u32[]{:S(2)}, u32[]{:S(2)}) collective-permute-start(bf16[1728,512]{1,0:T(8,128)(2,1)S(1)} %bitcast.153), channel_id=1, source_target_pairs={{0,1},{1,0},{2,3},{3,2},{4,5},{5,4},{6,7},{7,6},{8,9},{9,8},{10,11... | collective-permute-start | bytes 5308424 | tf_op jit(solution)/shard_map/ppermute | solution.py:95
  327.3 33.0 %collective-permute-start.34 = (bf16[2,2,2,2,32,576]{5,4,3,2,1,0:T(8,128)(2,1)}, bf16[2,2,2,2,32,576]{5,4,3,2,1,0:T(8,128)(2,1)}, u32[]{:S(2)}, u32[]{:S(2)}) collective-permute-start(bf16[2,2,2,2,32,576]{5,4,3,2,1,0:T(8,128)(2,1)} %bitcast.34), channel_id=1, source_target_pairs={{0,1},{1,0},{2,3},{3,2},{4,5},{5,4},{6,7},{7,6},{8,9},{9,8},{10,11... | collective-permute-start | bytes 1769480 | tf_op jit(solution)/shard_map/ppermute | solution.py:95
  355.5 21.8 %collective-permute-start.36 = (bf16[2,72,3072]{2,1,0:T(8,128)(2,1)S(1)}, bf16[2,72,3072]{2,1,0:T(8,128)(2,1)}, u32[]{:S(2)}, u32[]{:S(2)}) collective-permute-start(bf16[2,72,3072]{2,1,0:T(8,128)(2,1)S(1)} %get-tuple-element.200.refs_2_), channel_id=1, source_target_pairs={{0,4},{2,6},{4,0},{6,2},{8,12},{10,14},{12,8},{14,10},{16,20},{18,... | collective-permute-start | bytes 2654216 | tf_op jit(solution)/shard_map/ppermute | solution.py:87
  358.9 82.6 %collective-permute-start.52 = (bf16[2,2,72,1536]{3,2,0,1:T(8,128)(2,1)}, bf16[2,2,72,1536]{3,2,0,1:T(8,128)(2,1)}, u32[]{:S(2)}, u32[]{:S(2)}) collective-permute-start(bf16[2,2,72,1536]{3,2,0,1:T(8,128)(2,1)} %copy.148), channel_id=1, source_target_pairs={{0,16},{2,18},{4,20},{6,22},{8,24},{10,26},{12,28},{14,30},{16,0},... | collective-permute-start | bytes 2654216 | tf_op jit(solution)/shard_map/ppermute | solution.py:87
  359.7 44.8 %collective-permute-start.49 = (bf16[2,72,3072]{2,1,0:T(8,128)(2,1)}, bf16[2,72,3072]{2,1,0:T(8,128)(2,1)}, u32[]{:S(2)}, u32[]{:S(2)}) collective-permute-start(bf16[2,72,3072]{2,1,0:T(8,128)(2,1)} %get-tuple-element.138.refs_1_), channel_id=1, source_target_pairs={{0,2},{2,0},{4,6},{6,4},{8,10},{10,8},{12,14},{14,12},{16,18},{18,... | collective-permute-start | bytes 2654216 | tf_op jit(solution)/shard_map/ppermute | solution.py:87
  375.4 40.3 %collective-permute-start.39 = (bf16[4,72,2368]{2,1,0:T(8,128)(2,1)}, bf16[4,72,2368]{2,1,0:T(8,128)(2,1)}, u32[]{:S(2)}, u32[]{:S(2)}) collective-permute-start(bf16[4,72,2368]{2,1,0:T(8,128)(2,1)} %get-tuple-element.74.refs_2_), channel_id=1, source_target_pairs={{0,2},{2,0},{4,6},{6,4},{8,10},{10,8},{12,14},{14,12},{16,18},{18,... | collective-permute-start | bytes 4091912 | tf_op jit(solution)/shard_map/ppermute | solution.py:87
  376.9 43.2 %collective-permute-start.37 = (bf16[4,72,2368]{2,1,0:T(8,128)(2,1)}, bf16[4,72,2368]{2,1,0:T(8,128)(2,1)}, u32[]{:S(2)}, u32[]{:S(2)}) collective-permute-start(bf16[4,72,2368]{2,1,0:T(8,128)(2,1)} %get-tuple-element.73.refs_1_), channel_id=1, source_target_pairs={{0,4},{2,6},{4,0},{6,2},{8,12},{10,14},{12,8},{14,10},{16,20},{18,... | collective-permute-start | bytes 4091912 | tf_op jit(solution)/shard_map/ppermute | solution.py:87
  389.8 18.7 %collective-permute-start.35 = (bf16[512,1152]{1,0:T(8,128)(2,1)}, bf16[512,1152]{1,0:T(8,128)(2,1)}, u32[]{:S(2)}, u32[]{:S(2)}) collective-permute-start(bf16[512,1152]{1,0:T(8,128)(2,1)} %slice.533), channel_id=1, source_target_pairs={{0,1},{1,0},{2,3},{3,2},{4,5},{5,4},{6,7},{7,6},{8,9},{9,8},{10,11... | collective-permute-start | bytes 3538952 | tf_op jit(solution)/shard_map/ppermute | solution.py:95
  404.5 22.3 %collective-permute-start.50 = (bf16[2,72,3072]{2,1,0:T(8,128)(2,1)}, bf16[2,72,3072]{2,1,0:T(8,128)(2,1)}, u32[]{:S(2)}, u32[]{:S(2)}) collective-permute-start(bf16[2,72,3072]{2,1,0:T(8,128)(2,1)} %add_convert_fusion.10.refs_3_), channel_id=1, source_target_pairs={{0,8},{2,10},{4,12},{6,14},{8,0},{10,2},{12,4},{14,6},{16,24},{18,... | collective-permute-start | bytes 2654216 | tf_op jit(solution)/shard_map/ppermute | solution.py:87
  418.5 18.0 %collective-permute-start.40 = (bf16[2,72,2368]{2,1,0:T(8,128)(2,1)}, bf16[2,72,2368]{2,1,0:T(8,128)(2,1)}, u32[]{:S(2)}, u32[]{:S(2)}) collective-permute-start(bf16[2,72,2368]{2,1,0:T(8,128)(2,1)} %slice_bitcast_fusion.4.refs_4_.refs_2_), channel_id=1, source_target_pairs={{0,4},{2,6},{4,0},{6,2},{8,12},{10,14},{12,8},{14,10},{16,20},{18,... | collective-permute-start | bytes 2045960 | tf_op jit(solution)/shard_map/ppermute | solution.py:87
  423.8 57.4 %collective-permute-start.38 = (bf16[2,72,2368]{2,1,0:T(8,128)(2,1)}, bf16[2,72,2368]{2,1,0:T(8,128)(2,1)}, u32[]{:S(2)}, u32[]{:S(2)}) collective-permute-start(bf16[2,72,2368]{2,1,0:T(8,128)(2,1)} %slice_bitcast_fusion.6.refs_3_.refs_1_), channel_id=1, source_target_pairs={{0,2},{2,0},{4,6},{6,4},{8,10},{10,8},{12,14},{14,12},{16,18},{18,... | collective-permute-start | bytes 2045960 | tf_op jit(solution)/shard_map/ppermute | solution.py:87
  429.5 28.2 %collective-permute-start.51 = (bf16[72,3072]{1,0:T(8,128)(2,1)}, bf16[72,3072]{1,0:T(8,128)(2,1)}, u32[]{:S(2)}, u32[]{:S(2)}) collective-permute-start(bf16[72,3072]{1,0:T(8,128)(2,1)} %get-tuple-element.152), channel_id=1, source_target_pairs={{0,16},{2,18},{4,20},{6,22},{8,24},{10,26},{12,28},{14,30},{16,0},... | collective-permute-start | bytes 1327112 | tf_op jit(solution)/shard_map/ppermute | solution.py:87
  438.6 42.6 %collective-permute-start.41 = (bf16[2,72,2368]{2,1,0:T(8,128)(2,1)}, bf16[2,72,2368]{2,1,0:T(8,128)(2,1)}, u32[]{:S(2)}, u32[]{:S(2)}) collective-permute-start(bf16[2,72,2368]{2,1,0:T(8,128)(2,1)} %fusion.8.refs_5_.refs_1_), channel_id=1, source_target_pairs={{0,8},{2,10},{4,12},{6,14},{8,0},{10,2},{12,4},{14,6},{16,24},{18,... | collective-permute-start | bytes 2045960 | tf_op jit(solution)/shard_map/ppermute | solution.py:87
  444.7 25.1 %collective-permute-start.53 = (bf16[2,72,1536]{2,1,0:T(8,128)(2,1)}, bf16[2,72,1536]{2,1,0:T(8,128)(2,1)}, u32[]{:S(2)}, u32[]{:S(2)}) collective-permute-start(bf16[2,72,1536]{2,1,0:T(8,128)(2,1)} %slice_bitcast_fusion.8), channel_id=1, source_target_pairs={{0,2},{2,0},{4,6},{6,4},{8,10},{10,8},{12,14},{14,12},{16,18},{18,... | collective-permute-start | bytes 1327112 | tf_op jit(solution)/shard_map/ppermute | solution.py:87
  454.2 1.3 collective-permute-start.43
  456.2 6.3 %collective-permute-start.44 = (bf16[1,1,1,1,8,3456]{5,4,3,2,1,0:T(8,128)(2,1)}, bf16[1,1,1,1,8,3456]{5,4,3,2,1,0:T(8,128)(2,1)S(1)}, u32[]{:S(2)}, u32[]{:S(2)}) collective-permute-start(bf16[1,1,1,1,8,3456]{5,4,3,2,1,0:T(8,128)(2,1)} %after.38), channel_id=1, source_target_pairs={{0,16},{2,18},{4,20},{6,22},{8,24},{10,26},{12,28},{14,30},{16,0},... | collective-permute-start | bytes 165896 | tf_op jit(solution)/shard_map/ppermute | solution.py:87
  463.3 4.8 collective-permute-start.45
  468.2 6.1 %collective-permute-start.46 = (bf16[2,2,1,1,8,3456]{5,4,3,2,1,0:T(8,128)(2,1)S(1)}, bf16[2,2,1,1,8,3456]{5,4,3,2,1,0:T(8,128)(2,1)S(1)}, u32[]{:S(2)}, u32[]{:S(2)}) collective-permute-start(bf16[2,2,1,1,8,3456]{5,4,3,2,1,0:T(8,128)(2,1)S(1)} %pad_maximum_fusion.17), channel_id=1, source_target_pairs={{0,2},{2,0},{4,6},{6,4},{8,10},{10,8},{12,14},{14,12},{16,18},{18,... | collective-permute-start | bytes 663560 | tf_op jit(solution)/shard_map/ppermute | solution.py:87
  471.8 7.7 %collective-permute-start.54 = (bf16[72,1536]{1,0:T(8,128)(2,1)}, bf16[72,1536]{1,0:T(8,128)(2,1)S(1)}, u32[]{:S(2)}, u32[]{:S(2)}) collective-permute-start(bf16[72,1536]{1,0:T(8,128)(2,1)} %get-tuple-element.160), channel_id=1, source_target_pairs={{0,4},{2,6},{4,0},{6,2},{8,12},{10,14},{12,8},{14,10},{16,20},{18,... | collective-permute-start | bytes 663560 | tf_op jit(solution)/shard_map/ppermute | solution.py:87
  475.8 11.6 %collective-permute-start.47 = (bf16[2,2,1,2,8,3456]{5,4,3,2,1,0:T(8,128)(2,1)}, bf16[2,2,1,2,8,3456]{5,4,3,2,1,0:T(8,128)(2,1)S(1)}, u32[]{:S(2)}, u32[]{:S(2)}) collective-permute-start(bf16[2,2,1,2,8,3456]{5,4,3,2,1,0:T(8,128)(2,1)} %pad_maximum_fusion.15), channel_id=1, source_target_pairs={{0,4},{2,6},{4,0},{6,2},{8,12},{10,14},{12,8},{14,10},{16,20},{18,... | collective-permute-start | bytes 1327112 | tf_op jit(solution)/shard_map/ppermute | solution.py:87
  482.8 14.4 %collective-permute-start.42 = (bf16[72,2368]{1,0:T(8,128)(2,1)S(1)}, bf16[72,2368]{1,0:T(8,128)(2,1)S(1)}, u32[]{:S(2)}, u32[]{:S(2)}) collective-permute-start(bf16[72,2368]{1,0:T(8,128)(2,1)S(1)} %slice_bitcast_fusion.14), channel_id=1, source_target_pairs={{0,16},{2,18},{4,20},{6,22},{8,24},{10,26},{12,28},{14,30},{16,0},... | collective-permute-start | bytes 1022984 | tf_op jit(solution)/shard_map/ppermute | solution.py:87
  487.6 1.2 collective-permute-start.48
  502.6 1.3 collective-permute-start.55
  504.5 3.7 collective-permute-start.56
  508.8 3.7 collective-permute-start.57
  513.1 3.7 collective-permute-start.58
  517.4 4.6 collective-permute-start.59
  524.6 8.1 %collective-permute-start.60 = (f32[72,576]{1,0:T(8,128)S(1)}, f32[72,576]{1,0:T(8,128)S(1)}, u32[]{:S(2)}, u32[]{:S(2)}) collective-permute-start(f32[72,576]{1,0:T(8,128)S(1)} %get-tuple-element.155), channel_id=1, source_target_pairs={{0,1},{1,0},{2,3},{3,2},{4,5},{5,4},{6,7},{7,6},{8,9},{9,8},{10,11... | collective-permute-start | bytes 497672 | tf_op jit(solution)/shard_map/ppermute | solution.py:95
  (186 other events, 1131.6 us)

commit v6 on v5

--- a/solution.py
+++ b/solution.py
@@ -119,6 +119,7 @@
 
 
 SCORE_SCALE = HEAD ** (-0.5)
+PAIR = 2
 FEED_BLOCK = 512
 FEED_ROWS = 512
 TURN_BLOCK = 768
@@ -151,18 +152,19 @@
     out_ref, log_ref, q_out, k_out, v_out,
 ):
     cosine, up, down = cos_ref[...], up_ref[...], down_ref[...]
-    query = turn(q_ref[0, 0], cosine, up, down).astype(jnp.bfloat16)
-    key = turn(k_ref[0, 0], cosine, up, down).astype(jnp.bfloat16)
-    value = v_ref[0, 0].astype(jnp.bfloat16)
-    q_out[0], k_out[0], v_out[0] = query, key, value
-    scores = dots(key, query, 0, 0) * SCORE_SCALE
-    scores = jnp.where(col_ref[...] == row_ref[...], scores, MASKED)
-    top = jnp.max(scores, axis=0, keepdims=True)
-    weights = jnp.exp(scores - top)
-    total = jnp.sum(weights, axis=0, keepdims=True)
-    mixed = dots(value, weights.astype(jnp.bfloat16), 1, 0)
-    out_ref[0] = (mixed * (1.0 / total)).astype(jnp.bfloat16)
-    log_ref[0] = top + jnp.log(total)
+    for head in range(PAIR):
+        query = turn(q_ref[0, head], cosine, up, down).astype(jnp.bfloat16)
+        key = turn(k_ref[0, head], cosine, up, down).astype(jnp.bfloat16)
+        value = v_ref[0, head].astype(jnp.bfloat16)
+        q_out[head], k_out[head], v_out[head] = query, key, value
+        scores = dots(key, query, 0, 0) * SCORE_SCALE
+        scores = jnp.where(col_ref[...] == row_ref[...], scores, MASKED)
+        top = jnp.max(scores, axis=0, keepdims=True)
+        weights = jnp.exp(scores - top)
+        total = jnp.sum(weights, axis=0, keepdims=True)
+        mixed = dots(value, weights.astype(jnp.bfloat16), 1, 0)
+        out_ref[head] = (mixed * (1.0 / total)).astype(jnp.bfloat16)
+        log_ref[head] = top + jnp.log(total)
 
 
 def whole(value):
@@ -173,14 +175,14 @@
     _, heads, _, tokens = mixed.shape
 
     def part(place):
-        return pl.BlockSpec((1, 1, HEAD, tokens), lambda i: (place, i, 0, 0))
-
-    block = pl.BlockSpec((1, HEAD, tokens), lambda i: (i, 0, 0))
-    line = pl.BlockSpec((1, 1, tokens), lambda i: (i, 0, 0))
+        return pl.BlockSpec((1, PAIR, HEAD, tokens), lambda i: (place, i, 0, 0))
+
+    block = pl.BlockSpec((PAIR, HEAD, tokens), lambda i: (i, 0, 0))
+    line = pl.BlockSpec((PAIR, 1, tokens), lambda i: (i, 0, 0))
     shape = jax.ShapeDtypeStruct((heads, HEAD, tokens), jnp.bfloat16)
     return pl.pallas_call(
         attend_kernel,
-        grid=(heads,),
+        grid=(heads // PAIR,),
         in_specs=[part(0), part(1), part(2)] + [whole(value) for value in tables],
         out_specs=[block, line, block, block, block],
         out_shape=[
@@ -199,31 +201,32 @@
 def attend_back_kernel(
     q_ref, k_ref, v_ref, g_ref, log_ref, cos_ref, up_ref, down_ref, row_ref, col_ref, out_ref
 ):
-    query, key, value, grad = q_ref[0], k_ref[0], v_ref[0], g_ref[0]
-    scores = dots(key, query, 0, 0) * SCORE_SCALE
-    scores = jnp.where(col_ref[...] == row_ref[...], scores, MASKED)
-    probs = jnp.exp(scores - log_ref[0])
-    d_probs = dots(value, grad, 0, 0)
-    inner = jnp.sum(probs * d_probs, axis=0, keepdims=True)
-    d_scores = (probs * (d_probs - inner) * SCORE_SCALE).astype(jnp.bfloat16)
-    d_value = dots(grad, probs.astype(jnp.bfloat16), 1, 1)
-    d_key = dots(query, d_scores, 1, 1)
-    d_query = dots(key, d_scores, 1, 0)
-    cosine, up, down = cos_ref[...], -up_ref[...], -down_ref[...]
-    out_ref[0, 0] = turn(d_query, cosine, up, down).astype(jnp.bfloat16)
-    out_ref[1, 0] = turn(d_key, cosine, up, down).astype(jnp.bfloat16)
-    out_ref[2, 0] = d_value.astype(jnp.bfloat16)
+    for head in range(PAIR):
+        query, key, value, grad = q_ref[head], k_ref[head], v_ref[head], g_ref[head]
+        scores = dots(key, query, 0, 0) * SCORE_SCALE
+        scores = jnp.where(col_ref[...] == row_ref[...], scores, MASKED)
+        probs = jnp.exp(scores - log_ref[head])
+        d_probs = dots(value, grad, 0, 0)
+        inner = jnp.sum(probs * d_probs, axis=0, keepdims=True)
+        d_scores = (probs * (d_probs - inner) * SCORE_SCALE).astype(jnp.bfloat16)
+        d_value = dots(grad, probs.astype(jnp.bfloat16), 1, 1)
+        d_key = dots(query, d_scores, 1, 1)
+        d_query = dots(key, d_scores, 1, 0)
+        cosine, up, down = cos_ref[...], -up_ref[...], -down_ref[...]
+        out_ref[0, head] = turn(d_query, cosine, up, down).astype(jnp.bfloat16)
+        out_ref[1, head] = turn(d_key, cosine, up, down).astype(jnp.bfloat16)
+        out_ref[2, head] = d_value.astype(jnp.bfloat16)
 
 
 def attend_back(query, key, value, grad, logs, tables):
     heads, _, tokens = query.shape
-    block = pl.BlockSpec((1, HEAD, tokens), lambda i: (i, 0, 0))
-    line = pl.BlockSpec((1, 1, tokens), lambda i: (i, 0, 0))
+    block = pl.BlockSpec((PAIR, HEAD, tokens), lambda i: (i, 0, 0))
+    line = pl.BlockSpec((PAIR, 1, tokens), lambda i: (i, 0, 0))
     return pl.pallas_call(
         attend_back_kernel,
-        grid=(heads,),
+        grid=(heads // PAIR,),
         in_specs=[block] * 4 + [line] + [whole(item) for item in tables],
-        out_specs=pl.BlockSpec((3, 1, HEAD, tokens), lambda i: (0, i, 0, 0)),
+        out_specs=pl.BlockSpec((3, PAIR, HEAD, tokens), lambda i: (0, i, 0, 0)),
         out_shape=jax.ShapeDtypeStruct((3, heads, HEAD, tokens), jnp.bfloat16),
         compiler_params=pltpu.CompilerParams(vmem_limit_bytes=32 << 20),
         cost_estimate=cost(10),

time: 547 us -> 545 us (level)
  no operation moved by 1% of the time
where the time goes in v6:
time: 545 us; the launch traced here: 537 us
  waiting for transfers between devices  126 us (23%)
  other arithmetic  120 us (22%)
  Pallas kernels  118 us (22%)
  local copies, waits for them, and re-layouts  67.7 us (12%)
  starting transfers between devices  65.7 us (12%)
  matrix products  28.1 us (5%)
  between operations  11.9 us (2%)
    ppermute x44, waiting for transfers between devices, trade(): lax.ppermute(value, 'tok', [(place, place ^ 1 << bit) for place in range(...  124 us
    ppermute x44, starting transfers between devices, trade(): lax.ppermute(value, 'tok', [(place, place ^ 1 << bit) for place in range(...  61.1 us
    pallas_call x1, Pallas kernels, feed_both_ways(): pl.pallas_call(feed_kernel, grid=(steps,), in_specs=[fixed] * 4 + [weight...  30.2 us
    convert_element_type x12, other arithmetic, add(): return (one.astype(jnp.float32) + two.astype(jnp.float32)).astype(kept)  23.2 us
    unnamed x378, local copies, waits for them, and re-layouts  22.5 us
    pallas_call x2, Pallas kernels, turned_parts(): pl.pallas_call(kernel, grid=(steps * len(rights),), in_specs=[pl.BlockSpe...  20.9 us
    dynamic_update_slice x12, local copies, waits for them, and re-layouts, put(): return lax.dynamic_update_slice(out, value, tuple(start))  20.7 us
    pallas_call x2, Pallas kernels, attend_back(): pl.pallas_call(attend_back_kernel, grid=(heads // PAIR,), in_specs=[block...  17.1 us
  transfers between devices with their start and end apart: 61, of which 30 were waited for; matrix products, arithmetic and copies ran while one was open for 33% of the time, Pallas kernels for 22%

profile of v6, /device:TPU:0, one launch (start us, length us, event | category | flops | bytes accessed | tf_op | source)
XLA Modules:
  0.0 536.8 jit_solution(3137073386849548957)
XLA Ops:
  6.6 2.5 collective-permute-start.2
  17.5 3.1 collective-permute-start.4
  27.2 3.0 collective-permute-start.6
  35.2 6.9 %collective-permute-done.6 = bf16[1,1,1,1,72,2304]{5,4,3,2,1,0:T(8,128)(2,1)} collective-permute-done((bf16[1,1,1,1,72,2304]{5,4,3,2,1,0:T(8,128)(2,1)}, bf16[1,1,1,1,72,2304]{5,4,3,2,1,0:T(8,128)(2,1)}, u32[]{:S(2)}, u32[]{:S(2)}) %collective-permute-start.6) | collective-permute-done | bytes 331808 | tf_op jit(solution)/shard_map/ppermute | solution.py:87
  56.6 4.4 collective-permute-done.9
  64.0 2.6 pad_maximum_fusion.9
  66.6 3.3 collective-permute-start.22
  74.4 10.1 %collective-permute-done.12 = bf16[2,1,1,1,72,2304]{5,4,3,2,1,0:T(8,128)(2,1)S(1)} collective-permute-done((bf16[2,1,1,1,72,2304]{5,4,3,2,1,0:T(8,128)(2,1)S(1)}, bf16[2,1,1,1,72,2304]{5,4,3,2,1,0:T(8,128)(2,1)S(1)}, u32[]{:S(2)}, u32[]{:S(2)}) %collective-permute-start.12) | collective-permute-done | bytes 663584 | tf_op jit(solution)/shard_map/ppermute | solution.py:87
  88.1 6.2 %maximum_maximum_fusion.1.refs_0_ = bf16[2,2,2,2,72,2304]{5,4,3,2,1,0:T(8,128)(2,1)} fusion(bf16[2,1,2,1,72,2304]{5,4,3,2,1,0:T(8,128)(2,1)} %copy-done.61, bf16[2,1,1,2,72,2304]{5,4,3,2,1,0:T(8,128)(2,1)} %constant_dynamic-update-slice_fusion.9.refs_1_), kind=kLoop, calls=%fused_computation.1 | loop fusion | flops 7962624 | bytes 7962624 | tf_op jit(solution)/shard_map/concatenate | solution.py:670
  96.6 3.1 collective-permute-done.13
  102.3 3.3 collective-permute-done.14
  106.3 3.5 pad_maximum_fusion.1
  110.7 5.8 %add_convert_fusion.6.refs_1_.x_ref = bf16[512,1152]{1,0:T(8,128)(2,1)} fusion(bf16[512,1152]{1,0:T(8,128)(2,1)S(1)} %copy-done.49, f32[1152]{0:T(1024)S(1)} %get-tuple-element.90, f32[1152]{0:T(1024)S(1)} %get-tuple-element.91, f32[1152]{0:T(1024)S(1)} %get-tuple-element.92, f32[1152]{0:T(1024)S(1)} %get-tuple-element.93, f32[1152]{0:T(1024)S(1)} %get-tuple-element.94, ...), kind=kLoop, calls=%fused_computation.38 | loop fusion | flops 9437184 | bytes 2402308 | tf_op jit(solution)/shard_map/convert_element_type | solution.py:867
  117.2 4.8 collective-permute-done.16
  122.0 2.5 constant_dynamic-update-slice_fusion.7
  124.5 2.5 constant_dynamic-update-slice_fusion.6
  127.0 6.2 %heads_of.2 = (f32[1728,512]{1,0:T(8,128)S(1)}, bf16[1152,512]{1,0:T(8,128)(2,1)}) custom-call(bf16[512,1152]{1,0:T(8,128)(2,1)S(1)} %copy-done.7, bf16[1152,2304]{1,0:T(8,128)(2,1)} %bitcast.161), custom_call_target="tpu_custom_call" | custom-call | flops 2300000000 | bytes 1000 | tf_op jit(solution)/shard_map/heads_of/pallas_call | solution.py:261
  133.7 7.5 %collective-permute-done.23 = bf16[2,1,1,1,72,4608]{5,4,3,2,1,0:T(8,128)(2,1)} collective-permute-done((bf16[2,1,1,1,72,4608]{5,4,3,2,1,0:T(8,128)(2,1)}, bf16[2,1,1,1,72,4608]{5,4,3,2,1,0:T(8,128)(2,1)}, u32[]{:S(2)}, u32[]{:S(2)}) %collective-permute-start.23) | collective-permute-done | bytes 1327136 | tf_op jit(solution)/shard_map/ppermute | solution.py:87
  141.2 2.5 constant_dynamic-update-slice_fusion.4.refs_0_
  147.2 5.6 %attend.2 = (bf16[8,72,512]{2,1,0:T(8,128)(2,1)S(1)}, f32[8,1,512]{2,1,0:T(1,128)S(1)}, bf16[8,72,512]{2,1,0:T(8,128)(2,1)S(1)}, bf16[8,72,512]{2,1,0:T(8,128)(2,1)S(1)}, bf16[8,72,512]{2,1,0:T(8,128)(2,1)S(1)}) custom-call(f32[3,8,72,512]{3,2,1,0:T(8,128)S(1)} %bitcast.143, f32[3,8,72,512]{3,2,1,0:T(8,128)S(1)} %bitcast.144, ...), custom_call_target="tpu_custom_call" | custom-call | flops 2760000000 | bytes 1000 | tf_op jit(solution)/shard_map/attend/pallas_call | solution.py:183
  156.4 19.5 %collective-permute-done.24 = bf16[2,1,1,1,72,4608]{5,4,3,2,1,0:T(8,128)(2,1)S(1)} collective-permute-done((bf16[2,1,1,1,72,4608]{5,4,3,2,1,0:T(8,128)(2,1)S(1)}, bf16[2,1,1,1,72,4608]{5,4,3,2,1,0:T(8,128)(2,1)S(1)}, u32[]{:S(2)}, u32[]{:S(2)}) %collective-permute-start.24) | collective-permute-done | bytes 1327136 | tf_op jit(solution)/shard_map/ppermute | solution.py:87
  178.7 6.4 %collective-permute-done.25 = bf16[2,1,1,1,72,4608]{5,4,3,2,1,0:T(8,128)(2,1)S(1)} collective-permute-done((bf16[2,1,1,1,72,4608]{5,4,3,2,1,0:T(8,128)(2,1)S(1)}, bf16[2,1,1,1,72,4608]{5,4,3,2,1,0:T(8,128)(2,1)S(1)}, u32[]{:S(2)}, u32[]{:S(2)}) %collective-permute-start.25) | collective-permute-done | bytes 1327136 | tf_op jit(solution)/shard_map/ppermute | solution.py:87
  185.8 7.4 %maximum_maximum_fusion = bf16[2,2,2,2,72,4608]{5,4,3,2,1,0:T(8,128)(2,1)} fusion(bf16[2,1,2,1,72,4608]{5,4,3,2,1,0:T(8,128)(2,1)S(1)} %constant_dynamic-update-slice_fusion.2, bf16[2,1,1,2,72,4608]{5,4,3,2,1,0:T(8,128)(2,1)} %constant_dynamic-update-slice_fusion.3), kind=kLoop, calls=%fused_computation | loop fusion | flops 15925248 | bytes 15925248 | tf_op jit(solution)/shard_map/concatenate | solution.py:670
  193.2 7.4 %heads_of.3 = (f32[1728,512]{1,0:T(8,128)}, bf16[1152,512]{1,0:T(8,128)(2,1)}) custom-call(bf16[512,1152]{1,0:T(8,128)(2,1)S(1)} %copy-done.8, bf16[1152,2304]{1,0:T(8,128)(2,1)} %bitcast.16.w_ref.w_two_ref, bf16[1152,512]{1,0:T(8,128)(2,1)} %collective-permute-done.19.refs_0_.refs_1_), custom_call_target="tpu_custom_call" | custom-call | flops 2300000000 | bytes 1000 | tf_op jit(solution)/shard_map/heads_of/pallas_call | solution.py:261
  202.6 5.8 %attend.3 = (bf16[8,72,512]{2,1,0:T(8,128)(2,1)S(1)}, f32[8,1,512]{2,1,0:T(1,128)S(1)}, bf16[8,72,512]{2,1,0:T(8,128)(2,1)S(1)}, bf16[8,72,512]{2,1,0:T(8,128)(2,1)S(1)}, bf16[8,72,512]{2,1,0:T(8,128)(2,1)S(1)}) custom-call(f32[3,8,72,512]{3,2,1,0:T(8,128)S(1)} %bitcast.146, f32[3,8,72,512]{3,2,1,0:T(8,128)S(1)} %bitcast.147, ...), custom_call_target="tpu_custom_call" | custom-call | flops 2760000000 | bytes 1000 | tf_op jit(solution)/shard_map/attend/pallas_call | solution.py:183
  210.1 3.0 broadcast_select_fusion.1
  213.3 6.8 %fusion.62 = (f32[512]{0:T(512)S(1)}, f32[512,1152]{1,0:T(8,128)S(1)}, bf16[512,1152]{1,0:T(8,128)(2,1)S(1)}, f32[512,1152]{1,0:T(8,128)}) fusion(f32[1152]{0:T(1024)S(1)} %copy-done.165, pred[512]{0:T(512)(128)(4,1)S(1)} %copy-done.130, f32[1152]{0:T(1024)S(1)} %copy-done.167, pred[512]{0:T(512)(128)(4,1)S(1)} %copy-done.135, f32[1152]{0:T(1024)S(1)} %copy-done.169, ...), kind=kOutput, calls=%fused_computation.288 | convolution fusion | flops 1374289408 | bytes 12134404 | tf_op jit(solution)/shard_map/dot_general | solution.py:142
  221.2 4.0 add_convert_fusion.5.x_one.one_ref
  225.7 14.1 %collective-permute-done.26 = bf16[2,1,1,2,72,4608]{5,4,3,2,1,0:T(8,128)(2,1)} collective-permute-done((bf16[2,1,1,2,72,4608]{5,4,3,2,1,0:T(8,128)(2,1)}, bf16[2,1,1,2,72,4608]{5,4,3,2,1,0:T(8,128)(2,1)}, u32[]{:S(2)}, u32[]{:S(2)}) %collective-permute-start.26) | collective-permute-done | bytes 2654240 | tf_op jit(solution)/shard_map/ppermute | solution.py:87
  239.9 3.4 constant_dynamic-update-slice_fusion.1
  243.3 3.5 constant_dynamic-update-slice_fusion
  248.2 30.2 %feed_both_ways.1 = (bf16[1024,1536]{1,0:T(8,128)(2,1)}, bf16[1024,1536]{1,0:T(8,128)(2,1)}, bf16[1024,1536]{1,0:T(8,128)(2,1)}, f32[512,1152]{1,0:T(8,128)}, bf16[512,1152]{1,0:T(8,128)(2,1)}) custom-call(bf16[512,1152]{1,0:T(8,128)(2,1)} %copy-done.20, bf16[512,1152]{1,0:T(8,128)(2,1)} %copy-done.25, bf16[512,1152]{1,0:T(8,128)(2,1)} %copy-done.23, ...), custom_call_target="tpu_custom_call" | custom-call | flops 10119999488 | bytes 1000 | tf_op jit(solution)/shard_map/feed_both_ways/pallas_call | solution.py:356
  280.7 7.6 %turned_parts.2 = (bf16[8,72,1536]{2,1,0:T(8,128)(2,1)S(1)}, bf16[8,72,1536]{2,1,0:T(8,128)(2,1)}) custom-call(s32[1]{0:T(128)} %bitcast.25.tok_ref, bf16[512,1152]{1,0:T(8,128)(2,1)S(1)} %copy-done.24, bf16[512,1152]{1,0:T(8,128)(2,1)S(1)} %copy-done.28, bf16[1024,1536]{1,0:T(8,128)(2,1)} %get-tuple-element.54.refs_0_, ...), custom_call_target="tpu_custom_call" | custom-call | flops 2760000000 | bytes 1000 | tf_op jit(solution)/shard_map/turned_parts/pallas_call | solution.py:423
  289.0 13.3 %turned_parts.3 = (bf16[4,72,3072]{2,1,0:T(8,128)(2,1)}, bf16[4,72,3072]{2,1,0:T(8,128)(2,1)S(1)}, bf16[4,72,3072]{2,1,0:T(8,128)(2,1)}, bf16[4,72,3072]{2,1,0:T(8,128)(2,1)}) custom-call(s32[1]{0:T(128)} %bitcast.25.tok_ref, bf16[512,1152]{1,0:T(8,128)(2,1)S(1)} %copy-done.21, bf16[512,1152]{1,0:T(8,128)(2,1)S(1)} %copy-done.26, ...), custom_call_target="tpu_custom_call" | custom-call | flops 5520000000 | bytes 1000 | tf_op jit(solution)/shard_map/turned_parts/pallas_call | solution.py:423
  304.6 2.6 multiply_reduce_fusion.1
  307.3 2.9 fusion.61
  310.3 2.2 multiply_convert_fusion.5
  316.4 8.5 %attend_back.2 = bf16[3,8,72,512]{3,2,1,0:T(8,128)(2,1)S(1)} custom-call(bf16[8,72,512]{2,1,0:T(8,128)(2,1)S(1)} %copy-done.36, bf16[8,72,512]{2,1,0:T(8,128)(2,1)S(1)} %copy-done.38, bf16[8,72,512]{2,1,0:T(8,128)(2,1)S(1)} %copy-done.40, bf16[8,72,512]{2,1,0:T(8,128)(2,1)S(1)} %get-tuple-element.145.g_ref, f32[8,1,512]{2,1,0:T(1,128)S(1)} %copy-done.44, ...), custom_call_target="tpu_custom_call" | custom-call | flops 4600000000 | bytes 1000 | tf_op jit(solution)/shard_map/attend_back/pallas_call | solution.py:225
  326.7 2.2 collective-permute-done.30
  336.5 8.6 %attend_back.3 = bf16[3,8,72,512]{3,2,1,0:T(8,128)(2,1)S(1)} custom-call(bf16[8,72,512]{2,1,0:T(8,128)(2,1)S(1)} %copy-done.30, bf16[8,72,512]{2,1,0:T(8,128)(2,1)S(1)} %copy-done.32, bf16[8,72,512]{2,1,0:T(8,128)(2,1)S(1)} %copy-done.34, bf16[8,72,512]{2,1,0:T(8,128)(2,1)S(1)} %copy-done.13, f32[8,1,512]{2,1,0:T(1,128)S(1)} %copy-done.42, ...), custom_call_target="tpu_custom_call" | custom-call | flops 4600000000 | bytes 1000 | tf_op jit(solution)/shard_map/attend_back/pallas_call | solution.py:225
  347.9 2.1 add_convert_fusion
  350.0 2.1 add_convert_fusion.1
  358.5 15.1 %grad_parts.1 = (bf16[4,72,2368]{2,1,0:T(8,128)(2,1)}, bf16[4,72,2368]{2,1,0:T(8,128)(2,1)}, bf16[4,72,2368]{2,1,0:T(8,128)(2,1)}, bf16[4,72,2368]{2,1,0:T(8,128)(2,1)}) custom-call(s32[1]{0:T(128)} %bitcast.25.tok_ref, bf16[1152,512]{1,0:T(8,128)(2,1)} %get-tuple-element.51.refs_0_, bf16[1152,512]{1,0:T(8,128)(2,1)} %collective-permute-done.19.refs_0_.refs_1_, ...), custom_call_target="tpu_custom_call" | custom-call | flops 5980000256 | bytes 1000 | tf_op jit(solution)/shard_map/grad_parts/pallas_call | solution.py:498
  375.6 2.6 add_convert_fusion.10.refs_3_
  378.1 7.3 %fusion = f32[1024,1152]{1,0:T(8,128)S(1)} fusion(bf16[1024,1536]{1,0:T(8,128)(2,1)} %after.33, bf16[1152,4608]{1,0:T(8,128)(2,1)} %bitcast.167), kind=kOutput, calls=%fused_computation.3 | convolution fusion | flops 3623878656 | bytes 11403264 | tf_op jit(solution)/shard_map/dot_general | solution.py:60
  388.2 9.5 %back_through.1 = f32[512,1152]{1,0:T(8,128)S(1)} custom-call(bf16[1728,512]{1,0:T(8,128)(2,1)S(1)} %copy-done.4, bf16[1728,512]{1,0:T(8,128)(2,1)S(1)} %copy-done.6, bf16[1152,2304]{1,0:T(8,128)(2,1)} %bitcast.163, bf16[1152,2304]{1,0:T(8,128)(2,1)} %bitcast.16.w_ref.w_two_ref), custom_call_target="tpu_custom_call" | custom-call | flops 4140000000 | bytes 1000 | tf_op jit(solution)/shard_map/back_through/pallas_call | solution.py:294
  399.3 3.3 fusion.60
  404.1 2.6 add_convert_fusion.9.refs_0_
  406.8 7.2 %add_add_fusion.2 = (f32[512,1152]{1,0:T(8,128)}, bf16[512,1152]{1,0:T(8,128)(2,1)}) fusion(f32[512,1152]{1,0:T(8,128)} %get-tuple-element.126, f32[512]{0:T(512)S(1)} %negate_multiply_fusion, bf16[512,1152]{1,0:T(8,128)(2,1)} %param.27, f32[512]{0:T(512)S(1)} %copy-done.128, f32[512,1152]{1,0:T(8,128)} %copy-done.52, f32[512]{0:T(512)S(1)} %copy-done.161, ...), kind=kLoop, calls=%fused_computation.23 | loop fusion | flops 9437184 | bytes 15362048 | tf_op jit(solution)/shard_map/add | solution.py:954
  422.6 2.3 collective-permute-done.50
  429.6 5.2 collective-permute-done.40
  434.8 2.1 fusion.8.refs_5_.refs_1_
  449.2 2.7 convolution_convert_fusion.1
  456.9 3.3 collective-permute-done.44
  462.0 4.0 collective-permute-done.45
  481.8 3.2 collective-permute-done.47
  487.2 7.1 %collective-permute-done.42 = bf16[72,2368]{1,0:T(8,128)(2,1)S(1)} collective-permute-done((bf16[72,2368]{1,0:T(8,128)(2,1)S(1)}, bf16[72,2368]{1,0:T(8,128)(2,1)S(1)}, u32[]{:S(2)}, u32[]{:S(2)}) %collective-permute-start.42) | collective-permute-done | bytes 341024 | tf_op jit(solution)/shard_map/ppermute | solution.py:87
  505.8 2.4 collective-permute-start.57
  511.5 2.3 collective-permute-done.58
  515.8 3.2 collective-permute-done.59
  521.7 3.8 multiply_subtract_fusion.1
  525.6 2.1 multiply_subtract_fusion
  530.6 2.1 concatenate.159
  532.6 2.8 multiply_subtract_fusion.2
  (633 shorter events, 175.6 us)
Async XLA Ops:
  2.0 13.7 %collective-permute-start = (bf16[72,576]{1,0:T(8,128)(2,1)S(1)}, bf16[72,576]{1,0:T(8,128)(2,1)S(1)}, u32[]{:S(2)}, u32[]{:S(2)}) collective-permute-start(bf16[72,576]{1,0:T(8,128)(2,1)S(1)} %get-tuple-element.161), channel_id=1, source_target_pairs={{0,1},{1,0},{2,3},{3,2},{4,5},{5,4},{6,7},{7,6},{8,9},{9,8},{10,11... | collective-permute-start | bytes 248840 | tf_op jit(solution)/shard_map/ppermute | solution.py:95
  3.2 2.7 collective-permute-start.1
  3.9 11.1 %collective-permute-start.7 = (f32[216]{0:T(256)S(1)}, f32[216]{0:T(256)S(1)}, u32[]{:S(2)}, u32[]{:S(2)}) collective-permute-start(f32[216]{0:T(256)S(1)} %convert_convert_fusion.1), channel_id=1, source_target_pairs={{0,1},{1,0},{2,3},{3,2},{4,5},{5,4},{6,7},{7,6},{8,9},{9,8},{10,11... | collective-permute-start | bytes 2600 | tf_op jit(solution)/shard_map/ppermute | solution.py:95
  6.6 4.0 collective-permute-start.2
  10.7 3.6 collective-permute-start.3
  17.5 5.0 collective-permute-start.4
  22.6 3.7 collective-permute-start.5
  27.2 14.9 %collective-permute-start.6 = (bf16[1,1,1,1,72,2304]{5,4,3,2,1,0:T(8,128)(2,1)}, bf16[1,1,1,1,72,2304]{5,4,3,2,1,0:T(8,128)(2,1)}, u32[]{:S(2)}, u32[]{:S(2)}) collective-permute-start(bf16[1,1,1,1,72,2304]{5,4,3,2,1,0:T(8,128)(2,1)} %after.23), channel_id=1, source_target_pairs={{0,16},{2,18},{4,20},{6,22},{8,24},{10,26},{12,28},{14,30},{16,0},... | collective-permute-start | bytes 995336 | tf_op jit(solution)/shard_map/ppermute | solution.py:87
  33.6 20.2 %collective-permute-start.8 = (bf16[2,2,2,1,8,3456]{5,4,3,2,1,0:T(8,128)(2,1)}, bf16[2,2,2,1,8,3456]{5,4,3,2,1,0:T(8,128)(2,1)}, u32[]{:S(2)}, u32[]{:S(2)}) collective-permute-start(bf16[2,2,2,1,8,3456]{5,4,3,2,1,0:T(8,128)(2,1)} %slice.534), channel_id=1, source_target_pairs={{0,2},{2,0},{4,6},{6,4},{8,10},{10,8},{12,14},{14,12},{16,18},{18,... | collective-permute-start | bytes 1327112 | tf_op jit(solution)/shard_map/ppermute | solution.py:87
  44.7 17.1 %collective-permute-start.10 = (bf16[2,1,1,1,72,2304]{5,4,3,2,1,0:T(8,128)(2,1)S(1)}, bf16[2,1,1,1,72,2304]{5,4,3,2,1,0:T(8,128)(2,1)}, u32[]{:S(2)}, u32[]{:S(2)}) collective-permute-start(bf16[2,1,1,1,72,2304]{5,4,3,2,1,0:T(8,128)(2,1)S(1)} %constant_dynamic-update-slice_fusion.11), channel_id=1, source_target_pairs={{0,8},{2,10},{4,12},{6,14},{8,0},{10,2},{12,4},{14,6},{16,24},{18,... | collective-permute-start | bytes 1990664 | tf_op jit(solution)/shard_map/ppermute | solution.py:87
  49.6 61.0 %copy-start.134 = (pred[512]{0:T(512)(128)(4,1)}, pred[512]{0:T(512)(128)(4,1)S(1)}, u32[]{:S(2)}) copy-start(pred[512]{0:T(512)(128)(4,1)S(1)} %get-tuple-element.185) | copy-start | bytes 1540
  49.6 61.0 %copy-start.139 = (pred[512]{0:T(512)(128)(4,1)}, pred[512]{0:T(512)(128)(4,1)S(1)}, u32[]{:S(2)}) copy-start(pred[512]{0:T(512)(128)(4,1)S(1)} %get-tuple-element.186) | copy-start | bytes 1540
  49.6 61.0 %copy-start.144 = (pred[512]{0:T(512)(128)(4,1)}, pred[512]{0:T(512)(128)(4,1)S(1)}, u32[]{:S(2)}) copy-start(pred[512]{0:T(512)(128)(4,1)S(1)} %get-tuple-element.187) | copy-start | bytes 1540
  55.0 6.0 %collective-permute-start.9 = (bf16[2,2,1,1,8,3456]{5,4,3,2,1,0:T(8,128)(2,1)S(1)}, bf16[2,2,1,1,8,3456]{5,4,3,2,1,0:T(8,128)(2,1)S(1)}, u32[]{:S(2)}, u32[]{:S(2)}) collective-permute-start(bf16[2,2,1,1,8,3456]{5,4,3,2,1,0:T(8,128)(2,1)S(1)} %slice.535), channel_id=1, source_target_pairs={{0,4},{2,6},{4,0},{6,2},{8,12},{10,14},{12,8},{14,10},{16,20},{18,... | collective-permute-start | bytes 663560 | tf_op jit(solution)/shard_map/ppermute | solution.py:87
  66.6 33.7 %collective-permute-start.22 = (bf16[1,1,1,1,72,4608]{5,4,3,2,1,0:T(8,128)(2,1)}, bf16[1,1,1,1,72,4608]{5,4,3,2,1,0:T(8,128)(2,1)}, u32[]{:S(2)}, u32[]{:S(2)}) collective-permute-start(bf16[1,1,1,1,72,4608]{5,4,3,2,1,0:T(8,128)(2,1)} %bitcast.174), channel_id=1, source_target_pairs={{0,16},{2,18},{4,20},{6,22},{8,24},{10,26},{12,28},{14,30},{16,0},... | collective-permute-start | bytes 1990664 | tf_op jit(solution)/shard_map/ppermute | solution.py:87
  70.1 14.4 %collective-permute-start.12 = (bf16[2,1,1,1,72,2304]{5,4,3,2,1,0:T(8,128)(2,1)S(1)}, bf16[2,1,1,1,72,2304]{5,4,3,2,1,0:T(8,128)(2,1)S(1)}, u32[]{:S(2)}, u32[]{:S(2)}) collective-permute-start(bf16[2,1,1,1,72,2304]{5,4,3,2,1,0:T(8,128)(2,1)S(1)} %get-tuple-element.141), channel_id=1, source_target_pairs={{0,4},{2,6},{4,0},{6,2},{8,12},{10,14},{12,8},{14,10},{16,20},{18,... | collective-permute-start | bytes 1990664 | tf_op jit(solution)/shard_map/ppermute | solution.py:87
  71.6 14.1 %collective-permute-start.11 = (bf16[2,1,1,1,72,2304]{5,4,3,2,1,0:T(8,128)(2,1)S(1)}, bf16[2,1,1,1,72,2304]{5,4,3,2,1,0:T(8,128)(2,1)S(1)}, u32[]{:S(2)}, u32[]{:S(2)}) collective-permute-start(bf16[2,1,1,1,72,2304]{5,4,3,2,1,0:T(8,128)(2,1)S(1)} %get-tuple-element.142), channel_id=1, source_target_pairs={{0,2},{2,0},{4,6},{6,4},{8,10},{10,8},{12,14},{14,12},{16,18},{18,... | collective-permute-start | bytes 1990664 | tf_op jit(solution)/shard_map/ppermute | solution.py:87
  87.5 12.1 %collective-permute-start.13 = (bf16[2,1,1,1,8,3456]{5,4,3,2,1,0:T(8,128)(2,1)S(1)}, bf16[2,1,1,1,8,3456]{5,4,3,2,1,0:T(8,128)(2,1)S(1)}, u32[]{:S(2)}, u32[]{:S(2)}) collective-permute-start(bf16[2,1,1,1,8,3456]{5,4,3,2,1,0:T(8,128)(2,1)S(1)} %slice.536), channel_id=1, source_target_pairs={{0,8},{2,10},{4,12},{6,14},{8,0},{10,2},{12,4},{14,6},{16,24},{18,... | collective-permute-start | bytes 331784 | tf_op jit(solution)/shard_map/ppermute | solution.py:87
  94.3 27.7 %collective-permute-start.16 = (bf16[2,1,1,2,72,2304]{5,4,3,2,1,0:T(8,128)(2,1)}, bf16[2,1,1,2,72,2304]{5,4,3,2,1,0:T(8,128)(2,1)}, u32[]{:S(2)}, u32[]{:S(2)}) collective-permute-start(bf16[2,1,1,2,72,2304]{5,4,3,2,1,0:T(8,128)(2,1)} %constant_dynamic-update-slice_fusion.9.refs_1_), channel_id=1, source_target_pairs={{0,4},{2,6},{4,0},{6,2},{8,12},{10,14},{12,8},{14,10},{16,20},{18,... | collective-permute-start | bytes 3981320 | tf_op jit(solution)/shard_map/ppermute | solution.py:87
  95.1 29.4 %collective-permute-start.17 = (bf16[2,1,2,1,72,2304]{5,4,3,2,1,0:T(8,128)(2,1)S(1)}, bf16[2,1,2,1,72,2304]{5,4,3,2,1,0:T(8,128)(2,1)}, u32[]{:S(2)}, u32[]{:S(2)}) collective-permute-start(bf16[2,1,2,1,72,2304]{5,4,3,2,1,0:T(8,128)(2,1)S(1)} %copy-done.62), channel_id=1, source_target_pairs={{0,2},{2,0},{4,6},{6,4},{8,10},{10,8},{12,14},{14,12},{16,18},{18,... | collective-permute-start | bytes 3981320 | tf_op jit(solution)/shard_map/ppermute | solution.py:87
  99.7 6.0 %collective-permute-start.14 = (bf16[1,1,1,1,8,3456]{5,4,3,2,1,0:T(8,128)(2,1)S(1)}, bf16[1,1,1,1,8,3456]{5,4,3,2,1,0:T(8,128)(2,1)S(1)}, u32[]{:S(2)}, u32[]{:S(2)}) collective-permute-start(bf16[1,1,1,1,8,3456]{5,4,3,2,1,0:T(8,128)(2,1)S(1)} %slice.537), channel_id=1, source_target_pairs={{0,16},{2,18},{4,20},{6,22},{8,24},{10,26},{12,28},{14,30},{16,0},... | collective-permute-start | bytes 165896 | tf_op jit(solution)/shard_map/ppermute | solution.py:87
  105.7 4.1 collective-permute-start.15
  109.8 31.4 %collective-permute-start.23 = (bf16[2,1,1,1,72,4608]{5,4,3,2,1,0:T(8,128)(2,1)}, bf16[2,1,1,1,72,4608]{5,4,3,2,1,0:T(8,128)(2,1)}, u32[]{:S(2)}, u32[]{:S(2)}) collective-permute-start(bf16[2,1,1,1,72,4608]{5,4,3,2,1,0:T(8,128)(2,1)} %after.27), channel_id=1, source_target_pairs={{0,8},{2,10},{4,12},{6,14},{8,0},{10,2},{12,4},{14,6},{16,24},{18,... | collective-permute-start | bytes 3981320 | tf_op jit(solution)/shard_map/ppermute | solution.py:87
  127.0 66.2 %collective-permute-start.18 = (bf16[2,2,2,2,72,2304]{5,4,3,2,1,0:T(8,128)(2,1)}, bf16[2,2,2,2,72,2304]{5,4,3,2,1,0:T(8,128)(2,1)}, u32[]{:S(2)}, u32[]{:S(2)}) collective-permute-start(bf16[2,2,2,2,72,2304]{5,4,3,2,1,0:T(8,128)(2,1)} %constant_dynamic-update-slice_fusion.6), channel_id=1, source_target_pairs={{0,1},{1,0},{2,3},{3,2},{4,5},{5,4},{6,7},{7,6},{8,9},{9,8},{10,11... | collective-permute-start | bytes 15925256 | tf_op jit(solution)/shard_map/ppermute | solution.py:95
  133.2 60.0 %collective-permute-start.19 = (bf16[1152,512]{1,0:T(8,128)(2,1)}, bf16[1152,512]{1,0:T(8,128)(2,1)}, u32[]{:S(2)}, u32[]{:S(2)}) collective-permute-start(bf16[1152,512]{1,0:T(8,128)(2,1)} %get-tuple-element.51.refs_0_), channel_id=1, source_target_pairs={{0,1},{1,0},{2,3},{3,2},{4,5},{5,4},{6,7},{7,6},{8,9},{9,8},{10,11... | collective-permute-start | bytes 3538952 | tf_op jit(solution)/shard_map/ppermute | solution.py:95
  145.7 30.3 %collective-permute-start.24 = (bf16[2,1,1,1,72,4608]{5,4,3,2,1,0:T(8,128)(2,1)S(1)}, bf16[2,1,1,1,72,4608]{5,4,3,2,1,0:T(8,128)(2,1)S(1)}, u32[]{:S(2)}, u32[]{:S(2)}) collective-permute-start(bf16[2,1,1,1,72,4608]{5,4,3,2,1,0:T(8,128)(2,1)S(1)} %get-tuple-element.133), channel_id=1, source_target_pairs={{0,2},{2,0},{4,6},{6,4},{8,10},{10,8},{12,14},{14,12},{16,18},{18,... | collective-permute-start | bytes 3981320 | tf_op jit(solution)/shard_map/ppermute | solution.py:87
  152.9 32.1 %collective-permute-start.25 = (bf16[2,1,1,1,72,4608]{5,4,3,2,1,0:T(8,128)(2,1)S(1)}, bf16[2,1,1,1,72,4608]{5,4,3,2,1,0:T(8,128)(2,1)S(1)}, u32[]{:S(2)}, u32[]{:S(2)}) collective-permute-start(bf16[2,1,1,1,72,4608]{5,4,3,2,1,0:T(8,128)(2,1)S(1)} %get-tuple-element.134), channel_id=1, source_target_pairs={{0,4},{2,6},{4,0},{6,2},{8,12},{10,14},{12,8},{14,10},{16,20},{18,... | collective-permute-start | bytes 3981320 | tf_op jit(solution)/shard_map/ppermute | solution.py:87
  177.1 62.7 %collective-permute-start.26 = (bf16[2,1,1,2,72,4608]{5,4,3,2,1,0:T(8,128)(2,1)}, bf16[2,1,1,2,72,4608]{5,4,3,2,1,0:T(8,128)(2,1)}, u32[]{:S(2)}, u32[]{:S(2)}) collective-permute-start(bf16[2,1,1,2,72,4608]{5,4,3,2,1,0:T(8,128)(2,1)} %constant_dynamic-update-slice_fusion.3), channel_id=1, source_target_pairs={{0,4},{2,6},{4,0},{6,2},{8,12},{10,14},{12,8},{14,10},{16,20},{18,... | collective-permute-start | bytes 7962632 | tf_op jit(solution)/shard_map/ppermute | solution.py:87
  185.2 58.1 %collective-permute-start.27 = (bf16[2,1,2,1,72,4608]{5,4,3,2,1,0:T(8,128)(2,1)S(1)}, bf16[2,1,2,1,72,4608]{5,4,3,2,1,0:T(8,128)(2,1)}, u32[]{:S(2)}, u32[]{:S(2)}) collective-permute-start(bf16[2,1,2,1,72,4608]{5,4,3,2,1,0:T(8,128)(2,1)S(1)} %constant_dynamic-update-slice_fusion.2), channel_id=1, source_target_pairs={{0,2},{2,0},{4,6},{6,4},{8,10},{10,8},{12,14},{14,12},{16,18},{18,... | collective-permute-start | bytes 7962632 | tf_op jit(solution)/shard_map/ppermute | solution.py:87
  225.1 21.7 %collective-permute-start.20 = (bf16[512,1152]{1,0:T(8,128)(2,1)S(1)}, bf16[512,1152]{1,0:T(8,128)(2,1)S(1)}, u32[]{:S(2)}, u32[]{:S(2)}) collective-permute-start(bf16[512,1152]{1,0:T(8,128)(2,1)S(1)} %add_convert_fusion.5.x_one.one_ref), channel_id=1, source_target_pairs={{0,1},{1,0},{2,3},{3,2},{4,5},{5,4},{6,7},{7,6},{8,9},{9,8},{10,11... | collective-permute-start | bytes 3538952 | tf_op jit(solution)/shard_map/ppermute | solution.py:95
  225.2 21.6 %collective-permute-start.21 = (bf16[512,1152]{1,0:T(8,128)(2,1)S(1)}, bf16[512,1152]{1,0:T(8,128)(2,1)S(1)}, u32[]{:S(2)}, u32[]{:S(2)}) collective-permute-start(bf16[512,1152]{1,0:T(8,128)(2,1)S(1)} %get-tuple-element.182.r_one.one_ref), channel_id=1, source_target_pairs={{0,1},{1,0},{2,3},{3,2},{4,5},{5,4},{6,7},{7,6},{8,9},{9,8},{10,11... | collective-permute-start | bytes 3538952 | tf_op jit(solution)/shard_map/ppermute | solution.py:95
  246.8 32.2 %collective-permute-start.28 = (bf16[1152,512]{1,0:T(8,128)(2,1)}, bf16[1152,512]{1,0:T(8,128)(2,1)S(1)}, u32[]{:S(2)}, u32[]{:S(2)}) collective-permute-start(bf16[1152,512]{1,0:T(8,128)(2,1)} %bitcast.18.refs_2_), channel_id=1, source_target_pairs={{0,1},{1,0},{2,3},{3,2},{4,5},{5,4},{6,7},{7,6},{8,9},{9,8},{10,11... | collective-permute-start | bytes 3538952 | tf_op jit(solution)/shard_map/ppermute | solution.py:95
  278.4 26.0 %collective-permute-start.29 = (bf16[512,1152]{1,0:T(8,128)(2,1)}, bf16[512,1152]{1,0:T(8,128)(2,1)}, u32[]{:S(2)}, u32[]{:S(2)}) collective-permute-start(bf16[512,1152]{1,0:T(8,128)(2,1)} %get-tuple-element.59), channel_id=1, source_target_pairs={{0,1},{1,0},{2,3},{3,2},{4,5},{5,4},{6,7},{7,6},{8,9},{9,8},{10,11... | collective-permute-start | bytes 3538952 | tf_op jit(solution)/shard_map/ppermute | solution.py:95
  288.3 40.7 %collective-permute-start.30 = (bf16[8,72,1536]{2,1,0:T(8,128)(2,1)S(1)}, bf16[8,72,1536]{2,1,0:T(8,128)(2,1)}, u32[]{:S(2)}, u32[]{:S(2)}) collective-permute-start(bf16[8,72,1536]{2,1,0:T(8,128)(2,1)S(1)} %get-tuple-element.65), channel_id=1, source_target_pairs={{0,8},{2,10},{4,12},{6,14},{8,0},{10,2},{12,4},{14,6},{16,24},{18,... | collective-permute-start | bytes 5308424 | tf_op jit(solution)/shard_map/ppermute | solution.py:87
  302.3 44.1 %collective-permute-start.33 = (bf16[4,72,3072]{2,1,0:T(8,128)(2,1)}, bf16[4,72,3072]{2,1,0:T(8,128)(2,1)}, u32[]{:S(2)}, u32[]{:S(2)}) collective-permute-start(bf16[4,72,3072]{2,1,0:T(8,128)(2,1)} %get-tuple-element.72), channel_id=1, source_target_pairs={{0,2},{2,0},{4,6},{6,4},{8,10},{10,8},{12,14},{14,12},{16,18},{18,... | collective-permute-start | bytes 5308424 | tf_op jit(solution)/shard_map/ppermute | solution.py:87
  302.8 47.2 %collective-permute-start.32 = (bf16[4,72,3072]{2,1,0:T(8,128)(2,1)}, bf16[4,72,3072]{2,1,0:T(8,128)(2,1)}, u32[]{:S(2)}, u32[]{:S(2)}) collective-permute-start(bf16[4,72,3072]{2,1,0:T(8,128)(2,1)} %get-tuple-element.70), channel_id=1, source_target_pairs={{0,4},{2,6},{4,0},{6,2},{8,12},{10,14},{12,8},{14,10},{16,20},{18,... | collective-permute-start | bytes 5308424 | tf_op jit(solution)/shard_map/ppermute | solution.py:87
  326.2 32.3 %collective-permute-start.31 = (bf16[1728,512]{1,0:T(8,128)(2,1)S(1)}, bf16[1728,512]{1,0:T(8,128)(2,1)}, u32[]{:S(2)}, u32[]{:S(2)}) collective-permute-start(bf16[1728,512]{1,0:T(8,128)(2,1)S(1)} %bitcast.153), channel_id=1, source_target_pairs={{0,1},{1,0},{2,3},{3,2},{4,5},{5,4},{6,7},{7,6},{8,9},{9,8},{10,11... | collective-permute-start | bytes 5308424 | tf_op jit(solution)/shard_map/ppermute | solution.py:95
  326.2 32.3 %collective-permute-start.34 = (bf16[2,2,2,2,32,576]{5,4,3,2,1,0:T(8,128)(2,1)}, bf16[2,2,2,2,32,576]{5,4,3,2,1,0:T(8,128)(2,1)}, u32[]{:S(2)}, u32[]{:S(2)}) collective-permute-start(bf16[2,2,2,2,32,576]{5,4,3,2,1,0:T(8,128)(2,1)} %bitcast.34), channel_id=1, source_target_pairs={{0,1},{1,0},{2,3},{3,2},{4,5},{5,4},{6,7},{7,6},{8,9},{9,8},{10,11... | collective-permute-start | bytes 1769480 | tf_op jit(solution)/shard_map/ppermute | solution.py:95
  353.7 21.8 %collective-permute-start.36 = (bf16[2,72,3072]{2,1,0:T(8,128)(2,1)S(1)}, bf16[2,72,3072]{2,1,0:T(8,128)(2,1)}, u32[]{:S(2)}, u32[]{:S(2)}) collective-permute-start(bf16[2,72,3072]{2,1,0:T(8,128)(2,1)S(1)} %get-tuple-element.200.refs_2_), channel_id=1, source_target_pairs={{0,4},{2,6},{4,0},{6,2},{8,12},{10,14},{12,8},{14,10},{16,20},{18,... | collective-permute-start | bytes 2654216 | tf_op jit(solution)/shard_map/ppermute | solution.py:87
  357.2 82.6 %collective-permute-start.52 = (bf16[2,2,72,1536]{3,2,0,1:T(8,128)(2,1)}, bf16[2,2,72,1536]{3,2,0,1:T(8,128)(2,1)}, u32[]{:S(2)}, u32[]{:S(2)}) collective-permute-start(bf16[2,2,72,1536]{3,2,0,1:T(8,128)(2,1)} %copy.148), channel_id=1, source_target_pairs={{0,16},{2,18},{4,20},{6,22},{8,24},{10,26},{12,28},{14,30},{16,0},... | collective-permute-start | bytes 2654216 | tf_op jit(solution)/shard_map/ppermute | solution.py:87
  358.0 44.6 %collective-permute-start.49 = (bf16[2,72,3072]{2,1,0:T(8,128)(2,1)}, bf16[2,72,3072]{2,1,0:T(8,128)(2,1)}, u32[]{:S(2)}, u32[]{:S(2)}) collective-permute-start(bf16[2,72,3072]{2,1,0:T(8,128)(2,1)} %get-tuple-element.138.refs_1_), channel_id=1, source_target_pairs={{0,2},{2,0},{4,6},{6,4},{8,10},{10,8},{12,14},{14,12},{16,18},{18,... | collective-permute-start | bytes 2654216 | tf_op jit(solution)/shard_map/ppermute | solution.py:87
  373.6 40.4 %collective-permute-start.39 = (bf16[4,72,2368]{2,1,0:T(8,128)(2,1)}, bf16[4,72,2368]{2,1,0:T(8,128)(2,1)}, u32[]{:S(2)}, u32[]{:S(2)}) collective-permute-start(bf16[4,72,2368]{2,1,0:T(8,128)(2,1)} %get-tuple-element.74.refs_2_), channel_id=1, source_target_pairs={{0,2},{2,0},{4,6},{6,4},{8,10},{10,8},{12,14},{14,12},{16,18},{18,... | collective-permute-start | bytes 4091912 | tf_op jit(solution)/shard_map/ppermute | solution.py:87
  375.2 43.3 %collective-permute-start.37 = (bf16[4,72,2368]{2,1,0:T(8,128)(2,1)}, bf16[4,72,2368]{2,1,0:T(8,128)(2,1)}, u32[]{:S(2)}, u32[]{:S(2)}) collective-permute-start(bf16[4,72,2368]{2,1,0:T(8,128)(2,1)} %get-tuple-element.73.refs_1_), channel_id=1, source_target_pairs={{0,4},{2,6},{4,0},{6,2},{8,12},{10,14},{12,8},{14,10},{16,20},{18,... | collective-permute-start | bytes 4091912 | tf_op jit(solution)/shard_map/ppermute | solution.py:87
  388.1 18.6 %collective-permute-start.35 = (bf16[512,1152]{1,0:T(8,128)(2,1)}, bf16[512,1152]{1,0:T(8,128)(2,1)}, u32[]{:S(2)}, u32[]{:S(2)}) collective-permute-start(bf16[512,1152]{1,0:T(8,128)(2,1)} %slice.533), channel_id=1, source_target_pairs={{0,1},{1,0},{2,3},{3,2},{4,5},{5,4},{6,7},{7,6},{8,9},{9,8},{10,11... | collective-permute-start | bytes 3538952 | tf_op jit(solution)/shard_map/ppermute | solution.py:95
  402.6 22.3 %collective-permute-start.50 = (bf16[2,72,3072]{2,1,0:T(8,128)(2,1)}, bf16[2,72,3072]{2,1,0:T(8,128)(2,1)}, u32[]{:S(2)}, u32[]{:S(2)}) collective-permute-start(bf16[2,72,3072]{2,1,0:T(8,128)(2,1)} %add_convert_fusion.10.refs_3_), channel_id=1, source_target_pairs={{0,8},{2,10},{4,12},{6,14},{8,0},{10,2},{12,4},{14,6},{16,24},{18,... | collective-permute-start | bytes 2654216 | tf_op jit(solution)/shard_map/ppermute | solution.py:87
  416.8 18.0 %collective-permute-start.40 = (bf16[2,72,2368]{2,1,0:T(8,128)(2,1)}, bf16[2,72,2368]{2,1,0:T(8,128)(2,1)}, u32[]{:S(2)}, u32[]{:S(2)}) collective-permute-start(bf16[2,72,2368]{2,1,0:T(8,128)(2,1)} %slice_bitcast_fusion.4.refs_4_.refs_2_), channel_id=1, source_target_pairs={{0,4},{2,6},{4,0},{6,2},{8,12},{10,14},{12,8},{14,10},{16,20},{18,... | collective-permute-start | bytes 2045960 | tf_op jit(solution)/shard_map/ppermute | solution.py:87
  422.1 56.8 %collective-permute-start.38 = (bf16[2,72,2368]{2,1,0:T(8,128)(2,1)}, bf16[2,72,2368]{2,1,0:T(8,128)(2,1)}, u32[]{:S(2)}, u32[]{:S(2)}) collective-permute-start(bf16[2,72,2368]{2,1,0:T(8,128)(2,1)} %slice_bitcast_fusion.6.refs_3_.refs_1_), channel_id=1, source_target_pairs={{0,2},{2,0},{4,6},{6,4},{8,10},{10,8},{12,14},{14,12},{16,18},{18,... | collective-permute-start | bytes 2045960 | tf_op jit(solution)/shard_map/ppermute | solution.py:87
  427.5 28.1 %collective-permute-start.51 = (bf16[72,3072]{1,0:T(8,128)(2,1)}, bf16[72,3072]{1,0:T(8,128)(2,1)}, u32[]{:S(2)}, u32[]{:S(2)}) collective-permute-start(bf16[72,3072]{1,0:T(8,128)(2,1)} %get-tuple-element.152), channel_id=1, source_target_pairs={{0,16},{2,18},{4,20},{6,22},{8,24},{10,26},{12,28},{14,30},{16,0},... | collective-permute-start | bytes 1327112 | tf_op jit(solution)/shard_map/ppermute | solution.py:87
  436.9 42.0 %collective-permute-start.41 = (bf16[2,72,2368]{2,1,0:T(8,128)(2,1)}, bf16[2,72,2368]{2,1,0:T(8,128)(2,1)}, u32[]{:S(2)}, u32[]{:S(2)}) collective-permute-start(bf16[2,72,2368]{2,1,0:T(8,128)(2,1)} %fusion.8.refs_5_.refs_1_), channel_id=1, source_target_pairs={{0,8},{2,10},{4,12},{6,14},{8,0},{10,2},{12,4},{14,6},{16,24},{18,... | collective-permute-start | bytes 2045960 | tf_op jit(solution)/shard_map/ppermute | solution.py:87
  443.0 24.4 %collective-permute-start.53 = (bf16[2,72,1536]{2,1,0:T(8,128)(2,1)}, bf16[2,72,1536]{2,1,0:T(8,128)(2,1)}, u32[]{:S(2)}, u32[]{:S(2)}) collective-permute-start(bf16[2,72,1536]{2,1,0:T(8,128)(2,1)} %slice_bitcast_fusion.8), channel_id=1, source_target_pairs={{0,2},{2,0},{4,6},{6,4},{8,10},{10,8},{12,14},{14,12},{16,18},{18,... | collective-permute-start | bytes 1327112 | tf_op jit(solution)/shard_map/ppermute | solution.py:87
  451.9 1.3 collective-permute-start.43
  453.9 6.3 %collective-permute-start.44 = (bf16[1,1,1,1,8,3456]{5,4,3,2,1,0:T(8,128)(2,1)}, bf16[1,1,1,1,8,3456]{5,4,3,2,1,0:T(8,128)(2,1)S(1)}, u32[]{:S(2)}, u32[]{:S(2)}) collective-permute-start(bf16[1,1,1,1,8,3456]{5,4,3,2,1,0:T(8,128)(2,1)} %after.38), channel_id=1, source_target_pairs={{0,16},{2,18},{4,20},{6,22},{8,24},{10,26},{12,28},{14,30},{16,0},... | collective-permute-start | bytes 165896 | tf_op jit(solution)/shard_map/ppermute | solution.py:87
  461.0 5.0 collective-permute-start.45
  466.1 6.0 %collective-permute-start.46 = (bf16[2,2,1,1,8,3456]{5,4,3,2,1,0:T(8,128)(2,1)S(1)}, bf16[2,2,1,1,8,3456]{5,4,3,2,1,0:T(8,128)(2,1)S(1)}, u32[]{:S(2)}, u32[]{:S(2)}) collective-permute-start(bf16[2,2,1,1,8,3456]{5,4,3,2,1,0:T(8,128)(2,1)S(1)} %pad_maximum_fusion.17), channel_id=1, source_target_pairs={{0,2},{2,0},{4,6},{6,4},{8,10},{10,8},{12,14},{14,12},{16,18},{18,... | collective-permute-start | bytes 663560 | tf_op jit(solution)/shard_map/ppermute | solution.py:87
  469.4 7.8 %collective-permute-start.54 = (bf16[72,1536]{1,0:T(8,128)(2,1)}, bf16[72,1536]{1,0:T(8,128)(2,1)S(1)}, u32[]{:S(2)}, u32[]{:S(2)}) collective-permute-start(bf16[72,1536]{1,0:T(8,128)(2,1)} %get-tuple-element.160), channel_id=1, source_target_pairs={{0,4},{2,6},{4,0},{6,2},{8,12},{10,14},{12,8},{14,10},{16,20},{18,... | collective-permute-start | bytes 663560 | tf_op jit(solution)/shard_map/ppermute | solution.py:87
  473.6 11.4 %collective-permute-start.47 = (bf16[2,2,1,2,8,3456]{5,4,3,2,1,0:T(8,128)(2,1)}, bf16[2,2,1,2,8,3456]{5,4,3,2,1,0:T(8,128)(2,1)S(1)}, u32[]{:S(2)}, u32[]{:S(2)}) collective-permute-start(bf16[2,2,1,2,8,3456]{5,4,3,2,1,0:T(8,128)(2,1)} %pad_maximum_fusion.15), channel_id=1, source_target_pairs={{0,4},{2,6},{4,0},{6,2},{8,12},{10,14},{12,8},{14,10},{16,20},{18,... | collective-permute-start | bytes 1327112 | tf_op jit(solution)/shard_map/ppermute | solution.py:87
  480.5 13.8 %collective-permute-start.42 = (bf16[72,2368]{1,0:T(8,128)(2,1)S(1)}, bf16[72,2368]{1,0:T(8,128)(2,1)S(1)}, u32[]{:S(2)}, u32[]{:S(2)}) collective-permute-start(bf16[72,2368]{1,0:T(8,128)(2,1)S(1)} %slice_bitcast_fusion.14), channel_id=1, source_target_pairs={{0,16},{2,18},{4,20},{6,22},{8,24},{10,26},{12,28},{14,30},{16,0},... | collective-permute-start | bytes 1022984 | tf_op jit(solution)/shard_map/ppermute | solution.py:87
  485.2 1.2 collective-permute-start.48
  499.6 1.3 collective-permute-start.55
  501.5 3.7 collective-permute-start.56
  505.8 3.7 collective-permute-start.57
  510.1 3.7 collective-permute-start.58
  514.4 4.6 collective-permute-start.59
  521.7 8.1 %collective-permute-start.60 = (f32[72,576]{1,0:T(8,128)S(1)}, f32[72,576]{1,0:T(8,128)S(1)}, u32[]{:S(2)}, u32[]{:S(2)}) collective-permute-start(f32[72,576]{1,0:T(8,128)S(1)} %get-tuple-element.155), channel_id=1, source_target_pairs={{0,1},{1,0},{2,3},{3,2},{4,5},{5,4},{6,7},{7,6},{8,9},{9,8},{10,11... | collective-permute-start | bytes 497672 | tf_op jit(solution)/shard_map/ppermute | solution.py:95
  (186 other events, 1135.4 us)
